TPU v7x, 32 devices: a whole 2x2x4 slice. The times are simulated.
32 devices in a mesh: row: 8 (over z, core), col: 4 (over y, x).
Axes of the slice: x: 2, y: 2, z: 4, core: 2. Of those that a mesh axis runs over, the one named last changes fastest.
Arguments:
- tokens: bfloat16 [4, 16, 4, 73728], P(None, 'row', 'col'), may hold values from -6 to 6
- conditioning: float32 [4, 1152], P(None, 'row'), may hold values from -6 to 6
- ada_weight: bfloat16 [2, 8, 4, 248832], P(None, 'row', 'col'), may hold values from -0.1875 to 0.1875
- ada_bias: float32 [2, 6, 1152], P(None, None, 'col'), may hold values from -3 to 3
- qkv_weight: bfloat16 [2, 8, 4, 124416], P(None, 'row', 'col'), may hold values from -1 to 1
- attn_bias: float32 [2, 2, 1152], P(None, None, 'col'), may hold values from -3 to 3
- mixing_weight: bfloat16 [2, 4, 8, 41472], P(None, 'col', 'row'), may hold values from -0.5 to 0.5
- mixing_bias: float32 [2, 1152], P(None, 'col'), may hold values from -3 to 3
- hidden_weight: bfloat16 [2, 8, 4, 165888], P(None, 'row', 'col'), may hold values from -1 to 1
- hidden_bias: float32 [2, 4608], P(None, 'col'), may hold values from -3 to 3
- output_weight: bfloat16 [2, 4, 8, 165888], P(None, 'col', 'row'), may hold values from -0.09375 to 0.09375
- output_bias: float32 [2, 1152], P(None, 'col'), may hold values from -3 to 3
- cotangent: bfloat16 [4, 16, 4, 73728], P(None, None, 'col', 'row'), may hold values from -6 to 6
Outputs:
- result: bfloat16 [4, 16, 4, 73728], P(None, None, 'col', 'row')
- tokens_gradient: float32 [4, 16, 4, 73728], P(None, 'row', 'col')
- conditioning_gradient: float32 [4, 1152], P(None, 'row')
- ada_weight_grad: float32 [2, 8, 4, 248832], P(None, 'row', 'col')
- ada_bias_grad: float32 [2, 6, 1152], P(None, None, 'col')
- qkv_weight_grad: float32 [2, 8, 4, 124416], P(None, 'row', 'col')
- attn_bias_grad: float32 [2, 2, 1152], P(None, None, 'col')
- mixing_weight_grad: float32 [2, 4, 8, 41472], P(None, 'col', 'row')
- mixing_bias_grad: float32 [2, 1152], P(None, 'col')
- hidden_weight_grad: float32 [2, 8, 4, 165888], P(None, 'row', 'col')
- hidden_bias_grad: float32 [2, 4608], P(None, 'col')
- output_weight_grad: float32 [2, 4, 8, 165888], P(None, 'col', 'row')
- output_bias_grad: float32 [2, 1152], P(None, 'col')
All inputs are finite; a program needn't handle non-finite values.
Results may differ from a plain program's by a relative error of at most 0.035.
Values may be sent and summed in bfloat16 or wider, within the bound.
No kernel may reach another device: no remote copies, remote signals or barrier semaphores. Data moves between devices by JAX's collectives and lax.ppermute only.
A program may use at most 448 MiB of HBM per device.

v0:
```python
import jax
import jax.numpy as jnp
from jax import lax
from jax.sharding import PartitionSpec as P

HEAD_DIM = 72


epsilon = 1e-06
highest = lax.Precision.HIGHEST
spatial_forms = ("caqhe,cakhe->cahqk", "cahqk,cakhe->caqhe", "cahqk,caqhe->cakhe")
temporal_forms = ("cqbhe,ckbhe->cbhqk", "cbhqk,ckbhe->cqbhe", "cbhqk,cqbhe->ckbhe")


def matmul(pattern, left, right):
    return jnp.einsum(pattern, left, right, preferred_element_type=jnp.float32)


def split_heads(values):
    return values.reshape(values.shape[:-1] + (values.shape[-1] // HEAD_DIM, HEAD_DIM))


def merge_heads(values):
    return values.reshape(values.shape[:-2] + (values.shape[-2] * values.shape[-1],))


def gelu_tanh(values):
    return jax.nn.gelu(values, approximate=True)


def open_tokens(blocked, width):
    return blocked.reshape(blocked.shape[0], blocked.shape[1], blocked.shape[3] // width, width)


def close_tokens(plain_layout):
    return plain_layout.reshape(
        plain_layout.shape[0],
        plain_layout.shape[1],
        1,
        plain_layout.shape[2] * plain_layout.shape[3],
    )


def close_weight(plain_layout):
    return plain_layout.reshape(plain_layout.shape[0], 1, 1, -1)


def normalize(stream):
    feature_count = stream.shape[-1] * lax.axis_size("col")
    row_total, squares = lax.psum((jnp.sum(stream, -1), jnp.sum(stream * stream, -1)), "col")
    average = row_total / feature_count
    variance = squares / feature_count - average * average
    inverse = lax.rsqrt(variance + epsilon)
    return ((stream - average[..., None]) * inverse[..., None], inverse)


def normalize_back(grad_normed, normed, inverse):
    feature_count = grad_normed.shape[-1] * lax.axis_size("col")
    first, second = lax.psum((jnp.sum(grad_normed, -1), jnp.sum(grad_normed * normed, -1)), "col")
    return inverse[..., None] * (
        grad_normed - first[..., None] / feature_count - normed * second[..., None] / feature_count
    )


def spread(values):
    return lax.all_gather(values, "col", axis=3, tiled=True)


def collect(terms):
    return lax.psum_scatter(
        terms.astype(jnp.bfloat16), "col", scatter_dimension=3, tiled=True
    ).astype(jnp.float32)


def spread_grad(values):
    return lax.all_gather(values, "col", axis=3, tiled=True)


def collect_grad(terms):
    return lax.psum_scatter(
        terms.astype(jnp.bfloat16), "col", scatter_dimension=3, tiled=True
    ).astype(jnp.float32)


def fetch_weights(qkv_weight, mixing_weight, hidden_weight, output_weight, depth):
    return (
        lax.all_gather(qkv_weight[depth], "row", axis=0, tiled=True),
        lax.all_gather(mixing_weight[depth], "row", axis=1, tiled=True),
        lax.all_gather(hidden_weight[depth], "row", axis=0, tiled=True),
        lax.all_gather(output_weight[depth], "row", axis=1, tiled=True),
    )


def attend(queries, key_rows, value_rows, forms):
    softmax_scale = HEAD_DIM ** (-0.5)
    scores = matmul(forms[0], split_heads(queries), split_heads(key_rows)) * softmax_scale
    largest = jnp.max(scores, -1, keepdims=True)
    weights = jnp.exp(scores - largest)
    totals = jnp.sum(weights, -1, keepdims=True)
    probs = (weights / totals).astype(jnp.bfloat16)
    mixed = matmul(forms[1], probs, split_heads(value_rows))
    return (merge_heads(mixed).astype(jnp.bfloat16), largest + jnp.log(totals))


def attend_back(queries, key_rows, value_rows, grad_heads, log_totals, forms):
    softmax_scale = HEAD_DIM ** (-0.5)
    query_split = split_heads(queries)
    key_split = split_heads(key_rows)
    value_split = split_heads(value_rows)
    grad_split = split_heads(grad_heads)
    scores = matmul(forms[0], query_split, key_split) * softmax_scale
    probs = jnp.exp(scores - log_totals)
    grad_values = matmul(forms[2], probs.astype(jnp.bfloat16), grad_split)
    grad_probs = matmul(forms[0], grad_split, value_split)
    row_delta = jnp.sum(probs * grad_probs, -1, keepdims=True)
    grad_scores = (probs * (grad_probs - row_delta)).astype(jnp.bfloat16)
    grad_queries = matmul(forms[1], grad_scores, key_split) * softmax_scale
    grad_keys = matmul(forms[2], grad_scores, query_split) * softmax_scale
    return tuple(
        (
            merge_heads(part_grad).astype(jnp.bfloat16)
            for part_grad in (grad_queries, grad_keys, grad_values)
        )
    )


def residual_forward(stream, modulation, weights, biases, forms):
    qkv_full, mixing_full, hidden_full, output_full = weights
    attn_add, mixing_add, hidden_add, output_add = biases

    def piece_of(column):
        return modulation[:, column][:, None, None, :]

    normed_attn, inv_attn = normalize(stream)
    input_attn = spread((normed_attn * (1.0 + piece_of(1)) + piece_of(0)).astype(jnp.bfloat16))
    qkv_rows = matmul("cabd,dsk->cabsk", input_attn, qkv_full)
    queries = (qkv_rows[..., 0, :] + attn_add[0]).astype(jnp.bfloat16)
    key_rows = qkv_rows[..., 1, :].astype(jnp.bfloat16)
    value_rows = (qkv_rows[..., 2, :] + attn_add[1]).astype(jnp.bfloat16)
    heads_out, log_totals = attend(queries, key_rows, value_rows, forms)
    attn_out = collect(matmul("cabk,kd->cabd", heads_out, mixing_full)) + mixing_add
    stream_mid = stream + piece_of(2) * attn_out
    normed_mlp, inv_mlp = normalize(stream_mid)
    input_mlp = spread((normed_mlp * (1.0 + piece_of(4)) + piece_of(3)).astype(jnp.bfloat16))
    pre_gelu = matmul("cabd,df->cabf", input_mlp, hidden_full) + hidden_add
    activated = gelu_tanh(pre_gelu).astype(jnp.bfloat16)
    mlp_out = collect(matmul("cabf,fd->cabd", activated, output_full)) + output_add
    stream_out = stream_mid + piece_of(5) * mlp_out
    saved = (
        normed_attn,
        inv_attn,
        input_attn,
        queries,
        key_rows,
        value_rows,
        heads_out,
        log_totals,
        attn_out,
        normed_mlp,
        inv_mlp,
        input_mlp,
        pre_gelu,
        activated,
        mlp_out,
    )
    return (stream_out, saved)


def residual_backward(grad_stream, saved, modulation, weights, forms):
    (
        normed_attn,
        inv_attn,
        input_attn,
        queries,
        key_rows,
        value_rows,
        heads_out,
        log_totals,
        attn_out,
        normed_mlp,
        inv_mlp,
        input_mlp,
        pre_gelu,
        activated,
        mlp_out,
    ) = saved
    qkv_full, mixing_full, hidden_full, output_full = weights

    def piece_of(column):
        return modulation[:, column][:, None, None, :]

    grad_mlp = (grad_stream * piece_of(5)).astype(jnp.bfloat16)
    gate_mlp_grad = jnp.sum(grad_stream * mlp_out, (1, 2))
    grad_mlp_all = spread_grad(grad_mlp)
    output_weight_term = matmul("cabf,cabd->fd", activated, grad_mlp_all)
    grad_act = matmul("cabd,fd->cabf", grad_mlp_all, output_full)
    grad_pre = jax.vjp(gelu_tanh, pre_gelu)[1](grad_act)[0].astype(jnp.bfloat16)
    hidden_weight_term = matmul("cabd,cabf->df", input_mlp, grad_pre)
    grad_input_mlp = collect_grad(matmul("cabf,df->cabd", grad_pre, hidden_full))
    shift_mlp_grad = jnp.sum(grad_input_mlp, (1, 2))
    scale_mlp_grad = jnp.sum(grad_input_mlp * normed_mlp, (1, 2))
    grad_mid = grad_stream + normalize_back(
        grad_input_mlp * (1.0 + piece_of(4)), normed_mlp, inv_mlp
    )
    grad_attn = (grad_mid * piece_of(2)).astype(jnp.bfloat16)
    gate_attn_grad = jnp.sum(grad_mid * attn_out, (1, 2))
    grad_attn_all = spread_grad(grad_attn)
    mixing_weight_term = matmul("cabk,cabd->kd", heads_out, grad_attn_all)
    grad_heads = matmul("cabd,kd->cabk", grad_attn_all, mixing_full).astype(jnp.bfloat16)
    grad_queries, grad_keys, grad_values = attend_back(
        queries, key_rows, value_rows, grad_heads, log_totals, forms
    )
    grad_qkv = jnp.stack((grad_queries, grad_keys, grad_values), 3)
    qkv_weight_term = matmul("cabd,cabsk->dsk", input_attn, grad_qkv)
    grad_input_attn = collect_grad(matmul("cabsk,dsk->cabd", grad_qkv, qkv_full))
    shift_attn_grad = jnp.sum(grad_input_attn, (1, 2))
    scale_attn_grad = jnp.sum(grad_input_attn * normed_attn, (1, 2))
    grad_input = grad_mid + normalize_back(
        grad_input_attn * (1.0 + piece_of(1)), normed_attn, inv_attn
    )
    weight_terms = (
        lax.psum_scatter(
            qkv_weight_term.astype(jnp.bfloat16), "row", scatter_dimension=0, tiled=True
        ).astype(jnp.float32),
        lax.psum_scatter(
            mixing_weight_term.astype(jnp.bfloat16), "row", scatter_dimension=1, tiled=True
        ).astype(jnp.float32),
        lax.psum_scatter(
            hidden_weight_term.astype(jnp.bfloat16), "row", scatter_dimension=0, tiled=True
        ).astype(jnp.float32),
        lax.psum_scatter(
            output_weight_term.astype(jnp.bfloat16), "row", scatter_dimension=1, tiled=True
        ).astype(jnp.float32),
    )
    modulation_grad = jnp.stack(
        (
            shift_attn_grad,
            scale_attn_grad,
            gate_attn_grad,
            shift_mlp_grad,
            scale_mlp_grad,
            gate_mlp_grad,
        ),
        1,
    )
    attn_bias_term = jnp.stack(
        (
            jnp.sum(grad_queries.astype(jnp.float32), (0, 1, 2)),
            jnp.sum(grad_values.astype(jnp.float32), (0, 1, 2)),
        )
    )
    bias_terms = (
        attn_bias_term,
        jnp.sum(grad_attn.astype(jnp.float32), (0, 1, 2)),
        jnp.sum(grad_pre.astype(jnp.float32), (0, 1, 2)),
        jnp.sum(grad_mlp.astype(jnp.float32), (0, 1, 2)),
    )
    return (grad_input, weight_terms, modulation_grad, bias_terms)


def local(
    tokens,
    conditioning,
    ada_weight,
    ada_bias,
    qkv_weight,
    attn_bias,
    mixing_weight,
    mixing_bias,
    hidden_weight,
    hidden_bias,
    output_weight,
    output_bias,
    cotangent,
):
    col_width = ada_bias.shape[2]
    row_width = conditioning.shape[1]
    hidden_width = hidden_bias.shape[1]
    layer_count = ada_bias.shape[0]
    ada_weight = ada_weight.reshape(layer_count, row_width, 6, col_width)
    qkv_weight = qkv_weight.reshape(layer_count, row_width, 3, col_width)
    mixing_weight = mixing_weight.reshape(layer_count, col_width, row_width)
    hidden_weight = hidden_weight.reshape(layer_count, row_width, hidden_width)
    output_weight = output_weight.reshape(layer_count, hidden_width, row_width)
    tokens = open_tokens(tokens, col_width)
    cotangent = open_tokens(cotangent, col_width)
    cond_act = jax.nn.silu(conditioning).astype(jnp.bfloat16)
    modulation = lax.psum(
        (
            matmul("cr,rsk->csk", cond_act, ada_weight[0]),
            matmul("cr,rsk->csk", cond_act, ada_weight[1]),
        ),
        "row",
    )
    modulation = (modulation[0] + ada_bias[0][None], modulation[1] + ada_bias[1][None])

    def biases_of(depth):
        return (attn_bias[depth], mixing_bias[depth], hidden_bias[depth], output_bias[depth])

    stream_first = tokens.astype(jnp.float32)
    weights_first = fetch_weights(qkv_weight, mixing_weight, hidden_weight, output_weight, 0)
    output_first, saved_first = residual_forward(
        stream_first, modulation[0], weights_first, biases_of(0), spatial_forms
    )
    moved = lax.all_to_all(
        output_first.astype(jnp.bfloat16), "row", split_axis=2, concat_axis=1, tiled=True
    )
    stream_second = moved.astype(jnp.float32)
    weights_second = fetch_weights(qkv_weight, mixing_weight, hidden_weight, output_weight, 1)
    output_second, saved_second = residual_forward(
        stream_second, modulation[1], weights_second, biases_of(1), temporal_forms
    )
    result = output_second.astype(jnp.bfloat16)
    weights_second = fetch_weights(qkv_weight, mixing_weight, hidden_weight, output_weight, 1)
    saved_second = residual_forward(
        stream_second, modulation[1], weights_second, biases_of(1), temporal_forms
    )[1]
    grad_second, terms_second, modgrad_second, biasgrad_second = residual_backward(
        cotangent.astype(jnp.float32), saved_second, modulation[1], weights_second, temporal_forms
    )
    returned = lax.all_to_all(
        grad_second.astype(jnp.bfloat16), "row", split_axis=1, concat_axis=2, tiled=True
    )
    weights_first = fetch_weights(qkv_weight, mixing_weight, hidden_weight, output_weight, 0)
    saved_first = residual_forward(
        stream_first, modulation[0], weights_first, biases_of(0), spatial_forms
    )[1]
    grad_first, terms_first, modgrad_first, biasgrad_first = residual_backward(
        returned.astype(jnp.float32), saved_first, modulation[0], weights_first, spatial_forms
    )
    summed = (
        lax.psum(jnp.stack((modgrad_first, modgrad_second)).astype(jnp.bfloat16), "row").astype(
            jnp.float32
        ),
        lax.psum(
            jnp.stack((biasgrad_first[0], biasgrad_second[0])).astype(jnp.bfloat16), "row"
        ).astype(jnp.float32),
        lax.psum(
            jnp.stack((biasgrad_first[1], biasgrad_second[1])).astype(jnp.bfloat16), "row"
        ).astype(jnp.float32),
        lax.psum(
            jnp.stack((biasgrad_first[2], biasgrad_second[2])).astype(jnp.bfloat16), "row"
        ).astype(jnp.float32),
        lax.psum(
            jnp.stack((biasgrad_first[3], biasgrad_second[3])).astype(jnp.bfloat16), "row"
        ).astype(jnp.float32),
    )
    modulation_grad = summed[0]
    ada_bias_grad = jnp.sum(modulation_grad, 1)
    ada_weight_grad = jnp.einsum(
        "cr,lcsk->lrsk", cond_act.astype(jnp.float32), modulation_grad, precision=highest
    )
    cond_part = jnp.einsum(
        "lcsk,lrsk->cr", modulation_grad, ada_weight.astype(jnp.float32), precision=highest
    )
    cond_part = lax.psum(cond_part, "col")
    conditioning_gradient = jax.vjp(jax.nn.silu, conditioning)[1](cond_part)[0]
    qkv_weight_grad = jnp.stack((terms_first[0], terms_second[0]))
    mixing_weight_grad = jnp.stack((terms_first[1], terms_second[1]))
    hidden_weight_grad = jnp.stack((terms_first[2], terms_second[2]))
    output_weight_grad = jnp.stack((terms_first[3], terms_second[3]))
    return (
        close_tokens(result),
        close_tokens(grad_first),
        conditioning_gradient,
        close_weight(ada_weight_grad),
        ada_bias_grad,
        close_weight(qkv_weight_grad),
        summed[1],
        close_weight(mixing_weight_grad),
        summed[2],
        close_weight(hidden_weight_grad),
        summed[3],
        close_weight(output_weight_grad),
        summed[4],
    )


def solution(mesh):
    placed = (
        P(None, "row", "col", None),
        P(None, "row"),
        P(None, "row", "col", None),
        P(None, None, "col"),
        P(None, "row", "col", None),
        P(None, None, "col"),
        P(None, "col", "row", None),
        P(None, "col"),
        P(None, "row", "col", None),
        P(None, "col"),
        P(None, "col", "row", None),
        P(None, "col"),
        P(None, None, "col", "row"),
    )
    return jax.shard_map(
        local,
        mesh=mesh,
        in_specs=placed,
        out_specs=(
            P(None, None, "col", "row"),
            P(None, "row", "col", None),
            P(None, "row"),
            P(None, "row", "col", None),
            P(None, None, "col"),
            P(None, "row", "col", None),
            P(None, None, "col"),
            P(None, "col", "row", None),
            P(None, "col"),
            P(None, "row", "col", None),
            P(None, "col"),
            P(None, "col", "row", None),
            P(None, "col"),
        ),
        check_vma=False,
    )
```

profile of v0, /device:TPU:0, one launch (start us, length us, event | category | flops | bytes accessed | tf_op | source)
XLA Modules:
  0.0 2717.5 jit_solution(8599094409471579450)
XLA Ops:
  13.6 10.5 slice_reduce_fusion
  37.9 17.6 all-reduce.8
  57.1 26.8 all-reduce
  89.1 15.9 all_gather.62
  105.0 34.8 %all-gather.15.cloned.1.call-done = bf16[4,2,256,1152]{2,3,1,0:T(8,128)(2,1)} async-done(((bf16[4,2,256,288]{2,3,1,0:T(8,128)(2,1)}), bf16[4,2,256,1152]{2,3,1,0:T(8,128)(2,1)}) %all-gather.15.cloned.1.call-update) | async-done | bytes 4718608 | tf_op jit(solution)/shard_map/all_gather | solution.py:66
  171.4 46.6 %reduce-scatter.25.cloned.1.call-done = bf16[4,2,256,288]{2,3,1,0:T(8,128)(2,1)} async-done(((bf16[4,2,256,1152]{2,3,1,0:T(8,128)(2,1)}), bf16[4,2,256,288]{2,3,1,0:T(8,128)(2,1)}) %reduce-scatter.25.cloned.1.call-update) | async-done | bytes 1179664 | tf_op jit(solution)/shard_map/reduce_scatter | solution.py:70
  221.4 15.2 all-reduce.7
  254.3 58.3 %all-gather.19.cloned.1.call-done = bf16[4,2,256,1152]{2,3,1,0:T(8,128)(2,1)} async-done(((bf16[4,2,256,288]{2,3,1,0:T(8,128)(2,1)}), bf16[4,2,256,1152]{2,3,1,0:T(8,128)(2,1)}) %all-gather.19.cloned.1.call-update) | async-done | bytes 4718608 | tf_op jit(solution)/shard_map/all_gather | solution.py:66
  312.6 14.8 multiply_convert_fusion.1
  327.4 21.5 all-gather.23.cloned.1.call-done
  348.9 10.7 convolution_convert_fusion.5
  362.5 53.3 %reduce-scatter.27.cloned.1.call-done = bf16[4,2,256,288]{2,3,1,0:T(8,128)(2,1)} async-done(((bf16[4,2,256,1152]{2,3,1,0:T(8,128)(2,1)}), bf16[4,2,256,288]{2,3,1,0:T(8,128)(2,1)}) %reduce-scatter.27.cloned.1.call-update) | async-done | bytes 1179664 | tf_op jit(solution)/shard_map/reduce_scatter | solution.py:70
  425.9 58.5 %all-to-all-done = bf16[4,2,256,288]{3,1,0,2:T(2,128)(2,1)S(1)} async-done(((bf16[4,2,256,288]{3,1,0,2:T(2,128)(2,1)}), bf16[4,2,256,288]{3,1,0,2:T(2,128)(2,1)S(1)}, u32[]{:S(2)}, u32[]{:S(2)}) %all-to-all-start) | async-done | bytes 1179680 | tf_op jit(solution)/shard_map/all_to_all | solution.py:305
  485.8 16.0 all-reduce.6
  511.9 17.1 all_gather.68
  529.0 155.5 %all-gather.25.cloned.1.call-done = bf16[4,16,32,1152]{2,1,0,3:T(8,128)(2,1)} async-done(((bf16[4,16,32,288]{2,1,0,3:T(8,128)(2,1)}), bf16[4,16,32,1152]{2,1,0,3:T(8,128)(2,1)}) %all-gather.25.cloned.1.call-update) | async-done | bytes 4718608 | tf_op jit(solution)/shard_map/all_gather | solution.py:66
  684.5 13.8 fusion
  747.0 25.8 copy.402
  772.8 25.2 reshape.382
  800.3 55.0 %reduce-scatter.49.cloned.1.call-done = bf16[288,2048]{1,0:T(8,128)(2,1)} async-done(((bf16[1152,2048]{1,0:T(8,128)(2,1)}), bf16[288,2048]{1,0:T(8,128)(2,1)}) %reduce-scatter.49.cloned.1.call-update) | async-done | bytes 1179664
  872.1 15.9 all-reduce.5
  898.6 173.2 %all-gather.29.cloned.1.call-done = bf16[4,16,32,1152]{2,1,0,3:T(8,128)(2,1)} async-done(((bf16[4,16,32,288]{2,1,0,3:T(8,128)(2,1)}), bf16[4,16,32,1152]{2,1,0,3:T(8,128)(2,1)}) %all-gather.29.cloned.1.call-update) | async-done | bytes 4718608 | tf_op jit(solution)/shard_map/all_gather | solution.py:66
  1071.9 26.6 multiply_convert_fusion
  1098.4 9.8 all-gather.33.cloned.1.call-done
  1108.3 11.3 convolution_convert_fusion.3
  1119.6 25.7 copy.404
  1145.3 25.2 reshape.384
  1174.0 52.8 %reduce-scatter.51.cloned.1.call-done = bf16[288,2048]{1,0:T(8,128)(2,1)} async-done(((bf16[1152,2048]{1,0:T(8,128)(2,1)}), bf16[288,2048]{1,0:T(8,128)(2,1)}) %reduce-scatter.51.cloned.1.call-update) | async-done | bytes 1179664
  1250.3 176.0 %all-gather.35.cloned.1.call-done = bf16[4,16,32,1152]{2,1,0,3:T(8,128)(2,1)} async-done(((bf16[4,16,32,288]{2,1,0,3:T(8,128)(2,1)}), bf16[4,16,32,1152]{2,1,0,3:T(8,128)(2,1)}) %all-gather.35.cloned.1.call-update) | async-done | bytes 4718608 | tf_op jit(solution)/shard_map/all_gather | solution.py:76
  1426.3 29.0 %fusion.209 = (bf16[1152]{0:T(1024)(128)(2,1)}, bf16[4,16,32,1152]{3,2,1,0:T(8,128)(2,1)}) fusion(f32[4,16,32,1152]{3,2,1,0:T(8,128)} %get-tuple-element.193, f32[1152]{0:T(1024)S(1)} %copy-done.105, bf16[1152,1152]{0,1:T(8,128)(2,1)S(1)} %copy-done.123, bf16[4,16,32,1152]{2,1,0,3:T(8,128)(2,1)} %all-gather.35.cloned.1.call-done), kind=kOutput, calls=%fused_computation.334 | convolution fusion | flops 5487721472 | bytes 21535488 | tf_op jit(solution)/shard_map/cabd,fd->cabf/dot_general | solution.py:16
  1455.3 10.6 convolution_convert_fusion.2
  1465.9 25.8 copy.406
  1491.7 25.2 reshape.386
  1517.0 57.2 %reduce-scatter.53.cloned.1.call-done = bf16[288,2048]{1,0:T(8,128)(2,1)} async-done(((bf16[1152,2048]{1,0:T(8,128)(2,1)}), bf16[288,2048]{1,0:T(8,128)(2,1)}) %reduce-scatter.53.cloned.1.call-update) | async-done | bytes 1179664
  1592.3 16.7 all-reduce.4
  1622.7 174.9 %all-gather.37.cloned.1.call-done = bf16[4,16,32,1152]{2,1,0,3:T(8,128)(2,1)} async-done(((bf16[4,16,32,288]{2,1,0,3:T(8,128)(2,1)}), bf16[4,16,32,1152]{2,1,0,3:T(8,128)(2,1)}) %all-gather.37.cloned.1.call-update) | async-done | bytes 4718608 | tf_op jit(solution)/shard_map/all_gather | solution.py:76
  1797.5 16.1 fusion.148
  1817.9 8.2 multiply_reduce_fusion.2
  1859.1 10.2 bitcast_convert_fusion.1
  1869.3 25.8 copy.408
  1895.1 25.6 reshape.388
  1920.7 57.2 %reduce-scatter.55.cloned.1.call-done = bf16[288,2048]{1,0:T(8,128)(2,1)} async-done(((bf16[1152,2048]{1,0:T(8,128)(2,1)}), bf16[288,2048]{1,0:T(8,128)(2,1)}) %reduce-scatter.55.cloned.1.call-update) | async-done | bytes 1179664
  1994.7 16.1 all-reduce.3
  2015.4 42.3 %all_to_all.8 = bf16[4,16,32,288]{3,2,0,1:T(8,128)(2,1)S(1)} all-to-all(bf16[4,16,32,288]{3,2,0,1:T(8,128)(2,1)S(1)} %copy.332), channel_id=1, replica_groups=mesh['row'=8,'col'=4] {'row'}, dimensions={1} | all-to-all | bytes 2359296 | tf_op jit(solution)/shard_map/all_to_all | solution.py:321
  2066.0 31.6 %fusion.38 = bf16[1152,1152]{0,1:T(8,128)(2,1)} fusion(bf16[4,16,32,1152]{2,1,0,3:T(8,128)(2,1)} %all-gather.35.cloned.1.call-done, bf16[4,16,32,1152]{3,2,1,0:T(8,128)(2,1)} %get-tuple-element.192), kind=kOutput, calls=%fused_computation.47 | convolution fusion | flops 5437145088 | bytes 12091392 | tf_op jit(solution)/shard_map/cabf,cabd->fd/dot_general | solution.py:16
  2097.7 31.4 %fusion.41 = bf16[1152,1152]{1,0:T(8,128)(2,1)} fusion(bf16[4,16,32,1152]{2,1,0,3:T(8,128)(2,1)} %all-gather.29.cloned.1.call-done, bf16[4,16,32,1152]{3,2,1,0:T(8,128)(2,1)} %get-tuple-element.207), kind=kOutput, calls=%fused_computation.48 | convolution fusion | flops 5437145088 | bytes 12091392 | tf_op jit(solution)/shard_map/cabd,cabf->df/dot_general | solution.py:16
  2129.2 23.0 copy.348
  2152.2 24.5 fusion.107
  2176.9 11.3 bitcast_convert_fusion.3
  2188.3 10.6 fusion.37
  2199.2 17.2 fusion.210
  2226.6 10.6 fusion.36
  2260.2 11.9 reduce-scatter.35.cloned.1.call-done
  2282.9 28.3 %reduce-scatter.45.cloned.1.call-done = bf16[1152,144]{0,1:T(8,128)(2,1)} async-done(((bf16[1152,1152]{0,1:T(8,128)(2,1)}), bf16[1152,144]{0,1:T(8,128)(2,1)}) %reduce-scatter.45.cloned.1.call-update) | async-done | bytes 331792 | tf_op jit(solution)/shard_map/reduce_scatter | solution.py:231
  2314.4 56.2 %reduce-scatter.29.cloned.1.call-done = bf16[4,2,256,288]{2,3,1,0:T(8,128)(2,1)} async-done(((bf16[4,2,256,1152]{2,3,1,0:T(8,128)(2,1)}), bf16[4,2,256,288]{2,3,1,0:T(8,128)(2,1)}) %reduce-scatter.29.cloned.1.call-update) | async-done | bytes 1179664 | tf_op jit(solution)/shard_map/reduce_scatter | solution.py:80
  2373.7 16.3 all-reduce.2
  2399.7 11.0 reduce-scatter.41.cloned.1.call-done
  2412.7 56.6 %all-gather.41.cloned.1.call-done = bf16[4,2,256,1152]{2,3,1,0:T(8,128)(2,1)} async-done(((bf16[4,2,256,288]{2,3,1,0:T(8,128)(2,1)}), bf16[4,2,256,1152]{2,3,1,0:T(8,128)(2,1)}) %all-gather.41.cloned.1.call-update) | async-done | bytes 4718608 | tf_op jit(solution)/shard_map/all_gather | solution.py:76
  2493.3 9.5 bitcast_convert_fusion.2
  2509.6 9.0 bitcast_convert_fusion
  2527.7 35.9 %reduce-scatter.33.cloned.1.call-done = bf16[144,3,288]{2,0,1:T(8,128)(2,1)} async-done(((bf16[1152,3,288]{2,0,1:T(8,128)(2,1)}), bf16[144,3,288]{2,0,1:T(8,128)(2,1)}) %reduce-scatter.33.cloned.1.call-update) | async-done | bytes 248848 | tf_op jit(solution)/shard_map/reduce_scatter | solution.py:222
  2569.7 52.8 %reduce-scatter.31.cloned.1.call-done = bf16[4,2,256,288]{2,3,1,0:T(8,128)(2,1)} async-done(((bf16[4,2,256,1152]{2,3,1,0:T(8,128)(2,1)}), bf16[4,2,256,288]{2,3,1,0:T(8,128)(2,1)}) %reduce-scatter.31.cloned.1.call-update) | async-done | bytes 1179664 | tf_op jit(solution)/shard_map/reduce_scatter | solution.py:80
  2631.4 30.2 %all-reduce.9 = (bf16[2,4,6,288]{3,1,2,0:T(4,128)(2,1)}, bf16[2,2,288]{2,1,0:T(2,128)(2,1)}, bf16[2,288]{1,0:T(2,128)(2,1)}, bf16[2,1152]{1,0:T(2,128)(2,1)}, bf16[2,288]{1,0:T(2,128)(2,1)}) all-reduce(bf16[2,4,6,288]{3,1,2,0:T(4,128)(2,1)} %pad_maximum_fusion.4, ...), channel_id=1, replica_groups=mesh['row'=8,'col'=4] {'row'}, use_global_device_ids=true, to_apply=%region_60.61 | all-reduce | flops 18432 | bytes 73728 | tf_op jit(solution)/shard_map/psum | solution.py:332
  2670.2 16.9 all-reduce.1
  (529 shorter events, 456.0 us)
Async XLA Ops:
  7.2 97.8 %all-gather.17.cloned.1.call-start = ((), (), s32[]{:S(2)}) async-start(), calls=%async_computation.19 | async-start | bytes 2985984 | tf_op jit(solution)/shard_map/all_gather | solution.py:87
  13.3 126.4 %all-gather.15.cloned.1.call-start = ((), (), s32[]{:S(2)}) async-start(), calls=%async_computation.18 | async-start | bytes 5898240 | tf_op jit(solution)/shard_map/all_gather | solution.py:66
  34.5 183.5 %copy-start.5 = (f32[4,2,256,288]{2,3,1,0:T(8,128)}, f32[4,2,256,288]{2,3,1,0:T(8,128)S(1)}, u32[]{:S(2)}) copy-start(f32[4,2,256,288]{2,3,1,0:T(8,128)S(1)} %copy.297) | copy-start | bytes 7077892
  55.5 31.7 %copy-start.49 = (bf16[2,1,1,41472]{3,0,2,1:T(2,128)(2,1)S(1)}, bf16[2,1,1,41472]{3,0,2,1:T(2,128)(2,1)}, u32[]{:S(2)}) copy-start(bf16[2,1,1,41472]{3,0,2,1:T(2,128)(2,1)} %param.19) | copy-start | bytes 497668
  84.7 133.4 %copy-start.79 = (f32[4,288]{1,0:T(4,128)}, f32[4,288]{1,0:T(4,128)S(1)}, u32[]{:S(2)}) copy-start(f32[4,288]{1,0:T(4,128)S(1)} %get-tuple-element.175) | copy-start | bytes 13828
  84.7 151.9 %copy-start.75 = (f32[4,288]{1,0:T(4,128)}, f32[4,288]{1,0:T(4,128)S(1)}, u32[]{:S(2)}) copy-start(f32[4,288]{1,0:T(4,128)S(1)} %get-tuple-element.172) | copy-start | bytes 13828
  84.7 331.1 %copy-start.69 = (f32[4,288]{1,0:T(4,128)}, f32[4,288]{1,0:T(4,128)S(1)}, u32[]{:S(2)}) copy-start(f32[4,288]{1,0:T(4,128)S(1)} %get-tuple-element.170) | copy-start | bytes 13828
  86.2 131.9 %reduce-scatter.25.cloned.1.call-start = ((), (), s32[]{:S(2)}) async-start(), calls=%async_computation.20 | async-start | bytes 5898240 | tf_op jit(solution)/shard_map/reduce_scatter | solution.py:70
  87.1 60.8 %copy-start.81 = (f32[4,72]{1,0:T(4,128)}, f32[4,72]{1,0:T(4,128)S(1)}, u32[]{:S(2)}) copy-start(f32[4,72]{1,0:T(4,128)S(1)} %add.463) | copy-start | bytes 3460
  87.2 64.5 %copy-start.88 = (f32[4,72]{1,0:T(4,128)}, f32[4,72]{1,0:T(4,128)S(1)}, u32[]{:S(2)}) copy-start(f32[4,72]{1,0:T(4,128)S(1)} %add.460) | copy-start | bytes 3460
  105.0 50.6 %copy-start.45 = (bf16[288,1152]{0,1:T(8,128)(2,1)}, bf16[288,1152]{0,1:T(8,128)(2,1)S(1)}, u32[]{:S(2)}) copy-start(bf16[288,1152]{0,1:T(8,128)(2,1)S(1)} %all_gather.62) | copy-start | bytes 1990660
  160.9 93.4 %all-gather.21.cloned.1.call-start = ((), (), s32[]{:S(2)}) async-start(), calls=%async_computation.22 | async-start | bytes 2985984 | tf_op jit(solution)/shard_map/all_gather | solution.py:89
  170.8 141.9 %all-gather.19.cloned.1.call-start = ((), (), s32[]{:S(2)}) async-start(), calls=%async_computation.21 | async-start | bytes 5898240 | tf_op jit(solution)/shard_map/all_gather | solution.py:66
  171.4 68.9 %copy-start.86 = (f32[288]{0:T(512)}, f32[288]{0:T(512)S(1)}, u32[]{:S(2)}) copy-start(f32[288]{0:T(512)S(1)} %get-tuple-element.117) | copy-start | bytes 3460
  240.4 108.5 %all-gather.23.cloned.1.call-start = ((), (), s32[]{:S(2)}) async-start(), calls=%async_computation.23 | async-start | bytes 2985984 | tf_op jit(solution)/shard_map/all_gather | solution.py:90
  249.9 165.9 %reduce-scatter.27.cloned.1.call-start = ((), (), s32[]{:S(2)}) async-start(), calls=%async_computation.24 | async-start | bytes 5898240 | tf_op jit(solution)/shard_map/reduce_scatter | solution.py:70
  250.7 76.6 %copy-start.103 = (f32[1152]{0:T(1024)}, f32[1152]{0:T(1024)S(1)}, u32[]{:S(2)}) copy-start(f32[1152]{0:T(1024)S(1)} %get-tuple-element.109) | copy-start | bytes 13828
  359.6 56.2 %copy-start.7 = (f32[4,2,256,288]{2,3,1,0:T(8,128)S(1)}, f32[4,2,256,288]{2,3,1,0:T(8,128)}, u32[]{:S(2)}) copy-start(f32[4,2,256,288]{2,3,1,0:T(8,128)} %get-tuple-element.149) | copy-start | bytes 7077892
  359.6 169.4 %all-gather.27.cloned.1.call-start = ((), (), s32[]{:S(2)}) async-start(), calls=%async_computation.26 | async-start | bytes 2985984 | tf_op jit(solution)/shard_map/all_gather | solution.py:87
  362.5 58.1 %copy-start.84 = (f32[288]{0:T(512)}, f32[288]{0:T(512)S(1)}, u32[]{:S(2)}) copy-start(f32[288]{0:T(512)S(1)} %get-tuple-element.115) | copy-start | bytes 3460
  420.6 63.8 %all-to-all-start = ((bf16[4,2,256,288]{3,1,0,2:T(2,128)(2,1)}), bf16[4,2,256,288]{3,1,0,2:T(2,128)(2,1)S(1)}, u32[]{:S(2)}, u32[]{:S(2)}) async-start(bf16[4,2,256,288]{3,1,0,2:T(2,128)(2,1)} %copy.299), calls=%async_computation.2 | async-start | bytes 3145728 | tf_op jit(solution)/shard_map/all_to_all | solution.py:305
  425.2 259.3 %all-gather.25.cloned.1.call-start = ((), (), s32[]{:S(2)}) async-start(), calls=%async_computation.25 | async-start | bytes 23592960 | tf_op jit(solution)/shard_map/all_gather | solution.py:66
  425.9 76.0 %copy-start.76 = (f32[4,288]{1,0:T(4,128)}, f32[4,288]{1,0:T(4,128)S(1)}, u32[]{:S(2)}) copy-start(f32[4,288]{1,0:T(4,128)S(1)} %get-tuple-element.168) | copy-start | bytes 13828
  425.9 442.6 %copy-start.80 = (f32[4,288]{1,0:T(4,128)}, f32[4,288]{1,0:T(4,128)S(1)}, u32[]{:S(2)}) copy-start(f32[4,288]{1,0:T(4,128)S(1)} %get-tuple-element.169) | copy-start | bytes 13828
  425.9 1161.5 %copy-start.72 = (f32[4,288]{1,0:T(4,128)}, f32[4,288]{1,0:T(4,128)S(1)}, u32[]{:S(2)}) copy-start(f32[4,288]{1,0:T(4,128)S(1)} %get-tuple-element.164) | copy-start | bytes 13828
  485.8 382.7 %copy-start.3 = (f32[4,8,2,32,288]{4,3,2,1,0:T(8,128)}, f32[4,8,2,32,288]{4,3,2,1,0:T(8,128)S(1)}, u32[]{:S(2)}) copy-start(f32[4,8,2,32,288]{4,3,2,1,0:T(8,128)S(1)} %copy.301) | copy-start | bytes 7077892
  510.7 344.7 %reduce-scatter.49.cloned.1.call-start = ((), (), s32[]{:S(2)}) async-start(), calls=%async_computation.44 | async-start | bytes 5898240
  511.4 217.0 %copy-start.101 = (f32[4,72]{1,0:T(4,128)}, f32[4,72]{1,0:T(4,128)S(1)}, u32[]{:S(2)}) copy-start(f32[4,72]{1,0:T(4,128)S(1)} %add.494) | copy-start | bytes 3460
  511.5 208.1 %copy-start.90 = (f32[4,72]{1,0:T(4,128)}, f32[4,72]{1,0:T(4,128)S(1)}, u32[]{:S(2)}) copy-start(f32[4,72]{1,0:T(4,128)S(1)} %add.497) | copy-start | bytes 3460
  798.0 100.6 %all-gather.31.cloned.1.call-start = ((), (), s32[]{:S(2)}) async-start(), calls=%async_computation.28 | async-start | bytes 2985984 | tf_op jit(solution)/shard_map/all_gather | solution.py:89
  800.2 271.6 %all-gather.29.cloned.1.call-start = ((), (), s32[]{:S(2)}) async-start(), calls=%async_computation.27 | async-start | bytes 23592960 | tf_op jit(solution)/shard_map/all_gather | solution.py:66
  895.8 176.1 %copy-start.105 = (f32[1152]{0:T(1024)S(1)}, f32[1152]{0:T(1024)}, u32[]{:S(2)}) copy-start(f32[1152]{0:T(1024)} %get-tuple-element.108) | copy-start | bytes 13828
  895.8 212.4 %all-gather.33.cloned.1.call-start = ((), (), s32[]{:S(2)}) async-start(), calls=%async_computation.29 | async-start | bytes 2985984 | tf_op jit(solution)/shard_map/all_gather | solution.py:90
  898.5 328.3 %reduce-scatter.51.cloned.1.call-start = ((), (), s32[]{:S(2)}) async-start(), calls=%async_computation.45 | async-start | bytes 5898240
  1170.6 255.7 %all-gather.35.cloned.1.call-start = ((), (), s32[]{:S(2)}) async-start(), calls=%async_computation.30 | async-start | bytes 23592960 | tf_op jit(solution)/shard_map/all_gather | solution.py:76
  1174.0 65.9 %copy-start.13 = (f32[4,16,32,288]{3,2,1,0:T(8,128)}, f32[4,16,32,288]{3,2,1,0:T(8,128)S(1)}, u32[]{:S(2)}) copy-start(f32[4,16,32,288]{3,2,1,0:T(8,128)S(1)} %reshape.350) | copy-start | bytes 7077892
  1250.2 176.1 %copy-start.123 = (bf16[1152,1152]{0,1:T(8,128)(2,1)S(1)}, bf16[1152,1152]{0,1:T(8,128)(2,1)}, u32[]{:S(2)}) copy-start(bf16[1152,1152]{0,1:T(8,128)(2,1)} %all-gather.33.cloned.1.call-done) | copy-start | bytes 7962628
  1250.2 324.0 %reduce-scatter.53.cloned.1.call-start = ((), (), s32[]{:S(2)}) async-start(), calls=%async_computation.46 | async-start | bytes 5898240
  1516.9 280.6 %all-gather.37.cloned.1.call-start = ((), (), s32[]{:S(2)}) async-start(), calls=%async_computation.31 | async-start | bytes 23592960 | tf_op jit(solution)/shard_map/all_gather | solution.py:76
  1621.7 175.9 %copy-start.47 = (bf16[288,1152]{0,1:T(8,128)(2,1)S(1)}, bf16[288,1152]{0,1:T(8,128)(2,1)}, u32[]{:S(2)}) copy-start(bf16[288,1152]{0,1:T(8,128)(2,1)} %all_gather.68) | copy-start | bytes 1990660
  1621.7 356.2 %reduce-scatter.55.cloned.1.call-start = ((), (), s32[]{:S(2)}) async-start(), calls=%async_computation.47 | async-start | bytes 5898240
  1920.7 267.6 %all-gather.39.cloned.1.call-start = ((), (), s32[]{:S(2)}) async-start(), calls=%async_computation.32 | async-start | bytes 5898240 | tf_op jit(solution)/shard_map/all_gather | solution.py:76
  2063.6 34.0 %copy-start.14 = (f32[4,2,256,288]{2,3,1,0:T(8,128)}, f32[4,2,256,288]{2,3,1,0:T(8,128)S(1)}, u32[]{:S(2)}) copy-start(f32[4,2,256,288]{2,3,1,0:T(8,128)S(1)} %copy.335) | copy-start | bytes 7077892
  2066.0 177.3 %reduce-scatter.47.cloned.1.call-start = ((), (), s32[]{:S(2)}) async-start(), calls=%async_computation.43 | async-start | bytes 2985984 | tf_op jit(solution)/shard_map/reduce_scatter | solution.py:231
  2097.6 148.7 %reduce-scatter.43.cloned.1.call-start = ((), (), s32[]{:S(2)}) async-start(), calls=%async_computation.41 | async-start | bytes 2985984 | tf_op jit(solution)/shard_map/reduce_scatter | solution.py:228
  2129.2 129.0 %reduce-scatter.39.cloned.1.call-start = ((), (), s32[]{:S(2)}) async-start(), calls=%async_computation.39 | async-start | bytes 995328 | tf_op jit(solution)/shard_map/reduce_scatter | solution.py:225
  2176.7 95.4 %reduce-scatter.35.cloned.1.call-start = ((), (), s32[]{:S(2)}) async-start(), calls=%async_computation.37 | async-start | bytes 2985984 | tf_op jit(solution)/shard_map/reduce_scatter | solution.py:222
  2188.2 123.1 %reduce-scatter.45.cloned.1.call-start = ((), (), s32[]{:S(2)}) async-start(), calls=%async_computation.42 | async-start | bytes 2985984 | tf_op jit(solution)/shard_map/reduce_scatter | solution.py:231
  2198.9 171.7 %reduce-scatter.29.cloned.1.call-start = ((), (), s32[]{:S(2)}) async-start(), calls=%async_computation.33 | async-start | bytes 5898240 | tf_op jit(solution)/shard_map/reduce_scatter | solution.py:80
  2226.6 184.1 %reduce-scatter.41.cloned.1.call-start = ((), (), s32[]{:S(2)}) async-start(), calls=%async_computation.40 | async-start | bytes 2985984 | tf_op jit(solution)/shard_map/reduce_scatter | solution.py:228
  2237.3 232.0 %all-gather.41.cloned.1.call-start = ((), (), s32[]{:S(2)}) async-start(), calls=%async_computation.34 | async-start | bytes 5898240 | tf_op jit(solution)/shard_map/all_gather | solution.py:76
  2279.5 91.1 %copy-start.8 = (f32[4,2,256,288]{2,3,1,0:T(8,128)S(1)}, f32[4,2,256,288]{2,3,1,0:T(8,128)}, u32[]{:S(2)}) copy-start(f32[4,2,256,288]{2,3,1,0:T(8,128)} %get-tuple-element.149) | copy-start | bytes 7077892
  2279.5 91.1 %copy-start.60 = (f32[4,2,256]{2,1,0:T(2,128)S(1)}, f32[4,2,256]{2,1,0:T(2,128)}, u32[]{:S(2)}) copy-start(f32[4,2,256]{2,1,0:T(2,128)} %copy-done.59) | copy-start | bytes 24580
  2279.5 91.1 %copy-start.62 = (f32[4,2,256]{2,1,0:T(2,128)S(1)}, f32[4,2,256]{2,1,0:T(2,128)}, u32[]{:S(2)}) copy-start(f32[4,2,256]{2,1,0:T(2,128)} %copy-done.61) | copy-start | bytes 24580
  2395.3 73.9 %copy-start.46 = (bf16[288,1152]{0,1:T(8,128)(2,1)S(1)}, bf16[288,1152]{0,1:T(8,128)(2,1)}, u32[]{:S(2)}) copy-start(bf16[288,1152]{0,1:T(8,128)(2,1)} %copy-done.45) | copy-start | bytes 1990660
  2395.3 129.9 %reduce-scatter.37.cloned.1.call-start = ((), (), s32[]{:S(2)}) async-start(), calls=%async_computation.38 | async-start | bytes 995328 | tf_op jit(solution)/shard_map/reduce_scatter | solution.py:225
  2412.7 60.8 %copy-start.48 = (f32[4,1,8,256]{3,2,1,0:T(8,128)S(1)}, f32[4,1,8,256]{3,2,1,0:T(8,128)}, u32[]{:S(2)}) copy-start(f32[4,1,8,256]{3,2,1,0:T(8,128)} %log_add_fusion.1) | copy-start | bytes 98308
  2493.2 70.4 %reduce-scatter.33.cloned.1.call-start = ((), (), s32[]{:S(2)}) async-start(), calls=%async_computation.36 | async-start | bytes 2985984 | tf_op jit(solution)/shard_map/reduce_scatter | solution.py:222
  2502.8 119.7 %reduce-scatter.31.cloned.1.call-start = ((), (), s32[]{:S(2)}) async-start(), calls=%async_computation.35 | async-start | bytes 5898240 | tf_op jit(solution)/shard_map/reduce_scatter | solution.py:80
  2518.7 48.5 %copy-start.35 = (bf16[1,1,1,124416]{3,2,1,0:T(2,128)(2,1)S(1)}, bf16[1,1,1,124416]{3,2,1,0:T(2,128)(2,1)}, u32[]{:S(2)}) copy-start(bf16[1,1,1,124416]{3,2,1,0:T(2,128)(2,1)} %stack.216) | copy-start | bytes 746500
  2518.7 105.4 %copy-start.6 = (f32[4,2,256,288]{2,3,1,0:T(8,128)S(1)}, f32[4,2,256,288]{2,3,1,0:T(8,128)}, u32[]{:S(2)}) copy-start(f32[4,2,256,288]{2,3,1,0:T(8,128)} %copy-done.5) | copy-start | bytes 7077892
  2518.7 105.4 %copy-start.66 = (f32[4,2,256]{2,1,0:T(2,128)S(1)}, f32[4,2,256]{2,1,0:T(2,128)}, u32[]{:S(2)}) copy-start(f32[4,2,256]{2,1,0:T(2,128)} %copy-done.65) | copy-start | bytes 24580
  2518.7 105.4 %copy-start.68 = (f32[4,2,256]{2,1,0:T(2,128)S(1)}, f32[4,2,256]{2,1,0:T(2,128)}, u32[]{:S(2)}) copy-start(f32[4,2,256]{2,1,0:T(2,128)} %copy-done.67) | copy-start | bytes 24580
  2624.1 67.6 %copy-start.22 = (bf16[4,2,256,288]{2,3,1,0:T(8,128)(2,1)S(1)}, bf16[4,2,256,288]{2,3,1,0:T(8,128)(2,1)}, u32[]{:S(2)}) copy-start(bf16[4,2,256,288]{2,3,1,0:T(8,128)(2,1)} %reduce-scatter.31.cloned.1.call-done) | copy-start | bytes 3538948
  (96 other events, 702.9 us)
Sparse Core Ops, SparseCore 0:
  13.5 36.8 all-gather.16
  86.3 53.4 all-gather.14
  161.0 57.0 reduce-scatter.24
  220.1 34.1 all-gather.20
  256.5 56.0 all-gather.18
  314.7 34.1 all-gather.22
  359.7 56.0 reduce-scatter.26
  418.0 61.7 all-gather.26
  510.8 173.7 all-gather.24
  798.2 57.0 reduce-scatter.48
  857.5 34.1 all-gather.30
  895.9 175.8 all-gather.28
  1074.1 34.1 all-gather.32
  1170.7 56.0 reduce-scatter.50
  1250.3 175.9 all-gather.34
  1517.0 57.0 reduce-scatter.52
  1621.8 175.6 all-gather.36
  1920.8 57.0 reduce-scatter.54
  2066.1 54.6 all-gather.38
  2123.0 37.7 reduce-scatter.46
  2163.1 36.8 reduce-scatter.42
  2202.9 30.7 reduce-scatter.38
  2236.1 35.8 reduce-scatter.34
  2274.3 36.8 reduce-scatter.44
  2314.5 56.0 reduce-scatter.28
  2372.9 37.7 reduce-scatter.40
  2413.1 56.1 all-gather.40
  2493.3 31.8 reduce-scatter.36
  2527.5 36.0 reduce-scatter.32
  2566.4 56.0 reduce-scatter.30
where the time goes:
time: 2730 us; the launch traced here: 2720 us
  waiting for transfers between devices  1450 us (53%)
  local copies, waits for them, and re-layouts  487 us (18%)
  matrix products  387 us (14%)
  blocking collectives  263 us (10%)
  other arithmetic  109 us (4%)
    all_gather x4, waiting for transfers between devices, spread(): return lax.all_gather(values, 'col', axis=3, tiled=True)  422 us
    all_gather x4, waiting for transfers between devices, spread_grad(): return lax.all_gather(values, 'col', axis=3, tiled=True)  408 us
    dot_general x38, matrix products, matmul(): return jnp.einsum(pattern, left, right, preferred_element_type=jnp.float32)  382 us
    unnamed x289, local copies, waits for them, and re-layouts  277 us
    unnamed x34, waiting for transfers between devices  223 us
    reduce_scatter x2, waiting for transfers between devices, collect_grad(): lax.psum_scatter(terms.astype(jnp.bfloat16), 'col', scatter_dimension=3,...  109 us
    reduce_scatter x2, waiting for transfers between devices, collect(): lax.psum_scatter(terms.astype(jnp.bfloat16), 'col', scatter_dimension=3,...  99.9 us
    psum x4, blocking collectives, normalize_back(): lax.psum((jnp.sum(grad_normed, -1), jnp.sum(grad_normed * normed, -1)), '...  65.9 us
  transfers between devices with their start and end apart: 31, of which 24 were waited for; matrix products, arithmetic and copies ran while one was open for 15% of the time, Pallas kernels for 0%

commit v1 on v0

--- a/solution.py
+++ b/solution.py
@@ -258,7 +258,7 @@
     return (grad_input, weight_terms, modulation_grad, bias_terms)
 
 
-def local(
+def tensor_parallel(
     tokens,
     conditioning,
     ada_weight,
@@ -376,6 +376,494 @@
     )
 
 
+def exchange(values, axis, mask):
+    count = lax.axis_size(axis)
+    return lax.ppermute(values, axis, [(index, index ^ mask) for index in range(count)])
+
+
+def ordered(mine, theirs, upper):
+    return jnp.where(
+        upper, jnp.concatenate((theirs, mine), 0), jnp.concatenate((mine, theirs), 0)
+    )
+
+
+def add_low(first, second):
+    return (first.astype(jnp.float32) + second.astype(jnp.float32)).astype(jnp.bfloat16)
+
+
+def gather_weight(shard, place):
+    held = shard
+    for mask in place.depth_masks:
+        held = ordered(held, exchange(held, "row", mask), (place.row & mask) != 0)
+    half = held.shape[0] // 2
+    across = exchange(held, "col", 1)
+    above = exchange(held, "col", 2)
+    opposite = jnp.concatenate(
+        (exchange(across[:half], "col", 2), exchange(above[half:], "col", 1)), 0
+    )
+    own = (held, across, above, opposite)
+    return (own, tuple(exchange(block, "row", 1) for block in own))
+
+
+def scatter_weight(own, other, place):
+    held, across, above, opposite = (
+        add_low(mine, exchange(theirs, "row", 1)) for mine, theirs in zip(own, other)
+    )
+    half = held.shape[0] // 2
+    upper = exchange(opposite[:half], "col", 2)
+    lower = exchange(opposite[half:], "col", 1)
+    across = jnp.concatenate((add_low(across[:half], upper), across[half:]), 0)
+    above = jnp.concatenate((above[:half], add_low(above[half:], lower)), 0)
+    total = held.astype(jnp.float32) + exchange(across, "col", 1).astype(jnp.float32)
+    total = total + exchange(above, "col", 2).astype(jnp.float32)
+    for mask in reversed(place.depth_masks):
+        half = total.shape[0] // 2
+        total = total.astype(jnp.bfloat16)
+        upper = (place.row & mask) != 0
+        kept = jnp.where(upper, total[half:], total[:half])
+        sent = jnp.where(upper, total[:half], total[half:])
+        total = kept.astype(jnp.float32) + exchange(sent, "row", mask).astype(jnp.float32)
+    return total
+
+
+class Place:
+    def __init__(self):
+        self.row = lax.axis_index("row")
+        self.col = lax.axis_index("col")
+        self.row_count = lax.axis_size("row")
+        self.col_count = lax.axis_size("col")
+        self.core = self.row & 1
+        self.depth_masks = []
+        mask = 2
+        while mask < self.row_count:
+            self.depth_masks.append(mask)
+            mask *= 2
+
+
+def mine_first(halves, place, axis):
+    return jnp.where(place.core == 1, jnp.flip(halves, axis), halves)
+
+
+def to_halves(features, place):
+    width = features.shape[-1]
+    lead = features.shape[:-1]
+    split_up = features.reshape(lead + (place.row_count // 2, 2, width // place.row_count))
+    halves = jnp.swapaxes(split_up, -3, -2).reshape(lead + (2, width // 2))
+    return mine_first(halves, place, len(lead))
+
+
+def from_halves(halves, place):
+    lead = halves.shape[:-2]
+    half = halves.shape[-1]
+    halves = mine_first(halves, place, len(lead))
+    split_up = halves.reshape(lead + (2, place.row_count // 2, half // (place.row_count // 2)))
+    return jnp.swapaxes(split_up, -3, -2).reshape(lead + (2 * half,))
+
+
+def relative(stacked, place):
+    return [
+        lax.dynamic_index_in_dim(stacked, place.col ^ step, 0, keepdims=False)
+        for step in range(place.col_count)
+    ]
+
+
+def absolute(blocks, place):
+    return jnp.stack(relative(jnp.stack(blocks), place))
+
+
+def trade(blocks):
+    return [
+        block if step == 0 else exchange(block, "col", step) for step, block in enumerate(blocks)
+    ]
+
+
+def placing(width, place):
+    block = width // place.col_count
+    part = width // place.row_count
+    feature = lax.broadcasted_iota(jnp.int32, (block, width // 2), 0)
+    target = lax.broadcasted_iota(jnp.int32, (block, width // 2), 1)
+
+    def one(step, half):
+        whole = feature + (place.col ^ step) * block
+        row = whole // part
+        matches = ((row & 1) == (place.core ^ half)) & (
+            (row // 2) * part + whole % part == target
+        )
+        return matches.astype(jnp.bfloat16)
+
+    return [[one(step, half) for half in range(2)] for step in range(place.col_count)]
+
+
+def enter(blocks, placement):
+    return jnp.stack(
+        [
+            sum(matmul("ti,io->to", block, pair[half]) for block, pair in zip(blocks, placement))
+            for half in range(2)
+        ]
+    )
+
+
+def leave(halves, placement):
+    return [
+        sum(matmul("to,io->ti", halves[half], pair[half]) for half in range(2)).astype(
+            jnp.bfloat16
+        )
+        for pair in placement
+    ]
+
+
+def norm(stream):
+    count = stream.shape[0] * stream.shape[2]
+    average = jnp.sum(stream, (0, 2), keepdims=True) / count
+    centred = stream - average
+    variance = jnp.sum(centred * centred, (0, 2), keepdims=True) / count
+    inverse = lax.rsqrt(variance + epsilon)
+    return (centred * inverse, inverse)
+
+
+def norm_back(grad_normed, normed, inverse):
+    count = normed.shape[0] * normed.shape[2]
+    first = jnp.sum(grad_normed, (0, 2), keepdims=True) / count
+    second = jnp.sum(grad_normed * normed, (0, 2), keepdims=True) / count
+    return inverse * (grad_normed - first - normed * second)
+
+
+def inward(halves, own, other):
+    return matmul("td,dn->tn", halves[0], own) + matmul("td,dn->tn", halves[1], other)
+
+
+def outward(blocks, weight):
+    return jnp.stack(
+        [
+            sum(matmul("tn,dn->td", block, part) for block, part in zip(blocks, half))
+            for half in weight
+        ]
+    )
+
+
+def weight_terms(halves, blocks):
+    return tuple(
+        tuple(matmul("td,tn->dn", halves[half], block).astype(jnp.bfloat16) for block in blocks)
+        for half in range(2)
+    )
+
+
+def block_forward(stream, modulation, weights, biases, group, forms):
+    qkv, mixing, hidden, output = weights
+    attn_add, mixing_add, hidden_add, output_add = biases
+
+    def piece(column):
+        return modulation[column][:, None, :]
+
+    normed_attn, inv_attn = norm(stream)
+    input_attn = (normed_attn * (1.0 + piece(1)) + piece(0)).astype(jnp.bfloat16)
+    queries, keys, values, heads, logs = ([], [], [], [], [])
+    for step in range(len(qkv[0])):
+        rows = inward(input_attn, qkv[0][step], qkv[1][step])
+        width = rows.shape[1] // 3
+        query = (rows[:, :width] + attn_add[step][0]).astype(jnp.bfloat16).reshape((1,) + group + (width,))
+        key = rows[:, width : 2 * width].astype(jnp.bfloat16).reshape((1,) + group + (width,))
+        value = (rows[:, 2 * width :] + attn_add[step][1]).astype(jnp.bfloat16)
+        value = value.reshape((1,) + group + (width,))
+        out, log_total = attend(query, key, value, forms)
+        queries.append(query)
+        keys.append(key)
+        values.append(value)
+        heads.append(out.reshape(-1, width))
+        logs.append(log_total)
+    attn_out = outward(heads, mixing) + mixing_add[:, None, :]
+    mid = stream + piece(2) * attn_out
+    normed_mlp, inv_mlp = norm(mid)
+    input_mlp = (normed_mlp * (1.0 + piece(4)) + piece(3)).astype(jnp.bfloat16)
+    pre = [
+        inward(input_mlp, own, other) + added
+        for own, other, added in zip(hidden[0], hidden[1], hidden_add)
+    ]
+    active = [gelu_tanh(values_in).astype(jnp.bfloat16) for values_in in pre]
+    mlp_out = outward(active, output) + output_add[:, None, :]
+    saved = (
+        normed_attn,
+        inv_attn,
+        input_attn,
+        queries,
+        keys,
+        values,
+        heads,
+        logs,
+        attn_out,
+        normed_mlp,
+        inv_mlp,
+        input_mlp,
+        pre,
+        active,
+        mlp_out,
+    )
+    return (mid + piece(5) * mlp_out, saved)
+
+
+def block_backward(grad, saved, modulation, weights, group, forms):
+    (
+        normed_attn,
+        inv_attn,
+        input_attn,
+        queries,
+        keys,
+        values,
+        heads,
+        logs,
+        attn_out,
+        normed_mlp,
+        inv_mlp,
+        input_mlp,
+        pre,
+        active,
+        mlp_out,
+    ) = saved
+    qkv, mixing, hidden, output = weights
+
+    def piece(column):
+        return modulation[column][:, None, :]
+
+    grad_mlp = (piece(5) * grad).astype(jnp.bfloat16)
+    gate_mlp = jnp.sum(grad * mlp_out, 1)
+    output_terms = weight_terms(grad_mlp, active)
+    grad_pre = []
+    for own, other, before in zip(output[0], output[1], pre):
+        grad_act = inward(grad_mlp, own, other)
+        grad_pre.append(jax.vjp(gelu_tanh, before)[1](grad_act)[0].astype(jnp.bfloat16))
+    hidden_terms = weight_terms(input_mlp, grad_pre)
+    grad_input = outward(grad_pre, hidden)
+    shift_mlp = jnp.sum(grad_input, 1)
+    scale_mlp = jnp.sum(grad_input * normed_mlp, 1)
+    grad_mid = grad + norm_back(grad_input * (1.0 + piece(4)), normed_mlp, inv_mlp)
+    grad_attn = (piece(2) * grad_mid).astype(jnp.bfloat16)
+    gate_attn = jnp.sum(grad_mid * attn_out, 1)
+    mixing_terms = weight_terms(grad_attn, heads)
+    grad_qkv = []
+    for step in range(len(qkv[0])):
+        grad_heads = inward(grad_attn, mixing[0][step], mixing[1][step]).astype(jnp.bfloat16)
+        width = grad_heads.shape[1]
+        parts = attend_back(
+            queries[step],
+            keys[step],
+            values[step],
+            grad_heads.reshape((1,) + group + (width,)),
+            logs[step],
+            forms,
+        )
+        grad_qkv.append(jnp.concatenate([part.reshape(-1, width) for part in parts], 1))
+    qkv_terms = weight_terms(input_attn, grad_qkv)
+    grad_input = outward(grad_qkv, qkv)
+    shift_attn = jnp.sum(grad_input, 1)
+    scale_attn = jnp.sum(grad_input * normed_attn, 1)
+    grad_in = grad_mid + norm_back(grad_input * (1.0 + piece(1)), normed_attn, inv_attn)
+    modulation_grad = jnp.stack(
+        (shift_attn, scale_attn, gate_attn, shift_mlp, scale_mlp, gate_mlp)
+    )
+
+    def total(blocks):
+        return [jnp.sum(block.astype(jnp.float32), 0) for block in blocks]
+
+    bias_grads = (
+        total(grad_qkv),
+        jnp.sum(grad_attn.astype(jnp.float32), 1),
+        total(grad_pre),
+        jnp.sum(grad_mlp.astype(jnp.float32), 1),
+    )
+    return (grad_in, (qkv_terms, mixing_terms, hidden_terms, output_terms), modulation_grad, bias_grads)
+
+
+def token_parallel(
+    tokens,
+    conditioning,
+    ada_weight,
+    ada_bias,
+    qkv_weight,
+    attn_bias,
+    mixing_weight,
+    mixing_bias,
+    hidden_weight,
+    hidden_bias,
+    output_weight,
+    output_bias,
+    cotangent,
+):
+    place = Place()
+    col_width = ada_bias.shape[2]
+    row_width = conditioning.shape[1]
+    hidden_width = hidden_bias.shape[1]
+    layer_count = ada_bias.shape[0]
+    clip_count = conditioning.shape[0]
+    width = col_width * place.col_count
+    ada_weight = ada_weight.reshape(layer_count, row_width, 6, col_width)
+    qkv_weight = qkv_weight.reshape(layer_count, row_width, 3 * col_width)
+    mixing_weight = jnp.swapaxes(mixing_weight.reshape(layer_count, col_width, row_width), 1, 2)
+    hidden_weight = hidden_weight.reshape(layer_count, row_width, hidden_width)
+    output_weight = jnp.swapaxes(output_weight.reshape(layer_count, hidden_width, row_width), 1, 2)
+    tokens = open_tokens(tokens, col_width)
+    cotangent = open_tokens(cotangent, col_width)
+    first_group = tokens.shape[1:3]
+    second_group = cotangent.shape[1:3]
+    placement = placing(width, place)
+
+    def arrive(held):
+        flat = held.reshape(clip_count, -1, col_width)
+        return enter(trade(relative(flat, place)), placement)
+
+    def depart(halves, group):
+        blocks = trade(leave(halves.astype(jnp.bfloat16), placement))
+        return absolute(blocks, place).reshape((clip_count,) + group + (col_width,))
+
+    stream_first = arrive(tokens)
+    cond_act = jax.nn.silu(conditioning).astype(jnp.bfloat16)
+    modulation = jnp.stack(
+        [matmul("cr,rsk->csk", cond_act, ada_weight[depth]) for depth in range(layer_count)], 1
+    )
+    modulation = modulation + jnp.where(place.row == 0, ada_bias, 0.0)[None]
+    modulation = modulation.reshape(clip_count, -1)
+    vectors = jnp.concatenate(
+        [value.reshape(-1) for value in (attn_bias, hidden_bias, mixing_bias, output_bias)]
+    )
+    met = trade([jnp.concatenate((mine, vectors)) for mine in relative(modulation, place)])
+    cut = modulation.shape[1]
+    modulation = jnp.stack([block[:cut] for block in met])
+    mask = 1
+    while mask < place.row_count:
+        modulation = modulation + exchange(modulation, "row", mask)
+        mask *= 2
+    modulation = jnp.stack(relative(modulation, place)).reshape(-1, layer_count, 6, col_width)
+    modulation = jnp.moveaxis(modulation, 0, 2).reshape(layer_count, 6, width)
+    modulation = to_halves(modulation, place)
+    attn_add, hidden_add, mixing_add, output_add = ([], [], [], [])
+    for block in met:
+        rest = block[cut:]
+        for kept, value in (
+            (attn_add, attn_bias),
+            (hidden_add, hidden_bias),
+            (mixing_add, mixing_bias),
+            (output_add, output_bias),
+        ):
+            kept.append(rest[: value.size].reshape(value.shape))
+            rest = rest[value.size :]
+
+    def whole_vector(blocks):
+        joined = jnp.moveaxis(absolute(blocks, place), 0, 1).reshape(layer_count, width)
+        return to_halves(joined, place)
+
+    mixing_add = whole_vector(mixing_add)
+    output_add = whole_vector(output_add)
+
+    def biases_of(depth):
+        return (
+            [block[depth] for block in attn_add],
+            mixing_add[depth],
+            [block[depth] for block in hidden_add],
+            output_add[depth],
+        )
+
+    weights = [
+        tuple(
+            gather_weight(shard[depth], place)
+            for shard in (qkv_weight, mixing_weight, hidden_weight, output_weight)
+        )
+        for depth in range(layer_count)
+    ]
+    output_first, saved_first = block_forward(
+        stream_first, modulation[0], weights[0], biases_of(0), first_group, spatial_forms
+    )
+    moving = mine_first(output_first.astype(jnp.bfloat16), place, 0)
+    moving = moving.reshape((2,) + first_group + (width // 2,))
+    moved = lax.all_to_all(moving, "row", split_axis=2, concat_axis=1, tiled=True)
+    stream_second = mine_first(moved, place, 0).astype(jnp.float32).reshape(2, -1, width // 2)
+    output_second, saved_second = block_forward(
+        stream_second, modulation[1], weights[1], biases_of(1), second_group, temporal_forms
+    )
+    result = depart(output_second, second_group)
+    grad_second, terms_second, modgrad_second, biasgrad_second = block_backward(
+        arrive(cotangent), saved_second, modulation[1], weights[1], second_group, temporal_forms
+    )
+    moving = mine_first(grad_second.astype(jnp.bfloat16), place, 0)
+    moving = moving.reshape((2,) + second_group + (width // 2,))
+    moved = lax.all_to_all(moving, "row", split_axis=1, concat_axis=2, tiled=True)
+    returned = mine_first(moved, place, 0).astype(jnp.float32).reshape(2, -1, width // 2)
+    sums_second = [scatter_weight(own, other, place) for own, other in terms_second]
+    grad_first, terms_first, modgrad_first, biasgrad_first = block_backward(
+        returned, saved_first, modulation[0], weights[0], first_group, spatial_forms
+    )
+    tokens_gradient = depart(grad_first, first_group).astype(jnp.float32)
+    sums_first = [scatter_weight(own, other, place) for own, other in terms_first]
+
+    def by_block(halves):
+        features = from_halves(halves, place)
+        features = features.reshape(features.shape[:-1] + (place.col_count, col_width))
+        return relative(jnp.moveaxis(features, -2, 0), place)
+
+    modgrad = by_block(jnp.stack((modgrad_first, modgrad_second)))
+    mixgrad = by_block(jnp.stack((biasgrad_first[1], biasgrad_second[1])))
+    outgrad = by_block(jnp.stack((biasgrad_first[3], biasgrad_second[3])))
+    sending = []
+    for step in range(place.col_count):
+        pieces = [modgrad[step].reshape(-1)]
+        for grads in (biasgrad_first, biasgrad_second):
+            pieces.append(grads[0][step][:col_width])
+            pieces.append(grads[0][step][2 * col_width :])
+        for grads in (biasgrad_first, biasgrad_second):
+            pieces.append(grads[2][step])
+        pieces.append(mixgrad[step].reshape(-1))
+        pieces.append(outgrad[step].reshape(-1))
+        sending.append(jnp.concatenate(pieces))
+    met = trade(sending)
+    modgrad = jnp.concatenate([block[:cut] for block in met])
+    biasgrad = sum(block[cut:] for block in met)
+    small = jnp.concatenate((modgrad, biasgrad))
+    mask = 1
+    while mask < place.row_count:
+        small = small + exchange(small, "row", mask)
+        mask *= 2
+    modgrad = small[: cut * clip_count].reshape(clip_count, layer_count, 6, col_width)
+    modgrad = jnp.moveaxis(jnp.stack(relative(modgrad, place)), 1, 0)
+    rest = small[cut * clip_count :]
+    bias_grads = []
+    for value in (attn_bias, hidden_bias, mixing_bias, output_bias):
+        bias_grads.append(rest[: value.size].reshape(value.shape))
+        rest = rest[value.size :]
+    ada_bias_grad = jnp.sum(modgrad, 1)
+    ada_weight_grad = jnp.einsum(
+        "cr,lcsk->lrsk", cond_act.astype(jnp.float32), modgrad, precision=highest
+    )
+    cond_part = jnp.einsum(
+        "lcsk,lrsk->cr", modgrad, ada_weight.astype(jnp.float32), precision=highest
+    )
+    for mask in (1, 2):
+        cond_part = cond_part + exchange(cond_part, "col", mask)
+    conditioning_gradient = jax.vjp(jax.nn.silu, conditioning)[1](cond_part)[0]
+
+    def both(index, flip):
+        pair = jnp.stack((sums_first[index], sums_second[index]))
+        return close_weight(jnp.swapaxes(pair, 1, 2) if flip else pair)
+
+    return (
+        close_tokens(result),
+        close_tokens(tokens_gradient),
+        conditioning_gradient,
+        close_weight(ada_weight_grad),
+        ada_bias_grad,
+        both(0, False),
+        bias_grads[0],
+        both(1, True),
+        bias_grads[2],
+        both(2, False),
+        bias_grads[1],
+        both(3, True),
+        bias_grads[3],
+    )
+
+
+def suits_tokens(mesh):
+    rows, cols = (mesh.shape["row"], mesh.shape["col"])
+    return cols == 4 and rows >= 2 and rows & (rows - 1) == 0
+
+
 def solution(mesh):
     placed = (
         P(None, "row", "col", None),
@@ -393,7 +881,7 @@
         P(None, None, "col", "row"),
     )
     return jax.shard_map(
-        local,
+        token_parallel if suits_tokens(mesh) else tensor_parallel,
         mesh=mesh,
         in_specs=placed,
         out_specs=(

time: 2730 us -> 1900 us (0.70)
  waiting for transfers between devices: 1450 us -> 665 us
  blocking collectives: 263 us -> 0 us
  starting transfers between devices: 7.45 us -> 156 us
  matrix products: 387 us -> 489 us
  local copies, waits for them, and re-layouts: 487 us -> 406 us
  other arithmetic: 109 us -> 154 us
    all_gather x14 -> x0, waiting for transfers between devices: 864 us -> none  [the longest x4 422 us: spread(): return lax.all_gather(values, 'col', axis=3, tiled=True)]
    ppermute x0 -> x186, waiting for transfers between devices: none -> 665 us  [exchange(): lax.ppermute(values, axis, [(index, index ^ mask) for index in range(coun...]
    reduce_scatter x12 -> x0, waiting for transfers between devices: 301 us -> none  [the longest x2 109 us: collect_grad(): lax.psum_scatter(terms.astype(jnp.bfloat16), 'col', scatter_dimension=3,...]
    unnamed x34 -> x0, waiting for transfers between devices: 223 us -> none
    unnamed x289 -> x1243, local copies, waits for them, and re-layouts: 277 us -> 55.9 us
    psum x10 -> x0, blocking collectives: 188 us -> none  [the longest x4 65.9 us: normalize_back(): lax.psum((jnp.sum(grad_normed, -1), jnp.sum(grad_normed * normed, -1)), '...]
    ppermute x0 -> x186, starting transfers between devices: none -> 147 us  [exchange(): lax.ppermute(values, axis, [(index, index ^ mask) for index in range(coun...]
    dot_general x38 -> x274, matrix products: 382 us -> 487 us  [matmul(): return jnp.einsum(pattern, left, right, preferred_element_type=jnp.float32)]
  transfers between devices with their start and end apart: 31 -> 188, of which waited for: 24 -> 66; matrix products, arithmetic and copies ran while one was open for 15% -> 40% of each run, Pallas kernels for 0% -> 0%
where the time goes in v1:
time: 1900 us; the launch traced here: 1880 us
  waiting for transfers between devices  665 us (35%)
  matrix products  489 us (26%)
  local copies, waits for them, and re-layouts  406 us (21%)
  starting transfers between devices  156 us (8%)
  other arithmetic  154 us (8%)
    ppermute x186, waiting for transfers between devices, exchange(): lax.ppermute(values, axis, [(index, index ^ mask) for index in range(coun...  665 us
    dot_general x274, matrix products, matmul(): return jnp.einsum(pattern, left, right, preferred_element_type=jnp.float32)  487 us
    ppermute x186, starting transfers between devices, exchange(): lax.ppermute(values, axis, [(index, index ^ mask) for index in range(coun...  147 us
    unnamed x1243, local copies, waits for them, and re-layouts  55.9 us
    convert_element_type x36, local copies, waits for them, and re-layouts, attend_back(): merge_heads(part_grad).astype(jnp.bfloat16)  51.9 us
    another operation x35, local copies, waits for them, and re-layouts  45 us
  transfers between devices with their start and end apart: 188, of which 66 were waited for; matrix products, arithmetic and copies ran while one was open for 40% of the time, Pallas kernels for 0%

profile of v1, /device:TPU:0, one launch (start us, length us, event | category | flops | bytes accessed | tf_op | source)
XLA Modules:
  0.0 1881.1 jit_solution(4639470519062441179)
XLA Ops:
  10.1 11.4 slice_reduce_fusion.1
  57.3 7.0 slice_reduce_fusion.2
  92.2 5.1 collective-permute-done.7
  100.5 11.8 collective-permute-done.8
  113.0 9.0 rev.35
  148.9 9.0 collective-permute-done.94
  163.3 6.6 collective-permute-done.93
  211.9 60.5 %collective-permute-done.10 = bf16[288,864]{1,0:T(8,128)(2,1)S(1)} collective-permute-done((bf16[288,864]{1,0:T(8,128)(2,1)S(1)}, bf16[288,864]{1,0:T(8,128)(2,1)S(1)}, u32[]{:S(2)}, u32[]{:S(2)}) %collective-permute-start.10) | collective-permute-done | bytes 497696 | tf_op jit(solution)/shard_map/ppermute | solution.py:381
  272.9 17.8 collective-permute-done.50
  293.5 11.4 collective-permute-done.30
  306.4 12.6 collective-permute-done.33
  321.7 11.6 collective-permute-done.70
  335.9 8.1 collective-permute-done.73
  357.3 12.8 collective-permute-done.54
  381.7 51.9 %collective-permute-done.21 = bf16[288,864]{1,0:T(8,128)(2,1)} collective-permute-done((bf16[288,864]{1,0:T(8,128)(2,1)}, bf16[288,864]{1,0:T(8,128)(2,1)}, u32[]{:S(2)}, u32[]{:S(2)}) %collective-permute-start.21) | collective-permute-done | bytes 497696 | tf_op jit(solution)/shard_map/ppermute | solution.py:381
  439.8 9.0 collective-permute-done.61
  461.4 5.6 collective-permute-done.39
  471.9 9.2 collective-permute-done.76
  494.0 8.8 collective-permute-done.74
  506.2 12.1 collective-permute-done.79
  563.5 4.5 collective-permute-done.83
  569.0 7.9 collective-permute-done.41
  577.0 12.7 collective-permute-done.44
  612.1 4.6 multiply_convert_fusion.14
  650.2 6.0 copy.519
  656.2 4.3 all-to-all-start
  672.0 6.0 collective-permute-done.81
  813.9 4.3 multiply_convert_fusion.7
  821.0 4.3 multiply_convert_fusion.9
  834.0 5.2 convert_reduce_fusion.10
  842.0 4.4 multiply_convert_fusion.8
  846.4 4.9 convert_reduce_fusion.3
  896.0 4.2 multiply_reduce_fusion.8
  1098.6 4.8 all-to-all-start.1
  1123.3 10.1 collective-permute-done.139
  1134.0 5.7 collective-permute-done.142
  1143.5 6.9 collective-permute-done.91
  1168.8 8.3 collective-permute-done.144
  1197.6 5.4 collective-permute-done.119
  1207.3 10.0 collective-permute-done.179
  1220.3 10.7 collective-permute-done.159
  1255.1 4.8 convert_reduce_fusion.4
  1459.8 5.9 reshape.1738
  1481.3 8.0 reshape.1737
  1494.7 6.4 collective-permute-done.129
  1502.8 23.9 %collective-permute-done.132 = bf16[288,288]{0,1:T(8,128)(2,1)S(1)} collective-permute-done((bf16[288,288]{0,1:T(8,128)(2,1)S(1)}, bf16[288,288]{0,1:T(8,128)(2,1)S(1)}, u32[]{:S(2)}, u32[]{:S(2)}) %collective-permute-start.132) | collective-permute-done | bytes 165920 | tf_op jit(solution)/shard_map/ppermute | solution.py:381
  1532.6 5.5 collective-permute-done.130
  1540.6 23.9 %collective-permute-done.124 = bf16[288,864]{1,0:T(8,128)(2,1)S(1)} collective-permute-done((bf16[288,864]{1,0:T(8,128)(2,1)S(1)}, bf16[288,864]{1,0:T(8,128)(2,1)S(1)}, u32[]{:S(2)}, u32[]{:S(2)}) %collective-permute-start.124) | collective-permute-done | bytes 497696 | tf_op jit(solution)/shard_map/ppermute | solution.py:381
  1568.9 11.1 collective-permute-done.134
  1586.6 5.7 collective-permute-done.135
  1602.0 10.3 collective-permute-done.183
  1615.7 6.9 collective-permute-done.160
  1622.7 17.1 collective-permute-done.163
  1655.3 7.4 collective-permute-done.109
  1666.8 33.5 %collective-permute-done.184 = bf16[288,1152]{1,0:T(8,128)(2,1)S(1)} collective-permute-done((bf16[288,1152]{1,0:T(8,128)(2,1)S(1)}, bf16[288,1152]{1,0:T(8,128)(2,1)S(1)}, u32[]{:S(2)}, u32[]{:S(2)}) %collective-permute-start.184) | collective-permute-done | bytes 663584 | tf_op jit(solution)/shard_map/ppermute | solution.py:381
  1701.2 13.2 collective-permute-done.164
  1718.0 13.3 collective-permute-done.149
  1737.1 17.0 collective-permute-done.110
  1758.5 21.5 %collective-permute-done.114 = bf16[288,864]{1,0:T(8,128)(2,1)S(1)} collective-permute-done((bf16[288,864]{1,0:T(8,128)(2,1)S(1)}, bf16[288,864]{1,0:T(8,128)(2,1)S(1)}, u32[]{:S(2)}, u32[]{:S(2)}) %collective-permute-start.114) | collective-permute-done | bytes 497696 | tf_op jit(solution)/shard_map/ppermute | solution.py:381
  1783.0 4.7 collective-permute-done.115
  1794.7 17.7 collective-permute-done.173
  1815.6 21.3 %collective-permute-done.153 = bf16[576,1152]{1,0:T(8,128)(2,1)S(1)} collective-permute-done((bf16[576,1152]{1,0:T(8,128)(2,1)}, bf16[576,1152]{1,0:T(8,128)(2,1)S(1)}, u32[]{:S(2)}, u32[]{:S(2)}) %collective-permute-start.153) | collective-permute-done | bytes 1327136 | tf_op jit(solution)/shard_map/ppermute | solution.py:381
  1839.6 9.0 collective-permute-done.174
  1849.0 17.7 collective-permute-done.154
  (2394 shorter events, 1138.5 us)
Async XLA Ops:
  5.5 135.2 %collective-permute-start = (bf16[512,288]{1,0:T(8,128)(2,1)}, bf16[512,288]{1,0:T(8,128)(2,1)}, u32[]{:S(2)}, u32[]{:S(2)}) collective-permute-start(bf16[512,288]{1,0:T(8,128)(2,1)} %get-tuple-element.151), channel_id=1, source_target_pairs={{0,1},{1,0},{2,3},{3,2},{4,5},{5,4},{6,7},{7,6},{8,9},{9,8},{10,11... | collective-permute-start | bytes 884744 | tf_op jit(solution)/shard_map/ppermute | solution.py:381
  8.5 128.4 %collective-permute-start.2 = (bf16[512,288]{1,0:T(8,128)(2,1)}, bf16[512,288]{1,0:T(8,128)(2,1)}, u32[]{:S(2)}, u32[]{:S(2)}) collective-permute-start(bf16[512,288]{1,0:T(8,128)(2,1)} %get-tuple-element.150), channel_id=1, source_target_pairs={{0,3},{1,2},{2,1},{3,0},{4,7},{5,6},{6,5},{7,4},{8,11},{9,10},{10,... | collective-permute-start | bytes 884744 | tf_op jit(solution)/shard_map/ppermute | solution.py:381
  29.5 45.2 %collective-permute-start.3 = (f32[8064]{0:T(1024)}, f32[8064]{0:T(1024)S(1)}, u32[]{:S(2)}, u32[]{:S(2)}) collective-permute-start(f32[8064]{0:T(1024)} %concatenate.248), channel_id=1, source_target_pairs={{0,1},{1,0},{2,3},{3,2},{4,5},{5,4},{6,7},{7,6},{8,9},{9,8},{10,11... | collective-permute-start | bytes 96776 | tf_op jit(solution)/shard_map/ppermute | solution.py:381
  31.7 44.7 %collective-permute-start.4 = (f32[8064]{0:T(1024)}, f32[8064]{0:T(1024)}, u32[]{:S(2)}, u32[]{:S(2)}) collective-permute-start(f32[8064]{0:T(1024)} %concatenate.249), channel_id=1, source_target_pairs={{0,2},{1,3},{2,0},{3,1},{4,6},{5,7},{6,4},{7,5},{8,10},{9,11},{10,... | collective-permute-start | bytes 96776 | tf_op jit(solution)/shard_map/ppermute | solution.py:381
  32.9 44.7 %collective-permute-start.5 = (f32[8064]{0:T(1024)}, f32[8064]{0:T(1024)}, u32[]{:S(2)}, u32[]{:S(2)}) collective-permute-start(f32[8064]{0:T(1024)} %concatenate.250), channel_id=1, source_target_pairs={{0,3},{1,2},{2,1},{3,0},{4,7},{5,6},{6,5},{7,4},{8,11},{9,10},{10,... | collective-permute-start | bytes 96776 | tf_op jit(solution)/shard_map/ppermute | solution.py:381
  74.8 54.7 %collective-permute-start.9 = (bf16[144,864]{1,0:T(8,128)(2,1)S(1)}, bf16[144,864]{1,0:T(8,128)(2,1)S(1)}, u32[]{:S(2)}, u32[]{:S(2)}) collective-permute-start(bf16[144,864]{1,0:T(8,128)(2,1)S(1)} %squeeze.143), channel_id=1, source_target_pairs={{0,8},{4,12},{8,0},{12,4},{16,24},{20,28},{24,16},{28,20},{1,9},{5... | collective-permute-start | bytes 746504 | tf_op jit(solution)/shard_map/ppermute | solution.py:381
  129.4 53.8 %collective-permute-start.29 = (bf16[144,1152]{1,0:T(8,128)(2,1)}, bf16[144,1152]{1,0:T(8,128)(2,1)}, u32[]{:S(2)}, u32[]{:S(2)}) collective-permute-start(bf16[144,1152]{1,0:T(8,128)(2,1)} %squeeze.147), channel_id=1, source_target_pairs={{0,8},{4,12},{8,0},{12,4},{16,24},{20,28},{24,16},{28,20},{1,9},{5... | collective-permute-start | bytes 995336 | tf_op jit(solution)/shard_map/ppermute | solution.py:381
  133.9 51.3 %collective-permute-start.32 = (bf16[144,1152]{1,0:T(8,128)(2,1)}, bf16[144,1152]{1,0:T(8,128)(2,1)}, u32[]{:S(2)}, u32[]{:S(2)}) collective-permute-start(bf16[144,1152]{1,0:T(8,128)(2,1)} %get-tuple-element.174), channel_id=1, source_target_pairs={{0,8},{4,12},{8,0},{12,4},{16,24},{20,28},{24,16},{28,20},{1,9},{5... | collective-permute-start | bytes 995336 | tf_op jit(solution)/shard_map/ppermute | solution.py:381
  136.9 55.7 %collective-permute-start.69 = (bf16[144,1152]{1,0:T(8,128)(2,1)}, bf16[144,1152]{1,0:T(8,128)(2,1)}, u32[]{:S(2)}, u32[]{:S(2)}) collective-permute-start(bf16[144,1152]{1,0:T(8,128)(2,1)} %squeeze.155), channel_id=1, source_target_pairs={{0,8},{4,12},{8,0},{12,4},{16,24},{20,28},{24,16},{28,20},{1,9},{5... | collective-permute-start | bytes 995336 | tf_op jit(solution)/shard_map/ppermute | solution.py:381
  190.8 81.6 %collective-permute-start.10 = (bf16[288,864]{1,0:T(8,128)(2,1)S(1)}, bf16[288,864]{1,0:T(8,128)(2,1)S(1)}, u32[]{:S(2)}, u32[]{:S(2)}) collective-permute-start(bf16[288,864]{1,0:T(8,128)(2,1)S(1)} %copy-done.216), channel_id=1, source_target_pairs={{0,16},{4,20},{8,24},{12,28},{16,0},{20,4},{24,8},{28,12},{1,17},{... | collective-permute-start | bytes 1493000 | tf_op jit(solution)/shard_map/ppermute | solution.py:381
  197.1 93.5 %collective-permute-start.50 = (bf16[288,864]{1,0:T(8,128)(2,1)S(1)}, bf16[288,864]{1,0:T(8,128)(2,1)S(1)}, u32[]{:S(2)}, u32[]{:S(2)}) collective-permute-start(bf16[288,864]{1,0:T(8,128)(2,1)S(1)} %copy-done.217), channel_id=1, source_target_pairs={{0,16},{4,20},{8,24},{12,28},{16,0},{20,4},{24,8},{28,12},{1,17},{... | collective-permute-start | bytes 1493000 | tf_op jit(solution)/shard_map/ppermute | solution.py:381
  200.6 104.3 %collective-permute-start.30 = (bf16[288,1152]{1,0:T(8,128)(2,1)S(1)}, bf16[288,1152]{1,0:T(8,128)(2,1)S(1)}, u32[]{:S(2)}, u32[]{:S(2)}) collective-permute-start(bf16[288,1152]{1,0:T(8,128)(2,1)S(1)} %maximum_select_fusion.6), channel_id=1, source_target_pairs={{0,16},{4,20},{8,24},{12,28},{16,0},{20,4},{24,8},{28,12},{1,17},{... | collective-permute-start | bytes 1990664 | tf_op jit(solution)/shard_map/ppermute | solution.py:381
  207.2 111.9 %collective-permute-start.33 = (bf16[288,1152]{1,0:T(8,128)(2,1)S(1)}, bf16[288,1152]{1,0:T(8,128)(2,1)S(1)}, u32[]{:S(2)}, u32[]{:S(2)}) collective-permute-start(bf16[288,1152]{1,0:T(8,128)(2,1)S(1)} %maximum_select_fusion.7), channel_id=1, source_target_pairs={{0,16},{4,20},{8,24},{12,28},{16,0},{20,4},{24,8},{28,12},{1,17},{... | collective-permute-start | bytes 1990664 | tf_op jit(solution)/shard_map/ppermute | solution.py:381
  209.5 123.8 %collective-permute-start.70 = (bf16[288,1152]{1,0:T(8,128)(2,1)S(1)}, bf16[288,1152]{1,0:T(8,128)(2,1)S(1)}, u32[]{:S(2)}, u32[]{:S(2)}) collective-permute-start(bf16[288,1152]{1,0:T(8,128)(2,1)S(1)} %maximum_select_fusion.8), channel_id=1, source_target_pairs={{0,16},{4,20},{8,24},{12,28},{16,0},{20,4},{24,8},{28,12},{1,17},{... | collective-permute-start | bytes 1990664 | tf_op jit(solution)/shard_map/ppermute | solution.py:381
  272.4 71.5 %collective-permute-start.73 = (bf16[288,1152]{1,0:T(8,128)(2,1)S(1)}, bf16[288,1152]{1,0:T(8,128)(2,1)S(1)}, u32[]{:S(2)}, u32[]{:S(2)}) collective-permute-start(bf16[288,1152]{1,0:T(8,128)(2,1)S(1)} %maximum_select_fusion.9), channel_id=1, source_target_pairs={{0,16},{4,20},{8,24},{12,28},{16,0},{20,4},{24,8},{28,12},{1,17},{... | collective-permute-start | bytes 1990664 | tf_op jit(solution)/shard_map/ppermute | solution.py:381
  290.6 56.4 %collective-permute-start.14 = (bf16[576,864]{1,0:T(8,128)(2,1)S(1)}, bf16[576,864]{1,0:T(8,128)(2,1)}, u32[]{:S(2)}, u32[]{:S(2)}) collective-permute-start(bf16[576,864]{1,0:T(8,128)(2,1)S(1)} %maximum_select_fusion.4), channel_id=1, source_target_pairs={{0,1},{1,0},{2,3},{3,2},{4,5},{5,4},{6,7},{7,6},{8,9},{9,8},{10,11... | collective-permute-start | bytes 2985992 | tf_op jit(solution)/shard_map/ppermute | solution.py:381
  304.8 44.0 %collective-permute-start.11 = (bf16[576,864]{1,0:T(8,128)(2,1)S(1)}, bf16[576,864]{1,0:T(8,128)(2,1)S(1)}, u32[]{:S(2)}, u32[]{:S(2)}) collective-permute-start(bf16[576,864]{1,0:T(8,128)(2,1)S(1)} %maximum_select_fusion.4), channel_id=1, source_target_pairs={{0,4},{4,0},{8,12},{12,8},{16,20},{20,16},{24,28},{28,24},{1,5},{5... | collective-permute-start | bytes 2985992 | tf_op jit(solution)/shard_map/ppermute | solution.py:381
  319.1 34.8 %collective-permute-start.17 = (bf16[576,864]{1,0:T(8,128)(2,1)S(1)}, bf16[576,864]{1,0:T(8,128)(2,1)}, u32[]{:S(2)}, u32[]{:S(2)}) collective-permute-start(bf16[576,864]{1,0:T(8,128)(2,1)S(1)} %maximum_select_fusion.4), channel_id=1, source_target_pairs={{0,2},{1,3},{2,0},{3,1},{4,6},{5,7},{6,4},{7,5},{8,10},{9,11},{10,... | collective-permute-start | bytes 2985992 | tf_op jit(solution)/shard_map/ppermute | solution.py:381
  333.3 40.7 %collective-permute-start.57 = (bf16[576,864]{1,0:T(8,128)(2,1)}, bf16[576,864]{1,0:T(8,128)(2,1)}, u32[]{:S(2)}, u32[]{:S(2)}) collective-permute-start(bf16[576,864]{1,0:T(8,128)(2,1)} %maximum_select_fusion.5), channel_id=1, source_target_pairs={{0,2},{1,3},{2,0},{3,1},{4,6},{5,7},{6,4},{7,5},{8,10},{9,11},{10,... | collective-permute-start | bytes 2985992 | tf_op jit(solution)/shard_map/ppermute | solution.py:381
  353.9 97.9 %collective-permute-start.34 = (bf16[576,1152]{1,0:T(8,128)(2,1)}, bf16[576,1152]{1,0:T(8,128)(2,1)}, u32[]{:S(2)}, u32[]{:S(2)}) collective-permute-start(bf16[576,1152]{1,0:T(8,128)(2,1)} %maximum_select_fusion), channel_id=1, source_target_pairs={{0,1},{1,0},{2,3},{3,2},{4,5},{5,4},{6,7},{7,6},{8,9},{9,8},{10,11... | collective-permute-start | bytes 3981320 | tf_op jit(solution)/shard_map/ppermute | solution.py:381
  370.1 83.5 %collective-permute-start.37 = (bf16[576,1152]{1,0:T(8,128)(2,1)}, bf16[576,1152]{1,0:T(8,128)(2,1)}, u32[]{:S(2)}, u32[]{:S(2)}) collective-permute-start(bf16[576,1152]{1,0:T(8,128)(2,1)} %maximum_select_fusion), channel_id=1, source_target_pairs={{0,2},{1,3},{2,0},{3,1},{4,6},{5,7},{6,4},{7,5},{8,10},{9,11},{10,... | collective-permute-start | bytes 3981320 | tf_op jit(solution)/shard_map/ppermute | solution.py:381
  373.5 80.0 %collective-permute-start.36 = (bf16[576,1152]{1,0:T(8,128)(2,1)}, bf16[576,1152]{1,0:T(8,128)(2,1)}, u32[]{:S(2)}, u32[]{:S(2)}) collective-permute-start(bf16[576,1152]{1,0:T(8,128)(2,1)} %maximum_select_fusion.1), channel_id=1, source_target_pairs={{0,1},{1,0},{2,3},{3,2},{4,5},{5,4},{6,7},{7,6},{8,9},{9,8},{10,11... | collective-permute-start | bytes 3981320 | tf_op jit(solution)/shard_map/ppermute | solution.py:381
  374.0 59.6 %collective-permute-start.21 = (bf16[288,864]{1,0:T(8,128)(2,1)}, bf16[288,864]{1,0:T(8,128)(2,1)}, u32[]{:S(2)}, u32[]{:S(2)}) collective-permute-start(bf16[288,864]{1,0:T(8,128)(2,1)} %slice.1348), channel_id=1, source_target_pairs={{0,1},{1,0},{2,3},{3,2},{4,5},{5,4},{6,7},{7,6},{8,9},{9,8},{10,11... | collective-permute-start | bytes 1493000 | tf_op jit(solution)/shard_map/ppermute | solution.py:381
  375.9 60.8 %collective-permute-start.60 = (bf16[288,864]{1,0:T(8,128)(2,1)}, bf16[288,864]{1,0:T(8,128)(2,1)}, u32[]{:S(2)}, u32[]{:S(2)}) collective-permute-start(bf16[288,864]{1,0:T(8,128)(2,1)} %slice.1396), channel_id=1, source_target_pairs={{0,2},{1,3},{2,0},{3,1},{4,6},{5,7},{6,4},{7,5},{8,10},{9,11},{10,... | collective-permute-start | bytes 1493000 | tf_op jit(solution)/shard_map/ppermute | solution.py:381
  433.6 33.4 %collective-permute-start.39 = (bf16[576,1152]{1,0:T(8,128)(2,1)}, bf16[576,1152]{1,0:T(8,128)(2,1)S(1)}, u32[]{:S(2)}, u32[]{:S(2)}) collective-permute-start(bf16[576,1152]{1,0:T(8,128)(2,1)} %maximum_select_fusion.1), channel_id=1, source_target_pairs={{0,2},{1,3},{2,0},{3,1},{4,6},{5,7},{6,4},{7,5},{8,10},{9,11},{10,... | collective-permute-start | bytes 3981320 | tf_op jit(solution)/shard_map/ppermute | solution.py:381
  451.8 51.0 %collective-permute-start.74 = (bf16[576,1152]{1,0:T(8,128)(2,1)S(1)}, bf16[576,1152]{1,0:T(8,128)(2,1)}, u32[]{:S(2)}, u32[]{:S(2)}) collective-permute-start(bf16[576,1152]{1,0:T(8,128)(2,1)S(1)} %copy-done.72), channel_id=1, source_target_pairs={{0,1},{1,0},{2,3},{3,2},{4,5},{5,4},{6,7},{7,6},{8,9},{9,8},{10,11... | collective-permute-start | bytes 3981320 | tf_op jit(solution)/shard_map/ppermute | solution.py:381
  453.5 51.3 %collective-permute-start.77 = (bf16[576,1152]{1,0:T(8,128)(2,1)S(1)}, bf16[576,1152]{1,0:T(8,128)(2,1)S(1)}, u32[]{:S(2)}, u32[]{:S(2)}) collective-permute-start(bf16[576,1152]{1,0:T(8,128)(2,1)S(1)} %copy-done.72), channel_id=1, source_target_pairs={{0,2},{1,3},{2,0},{3,1},{4,6},{5,7},{6,4},{7,5},{8,10},{9,11},{10,... | collective-permute-start | bytes 3981320 | tf_op jit(solution)/shard_map/ppermute | solution.py:381
  453.6 64.8 %collective-permute-start.79 = (bf16[576,1152]{1,0:T(8,128)(2,1)}, bf16[576,1152]{1,0:T(8,128)(2,1)S(1)}, u32[]{:S(2)}, u32[]{:S(2)}) collective-permute-start(bf16[576,1152]{1,0:T(8,128)(2,1)} %maximum_select_fusion.3), channel_id=1, source_target_pairs={{0,2},{1,3},{2,0},{3,1},{4,6},{5,7},{6,4},{7,5},{8,10},{9,11},{10,... | collective-permute-start | bytes 3981320 | tf_op jit(solution)/shard_map/ppermute | solution.py:381
  467.0 55.1 %collective-permute-start.18 = (bf16[576,864]{1,0:T(8,128)(2,1)}, bf16[576,864]{1,0:T(8,128)(2,1)S(1)}, u32[]{:S(2)}, u32[]{:S(2)}) collective-permute-start(bf16[576,864]{1,0:T(8,128)(2,1)} %collective-permute-done.17), channel_id=1, source_target_pairs={{0,4},{4,0},{8,12},{12,8},{16,20},{20,16},{24,28},{28,24},{1,5},{5... | collective-permute-start | bytes 2985992 | tf_op jit(solution)/shard_map/ppermute | solution.py:381
  481.2 50.6 %collective-permute-start.15 = (bf16[576,864]{1,0:T(8,128)(2,1)}, bf16[576,864]{1,0:T(8,128)(2,1)}, u32[]{:S(2)}, u32[]{:S(2)}) collective-permute-start(bf16[576,864]{1,0:T(8,128)(2,1)} %collective-permute-done.14), channel_id=1, source_target_pairs={{0,4},{4,0},{8,12},{12,8},{16,20},{20,16},{24,28},{28,24},{1,5},{5... | collective-permute-start | bytes 2985992 | tf_op jit(solution)/shard_map/ppermute | solution.py:381
  502.8 275.9 %collective-permute-start.65 = (bf16[576,288]{0,1:T(8,128)(2,1)}, bf16[576,288]{0,1:T(8,128)(2,1)}, u32[]{:S(2)}, u32[]{:S(2)}) collective-permute-start(bf16[576,288]{0,1:T(8,128)(2,1)} %maximum_select_fusion.13), channel_id=1, source_target_pairs={{0,4},{4,0},{8,12},{12,8},{16,20},{20,16},{24,28},{28,24},{1,5},{5... | collective-permute-start | bytes 995336 | tf_op jit(solution)/shard_map/ppermute | solution.py:381
  504.8 43.6 %collective-permute-start.26 = (bf16[576,288]{0,1:T(8,128)(2,1)}, bf16[576,288]{0,1:T(8,128)(2,1)}, u32[]{:S(2)}, u32[]{:S(2)}) collective-permute-start(bf16[576,288]{0,1:T(8,128)(2,1)} %collective-permute-done.16), channel_id=1, source_target_pairs={{0,4},{4,0},{8,12},{12,8},{16,20},{20,16},{24,28},{28,24},{1,5},{5... | collective-permute-start | bytes 995336 | tf_op jit(solution)/shard_map/ppermute | solution.py:381
  518.4 71.4 %collective-permute-start.22 = (bf16[576,864]{1,0:T(8,128)(2,1)}, bf16[576,864]{1,0:T(8,128)(2,1)}, u32[]{:S(2)}, u32[]{:S(2)}) collective-permute-start(bf16[576,864]{1,0:T(8,128)(2,1)} %constant_dynamic-update-slice_fusion), channel_id=1, source_target_pairs={{0,4},{4,0},{8,12},{12,8},{16,20},{20,16},{24,28},{28,24},{1,5},{5... | collective-permute-start | bytes 2985992 | tf_op jit(solution)/shard_map/ppermute | solution.py:381
  522.1 36.9 %collective-permute-start.40 = (bf16[288,1152]{1,0:T(8,128)(2,1)}, bf16[288,1152]{1,0:T(8,128)(2,1)}, u32[]{:S(2)}, u32[]{:S(2)}) collective-permute-start(bf16[288,1152]{1,0:T(8,128)(2,1)} %slice.1368), channel_id=1, source_target_pairs={{0,2},{1,3},{2,0},{3,1},{4,6},{5,7},{6,4},{7,5},{8,10},{9,11},{10,... | collective-permute-start | bytes 1990664 | tf_op jit(solution)/shard_map/ppermute | solution.py:381
  568.0 34.2 %collective-permute-start.27 = (bf16[576,288]{0,1:T(8,128)(2,1)}, bf16[576,288]{0,1:T(8,128)(2,1)}, u32[]{:S(2)}, u32[]{:S(2)}) collective-permute-start(bf16[576,288]{0,1:T(8,128)(2,1)} %collective-permute-done.19), channel_id=1, source_target_pairs={{0,4},{4,0},{8,12},{12,8},{16,20},{20,16},{24,28},{28,24},{1,5},{5... | collective-permute-start | bytes 995336 | tf_op jit(solution)/shard_map/ppermute | solution.py:381
  576.9 209.1 %collective-permute-start.66 = (bf16[576,288]{0,1:T(8,128)(2,1)}, bf16[576,288]{0,1:T(8,128)(2,1)}, u32[]{:S(2)}, u32[]{:S(2)}) collective-permute-start(bf16[576,288]{0,1:T(8,128)(2,1)} %collective-permute-done.56), channel_id=1, source_target_pairs={{0,4},{4,0},{8,12},{12,8},{16,20},{20,16},{24,28},{28,24},{1,5},{5... | collective-permute-start | bytes 995336 | tf_op jit(solution)/shard_map/ppermute | solution.py:381
  627.0 37.2 %collective-permute-start.85 = (bf16[576,1152]{1,0:T(8,128)(2,1)}, bf16[576,1152]{1,0:T(8,128)(2,1)}, u32[]{:S(2)}, u32[]{:S(2)}) collective-permute-start(bf16[576,1152]{1,0:T(8,128)(2,1)} %maximum_select_fusion.3), channel_id=1, source_target_pairs={{0,4},{4,0},{8,12},{12,8},{16,20},{20,16},{24,28},{28,24},{1,5},{5... | collective-permute-start | bytes 3981320 | tf_op jit(solution)/shard_map/ppermute | solution.py:381
  656.2 36.5 %all-to-all-start = ((bf16[2,2,256,576]{3,1,0,2:T(2,128)(2,1)}), bf16[2,2,256,576]{3,1,0,2:T(2,128)(2,1)}, u32[]{:S(2)}, u32[]{:S(2)}) async-start(bf16[2,2,256,576]{3,1,0,2:T(2,128)(2,1)} %copy.519), calls=%async_computation | async-start | bytes 2621440 | tf_op jit(solution)/shard_map/all_to_all | solution.py:776
  669.6 118.6 %collective-permute-start.67 = (bf16[576,288]{0,1:T(8,128)(2,1)}, bf16[576,288]{0,1:T(8,128)(2,1)}, u32[]{:S(2)}, u32[]{:S(2)}) collective-permute-start(bf16[576,288]{0,1:T(8,128)(2,1)} %collective-permute-done.59), channel_id=1, source_target_pairs={{0,4},{4,0},{8,12},{12,8},{16,20},{20,16},{24,28},{28,24},{1,5},{5... | collective-permute-start | bytes 995336 | tf_op jit(solution)/shard_map/ppermute | solution.py:381
  715.7 65.7 %collective-permute-start.68 = (bf16[576,288]{0,1:T(8,128)(2,1)}, bf16[576,288]{0,1:T(8,128)(2,1)}, u32[]{:S(2)}, u32[]{:S(2)}) collective-permute-start(bf16[576,288]{0,1:T(8,128)(2,1)} %pad_maximum_fusion.30), channel_id=1, source_target_pairs={{0,4},{4,0},{8,12},{12,8},{16,20},{20,16},{24,28},{28,24},{1,5},{5... | collective-permute-start | bytes 995336 | tf_op jit(solution)/shard_map/ppermute | solution.py:381
  753.4 57.9 %collective-permute-start.71 = (bf16[576,1152]{1,0:T(8,128)(2,1)}, bf16[576,1152]{1,0:T(8,128)(2,1)}, u32[]{:S(2)}, u32[]{:S(2)}) collective-permute-start(bf16[576,1152]{1,0:T(8,128)(2,1)} %maximum_select_fusion.2), channel_id=1, source_target_pairs={{0,4},{4,0},{8,12},{12,8},{16,20},{20,16},{24,28},{28,24},{1,5},{5... | collective-permute-start | bytes 3981320 | tf_op jit(solution)/shard_map/ppermute | solution.py:381
  778.8 42.3 %collective-permute-start.75 = (bf16[576,1152]{1,0:T(8,128)(2,1)}, bf16[576,1152]{1,0:T(8,128)(2,1)}, u32[]{:S(2)}, u32[]{:S(2)}) collective-permute-start(bf16[576,1152]{1,0:T(8,128)(2,1)} %collective-permute-done.74), channel_id=1, source_target_pairs={{0,4},{4,0},{8,12},{12,8},{16,20},{20,16},{24,28},{28,24},{1,5},{5... | collective-permute-start | bytes 3981320 | tf_op jit(solution)/shard_map/ppermute | solution.py:381
  781.4 52.6 %collective-permute-start.86 = (bf16[576,1152]{1,0:T(8,128)(2,1)}, bf16[576,1152]{1,0:T(8,128)(2,1)}, u32[]{:S(2)}, u32[]{:S(2)}) collective-permute-start(bf16[576,1152]{1,0:T(8,128)(2,1)} %collective-permute-done.76), channel_id=1, source_target_pairs={{0,4},{4,0},{8,12},{12,8},{16,20},{20,16},{24,28},{28,24},{1,5},{5... | collective-permute-start | bytes 3981320 | tf_op jit(solution)/shard_map/ppermute | solution.py:381
  786.0 55.9 %collective-permute-start.78 = (bf16[576,1152]{1,0:T(8,128)(2,1)}, bf16[576,1152]{1,0:T(8,128)(2,1)}, u32[]{:S(2)}, u32[]{:S(2)}) collective-permute-start(bf16[576,1152]{1,0:T(8,128)(2,1)} %copy-done.309), channel_id=1, source_target_pairs={{0,4},{4,0},{8,12},{12,8},{16,20},{20,16},{24,28},{28,24},{1,5},{5... | collective-permute-start | bytes 3981320 | tf_op jit(solution)/shard_map/ppermute | solution.py:381
  808.6 42.7 %collective-permute-start.87 = (bf16[576,1152]{1,0:T(8,128)(2,1)S(1)}, bf16[576,1152]{1,0:T(8,128)(2,1)S(1)}, u32[]{:S(2)}, u32[]{:S(2)}) collective-permute-start(bf16[576,1152]{1,0:T(8,128)(2,1)S(1)} %copy-done.307), channel_id=1, source_target_pairs={{0,4},{4,0},{8,12},{12,8},{16,20},{20,16},{24,28},{28,24},{1,5},{5... | collective-permute-start | bytes 3981320 | tf_op jit(solution)/shard_map/ppermute | solution.py:381
  1098.6 137.5 %all-to-all-start.1 = ((bf16[2,16,32,576]{3,2,0,1:T(8,128)(2,1)}), bf16[2,16,32,576]{3,2,0,1:T(8,128)(2,1)}, u32[]{:S(2)}, u32[]{:S(2)}) async-start(bf16[2,16,32,576]{3,2,0,1:T(8,128)(2,1)} %copy.604), calls=%async_computation.1 | async-start | bytes 2621440 | tf_op jit(solution)/shard_map/all_to_all | solution.py:787
  1104.6 52.1 %collective-permute-start.136 = (bf16[576,288]{0,1:T(8,128)(2,1)}, bf16[576,288]{0,1:T(8,128)(2,1)}, u32[]{:S(2)}, u32[]{:S(2)}) collective-permute-start(bf16[576,288]{0,1:T(8,128)(2,1)} %convolution_convert_fusion.62), channel_id=1, source_target_pairs={{0,4},{4,0},{8,12},{12,8},{16,20},{20,16},{24,28},{28,24},{1,5},{5... | collective-permute-start | bytes 995336 | tf_op jit(solution)/shard_map/ppermute | solution.py:381
  1104.6 54.9 %collective-permute-start.116 = (bf16[576,864]{1,0:T(8,128)(2,1)}, bf16[576,864]{1,0:T(8,128)(2,1)}, u32[]{:S(2)}, u32[]{:S(2)}) collective-permute-start(bf16[576,864]{1,0:T(8,128)(2,1)} %convolution_convert_fusion.38), channel_id=1, source_target_pairs={{0,4},{4,0},{8,12},{12,8},{16,20},{20,16},{24,28},{28,24},{1,5},{5... | collective-permute-start | bytes 2985992 | tf_op jit(solution)/shard_map/ppermute | solution.py:381
  1185.6 401.0 %collective-permute-start.176 = (bf16[576,1152]{1,0:T(8,128)(2,1)}, bf16[576,1152]{1,0:T(8,128)(2,1)}, u32[]{:S(2)}, u32[]{:S(2)}) collective-permute-start(bf16[576,1152]{1,0:T(8,128)(2,1)} %convolution_convert_fusion.6), channel_id=1, source_target_pairs={{0,4},{4,0},{8,12},{12,8},{16,20},{20,16},{24,28},{28,24},{1,5},{5... | collective-permute-start | bytes 3981320 | tf_op jit(solution)/shard_map/ppermute | solution.py:381
  1434.5 38.9 %collective-permute-start.95 = (bf16[512,288]{0,1:T(8,128)(2,1)}, bf16[512,288]{0,1:T(8,128)(2,1)}, u32[]{:S(2)}, u32[]{:S(2)}) collective-permute-start(bf16[512,288]{0,1:T(8,128)(2,1)} %fusion.185), channel_id=1, source_target_pairs={{0,1},{1,0},{2,3},{3,2},{4,5},{5,4},{6,7},{7,6},{8,9},{9,8},{10,11... | collective-permute-start | bytes 884744 | tf_op jit(solution)/shard_map/ppermute | solution.py:381
  1438.6 35.6 %collective-permute-start.96 = (bf16[512,288]{0,1:T(8,128)(2,1)}, bf16[512,288]{0,1:T(8,128)(2,1)}, u32[]{:S(2)}, u32[]{:S(2)}) collective-permute-start(bf16[512,288]{0,1:T(8,128)(2,1)} %fusion.186), channel_id=1, source_target_pairs={{0,2},{1,3},{2,0},{3,1},{4,6},{5,7},{6,4},{7,5},{8,10},{9,11},{10,... | collective-permute-start | bytes 884744 | tf_op jit(solution)/shard_map/ppermute | solution.py:381
  1470.3 56.7 %collective-permute-start.120 = (bf16[576,864]{1,0:T(8,128)(2,1)}, bf16[576,864]{1,0:T(8,128)(2,1)}, u32[]{:S(2)}, u32[]{:S(2)}) collective-permute-start(bf16[576,864]{1,0:T(8,128)(2,1)} %pad_maximum_fusion.22), channel_id=1, source_target_pairs={{0,1},{1,0},{2,3},{3,2},{4,5},{5,4},{6,7},{7,6},{8,9},{9,8},{10,11... | collective-permute-start | bytes 2985992 | tf_op jit(solution)/shard_map/ppermute | solution.py:381
  1473.4 55.4 %collective-permute-start.123 = (bf16[576,864]{1,0:T(8,128)(2,1)}, bf16[576,864]{1,0:T(8,128)(2,1)}, u32[]{:S(2)}, u32[]{:S(2)}) collective-permute-start(bf16[576,864]{1,0:T(8,128)(2,1)} %pad_maximum_fusion.23), channel_id=1, source_target_pairs={{0,2},{1,3},{2,0},{3,1},{4,6},{5,7},{6,4},{7,5},{8,10},{9,11},{10,... | collective-permute-start | bytes 2985992 | tf_op jit(solution)/shard_map/ppermute | solution.py:381
  1489.4 112.5 %collective-permute-start.180 = (bf16[576,1152]{1,0:T(8,128)(2,1)}, bf16[576,1152]{1,0:T(8,128)(2,1)}, u32[]{:S(2)}, u32[]{:S(2)}) collective-permute-start(bf16[576,1152]{1,0:T(8,128)(2,1)} %pad_maximum_fusion.15), channel_id=1, source_target_pairs={{0,1},{1,0},{2,3},{3,2},{4,5},{5,4},{6,7},{7,6},{8,9},{9,8},{10,11... | collective-permute-start | bytes 3981320 | tf_op jit(solution)/shard_map/ppermute | solution.py:381
  1593.8 46.0 %collective-permute-start.163 = (bf16[576,1152]{1,0:T(8,128)(2,1)}, bf16[576,1152]{1,0:T(8,128)(2,1)}, u32[]{:S(2)}, u32[]{:S(2)}) collective-permute-start(bf16[576,1152]{1,0:T(8,128)(2,1)} %pad_maximum_fusion.11), channel_id=1, source_target_pairs={{0,2},{1,3},{2,0},{3,1},{4,6},{5,7},{6,4},{7,5},{8,10},{9,11},{10,... | collective-permute-start | bytes 3981320 | tf_op jit(solution)/shard_map/ppermute | solution.py:381
  1601.9 40.8 %collective-permute-start.167 = (bf16[576,1152]{1,0:T(8,128)(2,1)}, bf16[576,1152]{1,0:T(8,128)(2,1)S(1)}, u32[]{:S(2)}, u32[]{:S(2)}) collective-permute-start(bf16[576,1152]{1,0:T(8,128)(2,1)} %convolution_convert_fusion.12), channel_id=1, source_target_pairs={{0,4},{4,0},{8,12},{12,8},{16,20},{20,16},{24,28},{28,24},{1,5},{5... | collective-permute-start | bytes 3981320 | tf_op jit(solution)/shard_map/ppermute | solution.py:381
  1622.7 168.1 %collective-permute-start.166 = (bf16[576,1152]{1,0:T(8,128)(2,1)}, bf16[576,1152]{1,0:T(8,128)(2,1)}, u32[]{:S(2)}, u32[]{:S(2)}) collective-permute-start(bf16[576,1152]{1,0:T(8,128)(2,1)} %convolution_convert_fusion.14), channel_id=1, source_target_pairs={{0,4},{4,0},{8,12},{12,8},{16,20},{20,16},{24,28},{28,24},{1,5},{5... | collective-permute-start | bytes 3981320 | tf_op jit(solution)/shard_map/ppermute | solution.py:381
  1647.4 168.0 %collective-permute-start.146 = (bf16[576,1152]{1,0:T(8,128)(2,1)}, bf16[576,1152]{1,0:T(8,128)(2,1)}, u32[]{:S(2)}, u32[]{:S(2)}) collective-permute-start(bf16[576,1152]{1,0:T(8,128)(2,1)} %convolution_convert_fusion.30), channel_id=1, source_target_pairs={{0,4},{4,0},{8,12},{12,8},{16,20},{20,16},{24,28},{28,24},{1,5},{5... | collective-permute-start | bytes 3981320 | tf_op jit(solution)/shard_map/ppermute | solution.py:381
  1654.1 46.2 %collective-permute-start.184 = (bf16[288,1152]{1,0:T(8,128)(2,1)S(1)}, bf16[288,1152]{1,0:T(8,128)(2,1)S(1)}, u32[]{:S(2)}, u32[]{:S(2)}) collective-permute-start(bf16[288,1152]{1,0:T(8,128)(2,1)S(1)} %broadcast_select_fusion), channel_id=1, source_target_pairs={{0,16},{4,20},{8,24},{12,28},{16,0},{20,4},{24,8},{28,12},{1,17},{... | collective-permute-start | bytes 1990664 | tf_op jit(solution)/shard_map/ppermute | solution.py:381
  1662.7 51.8 %collective-permute-start.164 = (bf16[288,1152]{1,0:T(8,128)(2,1)S(1)}, bf16[288,1152]{1,0:T(8,128)(2,1)S(1)}, u32[]{:S(2)}, u32[]{:S(2)}) collective-permute-start(bf16[288,1152]{1,0:T(8,128)(2,1)S(1)} %broadcast_select_fusion.2), channel_id=1, source_target_pairs={{0,16},{4,20},{8,24},{12,28},{16,0},{20,4},{24,8},{28,12},{1,17},{... | collective-permute-start | bytes 1990664 | tf_op jit(solution)/shard_map/ppermute | solution.py:381
  1665.6 49.8 %collective-permute-start.169 = (bf16[288,1152]{1,0:T(8,128)(2,1)S(1)}, bf16[288,1152]{1,0:T(8,128)(2,1)S(1)}, u32[]{:S(2)}, u32[]{:S(2)}) collective-permute-start(bf16[288,1152]{1,0:T(8,128)(2,1)S(1)} %get-tuple-element.152), channel_id=1, source_target_pairs={{0,2},{1,3},{2,0},{3,1},{4,6},{5,7},{6,4},{7,5},{8,10},{9,11},{10,... | collective-permute-start | bytes 1990664 | tf_op jit(solution)/shard_map/ppermute | solution.py:381
  1717.1 37.0 %collective-permute-start.110 = (bf16[576,864]{1,0:T(8,128)(2,1)S(1)}, bf16[576,864]{1,0:T(8,128)(2,1)S(1)}, u32[]{:S(2)}, u32[]{:S(2)}) collective-permute-start(bf16[576,864]{1,0:T(8,128)(2,1)S(1)} %pad_maximum_fusion.20), channel_id=1, source_target_pairs={{0,1},{1,0},{2,3},{3,2},{4,5},{5,4},{6,7},{7,6},{8,9},{9,8},{10,11... | collective-permute-start | bytes 2985992 | tf_op jit(solution)/shard_map/ppermute | solution.py:381
  1755.2 39.6 %collective-permute-start.170 = (bf16[576,1152]{1,0:T(8,128)(2,1)}, bf16[576,1152]{1,0:T(8,128)(2,1)}, u32[]{:S(2)}, u32[]{:S(2)}) collective-permute-start(bf16[576,1152]{1,0:T(8,128)(2,1)} %pad_maximum_fusion.13), channel_id=1, source_target_pairs={{0,1},{1,0},{2,3},{3,2},{4,5},{5,4},{6,7},{7,6},{8,9},{9,8},{10,11... | collective-permute-start | bytes 3981320 | tf_op jit(solution)/shard_map/ppermute | solution.py:381
  1790.7 46.2 %collective-permute-start.153 = (bf16[576,1152]{1,0:T(8,128)(2,1)}, bf16[576,1152]{1,0:T(8,128)(2,1)S(1)}, u32[]{:S(2)}, u32[]{:S(2)}) collective-permute-start(bf16[576,1152]{1,0:T(8,128)(2,1)} %pad_maximum_fusion.9), channel_id=1, source_target_pairs={{0,2},{1,3},{2,0},{3,1},{4,6},{5,7},{6,4},{7,5},{8,10},{9,11},{10,... | collective-permute-start | bytes 3981320 | tf_op jit(solution)/shard_map/ppermute | solution.py:381
  (729 other events, 7515.7 us)

commit v2 on v0

--- a/solution.py
+++ b/solution.py
@@ -1,6 +1,10 @@
+import functools
+
 import jax
 import jax.numpy as jnp
 from jax import lax
+from jax.experimental import pallas as pl
+from jax.experimental.pallas import tpu as pltpu
 from jax.sharding import PartitionSpec as P
 
 HEAD_DIM = 72
@@ -258,7 +262,7 @@
     return (grad_input, weight_terms, modulation_grad, bias_terms)
 
 
-def local(
+def tensor_parallel(
     tokens,
     conditioning,
     ada_weight,
@@ -376,6 +380,1253 @@
     )
 
 
+def exchange(values, axis, mask):
+    count = lax.axis_size(axis)
+    return lax.ppermute(values, axis, [(index, index ^ mask) for index in range(count)])
+
+
+def add_low(first, second):
+    return (first.astype(jnp.float32) + second.astype(jnp.float32)).astype(jnp.bfloat16)
+
+
+def after(values, *others):
+    return lax.optimization_barrier((values,) + others)[0]
+
+
+def together(*values):
+    return lax.optimization_barrier(values)
+
+
+def over_depth(values, place):
+    groups = [list(range(core, place.row_count, 2)) for core in range(2)]
+    return lax.all_to_all(
+        values, "row", split_axis=0, concat_axis=0, tiled=True, axis_index_groups=groups
+    )
+
+
+def swap(values):
+    return exchange(values, "row", 1)
+
+
+class Gathering:
+    def __init__(self, place):
+        self.place = place
+        self.held = ()
+        self.plane = ()
+        self.corner = ()
+        self.sent = ()
+        self.done = []
+
+    def step(self, shard, *gates):
+        groups = (self.held, self.plane, self.corner)
+        values = list(together(*[value for group in groups for value in group], *gates))
+        held, plane, corner = [[values.pop(0) for _ in group] for group in groups]
+        across, above = ([], [])
+        if held:
+            across.append(held[0])
+            above.append(held[0])
+        if plane:
+            size = plane[0].shape[0]
+            across.append(plane[2][size // 2 : size])
+            above.append(plane[1][: size // 2])
+        across = [jnp.concatenate(across, 0)] if across else []
+        above = [jnp.concatenate(above, 0)] if above else []
+        self.sent = tuple(across + above)
+        self.held = ()
+        if shard is not None:
+            self.held = (over_depth(after(shard, *self.sent), self.place),)
+        if corner:
+            own = pack_blocks(after(corner, *self.sent))
+            self.done.append((own, swap(own)))
+        met = tuple(
+            exchange(value[0], "col", mask) for mask, value in ((1, across), (2, above)) if value
+        )
+        self.corner = tuple(plane) + met if plane else ()
+        self.plane = tuple(held) + met if held else ()
+
+
+def scatter_corner(blocks):
+    held, across_upper, across_first, above_first, above_lower = blocks
+    return (
+        held,
+        across_upper,
+        exchange(across_first, "col", 1),
+        exchange(above_first, "col", 2),
+        above_lower,
+    )
+
+
+def scatter_sides(blocks):
+    held, across_upper, across_first, above_first, above_lower = blocks
+    half = across_upper.shape[0]
+    return (
+        add_low(across_upper, above_first[half:]),
+        add_low(above_lower, across_first[half:]),
+    )
+
+
+def scatter_plane(blocks, sides):
+    held, _, across_first, above_first, _ = blocks
+    across, above = sides
+    return (held, exchange(across, "col", 1), across_first, above_first, exchange(above, "col", 2))
+
+
+def add_all(pieces, place):
+    count = place.row_count // 2
+    pieces = pieces.reshape((count, -1) + pieces.shape[1:])
+    return jnp.sum(pieces.astype(jnp.float32), 0)
+
+
+class Place:
+    def __init__(self):
+        self.row = lax.axis_index("row")
+        self.col = lax.axis_index("col")
+        self.row_count = lax.axis_size("row")
+        self.col_count = lax.axis_size("col")
+        self.core = self.row & 1
+        self.depth_masks = []
+        mask = 2
+        while mask < self.row_count:
+            self.depth_masks.append(mask)
+            mask *= 2
+
+
+def mine_first(halves, place, axis):
+    return jnp.where(place.core == 1, jnp.flip(halves, axis), halves)
+
+
+def to_halves(features, place):
+    width = features.shape[-1]
+    lead = features.shape[:-1]
+    split_up = features.reshape(lead + (place.row_count // 2, 2, width // place.row_count))
+    halves = jnp.swapaxes(split_up, -3, -2).reshape(lead + (2, width // 2))
+    return mine_first(halves, place, len(lead))
+
+
+def from_halves(halves, place):
+    lead = halves.shape[:-2]
+    half = halves.shape[-1]
+    halves = mine_first(halves, place, len(lead))
+    split_up = halves.reshape(lead + (2, place.row_count // 2, half // (place.row_count // 2)))
+    return jnp.swapaxes(split_up, -3, -2).reshape(lead + (2 * half,))
+
+
+def relative(stacked, place):
+    return [
+        lax.dynamic_index_in_dim(stacked, place.col ^ step, 0, keepdims=False)
+        for step in range(place.col_count)
+    ]
+
+
+def absolute(blocks, place):
+    return jnp.stack(relative(jnp.stack(blocks), place))
+
+
+def trade(blocks):
+    return [
+        block if step == 0 else exchange(block, "col", step) for step, block in enumerate(blocks)
+    ]
+
+
+PLAIN = ((1,), (0,))
+TURNED = ((1,), (1,))
+SUMMED = ((0,), (0,))
+VMEM_BYTES = 58 * 1024 * 1024
+LANES = 128
+IN_HBM = pl.BlockSpec(memory_space=pl.ANY)
+SMALL_COST = pl.CostEstimate(flops=0, bytes_accessed=0, transcendentals=0)
+
+
+def dot(left, right, dims):
+    return lax.dot_general(left, right, (dims, ((), ())), preferred_element_type=jnp.float32)
+
+
+def round_up(value):
+    return -(-value // LANES) * LANES
+
+
+def whole(shape):
+    return pl.BlockSpec(shape, lambda step: (0,) * len(shape))
+
+
+def stepped(shape):
+    return pl.BlockSpec((1,) + shape, lambda step: (step,) + (0,) * len(shape))
+
+
+def of(shape, dtype):
+    return jax.ShapeDtypeStruct(shape, dtype)
+
+
+def norm_parts(stream_ref):
+    first, second = (stream_ref[0], stream_ref[1])
+    count = 2 * first.shape[1]
+    average = (jnp.sum(first, 1, keepdims=True) + jnp.sum(second, 1, keepdims=True)) / count
+    first, second = (first - average, second - average)
+    variance = (
+        jnp.sum(first * first, 1, keepdims=True) + jnp.sum(second * second, 1, keepdims=True)
+    ) / count
+    inverse = lax.rsqrt(variance + epsilon)
+    return (first * inverse, second * inverse, inverse)
+
+
+def norm_grads(stream_ref, acc, mod_ref, scale_row, grad_ref, out_ref, small_ref):
+    normed = norm_parts(stream_ref)
+    inverse = normed[2]
+    count = 2 * normed[0].shape[1]
+    weighted = []
+    for half in range(2):
+        grad_input = acc[half]
+        small_ref[half, 0:1, :] = jnp.sum(grad_input, 0, keepdims=True)
+        small_ref[half, 1:2, :] = jnp.sum(grad_input * normed[half], 0, keepdims=True)
+        weighted.append(grad_input * (1.0 + mod_ref[half, scale_row : scale_row + 1, :]))
+    first = sum(jnp.sum(value, 1, keepdims=True) for value in weighted) / count
+    second = (
+        sum(jnp.sum(value * normed[half], 1, keepdims=True) for half, value in enumerate(weighted))
+        / count
+    )
+    for half in range(2):
+        out_ref[half] = grad_ref[half] + inverse * (
+            weighted[half] - first - normed[half] * second
+        )
+
+
+def same_place(size, period):
+    row = lax.broadcasted_iota(jnp.int32, (size, size), 0)
+    column = lax.broadcasted_iota(jnp.int32, (size, size), 1)
+    return (row % period) == (column % period)
+
+
+def attention_kernel(size, period, steps, *refs):
+    stream_ref, mod_ref, bias_ref, added_ref = refs[:4]
+    weights = refs[4:6]
+    mid_ref, mine_ref, other_ref, qkv_ref, heads_ref, log_ref, out_ref, acc = refs[6:]
+    input_refs = (mine_ref, other_ref)
+    step = pl.program_id(0)
+    tokens = stream_ref.shape[1]
+    used = qkv_ref.shape[2]
+    padded = heads_ref.shape[2]
+    columns = weights[0].shape[2]
+    width = columns // 4
+    count = width // HEAD_DIM
+    scale = HEAD_DIM ** (-0.5)
+
+    @pl.when(step == 0)
+    def _():
+        normed = norm_parts(stream_ref)
+        for half in range(2):
+            input_refs[half][...] = (
+                normed[half] * (1.0 + mod_ref[half, 1:2, :]) + mod_ref[half, 0:1, :]
+            ).astype(jnp.bfloat16)
+        acc[...] = jnp.zeros_like(acc)
+
+    rows = dot(input_refs[0][...], weights[0][0, :, :used], PLAIN)
+    rows = rows + dot(input_refs[1][...], weights[1][0, :, :used], PLAIN) + bias_ref[0]
+    lane = lax.broadcasted_iota(jnp.int32, rows.shape, 1)
+    qkv_ref[0] = jnp.where(lane < 3 * width, rows, 0.0).astype(jnp.bfloat16)
+    log_lane = lax.broadcasted_iota(jnp.int32, (size, LANES), 1)
+    for group in range(tokens // size):
+        block = qkv_ref[0, group * size : (group + 1) * size, :]
+        outs = [jnp.zeros((size, padded - width), jnp.float32)]
+        logs = jnp.zeros((size, LANES), jnp.float32)
+        for head in range(count):
+            start = head * HEAD_DIM
+            query = block[:, start : start + HEAD_DIM]
+            key = block[:, width + start : width + start + HEAD_DIM]
+            value = block[:, 2 * width + start : 2 * width + start + HEAD_DIM]
+            scores = dot(query, key, TURNED) * scale
+            if period:
+                scores = jnp.where(same_place(size, period), scores, -1e30)
+            largest = jnp.max(scores, 1, keepdims=True)
+            weight = jnp.exp(scores - largest)
+            total = jnp.sum(weight, 1, keepdims=True)
+            probs = (weight * (1.0 / total)).astype(jnp.bfloat16)
+            outs.append(dot(probs, value, PLAIN))
+            logs = jnp.where(log_lane == head, largest + jnp.log(total), logs)
+        heads_ref[0, group * size : (group + 1) * size, :] = jnp.concatenate(outs, 1).astype(
+            jnp.bfloat16
+        )
+        log_ref[0, group * size : (group + 1) * size, :] = logs
+    for half in range(2):
+        acc[half] += dot(heads_ref[0], weights[half][0, :, columns - padded :], TURNED)
+
+    @pl.when(step == steps - 1)
+    def _():
+        for half in range(2):
+            total = acc[half] + added_ref[half]
+            out_ref[half] = total.astype(jnp.bfloat16)
+            mid_ref[half] = stream_ref[half] + mod_ref[half, 2:3, :] * total
+
+
+def attention_forward(stream, modulation, weights, bias, added, size, period):
+    steps = weights[0].shape[0]
+    _, tokens, half = stream.shape
+    columns = weights[0].shape[2]
+    used = round_up(3 * columns // 4)
+    padded = columns - (3 * columns // 4) // LANES * LANES
+    bf16, f32 = (jnp.bfloat16, jnp.float32)
+    return pl.pallas_call(
+        functools.partial(attention_kernel, size, period, steps),
+        grid=(steps,),
+        in_specs=[
+            whole(stream.shape),
+            whole(modulation.shape),
+            stepped((1, used)),
+            whole(added.shape),
+        ]
+        + [stepped((half, columns))] * 2,
+        out_specs=[
+            whole(stream.shape),
+            whole((tokens, half)),
+            whole((tokens, half)),
+            stepped((tokens, used)),
+            stepped((tokens, padded)),
+            stepped((tokens, LANES)),
+            whole(stream.shape),
+        ],
+        out_shape=[
+            of(stream.shape, f32),
+            of((tokens, half), bf16),
+            of((tokens, half), bf16),
+            of((steps, tokens, used), bf16),
+            of((steps, tokens, padded), bf16),
+            of((steps, tokens, LANES), f32),
+            of(stream.shape, bf16),
+        ],
+        scratch_shapes=[
+            pltpu.VMEM(stream.shape, f32),
+        ],
+        compiler_params=pltpu.CompilerParams(vmem_limit_bytes=VMEM_BYTES),
+        cost_estimate=SMALL_COST,
+        name="attention_forward",
+    )(stream, modulation, bias, added, *weights)
+
+
+def mlp_kernel(steps, *refs):
+    mid_ref, mod_ref, bias_ref, added_ref = refs[:4]
+    hidden, output = (refs[4:6], refs[6:8])
+    stream_ref, mine_ref, other_ref, active_ref, slope_ref, out_ref, acc = refs[8:]
+    input_refs = (mine_ref, other_ref)
+    step = pl.program_id(0)
+
+    @pl.when(step == 0)
+    def _():
+        normed = norm_parts(mid_ref)
+        for half in range(2):
+            input_refs[half][...] = (
+                normed[half] * (1.0 + mod_ref[half, 4:5, :]) + mod_ref[half, 3:4, :]
+            ).astype(jnp.bfloat16)
+        acc[...] = jnp.zeros_like(acc)
+
+    pre = dot(input_refs[0][...], hidden[0][0], PLAIN)
+    pre = pre + dot(input_refs[1][...], hidden[1][0], PLAIN) + bias_ref[0]
+    root = (2.0 / jnp.pi) ** 0.5
+    square = pre * pre
+    bend = jnp.tanh(pre * (root + root * 0.044715 * square))
+    active_ref[0] = (0.5 * pre * (1.0 + bend)).astype(jnp.bfloat16)
+    slope_ref[0] = (
+        0.5 * (1.0 + bend)
+        + 0.5 * pre * (1.0 - bend * bend) * (root + 3.0 * root * 0.044715 * square)
+    ).astype(jnp.bfloat16)
+    for half in range(2):
+        acc[half] += dot(active_ref[0], output[half][0], TURNED)
+
+    @pl.when(step == steps - 1)
+    def _():
+        for half in range(2):
+            total = acc[half] + added_ref[half]
+            out_ref[half] = total.astype(jnp.bfloat16)
+            stream_ref[half] = mid_ref[half] + mod_ref[half, 5:6, :] * total
+
+
+def mlp_forward(mid, modulation, hidden, output, bias, added):
+    steps = hidden[0].shape[0]
+    _, tokens, half = mid.shape
+    columns = hidden[0].shape[2]
+    bf16, f32 = (jnp.bfloat16, jnp.float32)
+    return pl.pallas_call(
+        functools.partial(mlp_kernel, steps),
+        grid=(steps,),
+        in_specs=[
+            whole(mid.shape),
+            whole(modulation.shape),
+            stepped((1, columns)),
+            whole(added.shape),
+        ]
+        + [stepped((half, columns))] * 4,
+        out_specs=[
+            whole(mid.shape),
+            whole((tokens, half)),
+            whole((tokens, half)),
+            stepped((tokens, columns)),
+            stepped((tokens, columns)),
+            whole(mid.shape),
+        ],
+        out_shape=[
+            of(mid.shape, f32),
+            of((tokens, half), bf16),
+            of((tokens, half), bf16),
+            of((steps, tokens, columns), bf16),
+            of((steps, tokens, columns), bf16),
+            of(mid.shape, bf16),
+        ],
+        scratch_shapes=[
+            pltpu.VMEM(mid.shape, f32),
+        ],
+        compiler_params=pltpu.CompilerParams(vmem_limit_bytes=VMEM_BYTES),
+        cost_estimate=SMALL_COST,
+        name="mlp_forward",
+    )(mid, modulation, bias, added, *hidden, *output)
+
+
+def mlp_back_kernel(steps, *refs):
+    grad_ref, mid_ref, out_ref, slope_ref, mod_ref = refs[:5]
+    hidden, output = (refs[5:7], refs[7:9])
+    grad_mid_ref, mine_ref, other_ref, grad_pre_ref, small_ref, sum_ref, acc = refs[9:]
+    grad_mlp_refs = (mine_ref, other_ref)
+    step = pl.program_id(0)
+
+    @pl.when(step == 0)
+    def _():
+        for half in range(2):
+            grad = grad_ref[half]
+            scaled = (grad * mod_ref[half, 5:6, :]).astype(jnp.bfloat16)
+            grad_mlp_refs[half][...] = scaled
+            small_ref[half, 2:3, :] = jnp.sum(
+                grad * out_ref[half].astype(jnp.float32), 0, keepdims=True
+            )
+            small_ref[half, 3:4, :] = jnp.sum(scaled.astype(jnp.float32), 0, keepdims=True)
+        acc[...] = jnp.zeros_like(acc)
+
+    grad_act = dot(grad_mlp_refs[0][...], output[0][0], PLAIN)
+    grad_act = grad_act + dot(grad_mlp_refs[1][...], output[1][0], PLAIN)
+    grad_pre = (grad_act * slope_ref[0].astype(jnp.float32)).astype(jnp.bfloat16)
+    grad_pre_ref[0] = grad_pre
+    sum_ref[0] = jnp.sum(grad_pre.astype(jnp.float32), 0, keepdims=True)
+    for half in range(2):
+        acc[half] += dot(grad_pre, hidden[half][0], TURNED)
+
+    @pl.when(step == steps - 1)
+    def _():
+        norm_grads(mid_ref, acc, mod_ref, 4, grad_ref, grad_mid_ref, small_ref)
+
+
+def mlp_backward(grad, mid, out, slope, modulation, hidden, output):
+    steps = hidden[0].shape[0]
+    _, tokens, half = mid.shape
+    columns = hidden[0].shape[2]
+    bf16, f32 = (jnp.bfloat16, jnp.float32)
+    return pl.pallas_call(
+        functools.partial(mlp_back_kernel, steps),
+        grid=(steps,),
+        in_specs=[
+            whole(mid.shape),
+            whole(mid.shape),
+            whole(mid.shape),
+            stepped((tokens, columns)),
+            whole(modulation.shape),
+        ]
+        + [stepped((half, columns))] * 4,
+        out_specs=[
+            whole(mid.shape),
+            whole((tokens, half)),
+            whole((tokens, half)),
+            stepped((tokens, columns)),
+            whole((2, 8, half)),
+            stepped((1, columns)),
+        ],
+        out_shape=[
+            of(mid.shape, f32),
+            of((tokens, half), bf16),
+            of((tokens, half), bf16),
+            of((steps, tokens, columns), bf16),
+            of((2, 8, half), f32),
+            of((steps, 1, columns), f32),
+        ],
+        scratch_shapes=[
+            pltpu.VMEM(mid.shape, f32),
+        ],
+        compiler_params=pltpu.CompilerParams(vmem_limit_bytes=VMEM_BYTES),
+        cost_estimate=SMALL_COST,
+        name="mlp_backward",
+    )(grad, mid, out, slope, modulation, *hidden, *output)
+
+
+def attention_back_kernel(size, period, steps, *refs):
+    grad_ref, stream_ref, out_ref, qkv_ref, log_ref, mod_ref = refs[:6]
+    weights = refs[6:8]
+    grad_in_ref, mine_ref, other_ref, grad_qkv_ref, small_ref, sum_ref, acc = refs[8:]
+    grad_attn_refs = (mine_ref, other_ref)
+    step = pl.program_id(0)
+    tokens = stream_ref.shape[1]
+    used = qkv_ref.shape[2]
+    columns = weights[0].shape[2]
+    width = columns // 4
+    padded = columns - (3 * width) // LANES * LANES
+    count = width // HEAD_DIM
+    scale = HEAD_DIM ** (-0.5)
+
+    @pl.when(step == 0)
+    def _():
+        for half in range(2):
+            grad = grad_ref[half]
+            scaled = (grad * mod_ref[half, 2:3, :]).astype(jnp.bfloat16)
+            grad_attn_refs[half][...] = scaled
+            small_ref[half, 2:3, :] = jnp.sum(
+                grad * out_ref[half].astype(jnp.float32), 0, keepdims=True
+            )
+            small_ref[half, 3:4, :] = jnp.sum(scaled.astype(jnp.float32), 0, keepdims=True)
+        acc[...] = jnp.zeros_like(acc)
+
+    grad_heads = dot(grad_attn_refs[0][...], weights[0][0, :, columns - padded :], PLAIN)
+    grad_heads = grad_heads + dot(grad_attn_refs[1][...], weights[1][0, :, columns - padded :], PLAIN)
+    grad_heads = grad_heads.astype(jnp.bfloat16)
+    total = jnp.zeros((1, used), jnp.float32)
+    for group in range(tokens // size):
+        rows = slice(group * size, (group + 1) * size)
+        block = qkv_ref[0, rows, :]
+        logs = log_ref[0, rows, :]
+        grad_queries, grad_keys, grad_values = ([], [], [])
+        for head in range(count):
+            start = head * HEAD_DIM
+            query = block[:, start : start + HEAD_DIM]
+            key = block[:, width + start : width + start + HEAD_DIM]
+            value = block[:, 2 * width + start : 2 * width + start + HEAD_DIM]
+            start = padded - width + head * HEAD_DIM
+            grad_out = grad_heads[rows, start : start + HEAD_DIM]
+            scores = dot(query, key, TURNED) * scale - logs[:, head : head + 1]
+            if period:
+                scores = jnp.where(same_place(size, period), scores, -1e30)
+            probs = jnp.exp(scores)
+            grad_probs = dot(grad_out, value, TURNED)
+            delta = jnp.sum(probs * grad_probs, 1, keepdims=True)
+            grad_scores = (probs * (grad_probs - delta)).astype(jnp.bfloat16)
+            grad_values.append(dot(probs.astype(jnp.bfloat16), grad_out, SUMMED))
+            grad_queries.append(dot(grad_scores, key, PLAIN) * scale)
+            grad_keys.append(dot(grad_scores, query, SUMMED) * scale)
+        rest = [jnp.zeros((size, used - 3 * width), jnp.float32)]
+        joined = jnp.concatenate(grad_queries + grad_keys + grad_values + rest, 1)
+        joined = joined.astype(jnp.bfloat16)
+        grad_qkv_ref[0, rows, :] = joined
+        total = total + jnp.sum(joined.astype(jnp.float32), 0, keepdims=True)
+    sum_ref[0] = total
+    for half in range(2):
+        acc[half] += dot(grad_qkv_ref[0], weights[half][0, :, :used], TURNED)
+
+    @pl.when(step == steps - 1)
+    def _():
+        norm_grads(stream_ref, acc, mod_ref, 1, grad_ref, grad_in_ref, small_ref)
+
+
+def attention_backward(grad, stream, out, qkv, logs, modulation, weights, size, period):
+    steps = weights[0].shape[0]
+    _, tokens, half = stream.shape
+    columns = weights[0].shape[2]
+    used = qkv.shape[2]
+    bf16, f32 = (jnp.bfloat16, jnp.float32)
+    return pl.pallas_call(
+        functools.partial(attention_back_kernel, size, period, steps),
+        grid=(steps,),
+        in_specs=[
+            whole(stream.shape),
+            whole(stream.shape),
+            whole(stream.shape),
+            stepped((tokens, used)),
+            stepped((tokens, LANES)),
+            whole(modulation.shape),
+        ]
+        + [stepped((half, columns))] * 2,
+        out_specs=[
+            whole(stream.shape),
+            whole((tokens, half)),
+            whole((tokens, half)),
+            stepped((tokens, used)),
+            whole((2, 8, half)),
+            stepped((1, used)),
+        ],
+        out_shape=[
+            of(stream.shape, f32),
+            of((tokens, half), bf16),
+            of((tokens, half), bf16),
+            of((steps, tokens, used), bf16),
+            of((2, 8, half), f32),
+            of((steps, 1, used), f32),
+        ],
+        scratch_shapes=[
+            pltpu.VMEM(stream.shape, f32),
+        ],
+        compiler_params=pltpu.CompilerParams(vmem_limit_bytes=VMEM_BYTES),
+        cost_estimate=SMALL_COST,
+        name="attention_backward",
+    )(grad, stream, out, qkv, logs, modulation, *weights)
+
+
+def weight_kernel(pairs, overlap, steps, *refs):
+    inputs = refs[: 4 * pairs]
+    outs = refs[4 * pairs : 4 * pairs + 5]
+    turned = refs[4 * pairs + 5 : 6 * pairs + 5]
+    buffer, sems = refs[6 * pairs + 5 :]
+    step = pl.program_id(0)
+    slot = step % 2
+    for pair in range(pairs):
+        mine, theirs, _, _ = inputs[4 * pair : 4 * pair + 4]
+
+        @pl.when(step == 0)
+        def _():
+            turned[2 * pair][...] = mine[...].T
+            turned[2 * pair + 1][...] = theirs[...].T
+
+    @pl.when(step >= 2)
+    def _():
+        pltpu.make_async_copy(buffer.at[slot], outs[0], sems.at[slot]).wait()
+
+    sums = []
+    for pair in range(pairs):
+        _, _, mine, theirs = inputs[4 * pair : 4 * pair + 4]
+        total = dot(turned[2 * pair][...], mine[0], PLAIN)
+        sums.append(total + dot(turned[2 * pair + 1][...], theirs[0], PLAIN))
+    if pairs == 1:
+        buffer[slot] = sums[0].astype(jnp.bfloat16)
+    else:
+        first = sums[0].shape[1] - overlap
+        buffer[slot, :, :first] = sums[0][:, :first].astype(jnp.bfloat16)
+        buffer[slot, :, first : first + overlap] = (
+            sums[0][:, first:] + sums[1][:, :overlap]
+        ).astype(jnp.bfloat16)
+        buffer[slot, :, first + overlap :] = sums[1][:, overlap:].astype(jnp.bfloat16)
+    for index in range(steps):
+
+        @pl.when(step == index)
+        def _():
+            source = buffer.at[index % 2]
+            sem = sems.at[index % 2]
+            if index == 0:
+                pltpu.make_async_copy(source, outs[0], sem).start()
+            else:
+                rows = outs[1].shape[0]
+                upper, lower = (
+                    (outs[1], outs[2].at[:rows]),
+                    (outs[3].at[:rows], outs[4]),
+                    (outs[3].at[rows:], outs[2].at[rows:]),
+                )[index - 1]
+                pltpu.make_async_copy(source.at[:rows], upper, sem).start()
+                pltpu.make_async_copy(source.at[rows:], lower, sem).start()
+
+    @pl.when(step == steps - 1)
+    def _():
+        for index in range(2):
+            pltpu.make_async_copy(buffer.at[index], outs[0], sems.at[index]).wait()
+
+
+def weight_grads(columns, overlap, *pairs, flops=0):
+    steps, tokens, _ = pairs[0][2].shape
+    half = pairs[0][1].shape[1]
+    bf16 = jnp.bfloat16
+    specs, values, turned = ([], [], [])
+    for mine, theirs, blocks, their_blocks in pairs:
+        specs += [
+            whole(mine.shape),
+            whole(theirs.shape),
+            stepped(blocks.shape[1:]),
+            stepped(blocks.shape[1:]),
+        ]
+        values += [mine, theirs, blocks, their_blocks]
+        turned += [pltpu.VMEM((half, tokens), bf16)] * 2
+    return pl.pallas_call(
+        functools.partial(weight_kernel, len(pairs), overlap, steps),
+        grid=(steps,),
+        in_specs=specs,
+        out_specs=[IN_HBM] * 5,
+        out_shape=[
+            of((rows, columns), bf16) for rows in (half, half // 2, half, half, half // 2)
+        ],
+        scratch_shapes=turned
+        + [pltpu.VMEM((2, half, columns), bf16), pltpu.SemaphoreType.DMA((2,))],
+        compiler_params=pltpu.CompilerParams(vmem_limit_bytes=VMEM_BYTES),
+        cost_estimate=pl.CostEstimate(flops=flops, bytes_accessed=0, transcendentals=0),
+        name="weight_grads",
+    )(*values)
+
+
+def pack_kernel(held, across, above, lower, upper, out, buffer, sems):
+    size = held.shape[0]
+    half = size // 2
+    corner = pl.ds(lower.shape[0] - half, half)
+    incoming = [
+        pltpu.make_async_copy(source, target, sems.at[index])
+        for index, (source, target) in enumerate(
+            (
+                (held, buffer.at[0]),
+                (across.at[:size], buffer.at[1]),
+                (above.at[:size], buffer.at[2]),
+                (upper.at[corner], buffer.at[3, :half]),
+                (lower.at[corner], buffer.at[3, half:]),
+            )
+        )
+    ]
+    outgoing = [
+        pltpu.make_async_copy(buffer.at[index], out.at[index], sems.at[5 + index])
+        for index in range(4)
+    ]
+    for copy in incoming:
+        copy.start()
+    for index in range(3):
+        incoming[index].wait()
+        outgoing[index].start()
+    incoming[3].wait()
+    incoming[4].wait()
+    outgoing[3].start()
+    for copy in outgoing:
+        copy.wait()
+
+
+def pack_blocks(blocks):
+    shape = (4,) + blocks[0].shape
+    return pl.pallas_call(
+        pack_kernel,
+        in_specs=[IN_HBM] * 5,
+        out_specs=IN_HBM,
+        out_shape=of(shape, jnp.bfloat16),
+        scratch_shapes=[pltpu.VMEM(shape, jnp.bfloat16), pltpu.SemaphoreType.DMA((9,))],
+        compiler_params=pltpu.CompilerParams(vmem_limit_bytes=VMEM_BYTES // 4),
+        cost_estimate=SMALL_COST,
+        name="pack_blocks",
+    )(*blocks)
+
+
+def placing_matrix(core, part, block, half, shape):
+    feature = lax.broadcasted_iota(jnp.int32, shape, 0) + block * shape[0]
+    target = lax.broadcasted_iota(jnp.int32, shape, 1)
+    row = feature // part
+    match = (row & 1) == (core ^ half)
+    match &= (row // 2) * part + (feature - row * part) == target
+    return jnp.where(match, 1.0, 0.0).astype(jnp.bfloat16)
+
+
+def enter_kernel(part, where_ref, *refs):
+    *blocks, out_ref = refs
+    shape = (blocks[0].shape[1], out_ref.shape[2])
+    for half in range(2):
+        total = None
+        for step, block in enumerate(blocks):
+            matrix = placing_matrix(where_ref[0], part, where_ref[1] ^ step, half, shape)
+            term = dot(block[...], matrix, PLAIN)
+            total = term if total is None else total + term
+        out_ref[half] = total
+
+
+def leave_kernel(part, where_ref, halves_ref, *outs):
+    shape = (outs[0].shape[1], halves_ref.shape[2])
+    halves = [halves_ref[half].astype(jnp.bfloat16) for half in range(2)]
+    for step, out in enumerate(outs):
+        total = None
+        for half in range(2):
+            matrix = placing_matrix(where_ref[0], part, where_ref[1] ^ step, half, shape)
+            term = dot(halves[half], matrix, TURNED)
+            total = term if total is None else total + term
+        out[...] = total.astype(jnp.bfloat16)
+
+
+def assemble_kernel(where_ref, *refs):
+    *blocks, out_ref = refs
+    for step, block in enumerate(blocks):
+        out_ref[where_ref[1] ^ step] = block[...].astype(out_ref.dtype)
+
+
+def reorder(kernel, values, outs, place):
+    in_vmem = pl.BlockSpec(memory_space=pltpu.VMEM)
+    where = jnp.stack((place.core, place.col)).astype(jnp.int32)
+    return pl.pallas_call(
+        kernel,
+        in_specs=[pl.BlockSpec(memory_space=pltpu.SMEM)] + [in_vmem] * len(values),
+        out_specs=[in_vmem] * len(outs),
+        out_shape=outs,
+        compiler_params=pltpu.CompilerParams(vmem_limit_bytes=VMEM_BYTES // 2),
+        cost_estimate=SMALL_COST,
+        name="reorder",
+    )(where, *values)
+
+
+def add_kernel(held, across_upper, across_first, above_first, above_lower, out):
+    rows = across_upper.shape[0]
+    for start, pair in ((0, (across_upper, above_first)), (rows, (across_first, above_lower))):
+        total = held[start : start + rows].astype(jnp.float32)
+        for value in pair:
+            total += value[:rows].astype(jnp.float32)
+        out[start : start + rows] = total.astype(jnp.bfloat16)
+
+
+def add_blocks(blocks):
+    in_vmem = pl.BlockSpec(memory_space=pltpu.VMEM)
+    return pl.pallas_call(
+        add_kernel,
+        in_specs=[in_vmem] * 5,
+        out_specs=in_vmem,
+        out_shape=of(blocks[0].shape, jnp.bfloat16),
+        compiler_params=pltpu.CompilerParams(vmem_limit_bytes=VMEM_BYTES // 2),
+        cost_estimate=SMALL_COST,
+        name="add_blocks",
+    )(*blocks)
+
+
+def token_parallel(
+    tokens,
+    conditioning,
+    ada_weight,
+    ada_bias,
+    qkv_weight,
+    attn_bias,
+    mixing_weight,
+    mixing_bias,
+    hidden_weight,
+    hidden_bias,
+    output_weight,
+    output_bias,
+    cotangent,
+):
+    place = Place()
+    col_width = ada_bias.shape[2]
+    row_width = conditioning.shape[1]
+    hidden_width = hidden_bias.shape[1]
+    layer_count = ada_bias.shape[0]
+    clip_count = conditioning.shape[0]
+    width = col_width * place.col_count
+
+    copies = (place.row_count // 2, 1)
+
+    def attn_shards(*gate):
+        first, second = together(qkv_weight, mixing_weight, *gate)[:2]
+        return [
+            jnp.tile(
+                jnp.concatenate(
+                    (
+                        first[depth].reshape(row_width, 3 * col_width),
+                        second[depth].reshape(col_width, row_width).T,
+                    ),
+                    1,
+                ),
+                copies,
+            )
+            for depth in range(layer_count)
+        ]
+
+    def hidden_shards(*gate):
+        value = after(hidden_weight, *gate)
+        return [
+            jnp.tile(value[depth].reshape(row_width, hidden_width), copies)
+            for depth in range(layer_count)
+        ]
+
+    def output_shards(*gate):
+        value = after(output_weight, *gate)
+        return [
+            jnp.tile(value[depth].reshape(hidden_width, row_width).T, copies)
+            for depth in range(layer_count)
+        ]
+
+    def arriving(held):
+        return trade(relative(held.reshape(clip_count, -1, col_width), place))
+
+    def entered(blocks):
+        outs = [of((2, blocks[0].shape[0], width // 2), jnp.float32)]
+        return reorder(functools.partial(enter_kernel, row_width), blocks, outs, place)[0]
+
+    gathering = Gathering(place)
+    attn_ready = attn_shards()
+    tokens = after(open_tokens(tokens, col_width), attn_ready[0])
+    cotangent = open_tokens(cotangent, col_width)
+    gathering.step(attn_ready[0])
+    token_blocks = arriving(tokens)
+    hidden_ready = hidden_shards(attn_ready[0])
+    hidden_ready, attn_ready, token_blocks = together(hidden_ready, attn_ready, token_blocks)
+    gathering.step(hidden_ready[0], *token_blocks)
+    conditioning, ada_weight, attn_bias, token_blocks, output_gate = after(
+        (conditioning, ada_weight, attn_bias, token_blocks, output_weight), *gathering.sent
+    )
+    output_weight = output_gate
+    output_ready = output_shards()
+    stream_first = entered(token_blocks)
+    ada_weight = ada_weight.reshape(layer_count, row_width, 6, col_width)
+    frame_part, places = tokens.shape[1:3]
+    frames, place_part = cotangent.shape[1:3]
+    period = 16 if place_part % 16 == 0 else place_part
+    groups = place_part // period
+    first_size = places
+    second_size = frames * period
+
+    half = width // 2
+
+    def leaving(halves):
+        outs = [of((halves.shape[1], col_width), jnp.bfloat16)] * place.col_count
+        return reorder(functools.partial(leave_kernel, row_width), [halves], outs, place)
+
+    def assembled(blocks, dtype):
+        outs = [of((len(blocks),) + blocks[0].shape, dtype)]
+        return reorder(assemble_kernel, blocks, outs, place)[0]
+
+    cond_act = jax.nn.silu(conditioning).astype(jnp.bfloat16)
+    modulation = matmul("cr,lrsk->clsk", cond_act, ada_weight)
+    modulation = modulation.reshape(clip_count, -1)
+    cut = modulation.shape[1]
+    own = [modulation] + [
+        value.reshape(clip_count, -1)
+        for value in (attn_bias, hidden_bias, mixing_bias, output_bias, ada_bias)
+    ]
+    met = lax.all_gather(jnp.concatenate(own, 1), ("row", "col"), axis=0)
+    met = met.reshape(place.row_count, place.col_count, clip_count, -1)
+    modulation = lax.dynamic_index_in_dim(met, place.col, 2, keepdims=False)[:, :, :cut]
+    modulation = jnp.sum(modulation, 0).reshape(-1, layer_count, 6, col_width)
+    rest = met[0, :, :, cut:]
+    vectors = []
+    for value in (attn_bias, hidden_bias, mixing_bias, output_bias, ada_bias):
+        size = value.size // clip_count
+        vectors.append(rest[:, :, :size].reshape((place.col_count,) + value.shape))
+        rest = rest[:, :, size:]
+    modulation = modulation + vectors.pop()
+    modulation = jnp.moveaxis(modulation, 0, 2).reshape(layer_count, 6, width)
+    modulation = jnp.swapaxes(to_halves(modulation, place), 1, 2)
+    attn_add, hidden_add, mixing_add, output_add = vectors
+    attn_add, hidden_add = (relative(value, place) for value in (attn_add, hidden_add))
+
+    def whole_vector(blocks):
+        joined = jnp.moveaxis(blocks, 0, 1).reshape(layer_count, width)
+        return to_halves(joined, place)
+
+    mixing_add = whole_vector(mixing_add)
+    output_add = whole_vector(output_add)
+
+    blank = jnp.zeros((round_up(3 * col_width) - 3 * col_width,), jnp.float32)
+
+    def biases_of(depth):
+        attn_rows = [
+            jnp.concatenate((block[depth, 0], jnp.zeros_like(block[depth, 0]), block[depth, 1], blank))
+            for block in attn_add
+        ]
+        return (
+            jnp.stack(attn_rows)[:, None, :],
+            mixing_add[depth][:, None, :],
+            jnp.stack([block[depth] for block in hidden_add])[:, None, :],
+            output_add[depth][:, None, :],
+        )
+
+    attn_biases, mixing_biases, hidden_biases, output_biases = zip(biases_of(0), biases_of(1))
+    sizes = (first_size, second_size)
+    periods = (0, period)
+
+    def attn_part(depth, stream):
+        return attention_forward(
+            stream,
+            modulation[depth],
+            gathering.done[3 * depth],
+            attn_biases[depth],
+            mixing_biases[depth],
+            sizes[depth],
+            periods[depth],
+        )
+
+    def mlp_part(depth, mid):
+        return mlp_forward(
+            mid,
+            modulation[depth],
+            gathering.done[3 * depth + 1],
+            gathering.done[3 * depth + 2],
+            hidden_biases[depth],
+            output_biases[depth],
+        )
+
+    def mlp_grads(depth, grad, saved):
+        _, mid, _, (_, _, _, slope, mlp_out) = saved
+        return mlp_backward(
+            grad, mid, mlp_out, slope, modulation[depth], *gathering.done[3 * depth + 1 : 3 * depth + 3]
+        )
+
+    def attn_grads(depth, grad_mid, saved):
+        stream, _, (_, _, qkv, _, logs, attn_out), _ = saved
+        return attention_backward(
+            grad_mid,
+            stream,
+            attn_out,
+            qkv,
+            logs,
+            modulation[depth],
+            gathering.done[3 * depth],
+            sizes[depth],
+            periods[depth],
+        )
+
+    def attn_terms(saved, swapped, grad_attn, grad_qkv, received, flops=0):
+        input_attn, _, _, heads, _, _ = saved[2]
+        columns = 4 * col_width
+        return weight_grads(
+            columns,
+            grad_qkv.shape[2] + heads.shape[2] - columns,
+            (input_attn, swapped[0], grad_qkv, received[0]),
+            (grad_attn, received[1], heads, swapped[1]),
+            flops=flops,
+        )
+
+    def output_terms(saved, swapped, grad_mlp, received):
+        active = saved[3][2]
+        return weight_grads(active.shape[2], 0, (grad_mlp, received, active, swapped[3]))
+
+    def hidden_terms(saved, swapped, grad_pre, received):
+        return weight_grads(
+            grad_pre.shape[2], 0, (saved[3][0], swapped[2], grad_pre, received)
+        )
+
+    gathering.step(output_ready[0], stream_first, *output_ready)
+    gathering.step(attn_ready[1], modulation)
+    mid_first, *attn_first = attn_part(0, after(stream_first, *gathering.sent))
+    gathering.step(hidden_ready[1], mid_first)
+    gathering.step(output_ready[1])
+    input_attn, heads = after((attn_first[1], attn_first[3]), *gathering.sent)
+    swapped_first = [swap(input_attn), swap(heads)]
+    output_first, *mlp_first = mlp_part(0, after(mid_first, *gathering.sent))
+    saved_first = (stream_first, mid_first, attn_first, mlp_first)
+    gathering.step(None, output_first, *swapped_first)
+    input_mlp, active, moving = after(
+        (mlp_first[1], mlp_first[2], output_first), *gathering.sent
+    )
+    swapped_first += [swap(input_mlp), swap(active)]
+    moving = mine_first(moving.astype(jnp.bfloat16), place, 0)
+    moving = moving.reshape(2, frame_part, place.row_count, groups, period, half)
+    moving = moving.transpose(0, 2, 3, 1, 4, 5)
+    moved = lax.all_to_all(moving, "row", split_axis=1, concat_axis=3, tiled=True)
+    gathering.step(None, moved, *swapped_first[2:])
+    cotangent, moved = after((cotangent, moved), *gathering.sent)
+    cotangent = cotangent.reshape(clip_count, frames, groups, period, col_width)
+    gradient_blocks = arriving(jnp.swapaxes(cotangent, 1, 2))
+    moved = moved.reshape(2, -1, half)
+    stream_second = mine_first(moved, place, 0).astype(jnp.float32)
+    mid_second, *attn_second = attn_part(1, stream_second)
+    gathering.step(None, mid_second)
+    gradient_blocks, mid_second, input_attn, heads = together(
+        gradient_blocks, mid_second, attn_second[1], attn_second[3]
+    )
+    swapped_second = [swap(input_attn), swap(heads)]
+    output_second, *mlp_second = mlp_part(1, mid_second)
+    saved_second = (stream_second, mid_second, attn_second, mlp_second)
+    grad = entered(gradient_blocks)
+    grad, swapped_second, input_mlp, active, output_second = together(
+        grad, swapped_second, mlp_second[1], mlp_second[2], output_second
+    )
+    swapped_second += [swap(input_mlp), swap(active)]
+
+    grad_mid, grad_mlp, grad_sent, grad_pre, small_mlp_second, hidden_sum_second = mlp_grads(
+        1, grad, saved_second
+    )
+    grad_mid, grad_mlp, grad_sent, grad_pre, swapped_second, output_second = together(
+        grad_mid, grad_mlp, grad_sent, grad_pre, swapped_second, output_second
+    )
+    received = swap(grad_sent)
+    result_blocks = leaving(output_second)
+    received, result_blocks, grad_pre = together(received, result_blocks, grad_pre)
+    received_pre = swap(grad_pre)
+    output_part = output_terms(saved_second, swapped_second, grad_mlp, received)
+    output_part, received_pre, grad_mid = together(output_part, received_pre, grad_mid)
+    output_part = scatter_corner(output_part)
+    hidden_part = hidden_terms(saved_second, swapped_second, grad_pre, received_pre)
+    hidden_part, grad_mid = together(hidden_part, grad_mid)
+    hidden_part = scatter_corner(hidden_part)
+    grad_second, grad_attn, grad_sent, grad_qkv, small_attn_second, qkv_sum_second = attn_grads(
+        1, grad_mid, saved_second
+    )
+    grad_second, grad_attn, grad_sent, grad_qkv, output_part = together(
+        grad_second, grad_attn, grad_sent, grad_qkv, output_part
+    )
+    received = [swap(grad_qkv), swap(grad_sent)]
+    sides = scatter_sides(output_part)
+    moving = mine_first(grad_second.astype(jnp.bfloat16), place, 0)
+    moving = moving.reshape(2, 1, groups, frames, period, half)
+    moved = lax.all_to_all(moving, "row", split_axis=3, concat_axis=1, tiled=True)
+    received, grad_attn, grad_qkv, sides, moving = together(
+        received, grad_attn, grad_qkv, sides, moving
+    )
+    output_part = scatter_plane(output_part, sides)
+    attn_blocks = attn_terms(
+        saved_second, swapped_second, grad_attn, grad_qkv, received, 15 * 10**9
+    )
+    attn_blocks, hidden_part = together(attn_blocks, hidden_part)
+    attn_part_second = scatter_corner(attn_blocks)
+    sides = scatter_sides(hidden_part)
+    output_total = add_blocks(output_part)
+    moved, output_total, sides = together(moved, output_total, sides)
+    moved = moved.transpose(0, 3, 1, 2, 4, 5).reshape(2, -1, half)
+    returned = mine_first(moved, place, 0).astype(jnp.float32)
+    output_pieces = over_depth(output_total, place)
+    hidden_part = scatter_plane(hidden_part, sides)
+    grad_mid, grad_mlp, grad_sent, grad_pre, small_mlp_first, hidden_sum_first = mlp_grads(
+        0, returned, saved_first
+    )
+    grad_mid, grad_mlp, grad_sent, grad_pre, output_pieces, hidden_part = together(
+        grad_mid, grad_mlp, grad_sent, grad_pre, output_pieces, hidden_part
+    )
+    received = swap(grad_sent)
+    hidden_total = add_blocks(hidden_part)
+    received, hidden_total, grad_pre = together(received, hidden_total, grad_pre)
+    hidden_pieces = over_depth(hidden_total, place)
+    received_pre = swap(grad_pre)
+    output_blocks = output_terms(saved_first, swapped_first, grad_mlp, received)
+    output_blocks, received_pre, attn_part_second = together(
+        output_blocks, received_pre, attn_part_second
+    )
+    output_part = scatter_corner(output_blocks)
+    sides = scatter_sides(attn_part_second)
+    attn_part_second = scatter_plane(attn_part_second, sides)
+    received_pre, _ = together(received_pre, sides)
+    hidden_blocks = hidden_terms(saved_first, swapped_first, grad_pre, received_pre)
+    hidden_blocks, grad_mid = together(hidden_blocks, grad_mid)
+    hidden_part = scatter_corner(hidden_blocks)
+    grad_first, grad_attn, grad_sent, grad_qkv, small_attn_first, qkv_sum_first = attn_grads(
+        0, grad_mid, saved_first
+    )
+    (
+        grad_first,
+        grad_attn,
+        grad_sent,
+        grad_qkv,
+        output_part,
+        attn_part_second,
+        hidden_pieces,
+    ) = together(
+        grad_first, grad_attn, grad_sent, grad_qkv, output_part, attn_part_second, hidden_pieces
+    )
+    received = [swap(grad_qkv), swap(grad_sent)]
+    sides = scatter_sides(output_part)
+    output_part = scatter_plane(output_part, sides)
+    attn_total = add_blocks(attn_part_second)
+    attn_pieces = over_depth(attn_total, place)
+    received, _, grad_attn, grad_qkv = together(
+        received, (sides, attn_total), grad_attn, grad_qkv
+    )
+    attn_blocks = attn_terms(saved_first, swapped_first, grad_attn, grad_qkv, received)
+    attn_blocks, output_part, hidden_part, small_mlp_first, grad_first = together(
+        attn_blocks, output_part, hidden_part, small_mlp_first, grad_first
+    )
+    attn_part_first = scatter_corner(attn_blocks)
+    sides = scatter_sides(hidden_part)
+    output_total = add_blocks(output_part)
+    output_total, sides, grad_first, small_attn_first, attn_pieces = together(
+        output_total, sides, grad_first, small_attn_first, attn_pieces
+    )
+    hidden_part = scatter_plane(hidden_part, sides)
+    output_first_pieces = over_depth(output_total, place)
+    gradient_blocks = leaving(grad_first)
+
+    def small_grads(small_attn, small_mlp, qkv_sum, hidden_sum):
+        return (
+            jnp.concatenate((small_attn[:, :3], small_mlp[:, :3]), 1),
+            (qkv_sum[:, 0], small_attn[:, 3], hidden_sum[:, 0], small_mlp[:, 3]),
+        )
+
+    modgrad_first, biasgrad_first = small_grads(
+        small_attn_first, small_mlp_first, qkv_sum_first, hidden_sum_first
+    )
+    modgrad_second, biasgrad_second = small_grads(
+        small_attn_second, small_mlp_second, qkv_sum_second, hidden_sum_second
+    )
+    def by_block(halves):
+        features = from_halves(halves, place)
+        features = features.reshape(features.shape[:-1] + (place.col_count, col_width))
+        return relative(jnp.moveaxis(features, -2, 0), place)
+
+    modgrad = by_block(jnp.swapaxes(jnp.stack((modgrad_first, modgrad_second)), 1, 2))
+    mixgrad = by_block(jnp.stack((biasgrad_first[1], biasgrad_second[1])))
+    outgrad = by_block(jnp.stack((biasgrad_first[3], biasgrad_second[3])))
+    sending = []
+    for step in range(place.col_count):
+        pieces = [modgrad[step].reshape(-1)]
+        for grads in (biasgrad_first, biasgrad_second):
+            pieces.append(grads[0][step][:col_width])
+            pieces.append(grads[0][step][2 * col_width : 3 * col_width])
+        for grads in (biasgrad_first, biasgrad_second):
+            pieces.append(grads[2][step])
+        pieces.append(mixgrad[step].reshape(-1))
+        pieces.append(outgrad[step].reshape(-1))
+        sending.append(jnp.concatenate(pieces))
+    sending = [value.reshape(-1, LANES) for value in sending]
+    attn_part_first, hidden_part, gradient_blocks, sending = together(
+        attn_part_first, hidden_part, gradient_blocks, sending
+    )
+    sides = scatter_sides(attn_part_first)
+    hidden_total = add_blocks(hidden_part)
+    sides, hidden_total, sending, output_first_pieces = together(
+        sides, hidden_total, sending, output_first_pieces
+    )
+    attn_part_first = scatter_plane(attn_part_first, sides)
+    hidden_first_pieces = over_depth(hidden_total, place)
+    met = trade(sending)
+    sums = [add_all(pieces, place) for pieces in (attn_pieces, hidden_pieces, output_pieces)]
+    met, attn_part_first, sums, output_first_pieces = together(
+        met, attn_part_first, sums, output_first_pieces
+    )
+    attn_total = add_blocks(attn_part_first)
+    met = [value.reshape(-1) for value in met]
+    modgrad = jnp.concatenate([block[:cut] for block in met])
+    biasgrad = sum(block[cut:] for block in met)
+    small = jnp.concatenate((modgrad, biasgrad))
+    small = small + swap(small)
+    gradient_blocks, result_blocks, small, _ = together(
+        gradient_blocks, result_blocks, small, attn_total
+    )
+    gradient_blocks = trade(gradient_blocks)
+    for mask in place.depth_masks:
+        small = small + exchange(small, "row", mask)
+    gradient_blocks, hidden_first_pieces, attn_total, small = together(
+        gradient_blocks, hidden_first_pieces, attn_total, small
+    )
+    attn_first_pieces = over_depth(attn_total, place)
+    tokens_gradient = assembled(gradient_blocks, jnp.float32)
+    tokens_gradient = tokens_gradient.reshape(clip_count, frame_part, places, col_width)
+    result = assembled(trade(result_blocks), jnp.bfloat16)
+    result = result.reshape(clip_count, groups, frames, period, col_width)
+    result = jnp.swapaxes(result, 1, 2).reshape(clip_count, frames, place_part, col_width)
+    first_sums = [
+        add_all(pieces, place)
+        for pieces in (attn_first_pieces, hidden_first_pieces, output_first_pieces)
+    ]
+    modgrad = small[: cut * clip_count].reshape(clip_count, layer_count, 6, col_width)
+    modgrad = jnp.moveaxis(jnp.stack(relative(modgrad, place)), 1, 0)
+    rest = small[cut * clip_count :]
+    bias_grads = []
+    for value in (attn_bias, hidden_bias, mixing_bias, output_bias):
+        bias_grads.append(rest[: value.size].reshape(value.shape))
+        rest = rest[value.size :]
+    ada_bias_grad = jnp.sum(modgrad, 1)
+    ada_weight_grad = jnp.einsum(
+        "cr,lcsk->lrsk", cond_act.astype(jnp.float32), modgrad, precision=highest
+    )
+    cond_part = jnp.einsum(
+        "lcsk,lrsk->cr", modgrad, ada_weight.astype(jnp.float32), precision=highest
+    )
+    for mask in (1, 2):
+        cond_part = cond_part + exchange(cond_part, "col", mask)
+    conditioning_gradient = jax.vjp(jax.nn.silu, conditioning)[1](cond_part)[0]
+
+    attn_sums, hidden_sums, output_sums = (
+        jnp.stack((first_sums[index], sums[index])) for index in range(3)
+    )
+    return (
+        close_tokens(result),
+        close_tokens(tokens_gradient),
+        conditioning_gradient,
+        close_weight(ada_weight_grad),
+        ada_bias_grad,
+        close_weight(attn_sums[:, :, : 3 * col_width]),
+        bias_grads[0],
+        close_weight(jnp.swapaxes(attn_sums[:, :, 3 * col_width :], 1, 2)),
+        bias_grads[2],
+        close_weight(hidden_sums),
+        bias_grads[1],
+        close_weight(jnp.swapaxes(output_sums, 1, 2)),
+        bias_grads[3],
+    )
+
+
+def suits_tokens(mesh):
+    rows, cols = (mesh.shape["row"], mesh.shape["col"])
+    return cols == 4 and rows >= 2 and rows & (rows - 1) == 0
+
+
 def solution(mesh):
     placed = (
         P(None, "row", "col", None),
@@ -393,7 +1644,7 @@
         P(None, None, "col", "row"),
     )
     return jax.shard_map(
-        local,
+        token_parallel if suits_tokens(mesh) else tensor_parallel,
         mesh=mesh,
         in_specs=placed,
         out_specs=(

time: 2730 us -> 1050 us (0.38)
  waiting for transfers between devices: 1450 us -> 252 us
  matrix products: 387 us -> 2.62 us
  Pallas kernels: 0 us -> 366 us
  local copies, waits for them, and re-layouts: 487 us -> 205 us
  blocking collectives: 263 us -> 0 us
  starting transfers between devices: 7.45 us -> 141 us
  other arithmetic: 109 us -> 60.5 us
    all_gather x14 -> x1, waiting for transfers between devices: 864 us -> 24.7 us  [token_parallel(): met = lax.all_gather(jnp.concatenate(own, 1), ('row', 'col'), axis=0)]
    dot_general x38 -> x1, matrix products: 382 us -> 0.24 us  [matmul(): return jnp.einsum(pattern, left, right, preferred_element_type=jnp.float32)]
    pallas_call x0 -> x32, Pallas kernels: none -> 366 us  [the longest x6 69.5 us: weight_grads(): pl.pallas_call(functools.partial(weight_kernel, len(pairs), overlap, step...]
    reduce_scatter x12 -> x0, waiting for transfers between devices: 301 us -> none  [the longest x2 109 us: collect_grad(): lax.psum_scatter(terms.astype(jnp.bfloat16), 'col', scatter_dimension=3,...]
    unnamed x289 -> x231, local copies, waits for them, and re-layouts: 277 us -> 26 us
    unnamed x34 -> x1, waiting for transfers between devices: 223 us -> 0.02 us
    psum x10 -> x0, blocking collectives: 188 us -> none  [the longest x4 65.9 us: normalize_back(): lax.psum((jnp.sum(grad_normed, -1), jnp.sum(grad_normed * normed, -1)), '...]
    ppermute x0 -> x80, waiting for transfers between devices: none -> 174 us  [exchange(): lax.ppermute(values, axis, [(index, index ^ mask) for index in range(coun...]
  transfers between devices with their start and end apart: 31 -> 95, of which waited for: 24 -> 31; matrix products, arithmetic and copies ran while one was open for 15% -> 19% of each run, Pallas kernels for 0% -> 35%
where the time goes in v2:
time: 1050 us; the launch traced here: 1040 us
  Pallas kernels  366 us (35%)
  waiting for transfers between devices  252 us (24%)
  local copies, waits for them, and re-layouts  205 us (20%)
  starting transfers between devices  141 us (13%)
  other arithmetic  60.5 us (6%)
  between operations  16.2 us (2%)
    ppermute x80, waiting for transfers between devices, exchange(): lax.ppermute(values, axis, [(index, index ^ mask) for index in range(coun...  174 us
    ppermute x80, starting transfers between devices, exchange(): lax.ppermute(values, axis, [(index, index ^ mask) for index in range(coun...  73.7 us
    pallas_call x6, Pallas kernels, weight_grads(): pl.pallas_call(functools.partial(weight_kernel, len(pairs), overlap, step...  69.5 us
    pallas_call x2, Pallas kernels, attention_backward(): pl.pallas_call(functools.partial(attention_back_kernel, size, period, ste...  66.4 us
    pallas_call x2, Pallas kernels, attention_forward(): pl.pallas_call(functools.partial(attention_kernel, size, period, steps),...  57.6 us
    all_to_all x12, starting transfers between devices, over_depth(): lax.all_to_all(values, 'row', split_axis=0, concat_axis=0, tiled=True, ax...  56.9 us
    pallas_call x2, Pallas kernels, mlp_forward(): pl.pallas_call(functools.partial(mlp_kernel, steps), grid=(steps,), in_sp...  56.3 us
    pallas_call x2, Pallas kernels, mlp_backward(): pl.pallas_call(functools.partial(mlp_back_kernel, steps), grid=(steps,),...  55 us
  transfers between devices with their start and end apart: 95, of which 31 were waited for; matrix products, arithmetic and copies ran while one was open for 19% of the time, Pallas kernels for 35%

profile of v2, /device:TPU:0, one launch (start us, length us, event | category | flops | bytes accessed | tf_op | source)
XLA Modules:
  0.0 1043.2 jit_solution(2862298414023846699)
XLA Ops:
  7.2 4.7 slice_reduce_fusion.4
  14.8 6.4 all-to-all-start
  30.7 7.8 slice_reduce_fusion.2
  52.9 5.2 reshape.399
  65.0 3.8 all-to-all-start.1
  71.9 9.0 slice_reduce_fusion
  92.1 4.7 reorder.6.refs_0_.refs_1_
  112.6 3.9 all-to-all-start.2
  116.5 24.7 %all-gather.4.cloned.1.call-done = f32[32,4,5472]{2,1,0:T(4,128)} async-done(((f32[1,4,5472]{2,1,0:T(4,128)}), f32[32,4,5472]{2,1,0:T(4,128)}) %all-gather.4.cloned.1.call-update) | async-done | bytes 2801680 | tf_op jit(solution)/shard_map/all_gather | solution.py:1274
  145.4 13.9 %collective-permute-done.5.lower.across = bf16[864,1152]{1,0:T(8,128)(2,1)} collective-permute-done((bf16[864,1152]{1,0:T(8,128)(2,1)}, bf16[864,1152]{1,0:T(8,128)(2,1)}, u32[]{:S(2)}, u32[]{:S(2)}) %collective-permute-start.5) | collective-permute-done | bytes 1990688 | tf_op jit(solution)/shard_map/ppermute | solution.py:385
  165.3 4.0 pack_blocks.6.refs_4_.refs_6_
  169.4 3.6 all-to-all-start.3
  178.5 28.8 %attention_forward.2 = (f32[2,512,576]{2,1,0:T(8,128)}, bf16[512,576]{1,0:T(8,128)(2,1)}, bf16[512,576]{1,0:T(8,128)(2,1)}, bf16[4,512,896]{2,1,0:T(8,128)(2,1)}...) custom-call(f32[2,512,576]{2,1,0:T(8,128)} %copy-done, ...), custom_call_target="tpu_custom_call" | custom-call | tf_op jit(solution)/shard_map/attention_forward/pallas_call | solution.py:667
  207.3 11.8 %collective-permute-done.8.lower.across = bf16[864,1152]{1,0:T(8,128)(2,1)} collective-permute-done((bf16[864,1152]{1,0:T(8,128)(2,1)}, bf16[864,1152]{1,0:T(8,128)(2,1)}, u32[]{:S(2)}, u32[]{:S(2)}) %collective-permute-start.8) | collective-permute-done | bytes 1990688 | tf_op jit(solution)/shard_map/ppermute | solution.py:385
  226.8 4.7 all-to-all-start.4
  231.6 3.9 pack_blocks.7.refs_4_.refs_5_
  235.5 33.4 %collective-permute-done.10.lower.across = bf16[864,1152]{1,0:T(8,128)(2,1)} collective-permute-done((bf16[864,1152]{1,0:T(8,128)(2,1)}, bf16[864,1152]{1,0:T(8,128)(2,1)}, u32[]{:S(2)}, u32[]{:S(2)}) %collective-permute-start.10) | collective-permute-done | bytes 1990688 | tf_op jit(solution)/shard_map/ppermute | solution.py:385
  272.3 3.6 pad_maximum_fusion.6
  275.9 4.0 pack_blocks.8.refs_6_.refs_7_
  280.0 4.7 all-to-all-start.5
  291.0 28.2 %mlp_forward.2 = (f32[2,512,576]{2,1,0:T(8,128)}, bf16[512,576]{1,0:T(8,128)(2,1)}, bf16[512,576]{1,0:T(8,128)(2,1)}, bf16[4,512,1152]{2,1,0:T(8,128)(2,1)}, bf1...) custom-call(f32[2,512,576]{2,1,0:T(8,128)} %get-tuple-element.471.refs_0_.refs_1_, ...), custom_call_target="tpu_custom_call" | custom-call | tf_op jit(solution)/shard_map/mlp_forward/pallas_call | solution.py:746
  319.3 11.3 %collective-permute-done.15.lower.across = bf16[864,1152]{1,0:T(8,128)(2,1)} collective-permute-done((bf16[864,1152]{1,0:T(8,128)(2,1)}, bf16[864,1152]{1,0:T(8,128)(2,1)}, u32[]{:S(2)}, u32[]{:S(2)}) %collective-permute-start.15) | collective-permute-done | bytes 1990688 | tf_op jit(solution)/shard_map/ppermute | solution.py:385
  335.4 4.0 pack_blocks.9.refs_4_.refs_6_
  341.7 5.2 all-to-all-start.6
  352.0 27.1 %all-to-all-done.6 = bf16[2,8,2,2,16,576]{5,4,2,3,0,1:T(8,128)(2,1)} async-done(((bf16[2,8,2,2,16,576]{5,4,2,3,0,1:T(8,128)(2,1)}), bf16[2,8,2,2,16,576]{5,4,2,3,0,1:T(8,128)(2,1)}, u32[]{:S(2)}, u32[]{:S(2)}) %all-to-all-start.6) | async-done | bytes 1179680 | tf_op jit(solution)/shard_map/all_to_all | solution.py:1393
  381.7 11.3 %collective-permute-done.19.lower.across = bf16[864,1152]{1,0:T(8,128)(2,1)S(1)} collective-permute-done((bf16[864,1152]{1,0:T(8,128)(2,1)}, bf16[864,1152]{1,0:T(8,128)(2,1)S(1)}, u32[]{:S(2)}, u32[]{:S(2)}) %collective-permute-start.19) | collective-permute-done | bytes 1990688 | tf_op jit(solution)/shard_map/ppermute | solution.py:385
  399.2 4.3 reshape.415
  404.1 3.9 pack_blocks.10.refs_4_.refs_5_
  409.8 28.8 %attention_forward.3 = (f32[2,512,576]{2,1,0:T(8,128)}, bf16[512,576]{1,0:T(8,128)(2,1)}, bf16[512,576]{1,0:T(8,128)(2,1)}, bf16[4,512,896]{2,1,0:T(8,128)(2,1)}...) custom-call(f32[2,512,576]{2,1,0:T(8,128)} %fusion.2.refs_0_.refs_1_, ...), custom_call_target="tpu_custom_call" | custom-call | tf_op jit(solution)/shard_map/attention_forward/pallas_call | solution.py:667
  438.7 4.5 pack_blocks.11.refs_6_.refs_7_
  447.7 8.5 collective-permute-done.22.refs_1_
  456.2 8.6 collective-permute-done.23.refs_2_
  466.3 4.7 reorder.7.refs_0_
  472.5 28.1 %mlp_forward.3 = (f32[2,512,576]{2,1,0:T(8,128)}, bf16[512,576]{1,0:T(8,128)(2,1)}, bf16[512,576]{1,0:T(8,128)(2,1)}, bf16[4,512,1152]{2,1,0:T(8,128)(2,1)}, bf1...) custom-call(f32[2,512,576]{2,1,0:T(8,128)} %get-tuple-element.523.refs_0_.refs_1_, ...), custom_call_target="tpu_custom_call" | custom-call | tf_op jit(solution)/shard_map/mlp_forward/pallas_call | solution.py:746
  503.4 27.5 %mlp_backward.2 = (f32[2,512,576]{2,1,0:T(8,128)}, bf16[512,576]{1,0:T(8,128)(2,1)}, bf16[512,576]{1,0:T(8,128)(2,1)}, bf16[4,512,1152]{2,1,0:T(8,128)(2,1)}, f3...) custom-call(f32[2,512,576]{2,1,0:T(8,128)} %copy-done.3, f32[2,512,576]{2,1,0:T(8,128)} %get-tuple-element.523.refs_0_.refs_1_, ...), custom_call_target="tpu_custom_call" | custom-call | tf_op jit(solution)/shard_map/mlp_backward/pallas_call | solution.py:818
  533.4 4.4 reorder.8
  541.8 10.8 %weight_grads.6 = (bf16[576,1152]{1,0:T(8,128)(2,1)}, bf16[288,1152]{1,0:T(8,128)(2,1)}, bf16[576,1152]{1,0:T(8,128)(2,1)}, bf16[576,1152]{1,0:T(8,128)(2,1)}, bf16[288,1152]{1,0:T(8,128)(2,1)}) custom-call(bf16[512,576]{1,0:T(8,128)(2,1)} %get-tuple-element.576.refs_0_, bf16[512,576]{1,0:T(8,128)(2,1)} %copy.177.refs_1_, ...), custom_call_target="tpu_custom_call" | custom-call | tf_op jit(solution)/shard_map/weight_grads/pallas_call | solution.py:1034
  556.6 11.0 %weight_grads.7 = (bf16[576,1152]{1,0:T(8,128)(2,1)}, bf16[288,1152]{1,0:T(8,128)(2,1)}, bf16[576,1152]{1,0:T(8,128)(2,1)}, bf16[576,1152]{1,0:T(8,128)(2,1)}, bf16[288,1152]{1,0:T(8,128)(2,1)}) custom-call(bf16[512,576]{1,0:T(8,128)(2,1)} %get-tuple-element.545.refs_0_, bf16[512,576]{1,0:T(8,128)(2,1)} %copy.178.refs_1_, ...), custom_call_target="tpu_custom_call" | custom-call | tf_op jit(solution)/shard_map/weight_grads/pallas_call | solution.py:1034
  567.6 33.2 %attention_backward.2 = (f32[2,512,576]{2,1,0:T(8,128)}, bf16[512,576]{1,0:T(8,128)(2,1)}, bf16[512,576]{1,0:T(8,128)(2,1)}, bf16[4,512,896]{2,1,0:T(8,128)(2,1)...) custom-call(f32[2,512,576]{2,1,0:T(8,128)} %get-tuple-element.592.refs_0_, f32[2,512,576]{2,1,0:T(8,128)} %fusion.2.refs_0_.refs_1_, ...), custom_call_target="tpu_custom_call" | custom-call | tf_op jit(solution)/shard_map/attention_backward/pallas_call | solution.py:926
  604.4 5.5 all-to-all-start.7
  618.6 23.6 %all-to-all-done.7 = bf16[2,1,2,16,16,576]{5,4,2,0,1,3:T(8,128)(2,1)} async-done(((bf16[2,1,2,16,16,576]{5,4,2,0,1,3:T(8,128)(2,1)}), bf16[2,1,2,16,16,576]{5,4,2,0,1,3:T(8,128)(2,1)}, u32[]{:S(2)}, u32[]{:S(2)}) %all-to-all-start.7) | async-done | bytes 1179680 | tf_op jit(solution)/shard_map/all_to_all | solution.py:1440
  646.8 12.9 %weight_grads.8 = (bf16[576,1152]{1,0:T(8,128)(2,1)}, bf16[288,1152]{1,0:T(8,128)(2,1)}, bf16[576,1152]{1,0:T(8,128)(2,1)}, bf16[576,1152]{1,0:T(8,128)(2,1)}, bf16[288,1152]{1,0:T(8,128)(2,1)}) custom-call(bf16[512,576]{1,0:T(8,128)(2,1)} %get-tuple-element.616.refs_0_, bf16[512,576]{1,0:T(8,128)(2,1)} %copy.182.refs_1_, ...), custom_call_target="tpu_custom_call" | custom-call | flops 15000000512 | tf_op jit(solution)/shard_map/weight_grads/pallas_call | solution.py:1034
  666.5 9.8 collective-permute-done.40.across_upper
  678.4 4.4 all-to-all-start.8
  686.8 27.5 %mlp_backward.3 = (f32[2,512,576]{2,1,0:T(8,128)}, bf16[512,576]{1,0:T(8,128)(2,1)}, bf16[512,576]{1,0:T(8,128)(2,1)}, bf16[4,512,1152]{2,1,0:T(8,128)(2,1)}, f3...) custom-call(f32[2,512,576]{2,1,0:T(8,128)} %fusion.3.refs_0_, f32[2,512,576]{2,1,0:T(8,128)} %get-tuple-element.471.refs_0_.refs_1_, ...), custom_call_target="tpu_custom_call" | custom-call | tf_op jit(solution)/shard_map/mlp_backward/pallas_call | solution.py:818
  722.2 5.0 all-to-all-start.9
  728.3 10.9 %weight_grads.9 = (bf16[576,1152]{1,0:T(8,128)(2,1)}, bf16[288,1152]{1,0:T(8,128)(2,1)}, bf16[576,1152]{1,0:T(8,128)(2,1)}, bf16[576,1152]{1,0:T(8,128)(2,1)}, bf16[288,1152]{1,0:T(8,128)(2,1)}) custom-call(bf16[512,576]{1,0:T(8,128)(2,1)} %get-tuple-element.656.refs_0_, bf16[512,576]{1,0:T(8,128)(2,1)} %copy.186.refs_1_, ...), custom_call_target="tpu_custom_call" | custom-call | tf_op jit(solution)/shard_map/weight_grads/pallas_call | solution.py:1034
  739.2 12.3 %collective-permute-done.48.across_first = bf16[576,1152]{1,0:T(8,128)(2,1)S(1)} collective-permute-done((bf16[576,1152]{1,0:T(8,128)(2,1)}, bf16[576,1152]{1,0:T(8,128)(2,1)S(1)}, u32[]{:S(2)}, u32[]{:S(2)}) %collective-permute-start.48) | collective-permute-done | bytes 1327136 | tf_op jit(solution)/shard_map/ppermute | solution.py:385
  763.1 10.9 %weight_grads.10 = (bf16[576,1152]{1,0:T(8,128)(2,1)}, bf16[288,1152]{1,0:T(8,128)(2,1)}, bf16[576,1152]{1,0:T(8,128)(2,1)}, bf16[576,1152]{1,0:T(8,128)(2,1)}, bf16[288,1152]{1,0:T(8,128)(2,1)}) custom-call(bf16[512,576]{1,0:T(8,128)(2,1)} %get-tuple-element.492.refs_0_, bf16[512,576]{1,0:T(8,128)(2,1)} %copy.187.refs_1_, ...), custom_call_target="tpu_custom_call" | custom-call | tf_op jit(solution)/shard_map/weight_grads/pallas_call | solution.py:1034
  774.0 33.2 %attention_backward.3 = (f32[2,512,576]{2,1,0:T(8,128)}, bf16[512,576]{1,0:T(8,128)(2,1)}, bf16[512,576]{1,0:T(8,128)(2,1)}, bf16[4,512,896]{2,1,0:T(8,128)(2,1)...) custom-call(f32[2,512,576]{2,1,0:T(8,128)} %get-tuple-element.680.refs_0_, f32[2,512,576]{2,1,0:T(8,128)} %copy-done, ...), custom_call_target="tpu_custom_call" | custom-call | tf_op jit(solution)/shard_map/attention_backward/pallas_call | solution.py:926
  823.7 5.2 all-to-all-start.10
  836.3 12.9 %weight_grads.11 = (bf16[576,1152]{1,0:T(8,128)(2,1)}, bf16[288,1152]{1,0:T(8,128)(2,1)}, bf16[576,1152]{1,0:T(8,128)(2,1)}, bf16[576,1152]{1,0:T(8,128)(2,1)}, bf16[288,1152]{1,0:T(8,128)(2,1)}) custom-call(bf16[512,576]{1,0:T(8,128)(2,1)} %get-tuple-element.454.refs_0_, bf16[512,576]{1,0:T(8,128)(2,1)} %copy.189.refs_1_, ...), custom_call_target="tpu_custom_call" | custom-call | tf_op jit(solution)/shard_map/weight_grads/pallas_call | solution.py:1034
  849.2 6.8 collective-permute-done.57.above_lower
  863.9 5.1 all-to-all-start.11
  880.1 5.1 reorder.9
  889.0 17.6 %collective-permute-done.62.across_upper = bf16[288,1152]{1,0:T(8,128)(2,1)S(1)} collective-permute-done((bf16[288,1152]{1,0:T(8,128)(2,1)}, bf16[288,1152]{1,0:T(8,128)(2,1)S(1)}, u32[]{:S(2)}, u32[]{:S(2)}) %collective-permute-start.62) | collective-permute-done | bytes 663584 | tf_op jit(solution)/shard_map/ppermute | solution.py:385
  922.9 5.4 all-to-all-start.12
  948.2 4.5 collective-permute-start.77
  956.2 3.5 collective-permute-done.77
  967.6 4.9 reshape.465
  976.8 10.8 %collective-permute-done.71.refs_2_ = bf16[512,288]{1,0:T(8,128)(2,1)S(1)} collective-permute-done((bf16[512,288]{1,0:T(8,128)(2,1)S(1)}, bf16[512,288]{1,0:T(8,128)(2,1)S(1)}, u32[]{:S(2)}, u32[]{:S(2)}) %collective-permute-start.71) | collective-permute-done | bytes 294944 | tf_op jit(solution)/shard_map/ppermute | solution.py:385
  994.0 4.6 all-to-all-start.13
  1011.1 5.9 reshape.462
  1020.8 5.5 reshape_reshape.32
  (631 shorter events, 321.1 us)
Async XLA Ops:
  14.8 38.1 %all-to-all-start = ((bf16[4,144,1152]{2,1,0:T(8,128)(2,1)}), bf16[4,144,1152]{2,1,0:T(8,128)(2,1)S(1)}, u32[]{:S(2)}, u32[]{:S(2)}) async-start(bf16[4,144,1152]{2,1,0:T(8,128)(2,1)} %bitcast.13), calls=%async_computation | async-start | bytes 2654208 | tf_op jit(solution)/shard_map/all_to_all | solution.py:402
  21.2 120.0 %all-gather.4.cloned.1.call-start = ((), (), s32[]{:S(2)}) async-start(), calls=%async_computation.14 | async-start | bytes 2906112 | tf_op jit(solution)/shard_map/all_gather | solution.py:1274
  65.0 36.8 %all-to-all-start.1 = ((bf16[4,144,1152]{2,1,0:T(8,128)(2,1)}), bf16[4,144,1152]{2,1,0:T(8,128)(2,1)S(1)}, u32[]{:S(2)}, u32[]{:S(2)}) async-start(bf16[4,144,1152]{2,1,0:T(8,128)(2,1)} %tile.59), calls=%async_computation.1 | async-start | bytes 2654208 | tf_op jit(solution)/shard_map/all_to_all | solution.py:402
  68.8 30.9 %collective-permute-start.3 = (bf16[576,1152]{1,0:T(8,128)(2,1)S(1)}, bf16[576,1152]{1,0:T(8,128)(2,1)}, u32[]{:S(2)}, u32[]{:S(2)}) collective-permute-start(bf16[576,1152]{1,0:T(8,128)(2,1)S(1)} %bitcast.232), channel_id=1, source_target_pairs={{0,1},{1,0},{2,3},{3,2},{4,5},{5,4},{6,7},{7,6},{8,9},{9,8},{10,11... | collective-permute-start | bytes 3981320 | tf_op jit(solution)/shard_map/ppermute | solution.py:385
  70.3 30.6 %collective-permute-start.4 = (bf16[576,1152]{1,0:T(8,128)(2,1)S(1)}, bf16[576,1152]{1,0:T(8,128)(2,1)}, u32[]{:S(2)}, u32[]{:S(2)}) collective-permute-start(bf16[576,1152]{1,0:T(8,128)(2,1)S(1)} %bitcast.233), channel_id=1, source_target_pairs={{0,2},{1,3},{2,0},{3,1},{4,6},{5,7},{6,4},{7,5},{8,10},{9,11},{10,... | collective-permute-start | bytes 3981320 | tf_op jit(solution)/shard_map/ppermute | solution.py:385
  109.6 49.7 %collective-permute-start.5 = (bf16[864,1152]{1,0:T(8,128)(2,1)}, bf16[864,1152]{1,0:T(8,128)(2,1)}, u32[]{:S(2)}, u32[]{:S(2)}) collective-permute-start(bf16[864,1152]{1,0:T(8,128)(2,1)} %get-tuple-element.961), channel_id=1, source_target_pairs={{0,1},{1,0},{2,3},{3,2},{4,5},{5,4},{6,7},{7,6},{8,9},{9,8},{10,11... | collective-permute-start | bytes 5971976 | tf_op jit(solution)/shard_map/ppermute | solution.py:385
  111.1 49.3 %collective-permute-start.6 = (bf16[864,1152]{1,0:T(8,128)(2,1)}, bf16[864,1152]{1,0:T(8,128)(2,1)}, u32[]{:S(2)}, u32[]{:S(2)}) collective-permute-start(bf16[864,1152]{1,0:T(8,128)(2,1)} %get-tuple-element.960), channel_id=1, source_target_pairs={{0,2},{1,3},{2,0},{3,1},{4,6},{5,7},{6,4},{7,5},{8,10},{9,11},{10,... | collective-permute-start | bytes 5971976 | tf_op jit(solution)/shard_map/ppermute | solution.py:385
  112.6 47.8 %all-to-all-start.2 = ((bf16[4,144,1152]{2,1,0:T(8,128)(2,1)}), bf16[4,144,1152]{2,1,0:T(8,128)(2,1)S(1)}, u32[]{:S(2)}, u32[]{:S(2)}) async-start(bf16[4,144,1152]{2,1,0:T(8,128)(2,1)} %tile.66), calls=%async_computation.2 | async-start | bytes 2654208 | tf_op jit(solution)/shard_map/all_to_all | solution.py:402
  169.4 37.9 %all-to-all-start.3 = ((bf16[4,144,1152]{2,1,0:T(8,128)(2,1)}), bf16[4,144,1152]{2,1,0:T(8,128)(2,1)S(1)}, u32[]{:S(2)}, u32[]{:S(2)}) async-start(bf16[4,144,1152]{2,1,0:T(8,128)(2,1)} %tile.64), calls=%async_computation.3 | async-start | bytes 2654208 | tf_op jit(solution)/shard_map/all_to_all | solution.py:402
  172.9 46.1 %collective-permute-start.8 = (bf16[864,1152]{1,0:T(8,128)(2,1)}, bf16[864,1152]{1,0:T(8,128)(2,1)}, u32[]{:S(2)}, u32[]{:S(2)}) collective-permute-start(bf16[864,1152]{1,0:T(8,128)(2,1)} %get-tuple-element.959), channel_id=1, source_target_pairs={{0,1},{1,0},{2,3},{3,2},{4,5},{5,4},{6,7},{7,6},{8,9},{9,8},{10,11... | collective-permute-start | bytes 5971976 | tf_op jit(solution)/shard_map/ppermute | solution.py:385
  173.5 45.8 %collective-permute-start.9 = (bf16[864,1152]{1,0:T(8,128)(2,1)}, bf16[864,1152]{1,0:T(8,128)(2,1)}, u32[]{:S(2)}, u32[]{:S(2)}) collective-permute-start(bf16[864,1152]{1,0:T(8,128)(2,1)} %get-tuple-element.958), channel_id=1, source_target_pairs={{0,2},{1,3},{2,0},{3,1},{4,6},{5,7},{6,4},{7,5},{8,10},{9,11},{10,... | collective-permute-start | bytes 5971976 | tf_op jit(solution)/shard_map/ppermute | solution.py:385
  223.8 45.0 %collective-permute-start.10 = (bf16[864,1152]{1,0:T(8,128)(2,1)}, bf16[864,1152]{1,0:T(8,128)(2,1)}, u32[]{:S(2)}, u32[]{:S(2)}) collective-permute-start(bf16[864,1152]{1,0:T(8,128)(2,1)} %get-tuple-element.957), channel_id=1, source_target_pairs={{0,1},{1,0},{2,3},{3,2},{4,5},{5,4},{6,7},{7,6},{8,9},{9,8},{10,11... | collective-permute-start | bytes 5971976 | tf_op jit(solution)/shard_map/ppermute | solution.py:385
  225.3 44.7 %collective-permute-start.11 = (bf16[864,1152]{1,0:T(8,128)(2,1)}, bf16[864,1152]{1,0:T(8,128)(2,1)}, u32[]{:S(2)}, u32[]{:S(2)}) collective-permute-start(bf16[864,1152]{1,0:T(8,128)(2,1)} %get-tuple-element.956), channel_id=1, source_target_pairs={{0,2},{1,3},{2,0},{3,1},{4,6},{5,7},{6,4},{7,5},{8,10},{9,11},{10,... | collective-permute-start | bytes 5971976 | tf_op jit(solution)/shard_map/ppermute | solution.py:385
  226.8 43.2 %all-to-all-start.4 = ((bf16[4,144,1152]{2,1,0:T(8,128)(2,1)}), bf16[4,144,1152]{2,1,0:T(8,128)(2,1)}, u32[]{:S(2)}, u32[]{:S(2)}) async-start(bf16[4,144,1152]{2,1,0:T(8,128)(2,1)} %tile.62), calls=%async_computation.4 | async-start | bytes 2654208 | tf_op jit(solution)/shard_map/all_to_all | solution.py:402
  235.4 52.8 %collective-permute-start.13 = (bf16[4,576,1152]{2,1,0:T(8,128)(2,1)}, bf16[4,576,1152]{2,1,0:T(8,128)(2,1)}, u32[]{:S(2)}, u32[]{:S(2)}) collective-permute-start(bf16[4,576,1152]{2,1,0:T(8,128)(2,1)} %pack_blocks.7.refs_4_.refs_5_), channel_id=1, source_target_pairs={{0,4},{4,0},{8,12},{12,8},{16,20},{20,16},{24,28},{28,24},{1,5},{5... | collective-permute-start | bytes 15925256 | tf_op jit(solution)/shard_map/ppermute | solution.py:385
  280.0 39.3 %all-to-all-start.5 = ((bf16[4,144,1152]{2,1,0:T(8,128)(2,1)}), bf16[4,144,1152]{2,1,0:T(8,128)(2,1)S(1)}, u32[]{:S(2)}, u32[]{:S(2)}) async-start(bf16[4,144,1152]{2,1,0:T(8,128)(2,1)} %tile.68), calls=%async_computation.5 | async-start | bytes 2654208 | tf_op jit(solution)/shard_map/all_to_all | solution.py:402
  284.7 45.8 %collective-permute-start.15 = (bf16[864,1152]{1,0:T(8,128)(2,1)}, bf16[864,1152]{1,0:T(8,128)(2,1)}, u32[]{:S(2)}, u32[]{:S(2)}) collective-permute-start(bf16[864,1152]{1,0:T(8,128)(2,1)} %get-tuple-element.955), channel_id=1, source_target_pairs={{0,1},{1,0},{2,3},{3,2},{4,5},{5,4},{6,7},{7,6},{8,9},{9,8},{10,11... | collective-permute-start | bytes 5971976 | tf_op jit(solution)/shard_map/ppermute | solution.py:385
  285.4 45.5 %collective-permute-start.16 = (bf16[864,1152]{1,0:T(8,128)(2,1)}, bf16[864,1152]{1,0:T(8,128)(2,1)}, u32[]{:S(2)}, u32[]{:S(2)}) collective-permute-start(bf16[864,1152]{1,0:T(8,128)(2,1)} %get-tuple-element.954), channel_id=1, source_target_pairs={{0,2},{1,3},{2,0},{3,1},{4,6},{5,7},{6,4},{7,5},{8,10},{9,11},{10,... | collective-permute-start | bytes 5971976 | tf_op jit(solution)/shard_map/ppermute | solution.py:385
  286.9 32.3 %collective-permute-start.17 = (bf16[4,512,384]{2,1,0:T(8,128)(2,1)}, bf16[4,512,384]{2,1,0:T(8,128)(2,1)}, u32[]{:S(2)}, u32[]{:S(2)}) collective-permute-start(bf16[4,512,384]{2,1,0:T(8,128)(2,1)} %get-tuple-element.498.refs_6_), channel_id=1, source_target_pairs={{0,4},{4,0},{8,12},{12,8},{16,20},{20,16},{24,28},{28,24},{1,5},{5... | collective-permute-start | bytes 4718600 | tf_op jit(solution)/shard_map/ppermute | solution.py:385
  288.2 31.0 %collective-permute-start.12 = (bf16[512,576]{0,1:T(8,128)(2,1)}, bf16[512,576]{0,1:T(8,128)(2,1)S(1)}, u32[]{:S(2)}, u32[]{:S(2)}) collective-permute-start(bf16[512,576]{0,1:T(8,128)(2,1)} %copy.167), channel_id=1, source_target_pairs={{0,4},{4,0},{8,12},{12,8},{16,20},{20,16},{24,28},{28,24},{1,5},{5... | collective-permute-start | bytes 1769480 | tf_op jit(solution)/shard_map/ppermute | solution.py:385
  335.4 58.8 %collective-permute-start.21 = (bf16[4,512,1152]{2,1,0:T(8,128)(2,1)}, bf16[4,512,1152]{2,1,0:T(8,128)(2,1)}, u32[]{:S(2)}, u32[]{:S(2)}) collective-permute-start(bf16[4,512,1152]{2,1,0:T(8,128)(2,1)} %get-tuple-element.505.refs_2_), channel_id=1, source_target_pairs={{0,4},{4,0},{8,12},{12,8},{16,20},{20,16},{24,28},{28,24},{1,5},{5... | collective-permute-start | bytes 14155784 | tf_op jit(solution)/shard_map/ppermute | solution.py:385
  339.4 70.4 %collective-permute-start.25 = (bf16[4,576,1152]{2,1,0:T(8,128)(2,1)}, bf16[4,576,1152]{2,1,0:T(8,128)(2,1)}, u32[]{:S(2)}, u32[]{:S(2)}) collective-permute-start(bf16[4,576,1152]{2,1,0:T(8,128)(2,1)} %pack_blocks.9.refs_4_.refs_6_), channel_id=1, source_target_pairs={{0,4},{4,0},{8,12},{12,8},{16,20},{20,16},{24,28},{28,24},{1,5},{5... | collective-permute-start | bytes 15925256 | tf_op jit(solution)/shard_map/ppermute | solution.py:385
  341.7 37.5 %all-to-all-start.6 = ((bf16[2,8,2,2,16,576]{5,4,2,3,0,1:T(8,128)(2,1)}), bf16[2,8,2,2,16,576]{5,4,2,3,0,1:T(8,128)(2,1)}, u32[]{:S(2)}, u32[]{:S(2)}) async-start(bf16[2,8,2,2,16,576]{5,4,2,3,0,1:T(8,128)(2,1)} %bitcast.219), calls=%async_computation.6 | async-start | bytes 2621440 | tf_op jit(solution)/shard_map/all_to_all | solution.py:1393
  346.9 46.0 %collective-permute-start.19 = (bf16[864,1152]{1,0:T(8,128)(2,1)}, bf16[864,1152]{1,0:T(8,128)(2,1)S(1)}, u32[]{:S(2)}, u32[]{:S(2)}) collective-permute-start(bf16[864,1152]{1,0:T(8,128)(2,1)} %get-tuple-element.953), channel_id=1, source_target_pairs={{0,1},{1,0},{2,3},{3,2},{4,5},{5,4},{6,7},{7,6},{8,9},{9,8},{10,11... | collective-permute-start | bytes 5971976 | tf_op jit(solution)/shard_map/ppermute | solution.py:385
  348.4 45.8 %collective-permute-start.20 = (bf16[864,1152]{1,0:T(8,128)(2,1)}, bf16[864,1152]{1,0:T(8,128)(2,1)}, u32[]{:S(2)}, u32[]{:S(2)}) collective-permute-start(bf16[864,1152]{1,0:T(8,128)(2,1)} %get-tuple-element.952), channel_id=1, source_target_pairs={{0,2},{1,3},{2,0},{3,1},{4,6},{5,7},{6,4},{7,5},{8,10},{9,11},{10,... | collective-permute-start | bytes 5971976 | tf_op jit(solution)/shard_map/ppermute | solution.py:385
  352.0 29.6 %collective-permute-start.18 = (bf16[512,576]{0,1:T(8,128)(2,1)}, bf16[512,576]{0,1:T(8,128)(2,1)}, u32[]{:S(2)}, u32[]{:S(2)}) collective-permute-start(bf16[512,576]{0,1:T(8,128)(2,1)} %copy.170), channel_id=1, source_target_pairs={{0,4},{4,0},{8,12},{12,8},{16,20},{20,16},{24,28},{28,24},{1,5},{5... | collective-permute-start | bytes 1769480 | tf_op jit(solution)/shard_map/ppermute | solution.py:385
  397.0 41.6 %collective-permute-start.27 = (bf16[288,1152]{1,0:T(8,128)(2,1)}, bf16[288,1152]{1,0:T(8,128)(2,1)}, u32[]{:S(2)}, u32[]{:S(2)}) collective-permute-start(bf16[288,1152]{1,0:T(8,128)(2,1)} %slice.586), channel_id=1, source_target_pairs={{0,1},{1,0},{2,3},{3,2},{4,5},{5,4},{6,7},{7,6},{8,9},{9,8},{10,11... | collective-permute-start | bytes 1990664 | tf_op jit(solution)/shard_map/ppermute | solution.py:385
  397.6 41.0 %collective-permute-start.28 = (bf16[288,1152]{1,0:T(8,128)(2,1)}, bf16[288,1152]{1,0:T(8,128)(2,1)}, u32[]{:S(2)}, u32[]{:S(2)}) collective-permute-start(bf16[288,1152]{1,0:T(8,128)(2,1)} %slice.587), channel_id=1, source_target_pairs={{0,2},{1,3},{2,0},{3,1},{4,6},{5,7},{6,4},{7,5},{8,10},{9,11},{10,... | collective-permute-start | bytes 1990664 | tf_op jit(solution)/shard_map/ppermute | solution.py:385
  408.0 64.4 %collective-permute-start.26 = (bf16[4,576,1152]{2,1,0:T(8,128)(2,1)}, bf16[4,576,1152]{2,1,0:T(8,128)(2,1)}, u32[]{:S(2)}, u32[]{:S(2)}) collective-permute-start(bf16[4,576,1152]{2,1,0:T(8,128)(2,1)} %pack_blocks.10.refs_4_.refs_5_), channel_id=1, source_target_pairs={{0,4},{4,0},{8,12},{12,8},{16,20},{20,16},{24,28},{28,24},{1,5},{5... | collective-permute-start | bytes 15925256 | tf_op jit(solution)/shard_map/ppermute | solution.py:385
  464.8 35.8 %collective-permute-start.31 = (bf16[4,512,384]{2,1,0:T(8,128)(2,1)}, bf16[4,512,384]{2,1,0:T(8,128)(2,1)}, u32[]{:S(2)}, u32[]{:S(2)}) collective-permute-start(bf16[4,512,384]{2,1,0:T(8,128)(2,1)} %get-tuple-element.551.refs_6_), channel_id=1, source_target_pairs={{0,4},{4,0},{8,12},{12,8},{16,20},{20,16},{24,28},{28,24},{1,5},{5... | collective-permute-start | bytes 4718600 | tf_op jit(solution)/shard_map/ppermute | solution.py:385
  465.1 35.6 %collective-permute-start.30 = (bf16[512,576]{0,1:T(8,128)(2,1)S(1)}, bf16[512,576]{0,1:T(8,128)(2,1)S(1)}, u32[]{:S(2)}, u32[]{:S(2)}) collective-permute-start(bf16[512,576]{0,1:T(8,128)(2,1)S(1)} %copy.174), channel_id=1, source_target_pairs={{0,4},{4,0},{8,12},{12,8},{16,20},{20,16},{24,28},{28,24},{1,5},{5... | collective-permute-start | bytes 1769480 | tf_op jit(solution)/shard_map/ppermute | solution.py:385
  500.6 30.2 %collective-permute-start.33 = (bf16[4,512,1152]{2,1,0:T(8,128)(2,1)}, bf16[4,512,1152]{2,1,0:T(8,128)(2,1)}, u32[]{:S(2)}, u32[]{:S(2)}) collective-permute-start(bf16[4,512,1152]{2,1,0:T(8,128)(2,1)} %get-tuple-element.565.refs_2_), channel_id=1, source_target_pairs={{0,4},{4,0},{8,12},{12,8},{16,20},{20,16},{24,28},{28,24},{1,5},{5... | collective-permute-start | bytes 14155784 | tf_op jit(solution)/shard_map/ppermute | solution.py:385
  552.6 48.2 %collective-permute-start.36 = (bf16[576,1152]{1,0:T(8,128)(2,1)}, bf16[576,1152]{1,0:T(8,128)(2,1)S(1)}, u32[]{:S(2)}, u32[]{:S(2)}) collective-permute-start(bf16[576,1152]{1,0:T(8,128)(2,1)} %get-tuple-element.602), channel_id=1, source_target_pairs={{0,1},{1,0},{2,3},{3,2},{4,5},{5,4},{6,7},{7,6},{8,9},{9,8},{10,11... | collective-permute-start | bytes 3981320 | tf_op jit(solution)/shard_map/ppermute | solution.py:385
  553.3 47.6 %collective-permute-start.37 = (bf16[576,1152]{1,0:T(8,128)(2,1)}, bf16[576,1152]{1,0:T(8,128)(2,1)S(1)}, u32[]{:S(2)}, u32[]{:S(2)}) collective-permute-start(bf16[576,1152]{1,0:T(8,128)(2,1)} %get-tuple-element.603), channel_id=1, source_target_pairs={{0,2},{1,3},{2,0},{3,1},{4,6},{5,7},{6,4},{7,5},{8,10},{9,11},{10,... | collective-permute-start | bytes 3981320 | tf_op jit(solution)/shard_map/ppermute | solution.py:385
  600.9 43.8 %collective-permute-start.38 = (bf16[4,512,896]{2,1,0:T(8,128)(2,1)}, bf16[4,512,896]{2,1,0:T(8,128)(2,1)}, u32[]{:S(2)}, u32[]{:S(2)}) collective-permute-start(bf16[4,512,896]{2,1,0:T(8,128)(2,1)} %get-tuple-element.618.refs_2_), channel_id=1, source_target_pairs={{0,4},{4,0},{8,12},{12,8},{16,20},{20,16},{24,28},{28,24},{1,5},{5... | collective-permute-start | bytes 11010056 | tf_op jit(solution)/shard_map/ppermute | solution.py:385
  604.4 37.8 %all-to-all-start.7 = ((bf16[2,1,2,16,16,576]{5,4,2,0,1,3:T(8,128)(2,1)}), bf16[2,1,2,16,16,576]{5,4,2,0,1,3:T(8,128)(2,1)}, u32[]{:S(2)}, u32[]{:S(2)}) async-start(bf16[2,1,2,16,16,576]{5,4,2,0,1,3:T(8,128)(2,1)} %copy.179), calls=%async_computation.7 | async-start | bytes 2621440 | tf_op jit(solution)/shard_map/all_to_all | solution.py:1440
  611.0 48.8 %collective-permute-start.42 = (bf16[576,1152]{1,0:T(8,128)(2,1)}, bf16[576,1152]{1,0:T(8,128)(2,1)}, u32[]{:S(2)}, u32[]{:S(2)}) collective-permute-start(bf16[576,1152]{1,0:T(8,128)(2,1)} %get-tuple-element.630), channel_id=1, source_target_pairs={{0,1},{1,0},{2,3},{3,2},{4,5},{5,4},{6,7},{7,6},{8,9},{9,8},{10,11... | collective-permute-start | bytes 3981320 | tf_op jit(solution)/shard_map/ppermute | solution.py:385
  611.8 48.0 %collective-permute-start.43 = (bf16[576,1152]{1,0:T(8,128)(2,1)}, bf16[576,1152]{1,0:T(8,128)(2,1)}, u32[]{:S(2)}, u32[]{:S(2)}) collective-permute-start(bf16[576,1152]{1,0:T(8,128)(2,1)} %get-tuple-element.631), channel_id=1, source_target_pairs={{0,2},{1,3},{2,0},{3,1},{4,6},{5,7},{6,4},{7,5},{8,10},{9,11},{10,... | collective-permute-start | bytes 3981320 | tf_op jit(solution)/shard_map/ppermute | solution.py:385
  615.4 29.3 %collective-permute-start.39 = (bf16[512,576]{0,1:T(8,128)(2,1)}, bf16[512,576]{0,1:T(8,128)(2,1)}, u32[]{:S(2)}, u32[]{:S(2)}) collective-permute-start(bf16[512,576]{0,1:T(8,128)(2,1)} %copy.181), channel_id=1, source_target_pairs={{0,4},{4,0},{8,12},{12,8},{16,20},{20,16},{24,28},{28,24},{1,5},{5... | collective-permute-start | bytes 1769480 | tf_op jit(solution)/shard_map/ppermute | solution.py:385
  678.4 35.9 %all-to-all-start.8 = ((bf16[4,144,1152]{2,1,0:T(8,128)(2,1)}), bf16[4,144,1152]{2,1,0:T(8,128)(2,1)}, u32[]{:S(2)}, u32[]{:S(2)}) async-start(bf16[4,144,1152]{2,1,0:T(8,128)(2,1)} %bitcast.80), calls=%async_computation.8 | async-start | bytes 2654208 | tf_op jit(solution)/shard_map/all_to_all | solution.py:402
  682.9 31.5 %collective-permute-start.44 = (bf16[288,1152]{1,0:T(8,128)(2,1)}, bf16[288,1152]{1,0:T(8,128)(2,1)S(1)}, u32[]{:S(2)}, u32[]{:S(2)}) collective-permute-start(bf16[288,1152]{1,0:T(8,128)(2,1)} %add_convert_fusion.9), channel_id=1, source_target_pairs={{0,1},{1,0},{2,3},{3,2},{4,5},{5,4},{6,7},{7,6},{8,9},{9,8},{10,11... | collective-permute-start | bytes 1990664 | tf_op jit(solution)/shard_map/ppermute | solution.py:385
  684.2 30.2 %collective-permute-start.45 = (bf16[288,1152]{1,0:T(8,128)(2,1)S(1)}, bf16[288,1152]{1,0:T(8,128)(2,1)S(1)}, u32[]{:S(2)}, u32[]{:S(2)}) collective-permute-start(bf16[288,1152]{1,0:T(8,128)(2,1)S(1)} %copy-done.69), channel_id=1, source_target_pairs={{0,2},{1,3},{2,0},{3,1},{4,6},{5,7},{6,4},{7,5},{8,10},{9,11},{10,... | collective-permute-start | bytes 1990664 | tf_op jit(solution)/shard_map/ppermute | solution.py:385
  719.8 32.9 %collective-permute-start.47 = (bf16[4,512,1152]{2,1,0:T(8,128)(2,1)}, bf16[4,512,1152]{2,1,0:T(8,128)(2,1)}, u32[]{:S(2)}, u32[]{:S(2)}) collective-permute-start(bf16[4,512,1152]{2,1,0:T(8,128)(2,1)} %get-tuple-element.655.refs_2_), channel_id=1, source_target_pairs={{0,4},{4,0},{8,12},{12,8},{16,20},{20,16},{24,28},{28,24},{1,5},{5... | collective-permute-start | bytes 14155784 | tf_op jit(solution)/shard_map/ppermute | solution.py:385
  720.3 31.2 %collective-permute-start.48 = (bf16[576,1152]{1,0:T(8,128)(2,1)}, bf16[576,1152]{1,0:T(8,128)(2,1)S(1)}, u32[]{:S(2)}, u32[]{:S(2)}) collective-permute-start(bf16[576,1152]{1,0:T(8,128)(2,1)} %get-tuple-element.665), channel_id=1, source_target_pairs={{0,1},{1,0},{2,3},{3,2},{4,5},{5,4},{6,7},{7,6},{8,9},{9,8},{10,11... | collective-permute-start | bytes 3981320 | tf_op jit(solution)/shard_map/ppermute | solution.py:385
  721.7 31.0 %collective-permute-start.49 = (bf16[576,1152]{1,0:T(8,128)(2,1)}, bf16[576,1152]{1,0:T(8,128)(2,1)S(1)}, u32[]{:S(2)}, u32[]{:S(2)}) collective-permute-start(bf16[576,1152]{1,0:T(8,128)(2,1)} %get-tuple-element.666), channel_id=1, source_target_pairs={{0,2},{1,3},{2,0},{3,1},{4,6},{5,7},{6,4},{7,5},{8,10},{9,11},{10,... | collective-permute-start | bytes 3981320 | tf_op jit(solution)/shard_map/ppermute | solution.py:385
  722.2 85.0 %all-to-all-start.9 = ((bf16[4,144,1152]{2,1,0:T(8,128)(2,1)}), bf16[4,144,1152]{2,1,0:T(8,128)(2,1)}, u32[]{:S(2)}, u32[]{:S(2)}) async-start(bf16[4,144,1152]{2,1,0:T(8,128)(2,1)} %bitcast.82), calls=%async_computation.9 | async-start | bytes 2654208 | tf_op jit(solution)/shard_map/all_to_all | solution.py:402
  753.8 53.5 %collective-permute-start.50 = (bf16[576,1152]{1,0:T(8,128)(2,1)}, bf16[576,1152]{1,0:T(8,128)(2,1)S(1)}, u32[]{:S(2)}, u32[]{:S(2)}) collective-permute-start(bf16[576,1152]{1,0:T(8,128)(2,1)} %get-tuple-element.690), channel_id=1, source_target_pairs={{0,1},{1,0},{2,3},{3,2},{4,5},{5,4},{6,7},{7,6},{8,9},{9,8},{10,11... | collective-permute-start | bytes 3981320 | tf_op jit(solution)/shard_map/ppermute | solution.py:385
  754.5 52.8 %collective-permute-start.51 = (bf16[576,1152]{1,0:T(8,128)(2,1)}, bf16[576,1152]{1,0:T(8,128)(2,1)S(1)}, u32[]{:S(2)}, u32[]{:S(2)}) collective-permute-start(bf16[576,1152]{1,0:T(8,128)(2,1)} %get-tuple-element.691), channel_id=1, source_target_pairs={{0,2},{1,3},{2,0},{3,1},{4,6},{5,7},{6,4},{7,5},{8,10},{9,11},{10,... | collective-permute-start | bytes 3981320 | tf_op jit(solution)/shard_map/ppermute | solution.py:385
  757.6 49.6 %collective-permute-start.53 = (bf16[288,1152]{1,0:T(8,128)(2,1)}, bf16[288,1152]{1,0:T(8,128)(2,1)S(1)}, u32[]{:S(2)}, u32[]{:S(2)}) collective-permute-start(bf16[288,1152]{1,0:T(8,128)(2,1)} %add_convert_fusion.6), channel_id=1, source_target_pairs={{0,2},{1,3},{2,0},{3,1},{4,6},{5,7},{6,4},{7,5},{8,10},{9,11},{10,... | collective-permute-start | bytes 1990664 | tf_op jit(solution)/shard_map/ppermute | solution.py:385
  759.6 47.6 %collective-permute-start.52 = (bf16[288,1152]{1,0:T(8,128)(2,1)}, bf16[288,1152]{1,0:T(8,128)(2,1)}, u32[]{:S(2)}, u32[]{:S(2)}) collective-permute-start(bf16[288,1152]{1,0:T(8,128)(2,1)} %add_convert_fusion.7), channel_id=1, source_target_pairs={{0,1},{1,0},{2,3},{3,2},{4,5},{5,4},{6,7},{7,6},{8,9},{9,8},{10,11... | collective-permute-start | bytes 1990664 | tf_op jit(solution)/shard_map/ppermute | solution.py:385
  810.0 39.2 %collective-permute-start.58 = (bf16[576,1152]{1,0:T(8,128)(2,1)}, bf16[576,1152]{1,0:T(8,128)(2,1)S(1)}, u32[]{:S(2)}, u32[]{:S(2)}) collective-permute-start(bf16[576,1152]{1,0:T(8,128)(2,1)} %get-tuple-element.719), channel_id=1, source_target_pairs={{0,1},{1,0},{2,3},{3,2},{4,5},{5,4},{6,7},{7,6},{8,9},{9,8},{10,11... | collective-permute-start | bytes 3981320 | tf_op jit(solution)/shard_map/ppermute | solution.py:385
  810.8 38.5 %collective-permute-start.59 = (bf16[576,1152]{1,0:T(8,128)(2,1)}, bf16[576,1152]{1,0:T(8,128)(2,1)S(1)}, u32[]{:S(2)}, u32[]{:S(2)}) collective-permute-start(bf16[576,1152]{1,0:T(8,128)(2,1)} %get-tuple-element.720), channel_id=1, source_target_pairs={{0,2},{1,3},{2,0},{3,1},{4,6},{5,7},{6,4},{7,5},{8,10},{9,11},{10,... | collective-permute-start | bytes 3981320 | tf_op jit(solution)/shard_map/ppermute | solution.py:385
  816.3 39.7 %collective-permute-start.57 = (bf16[288,1152]{1,0:T(8,128)(2,1)}, bf16[288,1152]{1,0:T(8,128)(2,1)S(1)}, u32[]{:S(2)}, u32[]{:S(2)}) collective-permute-start(bf16[288,1152]{1,0:T(8,128)(2,1)} %add_convert_fusion.4), channel_id=1, source_target_pairs={{0,2},{1,3},{2,0},{3,1},{4,6},{5,7},{6,4},{7,5},{8,10},{9,11},{10,... | collective-permute-start | bytes 1990664 | tf_op jit(solution)/shard_map/ppermute | solution.py:385
  823.7 38.4 %all-to-all-start.10 = ((bf16[4,144,1152]{2,1,0:T(8,128)(2,1)}), bf16[4,144,1152]{2,1,0:T(8,128)(2,1)}, u32[]{:S(2)}, u32[]{:S(2)}) async-start(bf16[4,144,1152]{2,1,0:T(8,128)(2,1)} %bitcast.84), calls=%async_computation.10 | async-start | bytes 2654208 | tf_op jit(solution)/shard_map/all_to_all | solution.py:402
  862.1 45.6 %collective-permute-start.60 = (bf16[576,1152]{1,0:T(8,128)(2,1)}, bf16[576,1152]{1,0:T(8,128)(2,1)}, u32[]{:S(2)}, u32[]{:S(2)}) collective-permute-start(bf16[576,1152]{1,0:T(8,128)(2,1)} %get-tuple-element.726), channel_id=1, source_target_pairs={{0,1},{1,0},{2,3},{3,2},{4,5},{5,4},{6,7},{7,6},{8,9},{9,8},{10,11... | collective-permute-start | bytes 3981320 | tf_op jit(solution)/shard_map/ppermute | solution.py:385
  863.4 44.3 %collective-permute-start.61 = (bf16[576,1152]{1,0:T(8,128)(2,1)}, bf16[576,1152]{1,0:T(8,128)(2,1)}, u32[]{:S(2)}, u32[]{:S(2)}) collective-permute-start(bf16[576,1152]{1,0:T(8,128)(2,1)} %get-tuple-element.727), channel_id=1, source_target_pairs={{0,2},{1,3},{2,0},{3,1},{4,6},{5,7},{6,4},{7,5},{8,10},{9,11},{10,... | collective-permute-start | bytes 3981320 | tf_op jit(solution)/shard_map/ppermute | solution.py:385
  863.9 50.4 %all-to-all-start.11 = ((bf16[4,144,1152]{2,1,0:T(8,128)(2,1)}), bf16[4,144,1152]{2,1,0:T(8,128)(2,1)}, u32[]{:S(2)}, u32[]{:S(2)}) async-start(bf16[4,144,1152]{2,1,0:T(8,128)(2,1)} %bitcast.100), calls=%async_computation.11 | async-start | bytes 2654208 | tf_op jit(solution)/shard_map/all_to_all | solution.py:402
  869.3 37.3 %collective-permute-start.62 = (bf16[288,1152]{1,0:T(8,128)(2,1)}, bf16[288,1152]{1,0:T(8,128)(2,1)S(1)}, u32[]{:S(2)}, u32[]{:S(2)}) collective-permute-start(bf16[288,1152]{1,0:T(8,128)(2,1)} %add_convert_fusion.3), channel_id=1, source_target_pairs={{0,1},{1,0},{2,3},{3,2},{4,5},{5,4},{6,7},{7,6},{8,9},{9,8},{10,11... | collective-permute-start | bytes 1990664 | tf_op jit(solution)/shard_map/ppermute | solution.py:385
  870.6 37.2 %collective-permute-start.63 = (bf16[288,1152]{1,0:T(8,128)(2,1)}, bf16[288,1152]{1,0:T(8,128)(2,1)}, u32[]{:S(2)}, u32[]{:S(2)}) collective-permute-start(bf16[288,1152]{1,0:T(8,128)(2,1)} %add_convert_fusion.2), channel_id=1, source_target_pairs={{0,2},{1,3},{2,0},{3,1},{4,6},{5,7},{6,4},{7,5},{8,10},{9,11},{10,... | collective-permute-start | bytes 1990664 | tf_op jit(solution)/shard_map/ppermute | solution.py:385
  922.9 68.5 %all-to-all-start.12 = ((bf16[4,144,1152]{2,1,0:T(8,128)(2,1)}), bf16[4,144,1152]{2,1,0:T(8,128)(2,1)}, u32[]{:S(2)}, u32[]{:S(2)}) async-start(bf16[4,144,1152]{2,1,0:T(8,128)(2,1)} %bitcast.112), calls=%async_computation.12 | async-start | bytes 2654208 | tf_op jit(solution)/shard_map/all_to_all | solution.py:402
  952.7 38.7 %collective-permute-start.73 = (bf16[512,288]{1,0:T(8,128)(2,1)}, bf16[512,288]{1,0:T(8,128)(2,1)S(1)}, u32[]{:S(2)}, u32[]{:S(2)}) collective-permute-start(bf16[512,288]{1,0:T(8,128)(2,1)} %get-tuple-element.803), channel_id=1, source_target_pairs={{0,1},{1,0},{2,3},{3,2},{4,5},{5,4},{6,7},{7,6},{8,9},{9,8},{10,11... | collective-permute-start | bytes 884744 | tf_op jit(solution)/shard_map/ppermute | solution.py:385
  953.5 37.9 %collective-permute-start.74 = (bf16[512,288]{1,0:T(8,128)(2,1)}, bf16[512,288]{1,0:T(8,128)(2,1)S(1)}, u32[]{:S(2)}, u32[]{:S(2)}) collective-permute-start(bf16[512,288]{1,0:T(8,128)(2,1)} %get-tuple-element.804), channel_id=1, source_target_pairs={{0,2},{1,3},{2,0},{3,1},{4,6},{5,7},{6,4},{7,5},{8,10},{9,11},{10,... | collective-permute-start | bytes 884744 | tf_op jit(solution)/shard_map/ppermute | solution.py:385
  955.0 36.4 %collective-permute-start.75 = (bf16[512,288]{1,0:T(8,128)(2,1)}, bf16[512,288]{1,0:T(8,128)(2,1)S(1)}, u32[]{:S(2)}, u32[]{:S(2)}) collective-permute-start(bf16[512,288]{1,0:T(8,128)(2,1)} %get-tuple-element.805), channel_id=1, source_target_pairs={{0,3},{1,2},{2,1},{3,0},{4,7},{5,6},{6,5},{7,4},{8,11},{9,10},{10,... | collective-permute-start | bytes 884744 | tf_op jit(solution)/shard_map/ppermute | solution.py:385
  994.0 36.2 %all-to-all-start.13 = ((bf16[4,144,1152]{2,1,0:T(8,128)(2,1)}), bf16[4,144,1152]{2,1,0:T(8,128)(2,1)}, u32[]{:S(2)}, u32[]{:S(2)}) async-start(bf16[4,144,1152]{2,1,0:T(8,128)(2,1)} %bitcast.121), calls=%async_computation.13 | async-start | bytes 2654208 | tf_op jit(solution)/shard_map/all_to_all | solution.py:402
  (142 other events, 1278.7 us)
Sparse Core Ops, SparseCore 0:
  65.1 76.0 all-gather.3

commit v3 on v2

--- a/solution.py
+++ b/solution.py
@@ -599,8 +599,8 @@
 def attention_kernel(size, period, steps, *refs):
     stream_ref, mod_ref, bias_ref, added_ref = refs[:4]
     weights = refs[4:6]
-    mid_ref, mine_ref, other_ref, qkv_ref, heads_ref, log_ref, out_ref, acc = refs[6:]
-    input_refs = (mine_ref, other_ref)
+    mid_ref, mine_ref, other_ref, qkv_ref, heads_ref, log_ref, out_ref, acc, kept_ref = refs[6:]
+    input_refs = (mine_ref, kept_ref)
     step = pl.program_id(0)
     tokens = stream_ref.shape[1]
     used = qkv_ref.shape[2]
@@ -617,6 +617,7 @@
             input_refs[half][...] = (
                 normed[half] * (1.0 + mod_ref[half, 1:2, :]) + mod_ref[half, 0:1, :]
             ).astype(jnp.bfloat16)
+        other_ref[...] = kept_ref[...].T
         acc[...] = jnp.zeros_like(acc)
 
     rows = dot(input_refs[0][...], weights[0][0, :, :used], PLAIN)
@@ -677,7 +678,7 @@
         out_specs=[
             whole(stream.shape),
             whole((tokens, half)),
-            whole((tokens, half)),
+            whole((half, tokens)),
             stepped((tokens, used)),
             stepped((tokens, padded)),
             stepped((tokens, LANES)),
@@ -686,7 +687,7 @@
         out_shape=[
             of(stream.shape, f32),
             of((tokens, half), bf16),
-            of((tokens, half), bf16),
+            of((half, tokens), bf16),
             of((steps, tokens, used), bf16),
             of((steps, tokens, padded), bf16),
             of((steps, tokens, LANES), f32),
@@ -694,6 +695,7 @@
         ],
         scratch_shapes=[
             pltpu.VMEM(stream.shape, f32),
+            pltpu.VMEM((tokens, half), bf16),
         ],
         compiler_params=pltpu.CompilerParams(vmem_limit_bytes=VMEM_BYTES),
         cost_estimate=SMALL_COST,
@@ -704,8 +706,8 @@
 def mlp_kernel(steps, *refs):
     mid_ref, mod_ref, bias_ref, added_ref = refs[:4]
     hidden, output = (refs[4:6], refs[6:8])
-    stream_ref, mine_ref, other_ref, active_ref, slope_ref, out_ref, acc = refs[8:]
-    input_refs = (mine_ref, other_ref)
+    stream_ref, mine_ref, other_ref, active_ref, slope_ref, out_ref, acc, kept_ref = refs[8:]
+    input_refs = (mine_ref, kept_ref)
     step = pl.program_id(0)
 
     @pl.when(step == 0)
@@ -715,6 +717,7 @@
             input_refs[half][...] = (
                 normed[half] * (1.0 + mod_ref[half, 4:5, :]) + mod_ref[half, 3:4, :]
             ).astype(jnp.bfloat16)
+        other_ref[...] = kept_ref[...].T
         acc[...] = jnp.zeros_like(acc)
 
     pre = dot(input_refs[0][...], hidden[0][0], PLAIN)
@@ -756,7 +759,7 @@
         out_specs=[
             whole(mid.shape),
             whole((tokens, half)),
-            whole((tokens, half)),
+            whole((half, tokens)),
             stepped((tokens, columns)),
             stepped((tokens, columns)),
             whole(mid.shape),
@@ -764,13 +767,14 @@
         out_shape=[
             of(mid.shape, f32),
             of((tokens, half), bf16),
-            of((tokens, half), bf16),
+            of((half, tokens), bf16),
             of((steps, tokens, columns), bf16),
             of((steps, tokens, columns), bf16),
             of(mid.shape, bf16),
         ],
         scratch_shapes=[
             pltpu.VMEM(mid.shape, f32),
+            pltpu.VMEM((tokens, half), bf16),
         ],
         compiler_params=pltpu.CompilerParams(vmem_limit_bytes=VMEM_BYTES),
         cost_estimate=SMALL_COST,
@@ -781,8 +785,8 @@
 def mlp_back_kernel(steps, *refs):
     grad_ref, mid_ref, out_ref, slope_ref, mod_ref = refs[:5]
     hidden, output = (refs[5:7], refs[7:9])
-    grad_mid_ref, mine_ref, other_ref, grad_pre_ref, small_ref, sum_ref, acc = refs[9:]
-    grad_mlp_refs = (mine_ref, other_ref)
+    grad_mid_ref, mine_ref, other_ref, grad_pre_ref, small_ref, sum_ref, acc, kept_ref = refs[9:]
+    grad_mlp_refs = (mine_ref, kept_ref)
     step = pl.program_id(0)
 
     @pl.when(step == 0)
@@ -795,6 +799,7 @@
                 grad * out_ref[half].astype(jnp.float32), 0, keepdims=True
             )
             small_ref[half, 3:4, :] = jnp.sum(scaled.astype(jnp.float32), 0, keepdims=True)
+        other_ref[...] = kept_ref[...].T
         acc[...] = jnp.zeros_like(acc)
 
     grad_act = dot(grad_mlp_refs[0][...], output[0][0], PLAIN)
@@ -829,7 +834,7 @@
         out_specs=[
             whole(mid.shape),
             whole((tokens, half)),
-            whole((tokens, half)),
+            whole((half, tokens)),
             stepped((tokens, columns)),
             whole((2, 8, half)),
             stepped((1, columns)),
@@ -837,13 +842,14 @@
         out_shape=[
             of(mid.shape, f32),
             of((tokens, half), bf16),
-            of((tokens, half), bf16),
+            of((half, tokens), bf16),
             of((steps, tokens, columns), bf16),
             of((2, 8, half), f32),
             of((steps, 1, columns), f32),
         ],
         scratch_shapes=[
             pltpu.VMEM(mid.shape, f32),
+            pltpu.VMEM((tokens, half), bf16),
         ],
         compiler_params=pltpu.CompilerParams(vmem_limit_bytes=VMEM_BYTES),
         cost_estimate=SMALL_COST,
@@ -854,8 +860,8 @@
 def attention_back_kernel(size, period, steps, *refs):
     grad_ref, stream_ref, out_ref, qkv_ref, log_ref, mod_ref = refs[:6]
     weights = refs[6:8]
-    grad_in_ref, mine_ref, other_ref, grad_qkv_ref, small_ref, sum_ref, acc = refs[8:]
-    grad_attn_refs = (mine_ref, other_ref)
+    grad_in_ref, mine_ref, other_ref, grad_qkv_ref, small_ref, sum_ref, acc, kept_ref = refs[8:]
+    grad_attn_refs = (mine_ref, kept_ref)
     step = pl.program_id(0)
     tokens = stream_ref.shape[1]
     used = qkv_ref.shape[2]
@@ -875,6 +881,7 @@
                 grad * out_ref[half].astype(jnp.float32), 0, keepdims=True
             )
             small_ref[half, 3:4, :] = jnp.sum(scaled.astype(jnp.float32), 0, keepdims=True)
+        other_ref[...] = kept_ref[...].T
         acc[...] = jnp.zeros_like(acc)
 
     grad_heads = dot(grad_attn_refs[0][...], weights[0][0, :, columns - padded :], PLAIN)
@@ -938,7 +945,7 @@
         out_specs=[
             whole(stream.shape),
             whole((tokens, half)),
-            whole((tokens, half)),
+            whole((half, tokens)),
             stepped((tokens, used)),
             whole((2, 8, half)),
             stepped((1, used)),
@@ -946,13 +953,14 @@
         out_shape=[
             of(stream.shape, f32),
             of((tokens, half), bf16),
-            of((tokens, half), bf16),
+            of((half, tokens), bf16),
             of((steps, tokens, used), bf16),
             of((2, 8, half), f32),
             of((steps, 1, used), f32),
         ],
         scratch_shapes=[
             pltpu.VMEM(stream.shape, f32),
+            pltpu.VMEM((tokens, half), bf16),
         ],
         compiler_params=pltpu.CompilerParams(vmem_limit_bytes=VMEM_BYTES),
         cost_estimate=SMALL_COST,
@@ -963,17 +971,16 @@
 def weight_kernel(pairs, overlap, steps, *refs):
     inputs = refs[: 4 * pairs]
     outs = refs[4 * pairs : 4 * pairs + 5]
-    turned = refs[4 * pairs + 5 : 6 * pairs + 5]
-    buffer, sems = refs[6 * pairs + 5 :]
+    turned = refs[4 * pairs + 5 : 5 * pairs + 5]
+    buffer, sems = refs[5 * pairs + 5 :]
     step = pl.program_id(0)
     slot = step % 2
     for pair in range(pairs):
-        mine, theirs, _, _ = inputs[4 * pair : 4 * pair + 4]
+        mine = inputs[4 * pair]
 
         @pl.when(step == 0)
         def _():
-            turned[2 * pair][...] = mine[...].T
-            turned[2 * pair + 1][...] = theirs[...].T
+            turned[pair][...] = mine[...].T
 
     @pl.when(step >= 2)
     def _():
@@ -981,9 +988,9 @@
 
     sums = []
     for pair in range(pairs):
-        _, _, mine, theirs = inputs[4 * pair : 4 * pair + 4]
-        total = dot(turned[2 * pair][...], mine[0], PLAIN)
-        sums.append(total + dot(turned[2 * pair + 1][...], theirs[0], PLAIN))
+        _, rows, mine, theirs = inputs[4 * pair : 4 * pair + 4]
+        total = dot(turned[pair][...], mine[0], PLAIN)
+        sums.append(total + dot(rows[...], theirs[0], PLAIN))
     if pairs == 1:
         buffer[slot] = sums[0].astype(jnp.bfloat16)
     else:
@@ -1019,7 +1026,7 @@
 
 def weight_grads(columns, overlap, *pairs, flops=0):
     steps, tokens, _ = pairs[0][2].shape
-    half = pairs[0][1].shape[1]
+    half = pairs[0][1].shape[0]
     bf16 = jnp.bfloat16
     specs, values, turned = ([], [], [])
     for mine, theirs, blocks, their_blocks in pairs:
@@ -1030,7 +1037,7 @@
             stepped(blocks.shape[1:]),
         ]
         values += [mine, theirs, blocks, their_blocks]
-        turned += [pltpu.VMEM((half, tokens), bf16)] * 2
+        turned.append(pltpu.VMEM((half, tokens), bf16))
     return pl.pallas_call(
         functools.partial(weight_kernel, len(pairs), overlap, steps),
         grid=(steps,),
@@ -1234,6 +1241,12 @@
     attn_ready = attn_shards()
     tokens = after(open_tokens(tokens, col_width), attn_ready[0])
     cotangent = open_tokens(cotangent, col_width)
+    frame_part, places = tokens.shape[1:3]
+    frames, place_part = cotangent.shape[1:3]
+    period = 16 if place_part % 16 == 0 else place_part
+    groups = place_part // period
+    first_size = places
+    second_size = frames * period
     gathering.step(attn_ready[0])
     token_blocks = arriving(tokens)
     hidden_ready = hidden_shards(attn_ready[0])
@@ -1246,12 +1259,6 @@
     output_ready = output_shards()
     stream_first = entered(token_blocks)
     ada_weight = ada_weight.reshape(layer_count, row_width, 6, col_width)
-    frame_part, places = tokens.shape[1:3]
-    frames, place_part = cotangent.shape[1:3]
-    period = 16 if place_part % 16 == 0 else place_part
-    groups = place_part // period
-    first_size = places
-    second_size = frames * period
 
     half = width // 2
 
@@ -1377,7 +1384,12 @@
     gathering.step(attn_ready[1], modulation)
     mid_first, *attn_first = attn_part(0, after(stream_first, *gathering.sent))
     gathering.step(hidden_ready[1], mid_first)
-    gathering.step(output_ready[1])
+    cotangent = after(cotangent, *gathering.sent)
+    cotangent = cotangent.reshape(clip_count, frames, groups, period, col_width)
+    gradient_blocks = relative(
+        jnp.swapaxes(cotangent, 1, 2).reshape(clip_count, -1, col_width), place
+    )
+    gathering.step(output_ready[1], *gradient_blocks)
     input_attn, heads = after((attn_first[1], attn_first[3]), *gathering.sent)
     swapped_first = [swap(input_attn), swap(heads)]
     output_first, *mlp_first = mlp_part(0, after(mid_first, *gathering.sent))
@@ -1392,23 +1404,21 @@
     moving = moving.transpose(0, 2, 3, 1, 4, 5)
     moved = lax.all_to_all(moving, "row", split_axis=1, concat_axis=3, tiled=True)
     gathering.step(None, moved, *swapped_first[2:])
-    cotangent, moved = after((cotangent, moved), *gathering.sent)
-    cotangent = cotangent.reshape(clip_count, frames, groups, period, col_width)
-    gradient_blocks = arriving(jnp.swapaxes(cotangent, 1, 2))
+    moved = after(moved, *gathering.sent)
     moved = moved.reshape(2, -1, half)
     stream_second = mine_first(moved, place, 0).astype(jnp.float32)
+    gathering.step(None)
+    stream_second = after(stream_second, gathering.done[5][0])
     mid_second, *attn_second = attn_part(1, stream_second)
-    gathering.step(None, mid_second)
-    gradient_blocks, mid_second, input_attn, heads = together(
-        gradient_blocks, mid_second, attn_second[1], attn_second[3]
-    )
+    mid_second, input_attn, heads = together(mid_second, attn_second[1], attn_second[3])
     swapped_second = [swap(input_attn), swap(heads)]
+    gradient_blocks = trade(after(gradient_blocks, mid_second))
     output_second, *mlp_second = mlp_part(1, mid_second)
     saved_second = (stream_second, mid_second, attn_second, mlp_second)
+    gradient_blocks, swapped_second, input_mlp, active, output_second = together(
+        gradient_blocks, swapped_second, mlp_second[1], mlp_second[2], output_second
+    )
     grad = entered(gradient_blocks)
-    grad, swapped_second, input_mlp, active, output_second = together(
-        grad, swapped_second, mlp_second[1], mlp_second[2], output_second
-    )
     swapped_second += [swap(input_mlp), swap(active)]
 
     grad_mid, grad_mlp, grad_sent, grad_pre, small_mlp_second, hidden_sum_second = mlp_grads(
@@ -1418,8 +1428,7 @@
         grad_mid, grad_mlp, grad_sent, grad_pre, swapped_second, output_second
     )
     received = swap(grad_sent)
-    result_blocks = leaving(output_second)
-    received, result_blocks, grad_pre = together(received, result_blocks, grad_pre)
+    received, grad_pre = together(received, grad_pre)
     received_pre = swap(grad_pre)
     output_part = output_terms(saved_second, swapped_second, grad_mlp, received)
     output_part, received_pre, grad_mid = together(output_part, received_pre, grad_mid)
@@ -1430,35 +1439,37 @@
     grad_second, grad_attn, grad_sent, grad_qkv, small_attn_second, qkv_sum_second = attn_grads(
         1, grad_mid, saved_second
     )
-    grad_second, grad_attn, grad_sent, grad_qkv, output_part = together(
-        grad_second, grad_attn, grad_sent, grad_qkv, output_part
+    grad_second, grad_attn, grad_sent, grad_qkv, output_part, output_second = together(
+        grad_second, grad_attn, grad_sent, grad_qkv, output_part, output_second
     )
     received = [swap(grad_qkv), swap(grad_sent)]
     sides = scatter_sides(output_part)
+    result_blocks = leaving(output_second)
     moving = mine_first(grad_second.astype(jnp.bfloat16), place, 0)
     moving = moving.reshape(2, 1, groups, frames, period, half)
     moved = lax.all_to_all(moving, "row", split_axis=3, concat_axis=1, tiled=True)
-    received, grad_attn, grad_qkv, sides, moving = together(
-        received, grad_attn, grad_qkv, sides, moving
+    received, grad_attn, grad_qkv, sides, result_blocks = together(
+        received, grad_attn, grad_qkv, sides, result_blocks
     )
     output_part = scatter_plane(output_part, sides)
     attn_blocks = attn_terms(
         saved_second, swapped_second, grad_attn, grad_qkv, received, 15 * 10**9
     )
-    attn_blocks, hidden_part = together(attn_blocks, hidden_part)
+    attn_blocks, hidden_part, output_part = together(attn_blocks, hidden_part, output_part)
     attn_part_second = scatter_corner(attn_blocks)
     sides = scatter_sides(hidden_part)
     output_total = add_blocks(output_part)
     moved, output_total, sides = together(moved, output_total, sides)
+    hidden_part = scatter_plane(hidden_part, sides)
     moved = moved.transpose(0, 3, 1, 2, 4, 5).reshape(2, -1, half)
     returned = mine_first(moved, place, 0).astype(jnp.float32)
     output_pieces = over_depth(output_total, place)
-    hidden_part = scatter_plane(hidden_part, sides)
+    result_blocks = trade(after(result_blocks, output_total))
     grad_mid, grad_mlp, grad_sent, grad_pre, small_mlp_first, hidden_sum_first = mlp_grads(
         0, returned, saved_first
     )
-    grad_mid, grad_mlp, grad_sent, grad_pre, output_pieces, hidden_part = together(
-        grad_mid, grad_mlp, grad_sent, grad_pre, output_pieces, hidden_part
+    grad_mid, grad_mlp, grad_sent, grad_pre, output_pieces, hidden_part, result_blocks = together(
+        grad_mid, grad_mlp, grad_sent, grad_pre, output_pieces, hidden_part, result_blocks
     )
     received = swap(grad_sent)
     hidden_total = add_blocks(hidden_part)
@@ -1466,15 +1477,15 @@
     hidden_pieces = over_depth(hidden_total, place)
     received_pre = swap(grad_pre)
     output_blocks = output_terms(saved_first, swapped_first, grad_mlp, received)
-    output_blocks, received_pre, attn_part_second = together(
-        output_blocks, received_pre, attn_part_second
-    )
+    output_blocks, received_pre = together(output_blocks, received_pre)
     output_part = scatter_corner(output_blocks)
+    hidden_blocks = hidden_terms(saved_first, swapped_first, grad_pre, received_pre)
+    hidden_blocks, grad_mid, attn_part_second = together(
+        hidden_blocks, grad_mid, attn_part_second
+    )
     sides = scatter_sides(attn_part_second)
+    grad_mid, sides = together(grad_mid, sides)
     attn_part_second = scatter_plane(attn_part_second, sides)
-    received_pre, _ = together(received_pre, sides)
-    hidden_blocks = hidden_terms(saved_first, swapped_first, grad_pre, received_pre)
-    hidden_blocks, grad_mid = together(hidden_blocks, grad_mid)
     hidden_part = scatter_corner(hidden_blocks)
     grad_first, grad_attn, grad_sent, grad_qkv, small_attn_first, qkv_sum_first = attn_grads(
         0, grad_mid, saved_first
@@ -1492,26 +1503,13 @@
     )
     received = [swap(grad_qkv), swap(grad_sent)]
     sides = scatter_sides(output_part)
+    attn_total = add_blocks(attn_part_second)
+    received, sides, attn_total, grad_attn, grad_qkv = together(
+        received, sides, attn_total, grad_attn, grad_qkv
+    )
     output_part = scatter_plane(output_part, sides)
-    attn_total = add_blocks(attn_part_second)
     attn_pieces = over_depth(attn_total, place)
-    received, _, grad_attn, grad_qkv = together(
-        received, (sides, attn_total), grad_attn, grad_qkv
-    )
     attn_blocks = attn_terms(saved_first, swapped_first, grad_attn, grad_qkv, received)
-    attn_blocks, output_part, hidden_part, small_mlp_first, grad_first = together(
-        attn_blocks, output_part, hidden_part, small_mlp_first, grad_first
-    )
-    attn_part_first = scatter_corner(attn_blocks)
-    sides = scatter_sides(hidden_part)
-    output_total = add_blocks(output_part)
-    output_total, sides, grad_first, small_attn_first, attn_pieces = together(
-        output_total, sides, grad_first, small_attn_first, attn_pieces
-    )
-    hidden_part = scatter_plane(hidden_part, sides)
-    output_first_pieces = over_depth(output_total, place)
-    gradient_blocks = leaving(grad_first)
-
     def small_grads(small_attn, small_mlp, qkv_sum, hidden_sum):
         return (
             jnp.concatenate((small_attn[:, :3], small_mlp[:, :3]), 1),
@@ -1544,8 +1542,25 @@
         pieces.append(outgrad[step].reshape(-1))
         sending.append(jnp.concatenate(pieces))
     sending = [value.reshape(-1, LANES) for value in sending]
-    attn_part_first, hidden_part, gradient_blocks, sending = together(
-        attn_part_first, hidden_part, gradient_blocks, sending
+    attn_blocks, output_part, hidden_part, grad_first, result_blocks = together(
+        attn_blocks, output_part, hidden_part, grad_first, result_blocks
+    )
+    attn_part_first = scatter_corner(attn_blocks)
+    sides = scatter_sides(hidden_part)
+    output_total = add_blocks(output_part)
+    output_total, sides, grad_first, attn_pieces = together(
+        output_total, sides, grad_first, attn_pieces
+    )
+    hidden_part = scatter_plane(hidden_part, sides)
+    output_first_pieces = over_depth(output_total, place)
+    gradient_blocks = leaving(grad_first)
+
+    result = assembled(result_blocks, jnp.bfloat16)
+    result = result.reshape(clip_count, groups, frames, period, col_width)
+    result = jnp.swapaxes(result, 1, 2).reshape(clip_count, frames, place_part, col_width)
+    result = close_tokens(result)
+    attn_part_first, hidden_part, gradient_blocks, sending, result = together(
+        attn_part_first, hidden_part, gradient_blocks, sending, result
     )
     sides = scatter_sides(attn_part_first)
     hidden_total = add_blocks(hidden_part)
@@ -1553,33 +1568,26 @@
         sides, hidden_total, sending, output_first_pieces
     )
     attn_part_first = scatter_plane(attn_part_first, sides)
+    met = trade(sending)
     hidden_first_pieces = over_depth(hidden_total, place)
-    met = trade(sending)
-    sums = [add_all(pieces, place) for pieces in (attn_pieces, hidden_pieces, output_pieces)]
-    met, attn_part_first, sums, output_first_pieces = together(
-        met, attn_part_first, sums, output_first_pieces
-    )
-    attn_total = add_blocks(attn_part_first)
     met = [value.reshape(-1) for value in met]
     modgrad = jnp.concatenate([block[:cut] for block in met])
     biasgrad = sum(block[cut:] for block in met)
     small = jnp.concatenate((modgrad, biasgrad))
     small = small + swap(small)
-    gradient_blocks, result_blocks, small, _ = together(
-        gradient_blocks, result_blocks, small, attn_total
-    )
+    small, attn_part_first = together(small, attn_part_first)
+    attn_total = add_blocks(attn_part_first)
+    small, attn_total = together(small, attn_total)
     gradient_blocks = trade(gradient_blocks)
     for mask in place.depth_masks:
         small = small + exchange(small, "row", mask)
-    gradient_blocks, hidden_first_pieces, attn_total, small = together(
-        gradient_blocks, hidden_first_pieces, attn_total, small
+    sums = [add_all(pieces, place) for pieces in (attn_pieces, hidden_pieces, output_pieces)]
+    gradient_blocks, hidden_first_pieces, attn_total, small, sums = together(
+        gradient_blocks, hidden_first_pieces, attn_total, small, sums
     )
     attn_first_pieces = over_depth(attn_total, place)
     tokens_gradient = assembled(gradient_blocks, jnp.float32)
     tokens_gradient = tokens_gradient.reshape(clip_count, frame_part, places, col_width)
-    result = assembled(trade(result_blocks), jnp.bfloat16)
-    result = result.reshape(clip_count, groups, frames, period, col_width)
-    result = jnp.swapaxes(result, 1, 2).reshape(clip_count, frames, place_part, col_width)
     first_sums = [
         add_all(pieces, place)
         for pieces in (attn_first_pieces, hidden_first_pieces, output_first_pieces)
@@ -1606,7 +1614,7 @@
         jnp.stack((first_sums[index], sums[index])) for index in range(3)
     )
     return (
-        close_tokens(result),
+        result,
         close_tokens(tokens_gradient),
         conditioning_gradient,
         close_weight(ada_weight_grad),

time: 1050 us -> 994 us (0.947)
  local copies, waits for them, and re-layouts: 205 us -> 181 us
  waiting for transfers between devices: 252 us -> 232 us
    ppermute x80, waiting for transfers between devices: 174 us -> 133 us  [exchange(): lax.ppermute(values, axis, [(index, index ^ mask) for index in range(coun...]
    optimization_barrier x14 -> x0, local copies, waits for them, and re-layouts: 25.2 us -> none  [the longest x12 22 us: together(): return lax.optimization_barrier(values)]
    all_to_all x12, waiting for transfers between devices: 2.53 us -> 27.5 us  [over_depth(): lax.all_to_all(values, 'row', split_axis=0, concat_axis=0, tiled=True, ax...]
    unnamed x231 -> x227, local copies, waits for them, and re-layouts: 26 us -> 31.7 us
  transfers between devices with their start and end apart: 95 -> 95, of which waited for: 31 -> 40; matrix products, arithmetic and copies ran while one was open for 19% -> 17% of each run, Pallas kernels for 35% -> 36%
where the time goes in v3:
time: 994 us; the launch traced here: 986 us
  Pallas kernels  361 us (36%)
  waiting for transfers between devices  232 us (23%)
  local copies, waits for them, and re-layouts  181 us (18%)
  starting transfers between devices  136 us (14%)
  other arithmetic  55.9 us (6%)
  between operations  16.1 us (2%)
    ppermute x80, waiting for transfers between devices, exchange(): lax.ppermute(values, axis, [(index, index ^ mask) for index in range(coun...  133 us
    pallas_call x6, Pallas kernels, weight_grads(): pl.pallas_call(functools.partial(weight_kernel, len(pairs), overlap, step...  67.6 us
    ppermute x80, starting transfers between devices, exchange(): lax.ppermute(values, axis, [(index, index ^ mask) for index in range(coun...  67.5 us
    pallas_call x2, Pallas kernels, attention_backward(): pl.pallas_call(functools.partial(attention_back_kernel, size, period, ste...  67.2 us
    all_to_all x12, starting transfers between devices, over_depth(): lax.all_to_all(values, 'row', split_axis=0, concat_axis=0, tiled=True, ax...  58.9 us
    pallas_call x2, Pallas kernels, attention_forward(): pl.pallas_call(functools.partial(attention_kernel, size, period, steps),...  57.8 us
    pallas_call x2, Pallas kernels, mlp_forward(): pl.pallas_call(functools.partial(mlp_kernel, steps), grid=(steps,), in_sp...  56.7 us
    pallas_call x2, Pallas kernels, mlp_backward(): pl.pallas_call(functools.partial(mlp_back_kernel, steps), grid=(steps,),...  55.6 us
  transfers between devices with their start and end apart: 95, of which 40 were waited for; matrix products, arithmetic and copies ran while one was open for 17% of the time, Pallas kernels for 36%

profile of v3, /device:TPU:0, one launch (start us, length us, event | category | flops | bytes accessed | tf_op | source)
XLA Modules:
  0.0 985.7 jit_solution(17917545646095189294)
XLA Ops:
  14.5 6.4 all-to-all-start
  21.1 3.3 reshape.397
  30.4 7.8 slice_reduce_fusion.2
  52.6 5.2 reshape.399
  64.7 3.8 all-to-all-start.1
  71.6 9.0 slice_reduce_fusion
  91.8 4.7 reorder.6.refs_0_.refs_1_
  109.3 4.3 all-to-all-start.2
  116.3 25.8 %all-gather.4.cloned.1.call-done = f32[32,4,5472]{2,1,0:T(4,128)} async-done(((f32[1,4,5472]{2,1,0:T(4,128)}), f32[32,4,5472]{2,1,0:T(4,128)}) %all-gather.4.cloned.1.call-update) | async-done | bytes 2801680 | tf_op jit(solution)/shard_map/all_gather | solution.py:1281
  146.3 5.7 all-to-all-done.2
  152.0 11.0 %collective-permute-done.5.lower.across = bf16[864,1152]{1,0:T(8,128)(2,1)} collective-permute-done((bf16[864,1152]{1,0:T(8,128)(2,1)}, bf16[864,1152]{1,0:T(8,128)(2,1)}, u32[]{:S(2)}, u32[]{:S(2)}) %collective-permute-start.5) | collective-permute-done | bytes 1990688 | tf_op jit(solution)/shard_map/ppermute | solution.py:385
  168.6 3.9 pack_blocks.6.refs_4_.refs_6_
  172.6 4.8 all-to-all-start.3
  182.8 28.9 %attention_forward.2 = (f32[2,512,576]{2,1,0:T(8,128)}, bf16[512,576]{1,0:T(8,128)(2,1)}, bf16[576,512]{1,0:T(8,128)(2,1)}, bf16[4,512,896]{2,1,0:T(8,128)(2,1)}...) custom-call(f32[2,512,576]{2,1,0:T(8,128)} %copy-done.1, ...), custom_call_target="tpu_custom_call" | custom-call | tf_op jit(solution)/shard_map/attention_forward/pallas_call | solution.py:668
  211.6 11.6 %collective-permute-done.8.lower.across = bf16[864,1152]{1,0:T(8,128)(2,1)} collective-permute-done((bf16[864,1152]{1,0:T(8,128)(2,1)}, bf16[864,1152]{1,0:T(8,128)(2,1)}, u32[]{:S(2)}, u32[]{:S(2)}) %collective-permute-start.8) | collective-permute-done | bytes 1990688 | tf_op jit(solution)/shard_map/ppermute | solution.py:385
  228.0 4.8 all-to-all-start.4
  235.8 3.8 pack_blocks.7.refs_4_.refs_5_
  239.7 3.4 reshape.412
  244.4 19.2 %all-to-all-done.4 = bf16[4,144,1152]{2,1,0:T(8,128)(2,1)} async-done(((bf16[4,144,1152]{2,1,0:T(8,128)(2,1)}), bf16[4,144,1152]{2,1,0:T(8,128)(2,1)}, u32[]{:S(2)}, u32[]{:S(2)}) %all-to-all-start.4) | async-done | bytes 1327136 | tf_op jit(solution)/shard_map/all_to_all | solution.py:402
  263.6 13.4 %collective-permute-done.10.lower.across = bf16[864,1152]{1,0:T(8,128)(2,1)} collective-permute-done((bf16[864,1152]{1,0:T(8,128)(2,1)}, bf16[864,1152]{1,0:T(8,128)(2,1)}, u32[]{:S(2)}, u32[]{:S(2)}) %collective-permute-start.10) | collective-permute-done | bytes 1990688 | tf_op jit(solution)/shard_map/ppermute | solution.py:385
  280.5 3.6 pad_maximum_fusion.6
  284.1 4.0 pack_blocks.8.refs_6_.refs_7_
  288.2 4.9 all-to-all-start.5
  297.7 28.2 %mlp_forward.2 = (f32[2,512,576]{2,1,0:T(8,128)}, bf16[512,576]{1,0:T(8,128)(2,1)}, bf16[576,512]{1,0:T(8,128)(2,1)}, bf16[4,512,1152]{2,1,0:T(8,128)(2,1)}, bf1...) custom-call(f32[2,512,576]{2,1,0:T(8,128)} %get-tuple-element.482.refs_0_.refs_1_, ...), custom_call_target="tpu_custom_call" | custom-call | tf_op jit(solution)/shard_map/mlp_forward/pallas_call | solution.py:749
  325.9 13.2 %collective-permute-done.15.lower.across = bf16[864,1152]{1,0:T(8,128)(2,1)} collective-permute-done((bf16[864,1152]{1,0:T(8,128)(2,1)}, bf16[864,1152]{1,0:T(8,128)(2,1)}, u32[]{:S(2)}, u32[]{:S(2)}) %collective-permute-start.15) | collective-permute-done | bytes 1990688 | tf_op jit(solution)/shard_map/ppermute | solution.py:385
  346.3 5.1 all-to-all-start.6
  354.3 4.0 pack_blocks.10.refs_4_.refs_6_
  358.9 24.6 %all-to-all-done.6 = bf16[2,8,2,2,16,576]{5,4,2,3,0,1:T(8,128)(2,1)S(1)} async-done(((bf16[2,8,2,2,16,576]{5,4,2,3,0,1:T(8,128)(2,1)}), bf16[2,8,2,2,16,576]{5,4,2,3,0,1:T(8,128)(2,1)S(1)}, u32[]{:S(2)}, u32[]{:S(2)}) %all-to-all-start.6) | async-done | bytes 1179680 | tf_op jit(solution)/shard_map/all_to_all | solution.py:1405
  383.7 13.8 %collective-permute-done.19.across.lower = bf16[864,1152]{1,0:T(8,128)(2,1)} collective-permute-done((bf16[864,1152]{1,0:T(8,128)(2,1)}, bf16[864,1152]{1,0:T(8,128)(2,1)}, u32[]{:S(2)}, u32[]{:S(2)}) %collective-permute-start.19) | collective-permute-done | bytes 1990688 | tf_op jit(solution)/shard_map/ppermute | solution.py:385
  405.9 11.3 %collective-permute-done.22.lower = bf16[288,1152]{1,0:T(8,128)(2,1)S(1)} collective-permute-done((bf16[288,1152]{1,0:T(8,128)(2,1)S(1)}, bf16[288,1152]{1,0:T(8,128)(2,1)S(1)}, u32[]{:S(2)}, u32[]{:S(2)}) %collective-permute-start.22) | collective-permute-done | bytes 663584 | tf_op jit(solution)/shard_map/ppermute | solution.py:385
  417.5 3.9 pack_blocks.9.refs_6_.refs_7_
  424.0 28.9 %attention_forward.3 = (f32[2,512,576]{2,1,0:T(8,128)}, bf16[512,576]{1,0:T(8,128)(2,1)}, bf16[576,512]{1,0:T(8,128)(2,1)}, bf16[4,512,896]{2,1,0:T(8,128)(2,1)}...) custom-call(f32[2,512,576]{2,1,0:T(8,128)} %fusion.2.refs_0_.refs_1_, ...), custom_call_target="tpu_custom_call" | custom-call | tf_op jit(solution)/shard_map/attention_forward/pallas_call | solution.py:668
  457.7 28.5 %mlp_forward.3 = (f32[2,512,576]{2,1,0:T(8,128)}, bf16[512,576]{1,0:T(8,128)(2,1)}, bf16[576,512]{1,0:T(8,128)(2,1)}, bf16[4,512,1152]{2,1,0:T(8,128)(2,1)}, bf1...) custom-call(f32[2,512,576]{2,1,0:T(8,128)} %get-tuple-element.540.refs_0_.refs_1_, ...), custom_call_target="tpu_custom_call" | custom-call | tf_op jit(solution)/shard_map/mlp_forward/pallas_call | solution.py:749
  486.8 4.7 reorder.7.refs_0_
  493.0 27.9 %mlp_backward.2 = (f32[2,512,576]{2,1,0:T(8,128)}, bf16[512,576]{1,0:T(8,128)(2,1)}, bf16[576,512]{1,0:T(8,128)(2,1)}, bf16[4,512,1152]{2,1,0:T(8,128)(2,1)}, f3...) custom-call(f32[2,512,576]{2,1,0:T(8,128)} %copy-done.6, f32[2,512,576]{2,1,0:T(8,128)} %get-tuple-element.540.refs_0_.refs_1_, ...), custom_call_target="tpu_custom_call" | custom-call | tf_op jit(solution)/shard_map/mlp_backward/pallas_call | solution.py:823
  524.1 10.6 %weight_grads.6 = (bf16[576,1152]{1,0:T(8,128)(2,1)}, bf16[288,1152]{1,0:T(8,128)(2,1)}, bf16[576,1152]{1,0:T(8,128)(2,1)}, bf16[576,1152]{1,0:T(8,128)(2,1)}, bf16[288,1152]{1,0:T(8,128)(2,1)}) custom-call(bf16[512,576]{1,0:T(8,128)(2,1)} %get-tuple-element.580.refs_0_, bf16[576,512]{1,0:T(8,128)(2,1)} %copy-done.82, ...), custom_call_target="tpu_custom_call" | custom-call | tf_op jit(solution)/shard_map/weight_grads/pallas_call | solution.py:1041
  540.0 10.7 %weight_grads.7 = (bf16[576,1152]{1,0:T(8,128)(2,1)}, bf16[288,1152]{1,0:T(8,128)(2,1)}, bf16[576,1152]{1,0:T(8,128)(2,1)}, bf16[576,1152]{1,0:T(8,128)(2,1)}, bf16[288,1152]{1,0:T(8,128)(2,1)}) custom-call(bf16[512,576]{1,0:T(8,128)(2,1)} %get-tuple-element.551.refs_0_, bf16[576,512]{1,0:T(8,128)(2,1)} %copy-done.80, ...), custom_call_target="tpu_custom_call" | custom-call | tf_op jit(solution)/shard_map/weight_grads/pallas_call | solution.py:1041
  550.6 33.7 %attention_backward.2 = (f32[2,512,576]{2,1,0:T(8,128)}, bf16[512,576]{1,0:T(8,128)(2,1)}, bf16[576,512]{1,0:T(8,128)(2,1)}, bf16[4,512,896]{2,1,0:T(8,128)(2,1)...) custom-call(f32[2,512,576]{2,1,0:T(8,128)} %get-tuple-element.596.refs_0_, f32[2,512,576]{2,1,0:T(8,128)} %fusion.2.refs_0_.refs_1_, ...), custom_call_target="tpu_custom_call" | custom-call | tf_op jit(solution)/shard_map/attention_backward/pallas_call | solution.py:933
  588.7 4.7 all-to-all-start.7
  598.4 4.4 reorder.8
  604.7 20.9 %all-to-all-done.7 = bf16[2,1,2,16,16,576]{5,4,2,0,1,3:T(8,128)(2,1)} async-done(((bf16[2,1,2,16,16,576]{5,4,2,0,1,3:T(8,128)(2,1)}), bf16[2,1,2,16,16,576]{5,4,2,0,1,3:T(8,128)(2,1)}, u32[]{:S(2)}, u32[]{:S(2)}) %all-to-all-start.7) | async-done | bytes 1179680 | tf_op jit(solution)/shard_map/all_to_all | solution.py:1450
  629.4 12.5 %weight_grads.8 = (bf16[576,1152]{1,0:T(8,128)(2,1)}, bf16[288,1152]{1,0:T(8,128)(2,1)}, bf16[576,1152]{1,0:T(8,128)(2,1)}, bf16[576,1152]{1,0:T(8,128)(2,1)}, bf16[288,1152]{1,0:T(8,128)(2,1)}) custom-call(bf16[512,576]{1,0:T(8,128)(2,1)} %get-tuple-element.611.refs_0_, bf16[576,512]{1,0:T(8,128)(2,1)} %collective-permute-done.30.refs_1_, ...), custom_call_target="tpu_custom_call" | custom-call | flops 15000000512 | tf_op jit(solution)/shard_map/weight_grads/pallas_call | solution.py:1041
  650.6 4.6 all-to-all-start.8
  663.8 27.7 %mlp_backward.3 = (f32[2,512,576]{2,1,0:T(8,128)}, bf16[512,576]{1,0:T(8,128)(2,1)}, bf16[576,512]{1,0:T(8,128)(2,1)}, bf16[4,512,1152]{2,1,0:T(8,128)(2,1)}, f3...) custom-call(f32[2,512,576]{2,1,0:T(8,128)} %fusion.3.refs_0_, f32[2,512,576]{2,1,0:T(8,128)} %get-tuple-element.482.refs_0_.refs_1_, ...), custom_call_target="tpu_custom_call" | custom-call | tf_op jit(solution)/shard_map/mlp_backward/pallas_call | solution.py:823
  701.5 5.5 all-to-all-start.9
  707.1 10.6 %weight_grads.9 = (bf16[576,1152]{1,0:T(8,128)(2,1)}, bf16[288,1152]{1,0:T(8,128)(2,1)}, bf16[576,1152]{1,0:T(8,128)(2,1)}, bf16[576,1152]{1,0:T(8,128)(2,1)}, bf16[288,1152]{1,0:T(8,128)(2,1)}) custom-call(bf16[512,576]{1,0:T(8,128)(2,1)} %get-tuple-element.679.refs_0_, bf16[576,512]{1,0:T(8,128)(2,1)} %copy-done.81, ...), custom_call_target="tpu_custom_call" | custom-call | tf_op jit(solution)/shard_map/weight_grads/pallas_call | solution.py:1041
  717.7 10.7 %weight_grads.10 = (bf16[576,1152]{1,0:T(8,128)(2,1)}, bf16[288,1152]{1,0:T(8,128)(2,1)}, bf16[576,1152]{1,0:T(8,128)(2,1)}, bf16[576,1152]{1,0:T(8,128)(2,1)}, bf16[288,1152]{1,0:T(8,128)(2,1)}) custom-call(bf16[512,576]{1,0:T(8,128)(2,1)} %get-tuple-element.503.refs_0_, bf16[576,512]{1,0:T(8,128)(2,1)} %copy-done.79, ...), custom_call_target="tpu_custom_call" | custom-call | tf_op jit(solution)/shard_map/weight_grads/pallas_call | solution.py:1041
  737.5 33.5 %attention_backward.3 = (f32[2,512,576]{2,1,0:T(8,128)}, bf16[512,576]{1,0:T(8,128)(2,1)}, bf16[576,512]{1,0:T(8,128)(2,1)}, bf16[4,512,896]{2,1,0:T(8,128)(2,1)...) custom-call(f32[2,512,576]{2,1,0:T(8,128)} %get-tuple-element.703.refs_0_, f32[2,512,576]{2,1,0:T(8,128)} %copy-done.1, ...), custom_call_target="tpu_custom_call" | custom-call | tf_op jit(solution)/shard_map/attention_backward/pallas_call | solution.py:933
  771.1 5.4 collective-permute-done.55.across_upper
  786.5 5.2 all-to-all-start.10
  796.1 12.5 %weight_grads.11 = (bf16[576,1152]{1,0:T(8,128)(2,1)}, bf16[288,1152]{1,0:T(8,128)(2,1)}, bf16[576,1152]{1,0:T(8,128)(2,1)}, bf16[576,1152]{1,0:T(8,128)(2,1)}, bf16[288,1152]{1,0:T(8,128)(2,1)}) custom-call(bf16[512,576]{1,0:T(8,128)(2,1)} %get-tuple-element.464.refs_0_, bf16[576,512]{1,0:T(8,128)(2,1)} %collective-permute-done.12.refs_1_, ...), custom_call_target="tpu_custom_call" | custom-call | tf_op jit(solution)/shard_map/weight_grads/pallas_call | solution.py:1041
  811.4 13.1 %collective-permute-done.59.across_upper = bf16[288,1152]{1,0:T(8,128)(2,1)S(1)} collective-permute-done((bf16[288,1152]{1,0:T(8,128)(2,1)}, bf16[288,1152]{1,0:T(8,128)(2,1)S(1)}, u32[]{:S(2)}, u32[]{:S(2)}) %collective-permute-start.59) | collective-permute-done | bytes 663584 | tf_op jit(solution)/shard_map/ppermute | solution.py:385
  827.9 3.4 add_blocks.9
  833.5 5.1 all-to-all-start.11
  854.4 4.0 reshape_reshape.30
  860.0 4.4 reorder.9
  876.4 5.1 all-to-all-start.12
  889.0 3.4 convert_reduce_fusion.2
  896.0 6.8 collective-permute-done.74.across_upper
  903.2 3.3 add_blocks.11
  927.2 4.4 all-to-all-start.13
  948.6 5.5 reshape_reshape.32
  956.7 4.4 reshape.462
  967.0 3.7 reshape.465
  (609 shorter events, 302.1 us)
Async XLA Ops:
  14.5 38.1 %all-to-all-start = ((bf16[4,144,1152]{2,1,0:T(8,128)(2,1)}), bf16[4,144,1152]{2,1,0:T(8,128)(2,1)S(1)}, u32[]{:S(2)}, u32[]{:S(2)}) async-start(bf16[4,144,1152]{2,1,0:T(8,128)(2,1)} %bitcast.13), calls=%async_computation | async-start | bytes 2654208 | tf_op jit(solution)/shard_map/all_to_all | solution.py:402
  20.9 121.2 %all-gather.4.cloned.1.call-start = ((), (), s32[]{:S(2)}) async-start(), calls=%async_computation.14 | async-start | bytes 2906112 | tf_op jit(solution)/shard_map/all_gather | solution.py:1281
  64.7 36.8 %all-to-all-start.1 = ((bf16[4,144,1152]{2,1,0:T(8,128)(2,1)}), bf16[4,144,1152]{2,1,0:T(8,128)(2,1)S(1)}, u32[]{:S(2)}, u32[]{:S(2)}) async-start(bf16[4,144,1152]{2,1,0:T(8,128)(2,1)} %tile.59), calls=%async_computation.1 | async-start | bytes 2654208 | tf_op jit(solution)/shard_map/all_to_all | solution.py:402
  68.5 30.9 %collective-permute-start.3 = (bf16[576,1152]{1,0:T(8,128)(2,1)S(1)}, bf16[576,1152]{1,0:T(8,128)(2,1)}, u32[]{:S(2)}, u32[]{:S(2)}) collective-permute-start(bf16[576,1152]{1,0:T(8,128)(2,1)S(1)} %bitcast.240), channel_id=1, source_target_pairs={{0,1},{1,0},{2,3},{3,2},{4,5},{5,4},{6,7},{7,6},{8,9},{9,8},{10,11... | collective-permute-start | bytes 3981320 | tf_op jit(solution)/shard_map/ppermute | solution.py:385
  70.0 30.6 %collective-permute-start.4 = (bf16[576,1152]{1,0:T(8,128)(2,1)S(1)}, bf16[576,1152]{1,0:T(8,128)(2,1)}, u32[]{:S(2)}, u32[]{:S(2)}) collective-permute-start(bf16[576,1152]{1,0:T(8,128)(2,1)S(1)} %bitcast.241), channel_id=1, source_target_pairs={{0,2},{1,3},{2,0},{3,1},{4,6},{5,7},{6,4},{7,5},{8,10},{9,11},{10,... | collective-permute-start | bytes 3981320 | tf_op jit(solution)/shard_map/ppermute | solution.py:385
  109.3 42.7 %all-to-all-start.2 = ((bf16[4,144,1152]{2,1,0:T(8,128)(2,1)}), bf16[4,144,1152]{2,1,0:T(8,128)(2,1)S(1)}, u32[]{:S(2)}, u32[]{:S(2)}) async-start(bf16[4,144,1152]{2,1,0:T(8,128)(2,1)} %tile.66), calls=%async_computation.2 | async-start | bytes 2654208 | tf_op jit(solution)/shard_map/all_to_all | solution.py:402
  113.6 49.4 %collective-permute-start.5 = (bf16[864,1152]{1,0:T(8,128)(2,1)}, bf16[864,1152]{1,0:T(8,128)(2,1)}, u32[]{:S(2)}, u32[]{:S(2)}) collective-permute-start(bf16[864,1152]{1,0:T(8,128)(2,1)} %get-tuple-element.981), channel_id=1, source_target_pairs={{0,1},{1,0},{2,3},{3,2},{4,5},{5,4},{6,7},{7,6},{8,9},{9,8},{10,11... | collective-permute-start | bytes 5971976 | tf_op jit(solution)/shard_map/ppermute | solution.py:385
  114.8 49.3 %collective-permute-start.6 = (bf16[864,1152]{1,0:T(8,128)(2,1)}, bf16[864,1152]{1,0:T(8,128)(2,1)}, u32[]{:S(2)}, u32[]{:S(2)}) collective-permute-start(bf16[864,1152]{1,0:T(8,128)(2,1)} %get-tuple-element.980), channel_id=1, source_target_pairs={{0,2},{1,3},{2,0},{3,1},{4,6},{5,7},{6,4},{7,5},{8,10},{9,11},{10,... | collective-permute-start | bytes 5971976 | tf_op jit(solution)/shard_map/ppermute | solution.py:385
  172.6 39.0 %all-to-all-start.3 = ((bf16[4,144,1152]{2,1,0:T(8,128)(2,1)}), bf16[4,144,1152]{2,1,0:T(8,128)(2,1)S(1)}, u32[]{:S(2)}, u32[]{:S(2)}) async-start(bf16[4,144,1152]{2,1,0:T(8,128)(2,1)} %tile.64), calls=%async_computation.3 | async-start | bytes 2654208 | tf_op jit(solution)/shard_map/all_to_all | solution.py:402
  177.4 45.8 %collective-permute-start.8 = (bf16[864,1152]{1,0:T(8,128)(2,1)}, bf16[864,1152]{1,0:T(8,128)(2,1)}, u32[]{:S(2)}, u32[]{:S(2)}) collective-permute-start(bf16[864,1152]{1,0:T(8,128)(2,1)} %get-tuple-element.979), channel_id=1, source_target_pairs={{0,1},{1,0},{2,3},{3,2},{4,5},{5,4},{6,7},{7,6},{8,9},{9,8},{10,11... | collective-permute-start | bytes 5971976 | tf_op jit(solution)/shard_map/ppermute | solution.py:385
  178.0 45.5 %collective-permute-start.9 = (bf16[864,1152]{1,0:T(8,128)(2,1)}, bf16[864,1152]{1,0:T(8,128)(2,1)}, u32[]{:S(2)}, u32[]{:S(2)}) collective-permute-start(bf16[864,1152]{1,0:T(8,128)(2,1)} %get-tuple-element.978), channel_id=1, source_target_pairs={{0,2},{1,3},{2,0},{3,1},{4,6},{5,7},{6,4},{7,5},{8,10},{9,11},{10,... | collective-permute-start | bytes 5971976 | tf_op jit(solution)/shard_map/ppermute | solution.py:385
  228.0 35.6 %all-to-all-start.4 = ((bf16[4,144,1152]{2,1,0:T(8,128)(2,1)}), bf16[4,144,1152]{2,1,0:T(8,128)(2,1)}, u32[]{:S(2)}, u32[]{:S(2)}) async-start(bf16[4,144,1152]{2,1,0:T(8,128)(2,1)} %tile.62), calls=%async_computation.4 | async-start | bytes 2654208 | tf_op jit(solution)/shard_map/all_to_all | solution.py:402
  232.8 44.3 %collective-permute-start.10 = (bf16[864,1152]{1,0:T(8,128)(2,1)}, bf16[864,1152]{1,0:T(8,128)(2,1)}, u32[]{:S(2)}, u32[]{:S(2)}) collective-permute-start(bf16[864,1152]{1,0:T(8,128)(2,1)} %get-tuple-element.977), channel_id=1, source_target_pairs={{0,1},{1,0},{2,3},{3,2},{4,5},{5,4},{6,7},{7,6},{8,9},{9,8},{10,11... | collective-permute-start | bytes 5971976 | tf_op jit(solution)/shard_map/ppermute | solution.py:385
  234.3 43.9 %collective-permute-start.11 = (bf16[864,1152]{1,0:T(8,128)(2,1)}, bf16[864,1152]{1,0:T(8,128)(2,1)}, u32[]{:S(2)}, u32[]{:S(2)}) collective-permute-start(bf16[864,1152]{1,0:T(8,128)(2,1)} %get-tuple-element.976), channel_id=1, source_target_pairs={{0,2},{1,3},{2,0},{3,1},{4,6},{5,7},{6,4},{7,5},{8,10},{9,11},{10,... | collective-permute-start | bytes 5971976 | tf_op jit(solution)/shard_map/ppermute | solution.py:385
  239.6 55.9 %collective-permute-start.13 = (bf16[4,576,1152]{2,1,0:T(8,128)(2,1)}, bf16[4,576,1152]{2,1,0:T(8,128)(2,1)}, u32[]{:S(2)}, u32[]{:S(2)}) collective-permute-start(bf16[4,576,1152]{2,1,0:T(8,128)(2,1)} %pack_blocks.7.refs_4_.refs_5_), channel_id=1, source_target_pairs={{0,4},{4,0},{8,12},{12,8},{16,20},{20,16},{24,28},{28,24},{1,5},{5... | collective-permute-start | bytes 15925256 | tf_op jit(solution)/shard_map/ppermute | solution.py:385
  288.2 37.7 %all-to-all-start.5 = ((bf16[4,144,1152]{2,1,0:T(8,128)(2,1)}), bf16[4,144,1152]{2,1,0:T(8,128)(2,1)S(1)}, u32[]{:S(2)}, u32[]{:S(2)}) async-start(bf16[4,144,1152]{2,1,0:T(8,128)(2,1)} %tile.68), calls=%async_computation.5 | async-start | bytes 2654208 | tf_op jit(solution)/shard_map/all_to_all | solution.py:402
  293.1 46.0 %collective-permute-start.15 = (bf16[864,1152]{1,0:T(8,128)(2,1)}, bf16[864,1152]{1,0:T(8,128)(2,1)}, u32[]{:S(2)}, u32[]{:S(2)}) collective-permute-start(bf16[864,1152]{1,0:T(8,128)(2,1)} %get-tuple-element.975), channel_id=1, source_target_pairs={{0,1},{1,0},{2,3},{3,2},{4,5},{5,4},{6,7},{7,6},{8,9},{9,8},{10,11... | collective-permute-start | bytes 5971976 | tf_op jit(solution)/shard_map/ppermute | solution.py:385
  293.8 45.6 %collective-permute-start.16 = (bf16[864,1152]{1,0:T(8,128)(2,1)}, bf16[864,1152]{1,0:T(8,128)(2,1)}, u32[]{:S(2)}, u32[]{:S(2)}) collective-permute-start(bf16[864,1152]{1,0:T(8,128)(2,1)} %get-tuple-element.974), channel_id=1, source_target_pairs={{0,2},{1,3},{2,0},{3,1},{4,6},{5,7},{6,4},{7,5},{8,10},{9,11},{10,... | collective-permute-start | bytes 5971976 | tf_op jit(solution)/shard_map/ppermute | solution.py:385
  295.3 30.6 %collective-permute-start.17 = (bf16[4,512,384]{2,1,0:T(8,128)(2,1)}, bf16[4,512,384]{2,1,0:T(8,128)(2,1)}, u32[]{:S(2)}, u32[]{:S(2)}) collective-permute-start(bf16[4,512,384]{2,1,0:T(8,128)(2,1)} %get-tuple-element.509.refs_6_), channel_id=1, source_target_pairs={{0,4},{4,0},{8,12},{12,8},{16,20},{20,16},{24,28},{28,24},{1,5},{5... | collective-permute-start | bytes 4718600 | tf_op jit(solution)/shard_map/ppermute | solution.py:385
  343.9 54.7 %collective-permute-start.21 = (bf16[4,512,1152]{2,1,0:T(8,128)(2,1)}, bf16[4,512,1152]{2,1,0:T(8,128)(2,1)}, u32[]{:S(2)}, u32[]{:S(2)}) collective-permute-start(bf16[4,512,1152]{2,1,0:T(8,128)(2,1)} %get-tuple-element.516.refs_2_), channel_id=1, source_target_pairs={{0,4},{4,0},{8,12},{12,8},{16,20},{20,16},{24,28},{28,24},{1,5},{5... | collective-permute-start | bytes 14155784 | tf_op jit(solution)/shard_map/ppermute | solution.py:385
  346.3 37.2 %all-to-all-start.6 = ((bf16[2,8,2,2,16,576]{5,4,2,3,0,1:T(8,128)(2,1)}), bf16[2,8,2,2,16,576]{5,4,2,3,0,1:T(8,128)(2,1)S(1)}, u32[]{:S(2)}, u32[]{:S(2)}) async-start(bf16[2,8,2,2,16,576]{5,4,2,3,0,1:T(8,128)(2,1)} %bitcast.253), calls=%async_computation.6 | async-start | bytes 2621440 | tf_op jit(solution)/shard_map/all_to_all | solution.py:1405
  351.3 46.1 %collective-permute-start.19 = (bf16[864,1152]{1,0:T(8,128)(2,1)}, bf16[864,1152]{1,0:T(8,128)(2,1)}, u32[]{:S(2)}, u32[]{:S(2)}) collective-permute-start(bf16[864,1152]{1,0:T(8,128)(2,1)} %get-tuple-element.973), channel_id=1, source_target_pairs={{0,1},{1,0},{2,3},{3,2},{4,5},{5,4},{6,7},{7,6},{8,9},{9,8},{10,11... | collective-permute-start | bytes 5971976 | tf_op jit(solution)/shard_map/ppermute | solution.py:385
  352.8 45.8 %collective-permute-start.20 = (bf16[864,1152]{1,0:T(8,128)(2,1)}, bf16[864,1152]{1,0:T(8,128)(2,1)}, u32[]{:S(2)}, u32[]{:S(2)}) collective-permute-start(bf16[864,1152]{1,0:T(8,128)(2,1)} %get-tuple-element.972), channel_id=1, source_target_pairs={{0,2},{1,3},{2,0},{3,1},{4,6},{5,7},{6,4},{7,5},{8,10},{9,11},{10,... | collective-permute-start | bytes 5971976 | tf_op jit(solution)/shard_map/ppermute | solution.py:385
  358.3 65.7 %collective-permute-start.24 = (bf16[4,576,1152]{2,1,0:T(8,128)(2,1)}, bf16[4,576,1152]{2,1,0:T(8,128)(2,1)}, u32[]{:S(2)}, u32[]{:S(2)}) collective-permute-start(bf16[4,576,1152]{2,1,0:T(8,128)(2,1)} %pack_blocks.10.refs_4_.refs_6_), channel_id=1, source_target_pairs={{0,4},{4,0},{8,12},{12,8},{16,20},{20,16},{24,28},{28,24},{1,5},{5... | collective-permute-start | bytes 15925256 | tf_op jit(solution)/shard_map/ppermute | solution.py:385
  405.8 49.2 %collective-permute-start.25 = (bf16[4,576,1152]{2,1,0:T(8,128)(2,1)S(1)}, bf16[4,576,1152]{2,1,0:T(8,128)(2,1)}, u32[]{:S(2)}, u32[]{:S(2)}) collective-permute-start(bf16[4,576,1152]{2,1,0:T(8,128)(2,1)S(1)} %pack_blocks.11.refs_4_.refs_5_), channel_id=1, source_target_pairs={{0,4},{4,0},{8,12},{12,8},{16,20},{20,16},{24,28},{28,24},{1,5},{5... | collective-permute-start | bytes 15925256 | tf_op jit(solution)/shard_map/ppermute | solution.py:385
  421.5 35.0 %collective-permute-start.26 = (bf16[4,576,1152]{2,1,0:T(8,128)(2,1)}, bf16[4,576,1152]{2,1,0:T(8,128)(2,1)}, u32[]{:S(2)}, u32[]{:S(2)}) collective-permute-start(bf16[4,576,1152]{2,1,0:T(8,128)(2,1)} %pack_blocks.9.refs_6_.refs_7_), channel_id=1, source_target_pairs={{0,4},{4,0},{8,12},{12,8},{16,20},{20,16},{24,28},{28,24},{1,5},{5... | collective-permute-start | bytes 15925256 | tf_op jit(solution)/shard_map/ppermute | solution.py:385
  452.9 33.3 %collective-permute-start.31 = (bf16[4,512,384]{2,1,0:T(8,128)(2,1)}, bf16[4,512,384]{2,1,0:T(8,128)(2,1)}, u32[]{:S(2)}, u32[]{:S(2)}) collective-permute-start(bf16[4,512,384]{2,1,0:T(8,128)(2,1)} %get-tuple-element.557.refs_6_), channel_id=1, source_target_pairs={{0,4},{4,0},{8,12},{12,8},{16,20},{20,16},{24,28},{28,24},{1,5},{5... | collective-permute-start | bytes 4718600 | tf_op jit(solution)/shard_map/ppermute | solution.py:385
  453.5 32.8 %collective-permute-start.30 = (bf16[576,512]{1,0:T(8,128)(2,1)}, bf16[576,512]{1,0:T(8,128)(2,1)}, u32[]{:S(2)}, u32[]{:S(2)}) collective-permute-start(bf16[576,512]{1,0:T(8,128)(2,1)} %get-tuple-element.556), channel_id=1, source_target_pairs={{0,4},{4,0},{8,12},{12,8},{16,20},{20,16},{24,28},{28,24},{1,5},{5... | collective-permute-start | bytes 1769480 | tf_op jit(solution)/shard_map/ppermute | solution.py:385
  453.5 32.6 %collective-permute-start.27 = (bf16[512,288]{1,0:T(8,128)(2,1)}, bf16[512,288]{1,0:T(8,128)(2,1)S(1)}, u32[]{:S(2)}, u32[]{:S(2)}) collective-permute-start(bf16[512,288]{1,0:T(8,128)(2,1)} %get-tuple-element.553), channel_id=1, source_target_pairs={{0,1},{1,0},{2,3},{3,2},{4,5},{5,4},{6,7},{7,6},{8,9},{9,8},{10,11... | collective-permute-start | bytes 884744 | tf_op jit(solution)/shard_map/ppermute | solution.py:385
  455.0 31.2 %collective-permute-start.28 = (bf16[512,288]{1,0:T(8,128)(2,1)}, bf16[512,288]{1,0:T(8,128)(2,1)S(1)}, u32[]{:S(2)}, u32[]{:S(2)}) collective-permute-start(bf16[512,288]{1,0:T(8,128)(2,1)} %get-tuple-element.554), channel_id=1, source_target_pairs={{0,2},{1,3},{2,0},{3,1},{4,6},{5,7},{6,4},{7,5},{8,10},{9,11},{10,... | collective-permute-start | bytes 884744 | tf_op jit(solution)/shard_map/ppermute | solution.py:385
  486.2 34.7 %collective-permute-start.33 = (bf16[4,512,1152]{2,1,0:T(8,128)(2,1)}, bf16[4,512,1152]{2,1,0:T(8,128)(2,1)}, u32[]{:S(2)}, u32[]{:S(2)}) collective-permute-start(bf16[4,512,1152]{2,1,0:T(8,128)(2,1)} %get-tuple-element.574.refs_2_), channel_id=1, source_target_pairs={{0,4},{4,0},{8,12},{12,8},{16,20},{20,16},{24,28},{28,24},{1,5},{5... | collective-permute-start | bytes 14155784 | tf_op jit(solution)/shard_map/ppermute | solution.py:385
  486.3 34.6 %collective-permute-start.32 = (bf16[576,512]{1,0:T(8,128)(2,1)}, bf16[576,512]{1,0:T(8,128)(2,1)S(1)}, u32[]{:S(2)}, u32[]{:S(2)}) collective-permute-start(bf16[576,512]{1,0:T(8,128)(2,1)} %get-tuple-element.573), channel_id=1, source_target_pairs={{0,4},{4,0},{8,12},{12,8},{16,20},{20,16},{24,28},{28,24},{1,5},{5... | collective-permute-start | bytes 1769480 | tf_op jit(solution)/shard_map/ppermute | solution.py:385
  537.0 47.3 %collective-permute-start.36 = (bf16[576,1152]{1,0:T(8,128)(2,1)}, bf16[576,1152]{1,0:T(8,128)(2,1)S(1)}, u32[]{:S(2)}, u32[]{:S(2)}) collective-permute-start(bf16[576,1152]{1,0:T(8,128)(2,1)} %get-tuple-element.606), channel_id=1, source_target_pairs={{0,1},{1,0},{2,3},{3,2},{4,5},{5,4},{6,7},{7,6},{8,9},{9,8},{10,11... | collective-permute-start | bytes 3981320 | tf_op jit(solution)/shard_map/ppermute | solution.py:385
  538.4 45.9 %collective-permute-start.37 = (bf16[576,1152]{1,0:T(8,128)(2,1)}, bf16[576,1152]{1,0:T(8,128)(2,1)S(1)}, u32[]{:S(2)}, u32[]{:S(2)}) collective-permute-start(bf16[576,1152]{1,0:T(8,128)(2,1)} %get-tuple-element.607), channel_id=1, source_target_pairs={{0,2},{1,3},{2,0},{3,1},{4,6},{5,7},{6,4},{7,5},{8,10},{9,11},{10,... | collective-permute-start | bytes 3981320 | tf_op jit(solution)/shard_map/ppermute | solution.py:385
  584.3 43.8 %collective-permute-start.38 = (bf16[4,512,896]{2,1,0:T(8,128)(2,1)}, bf16[4,512,896]{2,1,0:T(8,128)(2,1)}, u32[]{:S(2)}, u32[]{:S(2)}) collective-permute-start(bf16[4,512,896]{2,1,0:T(8,128)(2,1)} %get-tuple-element.625.refs_2_), channel_id=1, source_target_pairs={{0,4},{4,0},{8,12},{12,8},{16,20},{20,16},{24,28},{28,24},{1,5},{5... | collective-permute-start | bytes 11010056 | tf_op jit(solution)/shard_map/ppermute | solution.py:385
  588.7 37.0 %all-to-all-start.7 = ((bf16[2,1,2,16,16,576]{5,4,2,0,1,3:T(8,128)(2,1)}), bf16[2,1,2,16,16,576]{5,4,2,0,1,3:T(8,128)(2,1)}, u32[]{:S(2)}, u32[]{:S(2)}) async-start(bf16[2,1,2,16,16,576]{5,4,2,0,1,3:T(8,128)(2,1)} %copy.156), calls=%async_computation.7 | async-start | bytes 2621440 | tf_op jit(solution)/shard_map/all_to_all | solution.py:1450
  593.4 48.5 %collective-permute-start.40 = (bf16[576,1152]{1,0:T(8,128)(2,1)}, bf16[576,1152]{1,0:T(8,128)(2,1)S(1)}, u32[]{:S(2)}, u32[]{:S(2)}) collective-permute-start(bf16[576,1152]{1,0:T(8,128)(2,1)} %get-tuple-element.637), channel_id=1, source_target_pairs={{0,1},{1,0},{2,3},{3,2},{4,5},{5,4},{6,7},{7,6},{8,9},{9,8},{10,11... | collective-permute-start | bytes 3981320 | tf_op jit(solution)/shard_map/ppermute | solution.py:385
  594.1 47.8 %collective-permute-start.41 = (bf16[576,1152]{1,0:T(8,128)(2,1)}, bf16[576,1152]{1,0:T(8,128)(2,1)S(1)}, u32[]{:S(2)}, u32[]{:S(2)}) collective-permute-start(bf16[576,1152]{1,0:T(8,128)(2,1)} %get-tuple-element.638), channel_id=1, source_target_pairs={{0,2},{1,3},{2,0},{3,1},{4,6},{5,7},{6,4},{7,5},{8,10},{9,11},{10,... | collective-permute-start | bytes 3981320 | tf_op jit(solution)/shard_map/ppermute | solution.py:385
  594.6 33.6 %collective-permute-start.39 = (bf16[576,512]{1,0:T(8,128)(2,1)}, bf16[576,512]{1,0:T(8,128)(2,1)}, u32[]{:S(2)}, u32[]{:S(2)}) collective-permute-start(bf16[576,512]{1,0:T(8,128)(2,1)} %get-tuple-element.614), channel_id=1, source_target_pairs={{0,4},{4,0},{8,12},{12,8},{16,20},{20,16},{24,28},{28,24},{1,5},{5... | collective-permute-start | bytes 1769480 | tf_op jit(solution)/shard_map/ppermute | solution.py:385
  650.6 44.1 %all-to-all-start.8 = ((bf16[4,144,1152]{2,1,0:T(8,128)(2,1)}), bf16[4,144,1152]{2,1,0:T(8,128)(2,1)}, u32[]{:S(2)}, u32[]{:S(2)}) async-start(bf16[4,144,1152]{2,1,0:T(8,128)(2,1)} %bitcast.80), calls=%async_computation.8 | async-start | bytes 2654208 | tf_op jit(solution)/shard_map/all_to_all | solution.py:402
  655.1 38.6 %collective-permute-start.44 = (bf16[288,1152]{1,0:T(8,128)(2,1)}, bf16[288,1152]{1,0:T(8,128)(2,1)S(1)}, u32[]{:S(2)}, u32[]{:S(2)}) collective-permute-start(bf16[288,1152]{1,0:T(8,128)(2,1)} %add_convert_fusion.9), channel_id=1, source_target_pairs={{0,1},{1,0},{2,3},{3,2},{4,5},{5,4},{6,7},{7,6},{8,9},{9,8},{10,11... | collective-permute-start | bytes 1990664 | tf_op jit(solution)/shard_map/ppermute | solution.py:385
  656.6 37.1 %collective-permute-start.45 = (bf16[288,1152]{1,0:T(8,128)(2,1)}, bf16[288,1152]{1,0:T(8,128)(2,1)S(1)}, u32[]{:S(2)}, u32[]{:S(2)}) collective-permute-start(bf16[288,1152]{1,0:T(8,128)(2,1)} %add_convert_fusion.8), channel_id=1, source_target_pairs={{0,2},{1,3},{2,0},{3,1},{4,6},{5,7},{6,4},{7,5},{8,10},{9,11},{10,... | collective-permute-start | bytes 1990664 | tf_op jit(solution)/shard_map/ppermute | solution.py:385
  658.6 32.9 %collective-permute-start.46 = (bf16[512,288]{1,0:T(8,128)(2,1)}, bf16[512,288]{1,0:T(8,128)(2,1)S(1)}, u32[]{:S(2)}, u32[]{:S(2)}) collective-permute-start(bf16[512,288]{1,0:T(8,128)(2,1)} %get-tuple-element.668), channel_id=1, source_target_pairs={{0,1},{1,0},{2,3},{3,2},{4,5},{5,4},{6,7},{7,6},{8,9},{9,8},{10,11... | collective-permute-start | bytes 884744 | tf_op jit(solution)/shard_map/ppermute | solution.py:385
  659.3 33.0 %collective-permute-start.47 = (bf16[512,288]{1,0:T(8,128)(2,1)S(1)}, bf16[512,288]{1,0:T(8,128)(2,1)S(1)}, u32[]{:S(2)}, u32[]{:S(2)}) collective-permute-start(bf16[512,288]{1,0:T(8,128)(2,1)S(1)} %copy-done.57), channel_id=1, source_target_pairs={{0,2},{1,3},{2,0},{3,1},{4,6},{5,7},{6,4},{7,5},{8,10},{9,11},{10,... | collective-permute-start | bytes 884744 | tf_op jit(solution)/shard_map/ppermute | solution.py:385
  660.8 32.2 %collective-permute-start.48 = (bf16[512,288]{1,0:T(8,128)(2,1)S(1)}, bf16[512,288]{1,0:T(8,128)(2,1)S(1)}, u32[]{:S(2)}, u32[]{:S(2)}) collective-permute-start(bf16[512,288]{1,0:T(8,128)(2,1)S(1)} %copy-done.55), channel_id=1, source_target_pairs={{0,3},{1,2},{2,1},{3,0},{4,7},{5,6},{6,5},{7,4},{8,11},{9,10},{10,... | collective-permute-start | bytes 884744 | tf_op jit(solution)/shard_map/ppermute | solution.py:385
  699.4 31.8 %collective-permute-start.51 = (bf16[576,1152]{1,0:T(8,128)(2,1)}, bf16[576,1152]{1,0:T(8,128)(2,1)S(1)}, u32[]{:S(2)}, u32[]{:S(2)}) collective-permute-start(bf16[576,1152]{1,0:T(8,128)(2,1)} %get-tuple-element.695), channel_id=1, source_target_pairs={{0,1},{1,0},{2,3},{3,2},{4,5},{5,4},{6,7},{7,6},{8,9},{9,8},{10,11... | collective-permute-start | bytes 3981320 | tf_op jit(solution)/shard_map/ppermute | solution.py:385
  700.0 31.5 %collective-permute-start.52 = (bf16[576,1152]{1,0:T(8,128)(2,1)}, bf16[576,1152]{1,0:T(8,128)(2,1)S(1)}, u32[]{:S(2)}, u32[]{:S(2)}) collective-permute-start(bf16[576,1152]{1,0:T(8,128)(2,1)} %get-tuple-element.696), channel_id=1, source_target_pairs={{0,2},{1,3},{2,0},{3,1},{4,6},{5,7},{6,4},{7,5},{8,10},{9,11},{10,... | collective-permute-start | bytes 3981320 | tf_op jit(solution)/shard_map/ppermute | solution.py:385
  701.5 69.6 %all-to-all-start.9 = ((bf16[4,144,1152]{2,1,0:T(8,128)(2,1)}), bf16[4,144,1152]{2,1,0:T(8,128)(2,1)}, u32[]{:S(2)}, u32[]{:S(2)}) async-start(bf16[4,144,1152]{2,1,0:T(8,128)(2,1)} %bitcast.82), calls=%async_computation.9 | async-start | bytes 2654208 | tf_op jit(solution)/shard_map/all_to_all | solution.py:402
  731.5 47.0 %collective-permute-start.53 = (bf16[576,1152]{1,0:T(8,128)(2,1)}, bf16[576,1152]{1,0:T(8,128)(2,1)}, u32[]{:S(2)}, u32[]{:S(2)}) collective-permute-start(bf16[576,1152]{1,0:T(8,128)(2,1)} %get-tuple-element.713), channel_id=1, source_target_pairs={{0,1},{1,0},{2,3},{3,2},{4,5},{5,4},{6,7},{7,6},{8,9},{9,8},{10,11... | collective-permute-start | bytes 3981320 | tf_op jit(solution)/shard_map/ppermute | solution.py:385
  732.9 45.5 %collective-permute-start.54 = (bf16[576,1152]{1,0:T(8,128)(2,1)}, bf16[576,1152]{1,0:T(8,128)(2,1)}, u32[]{:S(2)}, u32[]{:S(2)}) collective-permute-start(bf16[576,1152]{1,0:T(8,128)(2,1)} %get-tuple-element.714), channel_id=1, source_target_pairs={{0,2},{1,3},{2,0},{3,1},{4,6},{5,7},{6,4},{7,5},{8,10},{9,11},{10,... | collective-permute-start | bytes 3981320 | tf_op jit(solution)/shard_map/ppermute | solution.py:385
  736.4 40.1 %collective-permute-start.55 = (bf16[288,1152]{1,0:T(8,128)(2,1)}, bf16[288,1152]{1,0:T(8,128)(2,1)S(1)}, u32[]{:S(2)}, u32[]{:S(2)}) collective-permute-start(bf16[288,1152]{1,0:T(8,128)(2,1)} %add_convert_fusion.7), channel_id=1, source_target_pairs={{0,1},{1,0},{2,3},{3,2},{4,5},{5,4},{6,7},{7,6},{8,9},{9,8},{10,11... | collective-permute-start | bytes 1990664 | tf_op jit(solution)/shard_map/ppermute | solution.py:385
  737.0 40.6 %collective-permute-start.56 = (bf16[288,1152]{1,0:T(8,128)(2,1)}, bf16[288,1152]{1,0:T(8,128)(2,1)S(1)}, u32[]{:S(2)}, u32[]{:S(2)}) collective-permute-start(bf16[288,1152]{1,0:T(8,128)(2,1)} %add_convert_fusion.6), channel_id=1, source_target_pairs={{0,2},{1,3},{2,0},{3,1},{4,6},{5,7},{6,4},{7,5},{8,10},{9,11},{10,... | collective-permute-start | bytes 1990664 | tf_op jit(solution)/shard_map/ppermute | solution.py:385
  778.5 32.2 %collective-permute-start.61 = (bf16[576,1152]{1,0:T(8,128)(2,1)}, bf16[576,1152]{1,0:T(8,128)(2,1)S(1)}, u32[]{:S(2)}, u32[]{:S(2)}) collective-permute-start(bf16[576,1152]{1,0:T(8,128)(2,1)} %get-tuple-element.746), channel_id=1, source_target_pairs={{0,1},{1,0},{2,3},{3,2},{4,5},{5,4},{6,7},{7,6},{8,9},{9,8},{10,11... | collective-permute-start | bytes 3981320 | tf_op jit(solution)/shard_map/ppermute | solution.py:385
  779.3 32.2 %collective-permute-start.62 = (bf16[576,1152]{1,0:T(8,128)(2,1)}, bf16[576,1152]{1,0:T(8,128)(2,1)S(1)}, u32[]{:S(2)}, u32[]{:S(2)}) collective-permute-start(bf16[576,1152]{1,0:T(8,128)(2,1)} %get-tuple-element.747), channel_id=1, source_target_pairs={{0,2},{1,3},{2,0},{3,1},{4,6},{5,7},{6,4},{7,5},{8,10},{9,11},{10,... | collective-permute-start | bytes 3981320 | tf_op jit(solution)/shard_map/ppermute | solution.py:385
  786.5 46.9 %all-to-all-start.10 = ((bf16[4,144,1152]{2,1,0:T(8,128)(2,1)}), bf16[4,144,1152]{2,1,0:T(8,128)(2,1)}, u32[]{:S(2)}, u32[]{:S(2)}) async-start(bf16[4,144,1152]{2,1,0:T(8,128)(2,1)} %bitcast.84), calls=%async_computation.10 | async-start | bytes 2654208 | tf_op jit(solution)/shard_map/all_to_all | solution.py:402
  792.4 32.2 %collective-permute-start.59 = (bf16[288,1152]{1,0:T(8,128)(2,1)}, bf16[288,1152]{1,0:T(8,128)(2,1)S(1)}, u32[]{:S(2)}, u32[]{:S(2)}) collective-permute-start(bf16[288,1152]{1,0:T(8,128)(2,1)} %get-tuple-element.742), channel_id=1, source_target_pairs={{0,1},{1,0},{2,3},{3,2},{4,5},{5,4},{6,7},{7,6},{8,9},{9,8},{10,11... | collective-permute-start | bytes 1990664 | tf_op jit(solution)/shard_map/ppermute | solution.py:385
  793.8 31.2 %collective-permute-start.60 = (bf16[288,1152]{1,0:T(8,128)(2,1)}, bf16[288,1152]{1,0:T(8,128)(2,1)}, u32[]{:S(2)}, u32[]{:S(2)}) collective-permute-start(bf16[288,1152]{1,0:T(8,128)(2,1)} %get-tuple-element.743), channel_id=1, source_target_pairs={{0,2},{1,3},{2,0},{3,1},{4,6},{5,7},{6,4},{7,5},{8,10},{9,11},{10,... | collective-permute-start | bytes 1990664 | tf_op jit(solution)/shard_map/ppermute | solution.py:385
  825.0 42.4 %collective-permute-start.63 = (bf16[576,1152]{1,0:T(8,128)(2,1)}, bf16[576,1152]{1,0:T(8,128)(2,1)}, u32[]{:S(2)}, u32[]{:S(2)}) collective-permute-start(bf16[576,1152]{1,0:T(8,128)(2,1)} %get-tuple-element.756), channel_id=1, source_target_pairs={{0,1},{1,0},{2,3},{3,2},{4,5},{5,4},{6,7},{7,6},{8,9},{9,8},{10,11... | collective-permute-start | bytes 3981320 | tf_op jit(solution)/shard_map/ppermute | solution.py:385
  826.4 41.0 %collective-permute-start.64 = (bf16[576,1152]{1,0:T(8,128)(2,1)}, bf16[576,1152]{1,0:T(8,128)(2,1)}, u32[]{:S(2)}, u32[]{:S(2)}) collective-permute-start(bf16[576,1152]{1,0:T(8,128)(2,1)} %get-tuple-element.757), channel_id=1, source_target_pairs={{0,2},{1,3},{2,0},{3,1},{4,6},{5,7},{6,4},{7,5},{8,10},{9,11},{10,... | collective-permute-start | bytes 3981320 | tf_op jit(solution)/shard_map/ppermute | solution.py:385
  833.5 42.9 %all-to-all-start.11 = ((bf16[4,144,1152]{2,1,0:T(8,128)(2,1)}), bf16[4,144,1152]{2,1,0:T(8,128)(2,1)}, u32[]{:S(2)}, u32[]{:S(2)}) async-start(bf16[4,144,1152]{2,1,0:T(8,128)(2,1)} %bitcast.102), calls=%async_computation.11 | async-start | bytes 2654208 | tf_op jit(solution)/shard_map/all_to_all | solution.py:402
  839.3 30.6 %collective-permute-start.65 = (bf16[288,1152]{1,0:T(8,128)(2,1)}, bf16[288,1152]{1,0:T(8,128)(2,1)S(1)}, u32[]{:S(2)}, u32[]{:S(2)}) collective-permute-start(bf16[288,1152]{1,0:T(8,128)(2,1)} %add_convert_fusion.3), channel_id=1, source_target_pairs={{0,1},{1,0},{2,3},{3,2},{4,5},{5,4},{6,7},{7,6},{8,9},{9,8},{10,11... | collective-permute-start | bytes 1990664 | tf_op jit(solution)/shard_map/ppermute | solution.py:385
  840.0 31.1 %collective-permute-start.66 = (bf16[288,1152]{1,0:T(8,128)(2,1)}, bf16[288,1152]{1,0:T(8,128)(2,1)}, u32[]{:S(2)}, u32[]{:S(2)}) collective-permute-start(bf16[288,1152]{1,0:T(8,128)(2,1)} %add_convert_fusion.2), channel_id=1, source_target_pairs={{0,2},{1,3},{2,0},{3,1},{4,6},{5,7},{6,4},{7,5},{8,10},{9,11},{10,... | collective-permute-start | bytes 1990664 | tf_op jit(solution)/shard_map/ppermute | solution.py:385
  876.4 45.0 %all-to-all-start.12 = ((bf16[4,144,1152]{2,1,0:T(8,128)(2,1)}), bf16[4,144,1152]{2,1,0:T(8,128)(2,1)S(1)}, u32[]{:S(2)}, u32[]{:S(2)}) async-start(bf16[4,144,1152]{2,1,0:T(8,128)(2,1)} %bitcast.104), calls=%async_computation.12 | async-start | bytes 2654208 | tf_op jit(solution)/shard_map/all_to_all | solution.py:402
  927.2 45.4 %all-to-all-start.13 = ((bf16[4,144,1152]{2,1,0:T(8,128)(2,1)}), bf16[4,144,1152]{2,1,0:T(8,128)(2,1)}, u32[]{:S(2)}, u32[]{:S(2)}) async-start(bf16[4,144,1152]{2,1,0:T(8,128)(2,1)} %bitcast.121), calls=%async_computation.13 | async-start | bytes 2654208 | tf_op jit(solution)/shard_map/all_to_all | solution.py:402
  (139 other events, 1106.6 us)
Sparse Core Ops, SparseCore 0:
  64.8 77.2 all-gather.3

commit v4 on v3

--- a/solution.py
+++ b/solution.py
@@ -1444,22 +1444,22 @@
     )
     received = [swap(grad_qkv), swap(grad_sent)]
     sides = scatter_sides(output_part)
-    result_blocks = leaving(output_second)
     moving = mine_first(grad_second.astype(jnp.bfloat16), place, 0)
     moving = moving.reshape(2, 1, groups, frames, period, half)
+    received, grad_attn, grad_qkv, sides, moving = together(
+        received, grad_attn, grad_qkv, sides, moving
+    )
+    output_part = scatter_plane(output_part, sides)
+    attn_blocks = attn_terms(saved_second, swapped_second, grad_attn, grad_qkv, received)
+    attn_blocks, moving, hidden_part = together(attn_blocks, moving, hidden_part)
     moved = lax.all_to_all(moving, "row", split_axis=3, concat_axis=1, tiled=True)
-    received, grad_attn, grad_qkv, sides, result_blocks = together(
-        received, grad_attn, grad_qkv, sides, result_blocks
-    )
-    output_part = scatter_plane(output_part, sides)
-    attn_blocks = attn_terms(
-        saved_second, swapped_second, grad_attn, grad_qkv, received, 15 * 10**9
-    )
-    attn_blocks, hidden_part, output_part = together(attn_blocks, hidden_part, output_part)
     attn_part_second = scatter_corner(attn_blocks)
+    result_blocks = leaving(after(output_second, *attn_blocks))
     sides = scatter_sides(hidden_part)
     output_total = add_blocks(output_part)
-    moved, output_total, sides = together(moved, output_total, sides)
+    moved, output_total, sides, result_blocks = together(
+        moved, output_total, sides, result_blocks
+    )
     hidden_part = scatter_plane(hidden_part, sides)
     moved = moved.transpose(0, 3, 1, 2, 4, 5).reshape(2, -1, half)
     returned = mine_first(moved, place, 0).astype(jnp.float32)

time: 994 us -> 990 us (level)
    ppermute x80, waiting for transfers between devices: 133 us -> 168 us  [exchange(): lax.ppermute(values, axis, [(index, index ^ mask) for index in range(coun...]
    all_to_all x12, waiting for transfers between devices: 27.5 us -> 2.63 us  [over_depth(): lax.all_to_all(values, 'row', split_axis=0, concat_axis=0, tiled=True, ax...]
    unnamed x227 -> x221, local copies, waits for them, and re-layouts: 31.7 us -> 32.7 us
  transfers between devices with their start and end apart: 95 -> 95, of which waited for: 40 -> 42; matrix products, arithmetic and copies ran while one was open for 17% -> 16% of each run, Pallas kernels for 36% -> 36%
where the time goes in v4:
time: 990 us; the launch traced here: 982 us
  Pallas kernels  361 us (36%)
  waiting for transfers between devices  232 us (23%)
  local copies, waits for them, and re-layouts  185 us (19%)
  starting transfers between devices  135 us (14%)
  other arithmetic  49.8 us (5%)
  between operations  16.2 us (2%)
    ppermute x80, waiting for transfers between devices, exchange(): lax.ppermute(values, axis, [(index, index ^ mask) for index in range(coun...  168 us
    ppermute x80, starting transfers between devices, exchange(): lax.ppermute(values, axis, [(index, index ^ mask) for index in range(coun...  68.7 us
    pallas_call x6, Pallas kernels, weight_grads(): pl.pallas_call(functools.partial(weight_kernel, len(pairs), overlap, step...  67.6 us
    pallas_call x2, Pallas kernels, attention_backward(): pl.pallas_call(functools.partial(attention_back_kernel, size, period, ste...  67.2 us
    pallas_call x2, Pallas kernels, attention_forward(): pl.pallas_call(functools.partial(attention_kernel, size, period, steps),...  57.8 us
    pallas_call x2, Pallas kernels, mlp_forward(): pl.pallas_call(functools.partial(mlp_kernel, steps), grid=(steps,), in_sp...  56.7 us
    all_to_all x12, starting transfers between devices, over_depth(): lax.all_to_all(values, 'row', split_axis=0, concat_axis=0, tiled=True, ax...  56.4 us
    pallas_call x2, Pallas kernels, mlp_backward(): pl.pallas_call(functools.partial(mlp_back_kernel, steps), grid=(steps,),...  55.6 us
  transfers between devices with their start and end apart: 95, of which 42 were waited for; matrix products, arithmetic and copies ran while one was open for 16% of the time, Pallas kernels for 36%

profile of v4, /device:TPU:0, one launch (start us, length us, event | category | flops | bytes accessed | tf_op | source)
XLA Modules:
  0.0 981.7 jit_solution(8987826256284574843)
XLA Ops:
  7.2 4.7 slice_reduce_fusion.4
  14.8 6.4 all-to-all-start
  30.7 7.8 slice_reduce_fusion.2
  52.9 5.2 reshape.399
  65.0 3.8 all-to-all-start.1
  71.9 9.0 slice_reduce_fusion
  92.1 4.7 reorder.6.refs_0_.refs_1_
  112.6 3.9 all-to-all-start.2
  116.6 24.6 %all-gather.4.cloned.1.call-done = f32[32,4,5472]{2,1,0:T(4,128)} async-done(((f32[1,4,5472]{2,1,0:T(4,128)}), f32[32,4,5472]{2,1,0:T(4,128)}) %all-gather.4.cloned.1.call-update) | async-done | bytes 2801680 | tf_op jit(solution)/shard_map/all_gather | solution.py:1281
  145.4 13.9 %collective-permute-done.5.lower.across = bf16[864,1152]{1,0:T(8,128)(2,1)} collective-permute-done((bf16[864,1152]{1,0:T(8,128)(2,1)}, bf16[864,1152]{1,0:T(8,128)(2,1)}, u32[]{:S(2)}, u32[]{:S(2)}) %collective-permute-start.5) | collective-permute-done | bytes 1990688 | tf_op jit(solution)/shard_map/ppermute | solution.py:385
  165.3 4.0 pack_blocks.6.refs_4_.refs_6_
  169.4 3.6 all-to-all-start.3
  178.5 28.9 %attention_forward.2 = (f32[2,512,576]{2,1,0:T(8,128)}, bf16[512,576]{1,0:T(8,128)(2,1)}, bf16[576,512]{1,0:T(8,128)(2,1)}, bf16[4,512,896]{2,1,0:T(8,128)(2,1)}...) custom-call(f32[2,512,576]{2,1,0:T(8,128)} %copy-done.1, ...), custom_call_target="tpu_custom_call" | custom-call | tf_op jit(solution)/shard_map/attention_forward/pallas_call | solution.py:668
  207.4 11.7 %collective-permute-done.8.lower.across = bf16[864,1152]{1,0:T(8,128)(2,1)} collective-permute-done((bf16[864,1152]{1,0:T(8,128)(2,1)}, bf16[864,1152]{1,0:T(8,128)(2,1)}, u32[]{:S(2)}, u32[]{:S(2)}) %collective-permute-start.8) | collective-permute-done | bytes 1990688 | tf_op jit(solution)/shard_map/ppermute | solution.py:385
  226.8 4.7 all-to-all-start.4
  231.5 3.9 pack_blocks.7.refs_4_.refs_5_
  235.5 4.3 reshape.412
  242.5 26.4 %collective-permute-done.10.lower.across = bf16[864,1152]{1,0:T(8,128)(2,1)} collective-permute-done((bf16[864,1152]{1,0:T(8,128)(2,1)}, bf16[864,1152]{1,0:T(8,128)(2,1)}, u32[]{:S(2)}, u32[]{:S(2)}) %collective-permute-start.10) | collective-permute-done | bytes 1990688 | tf_op jit(solution)/shard_map/ppermute | solution.py:385
  272.3 3.6 pad_maximum_fusion.6
  275.9 3.9 pack_blocks.8.refs_6_.refs_7_
  280.0 4.6 all-to-all-start.5
  289.2 28.2 %mlp_forward.2 = (f32[2,512,576]{2,1,0:T(8,128)}, bf16[512,576]{1,0:T(8,128)(2,1)}, bf16[576,512]{1,0:T(8,128)(2,1)}, bf16[4,512,1152]{2,1,0:T(8,128)(2,1)}, bf1...) custom-call(f32[2,512,576]{2,1,0:T(8,128)} %get-tuple-element.480.refs_0_.refs_1_, ...), custom_call_target="tpu_custom_call" | custom-call | tf_op jit(solution)/shard_map/mlp_forward/pallas_call | solution.py:749
  317.4 13.1 %collective-permute-done.15.lower.across = bf16[864,1152]{1,0:T(8,128)(2,1)} collective-permute-done((bf16[864,1152]{1,0:T(8,128)(2,1)}, bf16[864,1152]{1,0:T(8,128)(2,1)}, u32[]{:S(2)}, u32[]{:S(2)}) %collective-permute-start.15) | collective-permute-done | bytes 1990688 | tf_op jit(solution)/shard_map/ppermute | solution.py:385
  337.7 5.1 all-to-all-start.6
  345.8 4.0 pack_blocks.10.refs_4_.refs_6_
  350.4 24.6 %all-to-all-done.6 = bf16[2,8,2,2,16,576]{5,4,2,3,0,1:T(8,128)(2,1)S(1)} async-done(((bf16[2,8,2,2,16,576]{5,4,2,3,0,1:T(8,128)(2,1)}), bf16[2,8,2,2,16,576]{5,4,2,3,0,1:T(8,128)(2,1)S(1)}, u32[]{:S(2)}, u32[]{:S(2)}) %all-to-all-start.6) | async-done | bytes 1179680 | tf_op jit(solution)/shard_map/all_to_all | solution.py:1405
  375.1 13.8 %collective-permute-done.19.across.lower = bf16[864,1152]{1,0:T(8,128)(2,1)} collective-permute-done((bf16[864,1152]{1,0:T(8,128)(2,1)}, bf16[864,1152]{1,0:T(8,128)(2,1)}, u32[]{:S(2)}, u32[]{:S(2)}) %collective-permute-start.19) | collective-permute-done | bytes 1990688 | tf_op jit(solution)/shard_map/ppermute | solution.py:385
  397.3 11.3 %collective-permute-done.22.lower = bf16[288,1152]{1,0:T(8,128)(2,1)S(1)} collective-permute-done((bf16[288,1152]{1,0:T(8,128)(2,1)S(1)}, bf16[288,1152]{1,0:T(8,128)(2,1)S(1)}, u32[]{:S(2)}, u32[]{:S(2)}) %collective-permute-start.22) | collective-permute-done | bytes 663584 | tf_op jit(solution)/shard_map/ppermute | solution.py:385
  409.0 3.9 pack_blocks.9.refs_6_.refs_7_
  415.4 28.9 %attention_forward.3 = (f32[2,512,576]{2,1,0:T(8,128)}, bf16[512,576]{1,0:T(8,128)(2,1)}, bf16[576,512]{1,0:T(8,128)(2,1)}, bf16[4,512,896]{2,1,0:T(8,128)(2,1)}...) custom-call(f32[2,512,576]{2,1,0:T(8,128)} %fusion.2.refs_0_.refs_1_, ...), custom_call_target="tpu_custom_call" | custom-call | tf_op jit(solution)/shard_map/attention_forward/pallas_call | solution.py:668
  449.1 28.5 %mlp_forward.3 = (f32[2,512,576]{2,1,0:T(8,128)}, bf16[512,576]{1,0:T(8,128)(2,1)}, bf16[576,512]{1,0:T(8,128)(2,1)}, bf16[4,512,1152]{2,1,0:T(8,128)(2,1)}, bf1...) custom-call(f32[2,512,576]{2,1,0:T(8,128)} %get-tuple-element.539.refs_0_.refs_1_, ...), custom_call_target="tpu_custom_call" | custom-call | tf_op jit(solution)/shard_map/mlp_forward/pallas_call | solution.py:749
  478.3 4.7 reorder.7.refs_0_
  484.4 27.9 %mlp_backward.2 = (f32[2,512,576]{2,1,0:T(8,128)}, bf16[512,576]{1,0:T(8,128)(2,1)}, bf16[576,512]{1,0:T(8,128)(2,1)}, bf16[4,512,1152]{2,1,0:T(8,128)(2,1)}, f3...) custom-call(f32[2,512,576]{2,1,0:T(8,128)} %copy-done.6, f32[2,512,576]{2,1,0:T(8,128)} %get-tuple-element.539.refs_0_.refs_1_, ...), custom_call_target="tpu_custom_call" | custom-call | tf_op jit(solution)/shard_map/mlp_backward/pallas_call | solution.py:823
  515.5 10.6 %weight_grads.6 = (bf16[576,1152]{1,0:T(8,128)(2,1)}, bf16[288,1152]{1,0:T(8,128)(2,1)}, bf16[576,1152]{1,0:T(8,128)(2,1)}, bf16[576,1152]{1,0:T(8,128)(2,1)}, bf16[288,1152]{1,0:T(8,128)(2,1)}) custom-call(bf16[512,576]{1,0:T(8,128)(2,1)} %get-tuple-element.580.refs_0_, bf16[576,512]{1,0:T(8,128)(2,1)} %copy-done.83, ...), custom_call_target="tpu_custom_call" | custom-call | tf_op jit(solution)/shard_map/weight_grads/pallas_call | solution.py:1041
  531.4 10.7 %weight_grads.7 = (bf16[576,1152]{1,0:T(8,128)(2,1)}, bf16[288,1152]{1,0:T(8,128)(2,1)}, bf16[576,1152]{1,0:T(8,128)(2,1)}, bf16[576,1152]{1,0:T(8,128)(2,1)}, bf16[288,1152]{1,0:T(8,128)(2,1)}) custom-call(bf16[512,576]{1,0:T(8,128)(2,1)} %get-tuple-element.575.refs_0_, bf16[576,512]{1,0:T(8,128)(2,1)} %copy-done.81, ...), custom_call_target="tpu_custom_call" | custom-call | tf_op jit(solution)/shard_map/weight_grads/pallas_call | solution.py:1041
  542.1 33.7 %attention_backward.2 = (f32[2,512,576]{2,1,0:T(8,128)}, bf16[512,576]{1,0:T(8,128)(2,1)}, bf16[576,512]{1,0:T(8,128)(2,1)}, bf16[4,512,896]{2,1,0:T(8,128)(2,1)...) custom-call(f32[2,512,576]{2,1,0:T(8,128)} %get-tuple-element.596.refs_0_, f32[2,512,576]{2,1,0:T(8,128)} %fusion.2.refs_0_.refs_1_, ...), custom_call_target="tpu_custom_call" | custom-call | tf_op jit(solution)/shard_map/attention_backward/pallas_call | solution.py:933
  583.2 12.4 %weight_grads.8 = (bf16[576,1152]{1,0:T(8,128)(2,1)}, bf16[288,1152]{1,0:T(8,128)(2,1)}, bf16[576,1152]{1,0:T(8,128)(2,1)}, bf16[576,1152]{1,0:T(8,128)(2,1)}, bf16[288,1152]{1,0:T(8,128)(2,1)}) custom-call(bf16[512,576]{1,0:T(8,128)(2,1)} %get-tuple-element.535.refs_0_, bf16[576,512]{1,0:T(8,128)(2,1)} %collective-permute-done.28.refs_1_, ...), custom_call_target="tpu_custom_call" | custom-call | tf_op jit(solution)/shard_map/weight_grads/pallas_call | solution.py:1041
  595.7 12.0 %collective-permute-done.40.across_first = bf16[576,1152]{1,0:T(8,128)(2,1)S(1)} collective-permute-done((bf16[576,1152]{1,0:T(8,128)(2,1)}, bf16[576,1152]{1,0:T(8,128)(2,1)S(1)}, u32[]{:S(2)}, u32[]{:S(2)}) %collective-permute-start.40) | collective-permute-done | bytes 1327136 | tf_op jit(solution)/shard_map/ppermute | solution.py:385
  609.2 4.7 all-to-all-start.7
  618.7 4.4 reorder.8
  625.6 5.9 collective-permute-done.42.across_upper
  634.3 11.9 %all-to-all-done.7 = bf16[2,1,2,16,16,576]{5,4,2,0,1,3:T(8,128)(2,1)} async-done(((bf16[2,1,2,16,16,576]{5,4,2,0,1,3:T(8,128)(2,1)}), bf16[2,1,2,16,16,576]{5,4,2,0,1,3:T(8,128)(2,1)}, u32[]{:S(2)}, u32[]{:S(2)}) %all-to-all-start.7) | async-done | bytes 1179680 | tf_op jit(solution)/shard_map/all_to_all | solution.py:1455
  648.7 4.3 all-to-all-start.8
  661.6 27.7 %mlp_backward.3 = (f32[2,512,576]{2,1,0:T(8,128)}, bf16[512,576]{1,0:T(8,128)(2,1)}, bf16[576,512]{1,0:T(8,128)(2,1)}, bf16[4,512,1152]{2,1,0:T(8,128)(2,1)}, f3...) custom-call(f32[2,512,576]{2,1,0:T(8,128)} %fusion.3.refs_0_, f32[2,512,576]{2,1,0:T(8,128)} %get-tuple-element.480.refs_0_.refs_1_, ...), custom_call_target="tpu_custom_call" | custom-call | tf_op jit(solution)/shard_map/mlp_backward/pallas_call | solution.py:823
  699.4 5.5 all-to-all-start.9
  704.8 10.6 %weight_grads.9 = (bf16[576,1152]{1,0:T(8,128)(2,1)}, bf16[288,1152]{1,0:T(8,128)(2,1)}, bf16[576,1152]{1,0:T(8,128)(2,1)}, bf16[576,1152]{1,0:T(8,128)(2,1)}, bf16[288,1152]{1,0:T(8,128)(2,1)}) custom-call(bf16[512,576]{1,0:T(8,128)(2,1)} %get-tuple-element.680.refs_0_, bf16[576,512]{1,0:T(8,128)(2,1)} %copy-done.82, ...), custom_call_target="tpu_custom_call" | custom-call | tf_op jit(solution)/shard_map/weight_grads/pallas_call | solution.py:1041
  715.5 10.7 %weight_grads.10 = (bf16[576,1152]{1,0:T(8,128)(2,1)}, bf16[288,1152]{1,0:T(8,128)(2,1)}, bf16[576,1152]{1,0:T(8,128)(2,1)}, bf16[576,1152]{1,0:T(8,128)(2,1)}, bf16[288,1152]{1,0:T(8,128)(2,1)}) custom-call(bf16[512,576]{1,0:T(8,128)(2,1)} %get-tuple-element.501.refs_0_, bf16[576,512]{1,0:T(8,128)(2,1)} %copy-done.80, ...), custom_call_target="tpu_custom_call" | custom-call | tf_op jit(solution)/shard_map/weight_grads/pallas_call | solution.py:1041
  735.4 33.5 %attention_backward.3 = (f32[2,512,576]{2,1,0:T(8,128)}, bf16[512,576]{1,0:T(8,128)(2,1)}, bf16[576,512]{1,0:T(8,128)(2,1)}, bf16[4,512,896]{2,1,0:T(8,128)(2,1)...) custom-call(f32[2,512,576]{2,1,0:T(8,128)} %get-tuple-element.699.refs_0_, f32[2,512,576]{2,1,0:T(8,128)} %copy-done.1, ...), custom_call_target="tpu_custom_call" | custom-call | tf_op jit(solution)/shard_map/attention_backward/pallas_call | solution.py:933
  768.9 5.5 collective-permute-done.55.across_upper
  784.4 5.1 all-to-all-start.10
  793.2 12.5 %weight_grads.11 = (bf16[576,1152]{1,0:T(8,128)(2,1)}, bf16[288,1152]{1,0:T(8,128)(2,1)}, bf16[576,1152]{1,0:T(8,128)(2,1)}, bf16[576,1152]{1,0:T(8,128)(2,1)}, bf16[288,1152]{1,0:T(8,128)(2,1)}) custom-call(bf16[512,576]{1,0:T(8,128)(2,1)} %get-tuple-element.462.refs_0_, bf16[576,512]{1,0:T(8,128)(2,1)} %collective-permute-done.12.refs_1_, ...), custom_call_target="tpu_custom_call" | custom-call | tf_op jit(solution)/shard_map/weight_grads/pallas_call | solution.py:1041
  809.3 13.1 %collective-permute-done.59.across_upper = bf16[288,1152]{1,0:T(8,128)(2,1)S(1)} collective-permute-done((bf16[288,1152]{1,0:T(8,128)(2,1)}, bf16[288,1152]{1,0:T(8,128)(2,1)S(1)}, u32[]{:S(2)}, u32[]{:S(2)}) %collective-permute-start.59) | collective-permute-done | bytes 663584 | tf_op jit(solution)/shard_map/ppermute | solution.py:385
  825.7 3.4 add_blocks.9
  831.4 5.1 all-to-all-start.11
  854.9 4.0 reshape_reshape.30
  860.6 4.4 reorder.9
  874.2 5.0 all-to-all-start.12
  886.8 3.4 convert_reduce_fusion.2
  893.7 6.8 collective-permute-done.74.across_upper
  913.3 3.7 collective-permute-done.77
  923.6 4.4 all-to-all-start.13
  941.4 4.9 reshape.465
  949.6 5.9 reshape.462
  959.2 5.5 reshape_reshape.32
  (603 shorter events, 296.4 us)
Async XLA Ops:
  14.8 38.1 %all-to-all-start = ((bf16[4,144,1152]{2,1,0:T(8,128)(2,1)}), bf16[4,144,1152]{2,1,0:T(8,128)(2,1)S(1)}, u32[]{:S(2)}, u32[]{:S(2)}) async-start(bf16[4,144,1152]{2,1,0:T(8,128)(2,1)} %bitcast.13), calls=%async_computation | async-start | bytes 2654208 | tf_op jit(solution)/shard_map/all_to_all | solution.py:402
  21.2 120.0 %all-gather.4.cloned.1.call-start = ((), (), s32[]{:S(2)}) async-start(), calls=%async_computation.14 | async-start | bytes 2906112 | tf_op jit(solution)/shard_map/all_gather | solution.py:1281
  65.0 36.8 %all-to-all-start.1 = ((bf16[4,144,1152]{2,1,0:T(8,128)(2,1)}), bf16[4,144,1152]{2,1,0:T(8,128)(2,1)S(1)}, u32[]{:S(2)}, u32[]{:S(2)}) async-start(bf16[4,144,1152]{2,1,0:T(8,128)(2,1)} %tile.59), calls=%async_computation.1 | async-start | bytes 2654208 | tf_op jit(solution)/shard_map/all_to_all | solution.py:402
  68.8 30.9 %collective-permute-start.3 = (bf16[576,1152]{1,0:T(8,128)(2,1)S(1)}, bf16[576,1152]{1,0:T(8,128)(2,1)}, u32[]{:S(2)}, u32[]{:S(2)}) collective-permute-start(bf16[576,1152]{1,0:T(8,128)(2,1)S(1)} %bitcast.240), channel_id=1, source_target_pairs={{0,1},{1,0},{2,3},{3,2},{4,5},{5,4},{6,7},{7,6},{8,9},{9,8},{10,11... | collective-permute-start | bytes 3981320 | tf_op jit(solution)/shard_map/ppermute | solution.py:385
  70.3 30.6 %collective-permute-start.4 = (bf16[576,1152]{1,0:T(8,128)(2,1)S(1)}, bf16[576,1152]{1,0:T(8,128)(2,1)}, u32[]{:S(2)}, u32[]{:S(2)}) collective-permute-start(bf16[576,1152]{1,0:T(8,128)(2,1)S(1)} %bitcast.241), channel_id=1, source_target_pairs={{0,2},{1,3},{2,0},{3,1},{4,6},{5,7},{6,4},{7,5},{8,10},{9,11},{10,... | collective-permute-start | bytes 3981320 | tf_op jit(solution)/shard_map/ppermute | solution.py:385
  109.6 49.7 %collective-permute-start.5 = (bf16[864,1152]{1,0:T(8,128)(2,1)}, bf16[864,1152]{1,0:T(8,128)(2,1)}, u32[]{:S(2)}, u32[]{:S(2)}) collective-permute-start(bf16[864,1152]{1,0:T(8,128)(2,1)} %get-tuple-element.977), channel_id=1, source_target_pairs={{0,1},{1,0},{2,3},{3,2},{4,5},{5,4},{6,7},{7,6},{8,9},{9,8},{10,11... | collective-permute-start | bytes 5971976 | tf_op jit(solution)/shard_map/ppermute | solution.py:385
  111.1 49.3 %collective-permute-start.6 = (bf16[864,1152]{1,0:T(8,128)(2,1)}, bf16[864,1152]{1,0:T(8,128)(2,1)}, u32[]{:S(2)}, u32[]{:S(2)}) collective-permute-start(bf16[864,1152]{1,0:T(8,128)(2,1)} %get-tuple-element.976), channel_id=1, source_target_pairs={{0,2},{1,3},{2,0},{3,1},{4,6},{5,7},{6,4},{7,5},{8,10},{9,11},{10,... | collective-permute-start | bytes 5971976 | tf_op jit(solution)/shard_map/ppermute | solution.py:385
  112.6 47.8 %all-to-all-start.2 = ((bf16[4,144,1152]{2,1,0:T(8,128)(2,1)}), bf16[4,144,1152]{2,1,0:T(8,128)(2,1)S(1)}, u32[]{:S(2)}, u32[]{:S(2)}) async-start(bf16[4,144,1152]{2,1,0:T(8,128)(2,1)} %tile.66), calls=%async_computation.2 | async-start | bytes 2654208 | tf_op jit(solution)/shard_map/all_to_all | solution.py:402
  169.4 38.0 %all-to-all-start.3 = ((bf16[4,144,1152]{2,1,0:T(8,128)(2,1)}), bf16[4,144,1152]{2,1,0:T(8,128)(2,1)S(1)}, u32[]{:S(2)}, u32[]{:S(2)}) async-start(bf16[4,144,1152]{2,1,0:T(8,128)(2,1)} %tile.64), calls=%async_computation.3 | async-start | bytes 2654208 | tf_op jit(solution)/shard_map/all_to_all | solution.py:402
  172.9 46.1 %collective-permute-start.8 = (bf16[864,1152]{1,0:T(8,128)(2,1)}, bf16[864,1152]{1,0:T(8,128)(2,1)}, u32[]{:S(2)}, u32[]{:S(2)}) collective-permute-start(bf16[864,1152]{1,0:T(8,128)(2,1)} %get-tuple-element.975), channel_id=1, source_target_pairs={{0,1},{1,0},{2,3},{3,2},{4,5},{5,4},{6,7},{7,6},{8,9},{9,8},{10,11... | collective-permute-start | bytes 5971976 | tf_op jit(solution)/shard_map/ppermute | solution.py:385
  173.5 45.8 %collective-permute-start.9 = (bf16[864,1152]{1,0:T(8,128)(2,1)}, bf16[864,1152]{1,0:T(8,128)(2,1)}, u32[]{:S(2)}, u32[]{:S(2)}) collective-permute-start(bf16[864,1152]{1,0:T(8,128)(2,1)} %get-tuple-element.974), channel_id=1, source_target_pairs={{0,2},{1,3},{2,0},{3,1},{4,6},{5,7},{6,4},{7,5},{8,10},{9,11},{10,... | collective-permute-start | bytes 5971976 | tf_op jit(solution)/shard_map/ppermute | solution.py:385
  223.8 45.0 %collective-permute-start.10 = (bf16[864,1152]{1,0:T(8,128)(2,1)}, bf16[864,1152]{1,0:T(8,128)(2,1)}, u32[]{:S(2)}, u32[]{:S(2)}) collective-permute-start(bf16[864,1152]{1,0:T(8,128)(2,1)} %get-tuple-element.973), channel_id=1, source_target_pairs={{0,1},{1,0},{2,3},{3,2},{4,5},{5,4},{6,7},{7,6},{8,9},{9,8},{10,11... | collective-permute-start | bytes 5971976 | tf_op jit(solution)/shard_map/ppermute | solution.py:385
  225.3 44.7 %collective-permute-start.11 = (bf16[864,1152]{1,0:T(8,128)(2,1)}, bf16[864,1152]{1,0:T(8,128)(2,1)}, u32[]{:S(2)}, u32[]{:S(2)}) collective-permute-start(bf16[864,1152]{1,0:T(8,128)(2,1)} %get-tuple-element.972), channel_id=1, source_target_pairs={{0,2},{1,3},{2,0},{3,1},{4,6},{5,7},{6,4},{7,5},{8,10},{9,11},{10,... | collective-permute-start | bytes 5971976 | tf_op jit(solution)/shard_map/ppermute | solution.py:385
  226.8 43.2 %all-to-all-start.4 = ((bf16[4,144,1152]{2,1,0:T(8,128)(2,1)}), bf16[4,144,1152]{2,1,0:T(8,128)(2,1)}, u32[]{:S(2)}, u32[]{:S(2)}) async-start(bf16[4,144,1152]{2,1,0:T(8,128)(2,1)} %tile.62), calls=%async_computation.4 | async-start | bytes 2654208 | tf_op jit(solution)/shard_map/all_to_all | solution.py:402
  235.4 51.6 %collective-permute-start.13 = (bf16[4,576,1152]{2,1,0:T(8,128)(2,1)}, bf16[4,576,1152]{2,1,0:T(8,128)(2,1)}, u32[]{:S(2)}, u32[]{:S(2)}) collective-permute-start(bf16[4,576,1152]{2,1,0:T(8,128)(2,1)} %pack_blocks.7.refs_4_.refs_5_), channel_id=1, source_target_pairs={{0,4},{4,0},{8,12},{12,8},{16,20},{20,16},{24,28},{28,24},{1,5},{5... | collective-permute-start | bytes 15925256 | tf_op jit(solution)/shard_map/ppermute | solution.py:385
  280.0 37.4 %all-to-all-start.5 = ((bf16[4,144,1152]{2,1,0:T(8,128)(2,1)}), bf16[4,144,1152]{2,1,0:T(8,128)(2,1)S(1)}, u32[]{:S(2)}, u32[]{:S(2)}) async-start(bf16[4,144,1152]{2,1,0:T(8,128)(2,1)} %tile.68), calls=%async_computation.5 | async-start | bytes 2654208 | tf_op jit(solution)/shard_map/all_to_all | solution.py:402
  284.6 46.0 %collective-permute-start.15 = (bf16[864,1152]{1,0:T(8,128)(2,1)}, bf16[864,1152]{1,0:T(8,128)(2,1)}, u32[]{:S(2)}, u32[]{:S(2)}) collective-permute-start(bf16[864,1152]{1,0:T(8,128)(2,1)} %get-tuple-element.971), channel_id=1, source_target_pairs={{0,1},{1,0},{2,3},{3,2},{4,5},{5,4},{6,7},{7,6},{8,9},{9,8},{10,11... | collective-permute-start | bytes 5971976 | tf_op jit(solution)/shard_map/ppermute | solution.py:385
  285.2 45.6 %collective-permute-start.16 = (bf16[864,1152]{1,0:T(8,128)(2,1)}, bf16[864,1152]{1,0:T(8,128)(2,1)}, u32[]{:S(2)}, u32[]{:S(2)}) collective-permute-start(bf16[864,1152]{1,0:T(8,128)(2,1)} %get-tuple-element.970), channel_id=1, source_target_pairs={{0,2},{1,3},{2,0},{3,1},{4,6},{5,7},{6,4},{7,5},{8,10},{9,11},{10,... | collective-permute-start | bytes 5971976 | tf_op jit(solution)/shard_map/ppermute | solution.py:385
  286.8 30.6 %collective-permute-start.17 = (bf16[4,512,384]{2,1,0:T(8,128)(2,1)}, bf16[4,512,384]{2,1,0:T(8,128)(2,1)}, u32[]{:S(2)}, u32[]{:S(2)}) collective-permute-start(bf16[4,512,384]{2,1,0:T(8,128)(2,1)} %get-tuple-element.507.refs_6_), channel_id=1, source_target_pairs={{0,4},{4,0},{8,12},{12,8},{16,20},{20,16},{24,28},{28,24},{1,5},{5... | collective-permute-start | bytes 4718600 | tf_op jit(solution)/shard_map/ppermute | solution.py:385
  287.0 30.3 %collective-permute-start.12 = (bf16[576,512]{1,0:T(8,128)(2,1)}, bf16[576,512]{1,0:T(8,128)(2,1)}, u32[]{:S(2)}, u32[]{:S(2)}) collective-permute-start(bf16[576,512]{1,0:T(8,128)(2,1)} %get-tuple-element.479), channel_id=1, source_target_pairs={{0,4},{4,0},{8,12},{12,8},{16,20},{20,16},{24,28},{28,24},{1,5},{5... | collective-permute-start | bytes 1769480 | tf_op jit(solution)/shard_map/ppermute | solution.py:385
  335.4 54.7 %collective-permute-start.21 = (bf16[4,512,1152]{2,1,0:T(8,128)(2,1)}, bf16[4,512,1152]{2,1,0:T(8,128)(2,1)}, u32[]{:S(2)}, u32[]{:S(2)}) collective-permute-start(bf16[4,512,1152]{2,1,0:T(8,128)(2,1)} %get-tuple-element.514.refs_2_), channel_id=1, source_target_pairs={{0,4},{4,0},{8,12},{12,8},{16,20},{20,16},{24,28},{28,24},{1,5},{5... | collective-permute-start | bytes 14155784 | tf_op jit(solution)/shard_map/ppermute | solution.py:385
  337.7 37.2 %all-to-all-start.6 = ((bf16[2,8,2,2,16,576]{5,4,2,3,0,1:T(8,128)(2,1)}), bf16[2,8,2,2,16,576]{5,4,2,3,0,1:T(8,128)(2,1)S(1)}, u32[]{:S(2)}, u32[]{:S(2)}) async-start(bf16[2,8,2,2,16,576]{5,4,2,3,0,1:T(8,128)(2,1)} %bitcast.254), calls=%async_computation.6 | async-start | bytes 2621440 | tf_op jit(solution)/shard_map/all_to_all | solution.py:1405
  342.8 46.1 %collective-permute-start.19 = (bf16[864,1152]{1,0:T(8,128)(2,1)}, bf16[864,1152]{1,0:T(8,128)(2,1)}, u32[]{:S(2)}, u32[]{:S(2)}) collective-permute-start(bf16[864,1152]{1,0:T(8,128)(2,1)} %get-tuple-element.969), channel_id=1, source_target_pairs={{0,1},{1,0},{2,3},{3,2},{4,5},{5,4},{6,7},{7,6},{8,9},{9,8},{10,11... | collective-permute-start | bytes 5971976 | tf_op jit(solution)/shard_map/ppermute | solution.py:385
  344.3 45.8 %collective-permute-start.20 = (bf16[864,1152]{1,0:T(8,128)(2,1)}, bf16[864,1152]{1,0:T(8,128)(2,1)}, u32[]{:S(2)}, u32[]{:S(2)}) collective-permute-start(bf16[864,1152]{1,0:T(8,128)(2,1)} %get-tuple-element.968), channel_id=1, source_target_pairs={{0,2},{1,3},{2,0},{3,1},{4,6},{5,7},{6,4},{7,5},{8,10},{9,11},{10,... | collective-permute-start | bytes 5971976 | tf_op jit(solution)/shard_map/ppermute | solution.py:385
  349.8 65.6 %collective-permute-start.24 = (bf16[4,576,1152]{2,1,0:T(8,128)(2,1)}, bf16[4,576,1152]{2,1,0:T(8,128)(2,1)}, u32[]{:S(2)}, u32[]{:S(2)}) collective-permute-start(bf16[4,576,1152]{2,1,0:T(8,128)(2,1)} %pack_blocks.10.refs_4_.refs_6_), channel_id=1, source_target_pairs={{0,4},{4,0},{8,12},{12,8},{16,20},{20,16},{24,28},{28,24},{1,5},{5... | collective-permute-start | bytes 15925256 | tf_op jit(solution)/shard_map/ppermute | solution.py:385
  397.3 49.2 %collective-permute-start.30 = (bf16[4,576,1152]{2,1,0:T(8,128)(2,1)S(1)}, bf16[4,576,1152]{2,1,0:T(8,128)(2,1)}, u32[]{:S(2)}, u32[]{:S(2)}) collective-permute-start(bf16[4,576,1152]{2,1,0:T(8,128)(2,1)S(1)} %pack_blocks.11.refs_4_.refs_5_), channel_id=1, source_target_pairs={{0,4},{4,0},{8,12},{12,8},{16,20},{20,16},{24,28},{28,24},{1,5},{5... | collective-permute-start | bytes 15925256 | tf_op jit(solution)/shard_map/ppermute | solution.py:385
  412.9 35.0 %collective-permute-start.31 = (bf16[4,576,1152]{2,1,0:T(8,128)(2,1)}, bf16[4,576,1152]{2,1,0:T(8,128)(2,1)}, u32[]{:S(2)}, u32[]{:S(2)}) collective-permute-start(bf16[4,576,1152]{2,1,0:T(8,128)(2,1)} %pack_blocks.9.refs_6_.refs_7_), channel_id=1, source_target_pairs={{0,4},{4,0},{8,12},{12,8},{16,20},{20,16},{24,28},{28,24},{1,5},{5... | collective-permute-start | bytes 15925256 | tf_op jit(solution)/shard_map/ppermute | solution.py:385
  444.4 33.3 %collective-permute-start.29 = (bf16[4,512,384]{2,1,0:T(8,128)(2,1)}, bf16[4,512,384]{2,1,0:T(8,128)(2,1)}, u32[]{:S(2)}, u32[]{:S(2)}) collective-permute-start(bf16[4,512,384]{2,1,0:T(8,128)(2,1)} %get-tuple-element.545.refs_6_), channel_id=1, source_target_pairs={{0,4},{4,0},{8,12},{12,8},{16,20},{20,16},{24,28},{28,24},{1,5},{5... | collective-permute-start | bytes 4718600 | tf_op jit(solution)/shard_map/ppermute | solution.py:385
  444.9 32.8 %collective-permute-start.28 = (bf16[576,512]{1,0:T(8,128)(2,1)}, bf16[576,512]{1,0:T(8,128)(2,1)}, u32[]{:S(2)}, u32[]{:S(2)}) collective-permute-start(bf16[576,512]{1,0:T(8,128)(2,1)} %get-tuple-element.544), channel_id=1, source_target_pairs={{0,4},{4,0},{8,12},{12,8},{16,20},{20,16},{24,28},{28,24},{1,5},{5... | collective-permute-start | bytes 1769480 | tf_op jit(solution)/shard_map/ppermute | solution.py:385
  445.0 32.6 %collective-permute-start.25 = (bf16[512,288]{1,0:T(8,128)(2,1)}, bf16[512,288]{1,0:T(8,128)(2,1)S(1)}, u32[]{:S(2)}, u32[]{:S(2)}) collective-permute-start(bf16[512,288]{1,0:T(8,128)(2,1)} %get-tuple-element.541), channel_id=1, source_target_pairs={{0,1},{1,0},{2,3},{3,2},{4,5},{5,4},{6,7},{7,6},{8,9},{9,8},{10,11... | collective-permute-start | bytes 884744 | tf_op jit(solution)/shard_map/ppermute | solution.py:385
  446.4 31.2 %collective-permute-start.26 = (bf16[512,288]{1,0:T(8,128)(2,1)}, bf16[512,288]{1,0:T(8,128)(2,1)S(1)}, u32[]{:S(2)}, u32[]{:S(2)}) collective-permute-start(bf16[512,288]{1,0:T(8,128)(2,1)} %get-tuple-element.542), channel_id=1, source_target_pairs={{0,2},{1,3},{2,0},{3,1},{4,6},{5,7},{6,4},{7,5},{8,10},{9,11},{10,... | collective-permute-start | bytes 884744 | tf_op jit(solution)/shard_map/ppermute | solution.py:385
  477.7 34.7 %collective-permute-start.33 = (bf16[4,512,1152]{2,1,0:T(8,128)(2,1)}, bf16[4,512,1152]{2,1,0:T(8,128)(2,1)}, u32[]{:S(2)}, u32[]{:S(2)}) collective-permute-start(bf16[4,512,1152]{2,1,0:T(8,128)(2,1)} %get-tuple-element.572.refs_2_), channel_id=1, source_target_pairs={{0,4},{4,0},{8,12},{12,8},{16,20},{20,16},{24,28},{28,24},{1,5},{5... | collective-permute-start | bytes 14155784 | tf_op jit(solution)/shard_map/ppermute | solution.py:385
  477.8 34.6 %collective-permute-start.32 = (bf16[576,512]{1,0:T(8,128)(2,1)}, bf16[576,512]{1,0:T(8,128)(2,1)S(1)}, u32[]{:S(2)}, u32[]{:S(2)}) collective-permute-start(bf16[576,512]{1,0:T(8,128)(2,1)} %get-tuple-element.571), channel_id=1, source_target_pairs={{0,4},{4,0},{8,12},{12,8},{16,20},{20,16},{24,28},{28,24},{1,5},{5... | collective-permute-start | bytes 1769480 | tf_op jit(solution)/shard_map/ppermute | solution.py:385
  528.4 47.3 %collective-permute-start.36 = (bf16[576,1152]{1,0:T(8,128)(2,1)}, bf16[576,1152]{1,0:T(8,128)(2,1)S(1)}, u32[]{:S(2)}, u32[]{:S(2)}) collective-permute-start(bf16[576,1152]{1,0:T(8,128)(2,1)} %get-tuple-element.606), channel_id=1, source_target_pairs={{0,1},{1,0},{2,3},{3,2},{4,5},{5,4},{6,7},{7,6},{8,9},{9,8},{10,11... | collective-permute-start | bytes 3981320 | tf_op jit(solution)/shard_map/ppermute | solution.py:385
  529.8 45.9 %collective-permute-start.37 = (bf16[576,1152]{1,0:T(8,128)(2,1)}, bf16[576,1152]{1,0:T(8,128)(2,1)S(1)}, u32[]{:S(2)}, u32[]{:S(2)}) collective-permute-start(bf16[576,1152]{1,0:T(8,128)(2,1)} %get-tuple-element.607), channel_id=1, source_target_pairs={{0,2},{1,3},{2,0},{3,1},{4,6},{5,7},{6,4},{7,5},{8,10},{9,11},{10,... | collective-permute-start | bytes 3981320 | tf_op jit(solution)/shard_map/ppermute | solution.py:385
  575.9 31.8 %collective-permute-start.40 = (bf16[576,1152]{1,0:T(8,128)(2,1)}, bf16[576,1152]{1,0:T(8,128)(2,1)S(1)}, u32[]{:S(2)}, u32[]{:S(2)}) collective-permute-start(bf16[576,1152]{1,0:T(8,128)(2,1)} %get-tuple-element.631), channel_id=1, source_target_pairs={{0,1},{1,0},{2,3},{3,2},{4,5},{5,4},{6,7},{7,6},{8,9},{9,8},{10,11... | collective-permute-start | bytes 3981320 | tf_op jit(solution)/shard_map/ppermute | solution.py:385
  576.5 31.4 %collective-permute-start.41 = (bf16[576,1152]{1,0:T(8,128)(2,1)}, bf16[576,1152]{1,0:T(8,128)(2,1)S(1)}, u32[]{:S(2)}, u32[]{:S(2)}) collective-permute-start(bf16[576,1152]{1,0:T(8,128)(2,1)} %get-tuple-element.632), channel_id=1, source_target_pairs={{0,2},{1,3},{2,0},{3,1},{4,6},{5,7},{6,4},{7,5},{8,10},{9,11},{10,... | collective-permute-start | bytes 3981320 | tf_op jit(solution)/shard_map/ppermute | solution.py:385
  609.2 37.0 %all-to-all-start.7 = ((bf16[2,1,2,16,16,576]{5,4,2,0,1,3:T(8,128)(2,1)}), bf16[2,1,2,16,16,576]{5,4,2,0,1,3:T(8,128)(2,1)}, u32[]{:S(2)}, u32[]{:S(2)}) async-start(bf16[2,1,2,16,16,576]{5,4,2,0,1,3:T(8,128)(2,1)} %copy.156), calls=%async_computation.7 | async-start | bytes 2621440 | tf_op jit(solution)/shard_map/all_to_all | solution.py:1455
  648.7 43.8 %all-to-all-start.8 = ((bf16[4,144,1152]{2,1,0:T(8,128)(2,1)}), bf16[4,144,1152]{2,1,0:T(8,128)(2,1)}, u32[]{:S(2)}, u32[]{:S(2)}) async-start(bf16[4,144,1152]{2,1,0:T(8,128)(2,1)} %bitcast.80), calls=%async_computation.8 | async-start | bytes 2654208 | tf_op jit(solution)/shard_map/all_to_all | solution.py:402
  653.0 38.6 %collective-permute-start.44 = (bf16[288,1152]{1,0:T(8,128)(2,1)}, bf16[288,1152]{1,0:T(8,128)(2,1)S(1)}, u32[]{:S(2)}, u32[]{:S(2)}) collective-permute-start(bf16[288,1152]{1,0:T(8,128)(2,1)} %add_convert_fusion.9), channel_id=1, source_target_pairs={{0,1},{1,0},{2,3},{3,2},{4,5},{5,4},{6,7},{7,6},{8,9},{9,8},{10,11... | collective-permute-start | bytes 1990664 | tf_op jit(solution)/shard_map/ppermute | solution.py:385
  654.5 37.1 %collective-permute-start.45 = (bf16[288,1152]{1,0:T(8,128)(2,1)}, bf16[288,1152]{1,0:T(8,128)(2,1)S(1)}, u32[]{:S(2)}, u32[]{:S(2)}) collective-permute-start(bf16[288,1152]{1,0:T(8,128)(2,1)} %add_convert_fusion.8), channel_id=1, source_target_pairs={{0,2},{1,3},{2,0},{3,1},{4,6},{5,7},{6,4},{7,5},{8,10},{9,11},{10,... | collective-permute-start | bytes 1990664 | tf_op jit(solution)/shard_map/ppermute | solution.py:385
  655.0 34.3 %collective-permute-start.46 = (bf16[512,288]{1,0:T(8,128)(2,1)}, bf16[512,288]{1,0:T(8,128)(2,1)S(1)}, u32[]{:S(2)}, u32[]{:S(2)}) collective-permute-start(bf16[512,288]{1,0:T(8,128)(2,1)} %copy-done.57), channel_id=1, source_target_pairs={{0,1},{1,0},{2,3},{3,2},{4,5},{5,4},{6,7},{7,6},{8,9},{9,8},{10,11... | collective-permute-start | bytes 884744 | tf_op jit(solution)/shard_map/ppermute | solution.py:385
  655.6 34.5 %collective-permute-start.47 = (bf16[512,288]{1,0:T(8,128)(2,1)}, bf16[512,288]{1,0:T(8,128)(2,1)S(1)}, u32[]{:S(2)}, u32[]{:S(2)}) collective-permute-start(bf16[512,288]{1,0:T(8,128)(2,1)} %copy-done.56), channel_id=1, source_target_pairs={{0,2},{1,3},{2,0},{3,1},{4,6},{5,7},{6,4},{7,5},{8,10},{9,11},{10,... | collective-permute-start | bytes 884744 | tf_op jit(solution)/shard_map/ppermute | solution.py:385
  657.1 33.7 %collective-permute-start.48 = (bf16[512,288]{1,0:T(8,128)(2,1)}, bf16[512,288]{1,0:T(8,128)(2,1)S(1)}, u32[]{:S(2)}, u32[]{:S(2)}) collective-permute-start(bf16[512,288]{1,0:T(8,128)(2,1)} %copy-done.55), channel_id=1, source_target_pairs={{0,3},{1,2},{2,1},{3,0},{4,7},{5,6},{6,5},{7,4},{8,11},{9,10},{10,... | collective-permute-start | bytes 884744 | tf_op jit(solution)/shard_map/ppermute | solution.py:385
  697.2 31.8 %collective-permute-start.51 = (bf16[576,1152]{1,0:T(8,128)(2,1)}, bf16[576,1152]{1,0:T(8,128)(2,1)S(1)}, u32[]{:S(2)}, u32[]{:S(2)}) collective-permute-start(bf16[576,1152]{1,0:T(8,128)(2,1)} %get-tuple-element.645), channel_id=1, source_target_pairs={{0,1},{1,0},{2,3},{3,2},{4,5},{5,4},{6,7},{7,6},{8,9},{9,8},{10,11... | collective-permute-start | bytes 3981320 | tf_op jit(solution)/shard_map/ppermute | solution.py:385
  697.8 31.5 %collective-permute-start.52 = (bf16[576,1152]{1,0:T(8,128)(2,1)}, bf16[576,1152]{1,0:T(8,128)(2,1)S(1)}, u32[]{:S(2)}, u32[]{:S(2)}) collective-permute-start(bf16[576,1152]{1,0:T(8,128)(2,1)} %get-tuple-element.646), channel_id=1, source_target_pairs={{0,2},{1,3},{2,0},{3,1},{4,6},{5,7},{6,4},{7,5},{8,10},{9,11},{10,... | collective-permute-start | bytes 3981320 | tf_op jit(solution)/shard_map/ppermute | solution.py:385
  699.4 69.5 %all-to-all-start.9 = ((bf16[4,144,1152]{2,1,0:T(8,128)(2,1)}), bf16[4,144,1152]{2,1,0:T(8,128)(2,1)}, u32[]{:S(2)}, u32[]{:S(2)}) async-start(bf16[4,144,1152]{2,1,0:T(8,128)(2,1)} %bitcast.82), calls=%async_computation.9 | async-start | bytes 2654208 | tf_op jit(solution)/shard_map/all_to_all | solution.py:402
  729.3 47.0 %collective-permute-start.53 = (bf16[576,1152]{1,0:T(8,128)(2,1)}, bf16[576,1152]{1,0:T(8,128)(2,1)}, u32[]{:S(2)}, u32[]{:S(2)}) collective-permute-start(bf16[576,1152]{1,0:T(8,128)(2,1)} %get-tuple-element.709), channel_id=1, source_target_pairs={{0,1},{1,0},{2,3},{3,2},{4,5},{5,4},{6,7},{7,6},{8,9},{9,8},{10,11... | collective-permute-start | bytes 3981320 | tf_op jit(solution)/shard_map/ppermute | solution.py:385
  730.7 45.5 %collective-permute-start.54 = (bf16[576,1152]{1,0:T(8,128)(2,1)}, bf16[576,1152]{1,0:T(8,128)(2,1)}, u32[]{:S(2)}, u32[]{:S(2)}) collective-permute-start(bf16[576,1152]{1,0:T(8,128)(2,1)} %get-tuple-element.710), channel_id=1, source_target_pairs={{0,2},{1,3},{2,0},{3,1},{4,6},{5,7},{6,4},{7,5},{8,10},{9,11},{10,... | collective-permute-start | bytes 3981320 | tf_op jit(solution)/shard_map/ppermute | solution.py:385
  734.2 40.1 %collective-permute-start.55 = (bf16[288,1152]{1,0:T(8,128)(2,1)}, bf16[288,1152]{1,0:T(8,128)(2,1)S(1)}, u32[]{:S(2)}, u32[]{:S(2)}) collective-permute-start(bf16[288,1152]{1,0:T(8,128)(2,1)} %add_convert_fusion.7), channel_id=1, source_target_pairs={{0,1},{1,0},{2,3},{3,2},{4,5},{5,4},{6,7},{7,6},{8,9},{9,8},{10,11... | collective-permute-start | bytes 1990664 | tf_op jit(solution)/shard_map/ppermute | solution.py:385
  734.9 40.6 %collective-permute-start.56 = (bf16[288,1152]{1,0:T(8,128)(2,1)}, bf16[288,1152]{1,0:T(8,128)(2,1)S(1)}, u32[]{:S(2)}, u32[]{:S(2)}) collective-permute-start(bf16[288,1152]{1,0:T(8,128)(2,1)} %add_convert_fusion.6), channel_id=1, source_target_pairs={{0,2},{1,3},{2,0},{3,1},{4,6},{5,7},{6,4},{7,5},{8,10},{9,11},{10,... | collective-permute-start | bytes 1990664 | tf_op jit(solution)/shard_map/ppermute | solution.py:385
  776.4 32.2 %collective-permute-start.61 = (bf16[576,1152]{1,0:T(8,128)(2,1)}, bf16[576,1152]{1,0:T(8,128)(2,1)S(1)}, u32[]{:S(2)}, u32[]{:S(2)}) collective-permute-start(bf16[576,1152]{1,0:T(8,128)(2,1)} %get-tuple-element.742), channel_id=1, source_target_pairs={{0,1},{1,0},{2,3},{3,2},{4,5},{5,4},{6,7},{7,6},{8,9},{9,8},{10,11... | collective-permute-start | bytes 3981320 | tf_op jit(solution)/shard_map/ppermute | solution.py:385
  777.1 32.2 %collective-permute-start.62 = (bf16[576,1152]{1,0:T(8,128)(2,1)}, bf16[576,1152]{1,0:T(8,128)(2,1)S(1)}, u32[]{:S(2)}, u32[]{:S(2)}) collective-permute-start(bf16[576,1152]{1,0:T(8,128)(2,1)} %get-tuple-element.743), channel_id=1, source_target_pairs={{0,2},{1,3},{2,0},{3,1},{4,6},{5,7},{6,4},{7,5},{8,10},{9,11},{10,... | collective-permute-start | bytes 3981320 | tf_op jit(solution)/shard_map/ppermute | solution.py:385
  784.4 47.0 %all-to-all-start.10 = ((bf16[4,144,1152]{2,1,0:T(8,128)(2,1)}), bf16[4,144,1152]{2,1,0:T(8,128)(2,1)}, u32[]{:S(2)}, u32[]{:S(2)}) async-start(bf16[4,144,1152]{2,1,0:T(8,128)(2,1)} %bitcast.84), calls=%async_computation.10 | async-start | bytes 2654208 | tf_op jit(solution)/shard_map/all_to_all | solution.py:402
  789.6 32.8 %collective-permute-start.59 = (bf16[288,1152]{1,0:T(8,128)(2,1)}, bf16[288,1152]{1,0:T(8,128)(2,1)S(1)}, u32[]{:S(2)}, u32[]{:S(2)}) collective-permute-start(bf16[288,1152]{1,0:T(8,128)(2,1)} %get-tuple-element.738), channel_id=1, source_target_pairs={{0,1},{1,0},{2,3},{3,2},{4,5},{5,4},{6,7},{7,6},{8,9},{9,8},{10,11... | collective-permute-start | bytes 1990664 | tf_op jit(solution)/shard_map/ppermute | solution.py:385
  791.0 31.8 %collective-permute-start.60 = (bf16[288,1152]{1,0:T(8,128)(2,1)}, bf16[288,1152]{1,0:T(8,128)(2,1)}, u32[]{:S(2)}, u32[]{:S(2)}) collective-permute-start(bf16[288,1152]{1,0:T(8,128)(2,1)} %get-tuple-element.739), channel_id=1, source_target_pairs={{0,2},{1,3},{2,0},{3,1},{4,6},{5,7},{6,4},{7,5},{8,10},{9,11},{10,... | collective-permute-start | bytes 1990664 | tf_op jit(solution)/shard_map/ppermute | solution.py:385
  822.9 42.1 %collective-permute-start.63 = (bf16[576,1152]{1,0:T(8,128)(2,1)}, bf16[576,1152]{1,0:T(8,128)(2,1)}, u32[]{:S(2)}, u32[]{:S(2)}) collective-permute-start(bf16[576,1152]{1,0:T(8,128)(2,1)} %get-tuple-element.752), channel_id=1, source_target_pairs={{0,1},{1,0},{2,3},{3,2},{4,5},{5,4},{6,7},{7,6},{8,9},{9,8},{10,11... | collective-permute-start | bytes 3981320 | tf_op jit(solution)/shard_map/ppermute | solution.py:385
  824.2 40.8 %collective-permute-start.64 = (bf16[576,1152]{1,0:T(8,128)(2,1)}, bf16[576,1152]{1,0:T(8,128)(2,1)}, u32[]{:S(2)}, u32[]{:S(2)}) collective-permute-start(bf16[576,1152]{1,0:T(8,128)(2,1)} %get-tuple-element.753), channel_id=1, source_target_pairs={{0,2},{1,3},{2,0},{3,1},{4,6},{5,7},{6,4},{7,5},{8,10},{9,11},{10,... | collective-permute-start | bytes 3981320 | tf_op jit(solution)/shard_map/ppermute | solution.py:385
  831.4 42.8 %all-to-all-start.11 = ((bf16[4,144,1152]{2,1,0:T(8,128)(2,1)}), bf16[4,144,1152]{2,1,0:T(8,128)(2,1)}, u32[]{:S(2)}, u32[]{:S(2)}) async-start(bf16[4,144,1152]{2,1,0:T(8,128)(2,1)} %bitcast.102), calls=%async_computation.11 | async-start | bytes 2654208 | tf_op jit(solution)/shard_map/all_to_all | solution.py:402
  836.5 31.2 %collective-permute-start.65 = (bf16[288,1152]{1,0:T(8,128)(2,1)}, bf16[288,1152]{1,0:T(8,128)(2,1)S(1)}, u32[]{:S(2)}, u32[]{:S(2)}) collective-permute-start(bf16[288,1152]{1,0:T(8,128)(2,1)} %add_convert_fusion.3), channel_id=1, source_target_pairs={{0,1},{1,0},{2,3},{3,2},{4,5},{5,4},{6,7},{7,6},{8,9},{9,8},{10,11... | collective-permute-start | bytes 1990664 | tf_op jit(solution)/shard_map/ppermute | solution.py:385
  837.2 31.7 %collective-permute-start.66 = (bf16[288,1152]{1,0:T(8,128)(2,1)}, bf16[288,1152]{1,0:T(8,128)(2,1)}, u32[]{:S(2)}, u32[]{:S(2)}) collective-permute-start(bf16[288,1152]{1,0:T(8,128)(2,1)} %add_convert_fusion.2), channel_id=1, source_target_pairs={{0,2},{1,3},{2,0},{3,1},{4,6},{5,7},{6,4},{7,5},{8,10},{9,11},{10,... | collective-permute-start | bytes 1990664 | tf_op jit(solution)/shard_map/ppermute | solution.py:385
  874.2 45.0 %all-to-all-start.12 = ((bf16[4,144,1152]{2,1,0:T(8,128)(2,1)}), bf16[4,144,1152]{2,1,0:T(8,128)(2,1)S(1)}, u32[]{:S(2)}, u32[]{:S(2)}) async-start(bf16[4,144,1152]{2,1,0:T(8,128)(2,1)} %bitcast.104), calls=%async_computation.12 | async-start | bytes 2654208 | tf_op jit(solution)/shard_map/all_to_all | solution.py:402
  923.6 45.1 %all-to-all-start.13 = ((bf16[4,144,1152]{2,1,0:T(8,128)(2,1)}), bf16[4,144,1152]{2,1,0:T(8,128)(2,1)}, u32[]{:S(2)}, u32[]{:S(2)}) async-start(bf16[4,144,1152]{2,1,0:T(8,128)(2,1)} %bitcast.121), calls=%async_computation.13 | async-start | bytes 2654208 | tf_op jit(solution)/shard_map/all_to_all | solution.py:402
  936.1 31.2 %collective-permute-start.79 = (f32[4,144]{1,0:T(4,128)}, f32[4,144]{1,0:T(4,128)}, u32[]{:S(2)}, u32[]{:S(2)}) collective-permute-start(f32[4,144]{1,0:T(4,128)} %add.146), channel_id=1, source_target_pairs={{0,2},{1,3},{2,0},{3,1},{4,6},{5,7},{6,4},{7,5},{8,10},{9,11},{10,... | collective-permute-start | bytes 6920 | tf_op jit(solution)/shard_map/ppermute | solution.py:385
  (136 other events, 1001.4 us)
Sparse Core Ops, SparseCore 0:
  65.1 76.0 all-gather.3

commit v5 on v4

--- a/solution.py
+++ b/solution.py
@@ -533,6 +533,7 @@
 SUMMED = ((0,), (0,))
 VMEM_BYTES = 58 * 1024 * 1024
 LANES = 128
+LOG2_E = 1.4426950408889634
 IN_HBM = pl.BlockSpec(memory_space=pl.ANY)
 SMALL_COST = pl.CostEstimate(flops=0, bytes_accessed=0, transcendentals=0)
 
@@ -609,6 +610,7 @@
     width = columns // 4
     count = width // HEAD_DIM
     scale = HEAD_DIM ** (-0.5)
+    binary = scale * LOG2_E
 
     @pl.when(step == 0)
     def _():
@@ -634,15 +636,15 @@
             query = block[:, start : start + HEAD_DIM]
             key = block[:, width + start : width + start + HEAD_DIM]
             value = block[:, 2 * width + start : 2 * width + start + HEAD_DIM]
-            scores = dot(query, key, TURNED) * scale
+            scores = dot(query, key, TURNED) * binary
             if period:
                 scores = jnp.where(same_place(size, period), scores, -1e30)
             largest = jnp.max(scores, 1, keepdims=True)
-            weight = jnp.exp(scores - largest)
+            weight = jnp.exp2(scores - largest)
             total = jnp.sum(weight, 1, keepdims=True)
             probs = (weight * (1.0 / total)).astype(jnp.bfloat16)
             outs.append(dot(probs, value, PLAIN))
-            logs = jnp.where(log_lane == head, largest + jnp.log(total), logs)
+            logs = jnp.where(log_lane == head, largest + jnp.log(total) * LOG2_E, logs)
         heads_ref[0, group * size : (group + 1) * size, :] = jnp.concatenate(outs, 1).astype(
             jnp.bfloat16
         )
@@ -870,6 +872,7 @@
     padded = columns - (3 * width) // LANES * LANES
     count = width // HEAD_DIM
     scale = HEAD_DIM ** (-0.5)
+    binary = scale * LOG2_E
 
     @pl.when(step == 0)
     def _():
@@ -900,10 +903,10 @@
             value = block[:, 2 * width + start : 2 * width + start + HEAD_DIM]
             start = padded - width + head * HEAD_DIM
             grad_out = grad_heads[rows, start : start + HEAD_DIM]
-            scores = dot(query, key, TURNED) * scale - logs[:, head : head + 1]
+            scores = dot(query, key, TURNED) * binary - logs[:, head : head + 1]
             if period:
                 scores = jnp.where(same_place(size, period), scores, -1e30)
-            probs = jnp.exp(scores)
+            probs = jnp.exp2(scores)
             grad_probs = dot(grad_out, value, TURNED)
             delta = jnp.sum(probs * grad_probs, 1, keepdims=True)
             grad_scores = (probs * (grad_probs - delta)).astype(jnp.bfloat16)

time: 990 us -> 989 us (level)
  no operation moved by 1% of the time
where the time goes in v5:
time: 989 us; the launch traced here: 980 us
  Pallas kernels  359 us (36%)
  waiting for transfers between devices  233 us (24%)
  local copies, waits for them, and re-layouts  185 us (19%)
  starting transfers between devices  135 us (14%)
  other arithmetic  49.8 us (5%)
  between operations  16.2 us (2%)
    ppermute x80, waiting for transfers between devices, exchange(): lax.ppermute(values, axis, [(index, index ^ mask) for index in range(coun...  169 us
    ppermute x80, starting transfers between devices, exchange(): lax.ppermute(values, axis, [(index, index ^ mask) for index in range(coun...  68.7 us
    pallas_call x2, Pallas kernels, attention_backward(): pl.pallas_call(functools.partial(attention_back_kernel, size, period, ste...  67.7 us
    pallas_call x6, Pallas kernels, weight_grads(): pl.pallas_call(functools.partial(weight_kernel, len(pairs), overlap, step...  67.6 us
    pallas_call x2, Pallas kernels, mlp_forward(): pl.pallas_call(functools.partial(mlp_kernel, steps), grid=(steps,), in_sp...  56.7 us
    all_to_all x12, starting transfers between devices, over_depth(): lax.all_to_all(values, 'row', split_axis=0, concat_axis=0, tiled=True, ax...  56.4 us
    pallas_call x2, Pallas kernels, mlp_backward(): pl.pallas_call(functools.partial(mlp_back_kernel, steps), grid=(steps,),...  55.6 us
    pallas_call x2, Pallas kernels, attention_forward(): pl.pallas_call(functools.partial(attention_kernel, size, period, steps),...  54.8 us
  transfers between devices with their start and end apart: 95, of which 42 were waited for; matrix products, arithmetic and copies ran while one was open for 16% of the time, Pallas kernels for 36%

profile of v5, /device:TPU:0, one launch (start us, length us, event | category | flops | bytes accessed | tf_op | source)
XLA Modules:
  0.0 980.4 jit_solution(6898914990025616863)
XLA Ops:
  7.2 4.7 slice_reduce_fusion.4
  14.8 6.4 all-to-all-start
  30.7 7.8 slice_reduce_fusion.2
  52.9 5.2 reshape.399
  65.0 3.8 all-to-all-start.1
  71.9 9.0 slice_reduce_fusion
  92.1 4.7 reorder.6.refs_0_.refs_1_
  112.6 3.9 all-to-all-start.2
  116.6 24.6 %all-gather.4.cloned.1.call-done = f32[32,4,5472]{2,1,0:T(4,128)} async-done(((f32[1,4,5472]{2,1,0:T(4,128)}), f32[32,4,5472]{2,1,0:T(4,128)}) %all-gather.4.cloned.1.call-update) | async-done | bytes 2801680 | tf_op jit(solution)/shard_map/all_gather | solution.py:1284
  145.4 13.9 %collective-permute-done.5.lower.across = bf16[864,1152]{1,0:T(8,128)(2,1)} collective-permute-done((bf16[864,1152]{1,0:T(8,128)(2,1)}, bf16[864,1152]{1,0:T(8,128)(2,1)}, u32[]{:S(2)}, u32[]{:S(2)}) %collective-permute-start.5) | collective-permute-done | bytes 1990688 | tf_op jit(solution)/shard_map/ppermute | solution.py:385
  165.3 4.0 pack_blocks.6.refs_4_.refs_6_
  169.4 3.6 all-to-all-start.3
  178.5 27.3 %attention_forward.2 = (f32[2,512,576]{2,1,0:T(8,128)}, bf16[512,576]{1,0:T(8,128)(2,1)}, bf16[576,512]{1,0:T(8,128)(2,1)}, bf16[4,512,896]{2,1,0:T(8,128)(2,1)}...) custom-call(f32[2,512,576]{2,1,0:T(8,128)} %copy-done.1, ...), custom_call_target="tpu_custom_call" | custom-call | tf_op jit(solution)/shard_map/attention_forward/pallas_call | solution.py:670
  205.8 13.2 %collective-permute-done.8.lower.across = bf16[864,1152]{1,0:T(8,128)(2,1)} collective-permute-done((bf16[864,1152]{1,0:T(8,128)(2,1)}, bf16[864,1152]{1,0:T(8,128)(2,1)}, u32[]{:S(2)}, u32[]{:S(2)}) %collective-permute-start.8) | collective-permute-done | bytes 1990688 | tf_op jit(solution)/shard_map/ppermute | solution.py:385
  226.8 4.7 all-to-all-start.4
  231.5 3.9 pack_blocks.7.refs_4_.refs_5_
  235.5 4.3 reshape.412
  242.5 26.4 %collective-permute-done.10.lower.across = bf16[864,1152]{1,0:T(8,128)(2,1)} collective-permute-done((bf16[864,1152]{1,0:T(8,128)(2,1)}, bf16[864,1152]{1,0:T(8,128)(2,1)}, u32[]{:S(2)}, u32[]{:S(2)}) %collective-permute-start.10) | collective-permute-done | bytes 1990688 | tf_op jit(solution)/shard_map/ppermute | solution.py:385
  272.3 3.6 pad_maximum_fusion.6
  275.9 3.9 pack_blocks.8.refs_6_.refs_7_
  280.0 4.6 all-to-all-start.5
  289.2 28.2 %mlp_forward.2 = (f32[2,512,576]{2,1,0:T(8,128)}, bf16[512,576]{1,0:T(8,128)(2,1)}, bf16[576,512]{1,0:T(8,128)(2,1)}, bf16[4,512,1152]{2,1,0:T(8,128)(2,1)}, bf1...) custom-call(f32[2,512,576]{2,1,0:T(8,128)} %get-tuple-element.480.refs_0_.refs_1_, ...), custom_call_target="tpu_custom_call" | custom-call | tf_op jit(solution)/shard_map/mlp_forward/pallas_call | solution.py:751
  317.4 13.1 %collective-permute-done.15.lower.across = bf16[864,1152]{1,0:T(8,128)(2,1)} collective-permute-done((bf16[864,1152]{1,0:T(8,128)(2,1)}, bf16[864,1152]{1,0:T(8,128)(2,1)}, u32[]{:S(2)}, u32[]{:S(2)}) %collective-permute-start.15) | collective-permute-done | bytes 1990688 | tf_op jit(solution)/shard_map/ppermute | solution.py:385
  337.7 5.1 all-to-all-start.6
  345.8 4.0 pack_blocks.10.refs_4_.refs_6_
  350.4 24.6 %all-to-all-done.6 = bf16[2,8,2,2,16,576]{5,4,2,3,0,1:T(8,128)(2,1)S(1)} async-done(((bf16[2,8,2,2,16,576]{5,4,2,3,0,1:T(8,128)(2,1)}), bf16[2,8,2,2,16,576]{5,4,2,3,0,1:T(8,128)(2,1)S(1)}, u32[]{:S(2)}, u32[]{:S(2)}) %all-to-all-start.6) | async-done | bytes 1179680 | tf_op jit(solution)/shard_map/all_to_all | solution.py:1408
  375.1 13.8 %collective-permute-done.19.across.lower = bf16[864,1152]{1,0:T(8,128)(2,1)} collective-permute-done((bf16[864,1152]{1,0:T(8,128)(2,1)}, bf16[864,1152]{1,0:T(8,128)(2,1)}, u32[]{:S(2)}, u32[]{:S(2)}) %collective-permute-start.19) | collective-permute-done | bytes 1990688 | tf_op jit(solution)/shard_map/ppermute | solution.py:385
  397.3 11.3 %collective-permute-done.22.lower = bf16[288,1152]{1,0:T(8,128)(2,1)S(1)} collective-permute-done((bf16[288,1152]{1,0:T(8,128)(2,1)S(1)}, bf16[288,1152]{1,0:T(8,128)(2,1)S(1)}, u32[]{:S(2)}, u32[]{:S(2)}) %collective-permute-start.22) | collective-permute-done | bytes 663584 | tf_op jit(solution)/shard_map/ppermute | solution.py:385
  409.0 3.9 pack_blocks.9.refs_6_.refs_7_
  415.4 27.4 %attention_forward.3 = (f32[2,512,576]{2,1,0:T(8,128)}, bf16[512,576]{1,0:T(8,128)(2,1)}, bf16[576,512]{1,0:T(8,128)(2,1)}, bf16[4,512,896]{2,1,0:T(8,128)(2,1)}...) custom-call(f32[2,512,576]{2,1,0:T(8,128)} %fusion.2.refs_0_.refs_1_, ...), custom_call_target="tpu_custom_call" | custom-call | tf_op jit(solution)/shard_map/attention_forward/pallas_call | solution.py:670
  447.6 28.5 %mlp_forward.3 = (f32[2,512,576]{2,1,0:T(8,128)}, bf16[512,576]{1,0:T(8,128)(2,1)}, bf16[576,512]{1,0:T(8,128)(2,1)}, bf16[4,512,1152]{2,1,0:T(8,128)(2,1)}, bf1...) custom-call(f32[2,512,576]{2,1,0:T(8,128)} %get-tuple-element.539.refs_0_.refs_1_, ...), custom_call_target="tpu_custom_call" | custom-call | tf_op jit(solution)/shard_map/mlp_forward/pallas_call | solution.py:751
  476.8 4.7 reorder.7.refs_0_
  482.9 27.9 %mlp_backward.2 = (f32[2,512,576]{2,1,0:T(8,128)}, bf16[512,576]{1,0:T(8,128)(2,1)}, bf16[576,512]{1,0:T(8,128)(2,1)}, bf16[4,512,1152]{2,1,0:T(8,128)(2,1)}, f3...) custom-call(f32[2,512,576]{2,1,0:T(8,128)} %copy-done.6, f32[2,512,576]{2,1,0:T(8,128)} %get-tuple-element.539.refs_0_.refs_1_, ...), custom_call_target="tpu_custom_call" | custom-call | tf_op jit(solution)/shard_map/mlp_backward/pallas_call | solution.py:825
  514.1 10.6 %weight_grads.6 = (bf16[576,1152]{1,0:T(8,128)(2,1)}, bf16[288,1152]{1,0:T(8,128)(2,1)}, bf16[576,1152]{1,0:T(8,128)(2,1)}, bf16[576,1152]{1,0:T(8,128)(2,1)}, bf16[288,1152]{1,0:T(8,128)(2,1)}) custom-call(bf16[512,576]{1,0:T(8,128)(2,1)} %get-tuple-element.580.refs_0_, bf16[576,512]{1,0:T(8,128)(2,1)} %copy-done.83, ...), custom_call_target="tpu_custom_call" | custom-call | tf_op jit(solution)/shard_map/weight_grads/pallas_call | solution.py:1044
  529.9 10.7 %weight_grads.7 = (bf16[576,1152]{1,0:T(8,128)(2,1)}, bf16[288,1152]{1,0:T(8,128)(2,1)}, bf16[576,1152]{1,0:T(8,128)(2,1)}, bf16[576,1152]{1,0:T(8,128)(2,1)}, bf16[288,1152]{1,0:T(8,128)(2,1)}) custom-call(bf16[512,576]{1,0:T(8,128)(2,1)} %get-tuple-element.575.refs_0_, bf16[576,512]{1,0:T(8,128)(2,1)} %copy-done.81, ...), custom_call_target="tpu_custom_call" | custom-call | tf_op jit(solution)/shard_map/weight_grads/pallas_call | solution.py:1044
  540.6 33.9 %attention_backward.2 = (f32[2,512,576]{2,1,0:T(8,128)}, bf16[512,576]{1,0:T(8,128)(2,1)}, bf16[576,512]{1,0:T(8,128)(2,1)}, bf16[4,512,896]{2,1,0:T(8,128)(2,1)...) custom-call(f32[2,512,576]{2,1,0:T(8,128)} %get-tuple-element.596.refs_0_, f32[2,512,576]{2,1,0:T(8,128)} %fusion.2.refs_0_.refs_1_, ...), custom_call_target="tpu_custom_call" | custom-call | tf_op jit(solution)/shard_map/attention_backward/pallas_call | solution.py:936
  581.9 12.4 %weight_grads.8 = (bf16[576,1152]{1,0:T(8,128)(2,1)}, bf16[288,1152]{1,0:T(8,128)(2,1)}, bf16[576,1152]{1,0:T(8,128)(2,1)}, bf16[576,1152]{1,0:T(8,128)(2,1)}, bf16[288,1152]{1,0:T(8,128)(2,1)}) custom-call(bf16[512,576]{1,0:T(8,128)(2,1)} %get-tuple-element.535.refs_0_, bf16[576,512]{1,0:T(8,128)(2,1)} %collective-permute-done.28.refs_1_, ...), custom_call_target="tpu_custom_call" | custom-call | tf_op jit(solution)/shard_map/weight_grads/pallas_call | solution.py:1044
  594.4 12.0 %collective-permute-done.40.across_first = bf16[576,1152]{1,0:T(8,128)(2,1)S(1)} collective-permute-done((bf16[576,1152]{1,0:T(8,128)(2,1)}, bf16[576,1152]{1,0:T(8,128)(2,1)S(1)}, u32[]{:S(2)}, u32[]{:S(2)}) %collective-permute-start.40) | collective-permute-done | bytes 1327136 | tf_op jit(solution)/shard_map/ppermute | solution.py:385
  607.9 4.7 all-to-all-start.7
  617.4 4.4 reorder.8
  624.4 5.9 collective-permute-done.42.across_upper
  633.0 11.9 %all-to-all-done.7 = bf16[2,1,2,16,16,576]{5,4,2,0,1,3:T(8,128)(2,1)} async-done(((bf16[2,1,2,16,16,576]{5,4,2,0,1,3:T(8,128)(2,1)}), bf16[2,1,2,16,16,576]{5,4,2,0,1,3:T(8,128)(2,1)}, u32[]{:S(2)}, u32[]{:S(2)}) %all-to-all-start.7) | async-done | bytes 1179680 | tf_op jit(solution)/shard_map/all_to_all | solution.py:1458
  647.4 4.3 all-to-all-start.8
  660.3 27.7 %mlp_backward.3 = (f32[2,512,576]{2,1,0:T(8,128)}, bf16[512,576]{1,0:T(8,128)(2,1)}, bf16[576,512]{1,0:T(8,128)(2,1)}, bf16[4,512,1152]{2,1,0:T(8,128)(2,1)}, f3...) custom-call(f32[2,512,576]{2,1,0:T(8,128)} %fusion.3.refs_0_, f32[2,512,576]{2,1,0:T(8,128)} %get-tuple-element.480.refs_0_.refs_1_, ...), custom_call_target="tpu_custom_call" | custom-call | tf_op jit(solution)/shard_map/mlp_backward/pallas_call | solution.py:825
  698.1 5.5 all-to-all-start.9
  703.5 10.6 %weight_grads.9 = (bf16[576,1152]{1,0:T(8,128)(2,1)}, bf16[288,1152]{1,0:T(8,128)(2,1)}, bf16[576,1152]{1,0:T(8,128)(2,1)}, bf16[576,1152]{1,0:T(8,128)(2,1)}, bf16[288,1152]{1,0:T(8,128)(2,1)}) custom-call(bf16[512,576]{1,0:T(8,128)(2,1)} %get-tuple-element.680.refs_0_, bf16[576,512]{1,0:T(8,128)(2,1)} %copy-done.82, ...), custom_call_target="tpu_custom_call" | custom-call | tf_op jit(solution)/shard_map/weight_grads/pallas_call | solution.py:1044
  714.2 10.7 %weight_grads.10 = (bf16[576,1152]{1,0:T(8,128)(2,1)}, bf16[288,1152]{1,0:T(8,128)(2,1)}, bf16[576,1152]{1,0:T(8,128)(2,1)}, bf16[576,1152]{1,0:T(8,128)(2,1)}, bf16[288,1152]{1,0:T(8,128)(2,1)}) custom-call(bf16[512,576]{1,0:T(8,128)(2,1)} %get-tuple-element.501.refs_0_, bf16[576,512]{1,0:T(8,128)(2,1)} %copy-done.80, ...), custom_call_target="tpu_custom_call" | custom-call | tf_op jit(solution)/shard_map/weight_grads/pallas_call | solution.py:1044
  734.1 33.9 %attention_backward.3 = (f32[2,512,576]{2,1,0:T(8,128)}, bf16[512,576]{1,0:T(8,128)(2,1)}, bf16[576,512]{1,0:T(8,128)(2,1)}, bf16[4,512,896]{2,1,0:T(8,128)(2,1)...) custom-call(f32[2,512,576]{2,1,0:T(8,128)} %get-tuple-element.699.refs_0_, f32[2,512,576]{2,1,0:T(8,128)} %copy-done.1, ...), custom_call_target="tpu_custom_call" | custom-call | tf_op jit(solution)/shard_map/attention_backward/pallas_call | solution.py:936
  768.0 5.1 collective-permute-done.55.across_upper
  783.1 5.1 all-to-all-start.10
  791.9 12.5 %weight_grads.11 = (bf16[576,1152]{1,0:T(8,128)(2,1)}, bf16[288,1152]{1,0:T(8,128)(2,1)}, bf16[576,1152]{1,0:T(8,128)(2,1)}, bf16[576,1152]{1,0:T(8,128)(2,1)}, bf16[288,1152]{1,0:T(8,128)(2,1)}) custom-call(bf16[512,576]{1,0:T(8,128)(2,1)} %get-tuple-element.462.refs_0_, bf16[576,512]{1,0:T(8,128)(2,1)} %collective-permute-done.12.refs_1_, ...), custom_call_target="tpu_custom_call" | custom-call | tf_op jit(solution)/shard_map/weight_grads/pallas_call | solution.py:1044
  808.0 13.1 %collective-permute-done.59.across_upper = bf16[288,1152]{1,0:T(8,128)(2,1)S(1)} collective-permute-done((bf16[288,1152]{1,0:T(8,128)(2,1)}, bf16[288,1152]{1,0:T(8,128)(2,1)S(1)}, u32[]{:S(2)}, u32[]{:S(2)}) %collective-permute-start.59) | collective-permute-done | bytes 663584 | tf_op jit(solution)/shard_map/ppermute | solution.py:385
  824.5 3.4 add_blocks.9
  830.1 5.1 all-to-all-start.11
  853.6 4.0 reshape_reshape.30
  859.3 4.4 reorder.9
  872.9 5.0 all-to-all-start.12
  885.5 3.4 convert_reduce_fusion.2
  892.5 6.8 collective-permute-done.74.across_upper
  912.0 3.7 collective-permute-done.77
  922.3 4.4 all-to-all-start.13
  940.2 4.9 reshape.465
  948.3 5.9 reshape.462
  957.9 5.5 reshape_reshape.32
  (603 shorter events, 296.4 us)
Async XLA Ops:
  14.8 38.1 %all-to-all-start = ((bf16[4,144,1152]{2,1,0:T(8,128)(2,1)}), bf16[4,144,1152]{2,1,0:T(8,128)(2,1)S(1)}, u32[]{:S(2)}, u32[]{:S(2)}) async-start(bf16[4,144,1152]{2,1,0:T(8,128)(2,1)} %bitcast.13), calls=%async_computation | async-start | bytes 2654208 | tf_op jit(solution)/shard_map/all_to_all | solution.py:402
  21.2 120.0 %all-gather.4.cloned.1.call-start = ((), (), s32[]{:S(2)}) async-start(), calls=%async_computation.14 | async-start | bytes 2906112 | tf_op jit(solution)/shard_map/all_gather | solution.py:1284
  65.0 36.8 %all-to-all-start.1 = ((bf16[4,144,1152]{2,1,0:T(8,128)(2,1)}), bf16[4,144,1152]{2,1,0:T(8,128)(2,1)S(1)}, u32[]{:S(2)}, u32[]{:S(2)}) async-start(bf16[4,144,1152]{2,1,0:T(8,128)(2,1)} %tile.59), calls=%async_computation.1 | async-start | bytes 2654208 | tf_op jit(solution)/shard_map/all_to_all | solution.py:402
  68.8 30.9 %collective-permute-start.3 = (bf16[576,1152]{1,0:T(8,128)(2,1)S(1)}, bf16[576,1152]{1,0:T(8,128)(2,1)}, u32[]{:S(2)}, u32[]{:S(2)}) collective-permute-start(bf16[576,1152]{1,0:T(8,128)(2,1)S(1)} %bitcast.240), channel_id=1, source_target_pairs={{0,1},{1,0},{2,3},{3,2},{4,5},{5,4},{6,7},{7,6},{8,9},{9,8},{10,11... | collective-permute-start | bytes 3981320 | tf_op jit(solution)/shard_map/ppermute | solution.py:385
  70.3 30.6 %collective-permute-start.4 = (bf16[576,1152]{1,0:T(8,128)(2,1)S(1)}, bf16[576,1152]{1,0:T(8,128)(2,1)}, u32[]{:S(2)}, u32[]{:S(2)}) collective-permute-start(bf16[576,1152]{1,0:T(8,128)(2,1)S(1)} %bitcast.241), channel_id=1, source_target_pairs={{0,2},{1,3},{2,0},{3,1},{4,6},{5,7},{6,4},{7,5},{8,10},{9,11},{10,... | collective-permute-start | bytes 3981320 | tf_op jit(solution)/shard_map/ppermute | solution.py:385
  109.6 49.7 %collective-permute-start.5 = (bf16[864,1152]{1,0:T(8,128)(2,1)}, bf16[864,1152]{1,0:T(8,128)(2,1)}, u32[]{:S(2)}, u32[]{:S(2)}) collective-permute-start(bf16[864,1152]{1,0:T(8,128)(2,1)} %get-tuple-element.977), channel_id=1, source_target_pairs={{0,1},{1,0},{2,3},{3,2},{4,5},{5,4},{6,7},{7,6},{8,9},{9,8},{10,11... | collective-permute-start | bytes 5971976 | tf_op jit(solution)/shard_map/ppermute | solution.py:385
  111.1 49.3 %collective-permute-start.6 = (bf16[864,1152]{1,0:T(8,128)(2,1)}, bf16[864,1152]{1,0:T(8,128)(2,1)}, u32[]{:S(2)}, u32[]{:S(2)}) collective-permute-start(bf16[864,1152]{1,0:T(8,128)(2,1)} %get-tuple-element.976), channel_id=1, source_target_pairs={{0,2},{1,3},{2,0},{3,1},{4,6},{5,7},{6,4},{7,5},{8,10},{9,11},{10,... | collective-permute-start | bytes 5971976 | tf_op jit(solution)/shard_map/ppermute | solution.py:385
  112.6 47.8 %all-to-all-start.2 = ((bf16[4,144,1152]{2,1,0:T(8,128)(2,1)}), bf16[4,144,1152]{2,1,0:T(8,128)(2,1)S(1)}, u32[]{:S(2)}, u32[]{:S(2)}) async-start(bf16[4,144,1152]{2,1,0:T(8,128)(2,1)} %tile.66), calls=%async_computation.2 | async-start | bytes 2654208 | tf_op jit(solution)/shard_map/all_to_all | solution.py:402
  169.4 36.4 %all-to-all-start.3 = ((bf16[4,144,1152]{2,1,0:T(8,128)(2,1)}), bf16[4,144,1152]{2,1,0:T(8,128)(2,1)S(1)}, u32[]{:S(2)}, u32[]{:S(2)}) async-start(bf16[4,144,1152]{2,1,0:T(8,128)(2,1)} %tile.64), calls=%async_computation.3 | async-start | bytes 2654208 | tf_op jit(solution)/shard_map/all_to_all | solution.py:402
  172.9 46.1 %collective-permute-start.8 = (bf16[864,1152]{1,0:T(8,128)(2,1)}, bf16[864,1152]{1,0:T(8,128)(2,1)}, u32[]{:S(2)}, u32[]{:S(2)}) collective-permute-start(bf16[864,1152]{1,0:T(8,128)(2,1)} %get-tuple-element.975), channel_id=1, source_target_pairs={{0,1},{1,0},{2,3},{3,2},{4,5},{5,4},{6,7},{7,6},{8,9},{9,8},{10,11... | collective-permute-start | bytes 5971976 | tf_op jit(solution)/shard_map/ppermute | solution.py:385
  173.5 45.8 %collective-permute-start.9 = (bf16[864,1152]{1,0:T(8,128)(2,1)}, bf16[864,1152]{1,0:T(8,128)(2,1)}, u32[]{:S(2)}, u32[]{:S(2)}) collective-permute-start(bf16[864,1152]{1,0:T(8,128)(2,1)} %get-tuple-element.974), channel_id=1, source_target_pairs={{0,2},{1,3},{2,0},{3,1},{4,6},{5,7},{6,4},{7,5},{8,10},{9,11},{10,... | collective-permute-start | bytes 5971976 | tf_op jit(solution)/shard_map/ppermute | solution.py:385
  223.8 45.0 %collective-permute-start.10 = (bf16[864,1152]{1,0:T(8,128)(2,1)}, bf16[864,1152]{1,0:T(8,128)(2,1)}, u32[]{:S(2)}, u32[]{:S(2)}) collective-permute-start(bf16[864,1152]{1,0:T(8,128)(2,1)} %get-tuple-element.973), channel_id=1, source_target_pairs={{0,1},{1,0},{2,3},{3,2},{4,5},{5,4},{6,7},{7,6},{8,9},{9,8},{10,11... | collective-permute-start | bytes 5971976 | tf_op jit(solution)/shard_map/ppermute | solution.py:385
  225.3 44.7 %collective-permute-start.11 = (bf16[864,1152]{1,0:T(8,128)(2,1)}, bf16[864,1152]{1,0:T(8,128)(2,1)}, u32[]{:S(2)}, u32[]{:S(2)}) collective-permute-start(bf16[864,1152]{1,0:T(8,128)(2,1)} %get-tuple-element.972), channel_id=1, source_target_pairs={{0,2},{1,3},{2,0},{3,1},{4,6},{5,7},{6,4},{7,5},{8,10},{9,11},{10,... | collective-permute-start | bytes 5971976 | tf_op jit(solution)/shard_map/ppermute | solution.py:385
  226.8 43.2 %all-to-all-start.4 = ((bf16[4,144,1152]{2,1,0:T(8,128)(2,1)}), bf16[4,144,1152]{2,1,0:T(8,128)(2,1)}, u32[]{:S(2)}, u32[]{:S(2)}) async-start(bf16[4,144,1152]{2,1,0:T(8,128)(2,1)} %tile.62), calls=%async_computation.4 | async-start | bytes 2654208 | tf_op jit(solution)/shard_map/all_to_all | solution.py:402
  235.4 51.6 %collective-permute-start.13 = (bf16[4,576,1152]{2,1,0:T(8,128)(2,1)}, bf16[4,576,1152]{2,1,0:T(8,128)(2,1)}, u32[]{:S(2)}, u32[]{:S(2)}) collective-permute-start(bf16[4,576,1152]{2,1,0:T(8,128)(2,1)} %pack_blocks.7.refs_4_.refs_5_), channel_id=1, source_target_pairs={{0,4},{4,0},{8,12},{12,8},{16,20},{20,16},{24,28},{28,24},{1,5},{5... | collective-permute-start | bytes 15925256 | tf_op jit(solution)/shard_map/ppermute | solution.py:385
  280.0 37.4 %all-to-all-start.5 = ((bf16[4,144,1152]{2,1,0:T(8,128)(2,1)}), bf16[4,144,1152]{2,1,0:T(8,128)(2,1)S(1)}, u32[]{:S(2)}, u32[]{:S(2)}) async-start(bf16[4,144,1152]{2,1,0:T(8,128)(2,1)} %tile.68), calls=%async_computation.5 | async-start | bytes 2654208 | tf_op jit(solution)/shard_map/all_to_all | solution.py:402
  284.6 46.0 %collective-permute-start.15 = (bf16[864,1152]{1,0:T(8,128)(2,1)}, bf16[864,1152]{1,0:T(8,128)(2,1)}, u32[]{:S(2)}, u32[]{:S(2)}) collective-permute-start(bf16[864,1152]{1,0:T(8,128)(2,1)} %get-tuple-element.971), channel_id=1, source_target_pairs={{0,1},{1,0},{2,3},{3,2},{4,5},{5,4},{6,7},{7,6},{8,9},{9,8},{10,11... | collective-permute-start | bytes 5971976 | tf_op jit(solution)/shard_map/ppermute | solution.py:385
  285.2 45.6 %collective-permute-start.16 = (bf16[864,1152]{1,0:T(8,128)(2,1)}, bf16[864,1152]{1,0:T(8,128)(2,1)}, u32[]{:S(2)}, u32[]{:S(2)}) collective-permute-start(bf16[864,1152]{1,0:T(8,128)(2,1)} %get-tuple-element.970), channel_id=1, source_target_pairs={{0,2},{1,3},{2,0},{3,1},{4,6},{5,7},{6,4},{7,5},{8,10},{9,11},{10,... | collective-permute-start | bytes 5971976 | tf_op jit(solution)/shard_map/ppermute | solution.py:385
  286.8 30.6 %collective-permute-start.17 = (bf16[4,512,384]{2,1,0:T(8,128)(2,1)}, bf16[4,512,384]{2,1,0:T(8,128)(2,1)}, u32[]{:S(2)}, u32[]{:S(2)}) collective-permute-start(bf16[4,512,384]{2,1,0:T(8,128)(2,1)} %get-tuple-element.507.refs_6_), channel_id=1, source_target_pairs={{0,4},{4,0},{8,12},{12,8},{16,20},{20,16},{24,28},{28,24},{1,5},{5... | collective-permute-start | bytes 4718600 | tf_op jit(solution)/shard_map/ppermute | solution.py:385
  287.0 30.3 %collective-permute-start.12 = (bf16[576,512]{1,0:T(8,128)(2,1)}, bf16[576,512]{1,0:T(8,128)(2,1)}, u32[]{:S(2)}, u32[]{:S(2)}) collective-permute-start(bf16[576,512]{1,0:T(8,128)(2,1)} %get-tuple-element.479), channel_id=1, source_target_pairs={{0,4},{4,0},{8,12},{12,8},{16,20},{20,16},{24,28},{28,24},{1,5},{5... | collective-permute-start | bytes 1769480 | tf_op jit(solution)/shard_map/ppermute | solution.py:385
  335.4 54.7 %collective-permute-start.21 = (bf16[4,512,1152]{2,1,0:T(8,128)(2,1)}, bf16[4,512,1152]{2,1,0:T(8,128)(2,1)}, u32[]{:S(2)}, u32[]{:S(2)}) collective-permute-start(bf16[4,512,1152]{2,1,0:T(8,128)(2,1)} %get-tuple-element.514.refs_2_), channel_id=1, source_target_pairs={{0,4},{4,0},{8,12},{12,8},{16,20},{20,16},{24,28},{28,24},{1,5},{5... | collective-permute-start | bytes 14155784 | tf_op jit(solution)/shard_map/ppermute | solution.py:385
  337.7 37.2 %all-to-all-start.6 = ((bf16[2,8,2,2,16,576]{5,4,2,3,0,1:T(8,128)(2,1)}), bf16[2,8,2,2,16,576]{5,4,2,3,0,1:T(8,128)(2,1)S(1)}, u32[]{:S(2)}, u32[]{:S(2)}) async-start(bf16[2,8,2,2,16,576]{5,4,2,3,0,1:T(8,128)(2,1)} %bitcast.254), calls=%async_computation.6 | async-start | bytes 2621440 | tf_op jit(solution)/shard_map/all_to_all | solution.py:1408
  342.8 46.1 %collective-permute-start.19 = (bf16[864,1152]{1,0:T(8,128)(2,1)}, bf16[864,1152]{1,0:T(8,128)(2,1)}, u32[]{:S(2)}, u32[]{:S(2)}) collective-permute-start(bf16[864,1152]{1,0:T(8,128)(2,1)} %get-tuple-element.969), channel_id=1, source_target_pairs={{0,1},{1,0},{2,3},{3,2},{4,5},{5,4},{6,7},{7,6},{8,9},{9,8},{10,11... | collective-permute-start | bytes 5971976 | tf_op jit(solution)/shard_map/ppermute | solution.py:385
  344.3 45.8 %collective-permute-start.20 = (bf16[864,1152]{1,0:T(8,128)(2,1)}, bf16[864,1152]{1,0:T(8,128)(2,1)}, u32[]{:S(2)}, u32[]{:S(2)}) collective-permute-start(bf16[864,1152]{1,0:T(8,128)(2,1)} %get-tuple-element.968), channel_id=1, source_target_pairs={{0,2},{1,3},{2,0},{3,1},{4,6},{5,7},{6,4},{7,5},{8,10},{9,11},{10,... | collective-permute-start | bytes 5971976 | tf_op jit(solution)/shard_map/ppermute | solution.py:385
  349.8 65.6 %collective-permute-start.24 = (bf16[4,576,1152]{2,1,0:T(8,128)(2,1)}, bf16[4,576,1152]{2,1,0:T(8,128)(2,1)}, u32[]{:S(2)}, u32[]{:S(2)}) collective-permute-start(bf16[4,576,1152]{2,1,0:T(8,128)(2,1)} %pack_blocks.10.refs_4_.refs_6_), channel_id=1, source_target_pairs={{0,4},{4,0},{8,12},{12,8},{16,20},{20,16},{24,28},{28,24},{1,5},{5... | collective-permute-start | bytes 15925256 | tf_op jit(solution)/shard_map/ppermute | solution.py:385
  397.3 47.7 %collective-permute-start.30 = (bf16[4,576,1152]{2,1,0:T(8,128)(2,1)S(1)}, bf16[4,576,1152]{2,1,0:T(8,128)(2,1)}, u32[]{:S(2)}, u32[]{:S(2)}) collective-permute-start(bf16[4,576,1152]{2,1,0:T(8,128)(2,1)S(1)} %pack_blocks.11.refs_4_.refs_5_), channel_id=1, source_target_pairs={{0,4},{4,0},{8,12},{12,8},{16,20},{20,16},{24,28},{28,24},{1,5},{5... | collective-permute-start | bytes 15925256 | tf_op jit(solution)/shard_map/ppermute | solution.py:385
  412.9 33.5 %collective-permute-start.31 = (bf16[4,576,1152]{2,1,0:T(8,128)(2,1)}, bf16[4,576,1152]{2,1,0:T(8,128)(2,1)}, u32[]{:S(2)}, u32[]{:S(2)}) collective-permute-start(bf16[4,576,1152]{2,1,0:T(8,128)(2,1)} %pack_blocks.9.refs_6_.refs_7_), channel_id=1, source_target_pairs={{0,4},{4,0},{8,12},{12,8},{16,20},{20,16},{24,28},{28,24},{1,5},{5... | collective-permute-start | bytes 15925256 | tf_op jit(solution)/shard_map/ppermute | solution.py:385
  442.9 33.3 %collective-permute-start.29 = (bf16[4,512,384]{2,1,0:T(8,128)(2,1)}, bf16[4,512,384]{2,1,0:T(8,128)(2,1)}, u32[]{:S(2)}, u32[]{:S(2)}) collective-permute-start(bf16[4,512,384]{2,1,0:T(8,128)(2,1)} %get-tuple-element.545.refs_6_), channel_id=1, source_target_pairs={{0,4},{4,0},{8,12},{12,8},{16,20},{20,16},{24,28},{28,24},{1,5},{5... | collective-permute-start | bytes 4718600 | tf_op jit(solution)/shard_map/ppermute | solution.py:385
  443.4 32.8 %collective-permute-start.28 = (bf16[576,512]{1,0:T(8,128)(2,1)}, bf16[576,512]{1,0:T(8,128)(2,1)}, u32[]{:S(2)}, u32[]{:S(2)}) collective-permute-start(bf16[576,512]{1,0:T(8,128)(2,1)} %get-tuple-element.544), channel_id=1, source_target_pairs={{0,4},{4,0},{8,12},{12,8},{16,20},{20,16},{24,28},{28,24},{1,5},{5... | collective-permute-start | bytes 1769480 | tf_op jit(solution)/shard_map/ppermute | solution.py:385
  443.5 32.6 %collective-permute-start.25 = (bf16[512,288]{1,0:T(8,128)(2,1)}, bf16[512,288]{1,0:T(8,128)(2,1)S(1)}, u32[]{:S(2)}, u32[]{:S(2)}) collective-permute-start(bf16[512,288]{1,0:T(8,128)(2,1)} %get-tuple-element.541), channel_id=1, source_target_pairs={{0,1},{1,0},{2,3},{3,2},{4,5},{5,4},{6,7},{7,6},{8,9},{9,8},{10,11... | collective-permute-start | bytes 884744 | tf_op jit(solution)/shard_map/ppermute | solution.py:385
  444.9 31.2 %collective-permute-start.26 = (bf16[512,288]{1,0:T(8,128)(2,1)}, bf16[512,288]{1,0:T(8,128)(2,1)S(1)}, u32[]{:S(2)}, u32[]{:S(2)}) collective-permute-start(bf16[512,288]{1,0:T(8,128)(2,1)} %get-tuple-element.542), channel_id=1, source_target_pairs={{0,2},{1,3},{2,0},{3,1},{4,6},{5,7},{6,4},{7,5},{8,10},{9,11},{10,... | collective-permute-start | bytes 884744 | tf_op jit(solution)/shard_map/ppermute | solution.py:385
  476.2 34.7 %collective-permute-start.33 = (bf16[4,512,1152]{2,1,0:T(8,128)(2,1)}, bf16[4,512,1152]{2,1,0:T(8,128)(2,1)}, u32[]{:S(2)}, u32[]{:S(2)}) collective-permute-start(bf16[4,512,1152]{2,1,0:T(8,128)(2,1)} %get-tuple-element.572.refs_2_), channel_id=1, source_target_pairs={{0,4},{4,0},{8,12},{12,8},{16,20},{20,16},{24,28},{28,24},{1,5},{5... | collective-permute-start | bytes 14155784 | tf_op jit(solution)/shard_map/ppermute | solution.py:385
  476.3 34.6 %collective-permute-start.32 = (bf16[576,512]{1,0:T(8,128)(2,1)}, bf16[576,512]{1,0:T(8,128)(2,1)S(1)}, u32[]{:S(2)}, u32[]{:S(2)}) collective-permute-start(bf16[576,512]{1,0:T(8,128)(2,1)} %get-tuple-element.571), channel_id=1, source_target_pairs={{0,4},{4,0},{8,12},{12,8},{16,20},{20,16},{24,28},{28,24},{1,5},{5... | collective-permute-start | bytes 1769480 | tf_op jit(solution)/shard_map/ppermute | solution.py:385
  526.9 47.5 %collective-permute-start.36 = (bf16[576,1152]{1,0:T(8,128)(2,1)}, bf16[576,1152]{1,0:T(8,128)(2,1)S(1)}, u32[]{:S(2)}, u32[]{:S(2)}) collective-permute-start(bf16[576,1152]{1,0:T(8,128)(2,1)} %get-tuple-element.606), channel_id=1, source_target_pairs={{0,1},{1,0},{2,3},{3,2},{4,5},{5,4},{6,7},{7,6},{8,9},{9,8},{10,11... | collective-permute-start | bytes 3981320 | tf_op jit(solution)/shard_map/ppermute | solution.py:385
  528.4 46.1 %collective-permute-start.37 = (bf16[576,1152]{1,0:T(8,128)(2,1)}, bf16[576,1152]{1,0:T(8,128)(2,1)S(1)}, u32[]{:S(2)}, u32[]{:S(2)}) collective-permute-start(bf16[576,1152]{1,0:T(8,128)(2,1)} %get-tuple-element.607), channel_id=1, source_target_pairs={{0,2},{1,3},{2,0},{3,1},{4,6},{5,7},{6,4},{7,5},{8,10},{9,11},{10,... | collective-permute-start | bytes 3981320 | tf_op jit(solution)/shard_map/ppermute | solution.py:385
  574.6 31.8 %collective-permute-start.40 = (bf16[576,1152]{1,0:T(8,128)(2,1)}, bf16[576,1152]{1,0:T(8,128)(2,1)S(1)}, u32[]{:S(2)}, u32[]{:S(2)}) collective-permute-start(bf16[576,1152]{1,0:T(8,128)(2,1)} %get-tuple-element.631), channel_id=1, source_target_pairs={{0,1},{1,0},{2,3},{3,2},{4,5},{5,4},{6,7},{7,6},{8,9},{9,8},{10,11... | collective-permute-start | bytes 3981320 | tf_op jit(solution)/shard_map/ppermute | solution.py:385
  575.2 31.4 %collective-permute-start.41 = (bf16[576,1152]{1,0:T(8,128)(2,1)}, bf16[576,1152]{1,0:T(8,128)(2,1)S(1)}, u32[]{:S(2)}, u32[]{:S(2)}) collective-permute-start(bf16[576,1152]{1,0:T(8,128)(2,1)} %get-tuple-element.632), channel_id=1, source_target_pairs={{0,2},{1,3},{2,0},{3,1},{4,6},{5,7},{6,4},{7,5},{8,10},{9,11},{10,... | collective-permute-start | bytes 3981320 | tf_op jit(solution)/shard_map/ppermute | solution.py:385
  607.9 37.0 %all-to-all-start.7 = ((bf16[2,1,2,16,16,576]{5,4,2,0,1,3:T(8,128)(2,1)}), bf16[2,1,2,16,16,576]{5,4,2,0,1,3:T(8,128)(2,1)}, u32[]{:S(2)}, u32[]{:S(2)}) async-start(bf16[2,1,2,16,16,576]{5,4,2,0,1,3:T(8,128)(2,1)} %copy.156), calls=%async_computation.7 | async-start | bytes 2621440 | tf_op jit(solution)/shard_map/all_to_all | solution.py:1458
  647.4 43.8 %all-to-all-start.8 = ((bf16[4,144,1152]{2,1,0:T(8,128)(2,1)}), bf16[4,144,1152]{2,1,0:T(8,128)(2,1)}, u32[]{:S(2)}, u32[]{:S(2)}) async-start(bf16[4,144,1152]{2,1,0:T(8,128)(2,1)} %bitcast.80), calls=%async_computation.8 | async-start | bytes 2654208 | tf_op jit(solution)/shard_map/all_to_all | solution.py:402
  651.7 38.6 %collective-permute-start.44 = (bf16[288,1152]{1,0:T(8,128)(2,1)}, bf16[288,1152]{1,0:T(8,128)(2,1)S(1)}, u32[]{:S(2)}, u32[]{:S(2)}) collective-permute-start(bf16[288,1152]{1,0:T(8,128)(2,1)} %add_convert_fusion.9), channel_id=1, source_target_pairs={{0,1},{1,0},{2,3},{3,2},{4,5},{5,4},{6,7},{7,6},{8,9},{9,8},{10,11... | collective-permute-start | bytes 1990664 | tf_op jit(solution)/shard_map/ppermute | solution.py:385
  653.2 37.1 %collective-permute-start.45 = (bf16[288,1152]{1,0:T(8,128)(2,1)}, bf16[288,1152]{1,0:T(8,128)(2,1)S(1)}, u32[]{:S(2)}, u32[]{:S(2)}) collective-permute-start(bf16[288,1152]{1,0:T(8,128)(2,1)} %add_convert_fusion.8), channel_id=1, source_target_pairs={{0,2},{1,3},{2,0},{3,1},{4,6},{5,7},{6,4},{7,5},{8,10},{9,11},{10,... | collective-permute-start | bytes 1990664 | tf_op jit(solution)/shard_map/ppermute | solution.py:385
  653.7 34.3 %collective-permute-start.46 = (bf16[512,288]{1,0:T(8,128)(2,1)}, bf16[512,288]{1,0:T(8,128)(2,1)S(1)}, u32[]{:S(2)}, u32[]{:S(2)}) collective-permute-start(bf16[512,288]{1,0:T(8,128)(2,1)} %copy-done.57), channel_id=1, source_target_pairs={{0,1},{1,0},{2,3},{3,2},{4,5},{5,4},{6,7},{7,6},{8,9},{9,8},{10,11... | collective-permute-start | bytes 884744 | tf_op jit(solution)/shard_map/ppermute | solution.py:385
  654.3 34.5 %collective-permute-start.47 = (bf16[512,288]{1,0:T(8,128)(2,1)}, bf16[512,288]{1,0:T(8,128)(2,1)S(1)}, u32[]{:S(2)}, u32[]{:S(2)}) collective-permute-start(bf16[512,288]{1,0:T(8,128)(2,1)} %copy-done.56), channel_id=1, source_target_pairs={{0,2},{1,3},{2,0},{3,1},{4,6},{5,7},{6,4},{7,5},{8,10},{9,11},{10,... | collective-permute-start | bytes 884744 | tf_op jit(solution)/shard_map/ppermute | solution.py:385
  655.9 33.7 %collective-permute-start.48 = (bf16[512,288]{1,0:T(8,128)(2,1)}, bf16[512,288]{1,0:T(8,128)(2,1)S(1)}, u32[]{:S(2)}, u32[]{:S(2)}) collective-permute-start(bf16[512,288]{1,0:T(8,128)(2,1)} %copy-done.55), channel_id=1, source_target_pairs={{0,3},{1,2},{2,1},{3,0},{4,7},{5,6},{6,5},{7,4},{8,11},{9,10},{10,... | collective-permute-start | bytes 884744 | tf_op jit(solution)/shard_map/ppermute | solution.py:385
  695.9 31.8 %collective-permute-start.51 = (bf16[576,1152]{1,0:T(8,128)(2,1)}, bf16[576,1152]{1,0:T(8,128)(2,1)S(1)}, u32[]{:S(2)}, u32[]{:S(2)}) collective-permute-start(bf16[576,1152]{1,0:T(8,128)(2,1)} %get-tuple-element.645), channel_id=1, source_target_pairs={{0,1},{1,0},{2,3},{3,2},{4,5},{5,4},{6,7},{7,6},{8,9},{9,8},{10,11... | collective-permute-start | bytes 3981320 | tf_op jit(solution)/shard_map/ppermute | solution.py:385
  696.5 31.5 %collective-permute-start.52 = (bf16[576,1152]{1,0:T(8,128)(2,1)}, bf16[576,1152]{1,0:T(8,128)(2,1)S(1)}, u32[]{:S(2)}, u32[]{:S(2)}) collective-permute-start(bf16[576,1152]{1,0:T(8,128)(2,1)} %get-tuple-element.646), channel_id=1, source_target_pairs={{0,2},{1,3},{2,0},{3,1},{4,6},{5,7},{6,4},{7,5},{8,10},{9,11},{10,... | collective-permute-start | bytes 3981320 | tf_op jit(solution)/shard_map/ppermute | solution.py:385
  698.1 69.9 %all-to-all-start.9 = ((bf16[4,144,1152]{2,1,0:T(8,128)(2,1)}), bf16[4,144,1152]{2,1,0:T(8,128)(2,1)}, u32[]{:S(2)}, u32[]{:S(2)}) async-start(bf16[4,144,1152]{2,1,0:T(8,128)(2,1)} %bitcast.82), calls=%async_computation.9 | async-start | bytes 2654208 | tf_op jit(solution)/shard_map/all_to_all | solution.py:402
  728.0 47.0 %collective-permute-start.53 = (bf16[576,1152]{1,0:T(8,128)(2,1)}, bf16[576,1152]{1,0:T(8,128)(2,1)}, u32[]{:S(2)}, u32[]{:S(2)}) collective-permute-start(bf16[576,1152]{1,0:T(8,128)(2,1)} %get-tuple-element.709), channel_id=1, source_target_pairs={{0,1},{1,0},{2,3},{3,2},{4,5},{5,4},{6,7},{7,6},{8,9},{9,8},{10,11... | collective-permute-start | bytes 3981320 | tf_op jit(solution)/shard_map/ppermute | solution.py:385
  729.4 45.5 %collective-permute-start.54 = (bf16[576,1152]{1,0:T(8,128)(2,1)}, bf16[576,1152]{1,0:T(8,128)(2,1)}, u32[]{:S(2)}, u32[]{:S(2)}) collective-permute-start(bf16[576,1152]{1,0:T(8,128)(2,1)} %get-tuple-element.710), channel_id=1, source_target_pairs={{0,2},{1,3},{2,0},{3,1},{4,6},{5,7},{6,4},{7,5},{8,10},{9,11},{10,... | collective-permute-start | bytes 3981320 | tf_op jit(solution)/shard_map/ppermute | solution.py:385
  733.0 40.1 %collective-permute-start.55 = (bf16[288,1152]{1,0:T(8,128)(2,1)}, bf16[288,1152]{1,0:T(8,128)(2,1)S(1)}, u32[]{:S(2)}, u32[]{:S(2)}) collective-permute-start(bf16[288,1152]{1,0:T(8,128)(2,1)} %add_convert_fusion.7), channel_id=1, source_target_pairs={{0,1},{1,0},{2,3},{3,2},{4,5},{5,4},{6,7},{7,6},{8,9},{9,8},{10,11... | collective-permute-start | bytes 1990664 | tf_op jit(solution)/shard_map/ppermute | solution.py:385
  733.6 40.6 %collective-permute-start.56 = (bf16[288,1152]{1,0:T(8,128)(2,1)}, bf16[288,1152]{1,0:T(8,128)(2,1)S(1)}, u32[]{:S(2)}, u32[]{:S(2)}) collective-permute-start(bf16[288,1152]{1,0:T(8,128)(2,1)} %add_convert_fusion.6), channel_id=1, source_target_pairs={{0,2},{1,3},{2,0},{3,1},{4,6},{5,7},{6,4},{7,5},{8,10},{9,11},{10,... | collective-permute-start | bytes 1990664 | tf_op jit(solution)/shard_map/ppermute | solution.py:385
  775.1 32.2 %collective-permute-start.61 = (bf16[576,1152]{1,0:T(8,128)(2,1)}, bf16[576,1152]{1,0:T(8,128)(2,1)S(1)}, u32[]{:S(2)}, u32[]{:S(2)}) collective-permute-start(bf16[576,1152]{1,0:T(8,128)(2,1)} %get-tuple-element.742), channel_id=1, source_target_pairs={{0,1},{1,0},{2,3},{3,2},{4,5},{5,4},{6,7},{7,6},{8,9},{9,8},{10,11... | collective-permute-start | bytes 3981320 | tf_op jit(solution)/shard_map/ppermute | solution.py:385
  775.8 32.2 %collective-permute-start.62 = (bf16[576,1152]{1,0:T(8,128)(2,1)}, bf16[576,1152]{1,0:T(8,128)(2,1)S(1)}, u32[]{:S(2)}, u32[]{:S(2)}) collective-permute-start(bf16[576,1152]{1,0:T(8,128)(2,1)} %get-tuple-element.743), channel_id=1, source_target_pairs={{0,2},{1,3},{2,0},{3,1},{4,6},{5,7},{6,4},{7,5},{8,10},{9,11},{10,... | collective-permute-start | bytes 3981320 | tf_op jit(solution)/shard_map/ppermute | solution.py:385
  783.1 47.0 %all-to-all-start.10 = ((bf16[4,144,1152]{2,1,0:T(8,128)(2,1)}), bf16[4,144,1152]{2,1,0:T(8,128)(2,1)}, u32[]{:S(2)}, u32[]{:S(2)}) async-start(bf16[4,144,1152]{2,1,0:T(8,128)(2,1)} %bitcast.84), calls=%async_computation.10 | async-start | bytes 2654208 | tf_op jit(solution)/shard_map/all_to_all | solution.py:402
  788.3 32.8 %collective-permute-start.59 = (bf16[288,1152]{1,0:T(8,128)(2,1)}, bf16[288,1152]{1,0:T(8,128)(2,1)S(1)}, u32[]{:S(2)}, u32[]{:S(2)}) collective-permute-start(bf16[288,1152]{1,0:T(8,128)(2,1)} %get-tuple-element.738), channel_id=1, source_target_pairs={{0,1},{1,0},{2,3},{3,2},{4,5},{5,4},{6,7},{7,6},{8,9},{9,8},{10,11... | collective-permute-start | bytes 1990664 | tf_op jit(solution)/shard_map/ppermute | solution.py:385
  789.7 31.8 %collective-permute-start.60 = (bf16[288,1152]{1,0:T(8,128)(2,1)}, bf16[288,1152]{1,0:T(8,128)(2,1)}, u32[]{:S(2)}, u32[]{:S(2)}) collective-permute-start(bf16[288,1152]{1,0:T(8,128)(2,1)} %get-tuple-element.739), channel_id=1, source_target_pairs={{0,2},{1,3},{2,0},{3,1},{4,6},{5,7},{6,4},{7,5},{8,10},{9,11},{10,... | collective-permute-start | bytes 1990664 | tf_op jit(solution)/shard_map/ppermute | solution.py:385
  821.6 42.1 %collective-permute-start.63 = (bf16[576,1152]{1,0:T(8,128)(2,1)}, bf16[576,1152]{1,0:T(8,128)(2,1)}, u32[]{:S(2)}, u32[]{:S(2)}) collective-permute-start(bf16[576,1152]{1,0:T(8,128)(2,1)} %get-tuple-element.752), channel_id=1, source_target_pairs={{0,1},{1,0},{2,3},{3,2},{4,5},{5,4},{6,7},{7,6},{8,9},{9,8},{10,11... | collective-permute-start | bytes 3981320 | tf_op jit(solution)/shard_map/ppermute | solution.py:385
  822.9 40.8 %collective-permute-start.64 = (bf16[576,1152]{1,0:T(8,128)(2,1)}, bf16[576,1152]{1,0:T(8,128)(2,1)}, u32[]{:S(2)}, u32[]{:S(2)}) collective-permute-start(bf16[576,1152]{1,0:T(8,128)(2,1)} %get-tuple-element.753), channel_id=1, source_target_pairs={{0,2},{1,3},{2,0},{3,1},{4,6},{5,7},{6,4},{7,5},{8,10},{9,11},{10,... | collective-permute-start | bytes 3981320 | tf_op jit(solution)/shard_map/ppermute | solution.py:385
  830.1 42.8 %all-to-all-start.11 = ((bf16[4,144,1152]{2,1,0:T(8,128)(2,1)}), bf16[4,144,1152]{2,1,0:T(8,128)(2,1)}, u32[]{:S(2)}, u32[]{:S(2)}) async-start(bf16[4,144,1152]{2,1,0:T(8,128)(2,1)} %bitcast.102), calls=%async_computation.11 | async-start | bytes 2654208 | tf_op jit(solution)/shard_map/all_to_all | solution.py:402
  835.2 31.2 %collective-permute-start.65 = (bf16[288,1152]{1,0:T(8,128)(2,1)}, bf16[288,1152]{1,0:T(8,128)(2,1)S(1)}, u32[]{:S(2)}, u32[]{:S(2)}) collective-permute-start(bf16[288,1152]{1,0:T(8,128)(2,1)} %add_convert_fusion.3), channel_id=1, source_target_pairs={{0,1},{1,0},{2,3},{3,2},{4,5},{5,4},{6,7},{7,6},{8,9},{9,8},{10,11... | collective-permute-start | bytes 1990664 | tf_op jit(solution)/shard_map/ppermute | solution.py:385
  835.9 31.7 %collective-permute-start.66 = (bf16[288,1152]{1,0:T(8,128)(2,1)}, bf16[288,1152]{1,0:T(8,128)(2,1)}, u32[]{:S(2)}, u32[]{:S(2)}) collective-permute-start(bf16[288,1152]{1,0:T(8,128)(2,1)} %add_convert_fusion.2), channel_id=1, source_target_pairs={{0,2},{1,3},{2,0},{3,1},{4,6},{5,7},{6,4},{7,5},{8,10},{9,11},{10,... | collective-permute-start | bytes 1990664 | tf_op jit(solution)/shard_map/ppermute | solution.py:385
  872.9 45.0 %all-to-all-start.12 = ((bf16[4,144,1152]{2,1,0:T(8,128)(2,1)}), bf16[4,144,1152]{2,1,0:T(8,128)(2,1)S(1)}, u32[]{:S(2)}, u32[]{:S(2)}) async-start(bf16[4,144,1152]{2,1,0:T(8,128)(2,1)} %bitcast.104), calls=%async_computation.12 | async-start | bytes 2654208 | tf_op jit(solution)/shard_map/all_to_all | solution.py:402
  922.3 45.1 %all-to-all-start.13 = ((bf16[4,144,1152]{2,1,0:T(8,128)(2,1)}), bf16[4,144,1152]{2,1,0:T(8,128)(2,1)}, u32[]{:S(2)}, u32[]{:S(2)}) async-start(bf16[4,144,1152]{2,1,0:T(8,128)(2,1)} %bitcast.121), calls=%async_computation.13 | async-start | bytes 2654208 | tf_op jit(solution)/shard_map/all_to_all | solution.py:402
  934.9 31.2 %collective-permute-start.79 = (f32[4,144]{1,0:T(4,128)}, f32[4,144]{1,0:T(4,128)}, u32[]{:S(2)}, u32[]{:S(2)}) collective-permute-start(f32[4,144]{1,0:T(4,128)} %add.146), channel_id=1, source_target_pairs={{0,2},{1,3},{2,0},{3,1},{4,6},{5,7},{6,4},{7,5},{8,10},{9,11},{10,... | collective-permute-start | bytes 6920 | tf_op jit(solution)/shard_map/ppermute | solution.py:385
  (136 other events, 1001.4 us)
Sparse Core Ops, SparseCore 0:
  65.1 76.0 all-gather.3
